TPU v7x, 512 devices: a whole 4x4x16 slice. The times are simulated.
512 devices in a mesh: band: 32 (over z, x_lo), dom: 16 (over x_hi, y, core).
Axes of the slice: x: 4 (x_hi: 2, x_lo: 2; x = x_hi * 2 + x_lo), y: 4, z: 16, core: 2. Of those that a mesh axis runs over, the one named last changes fastest.
Arguments:
- targets: bfloat16 [1024, 262144], P('band', 'dom'), as said below
- sources: bfloat16 [2, 128, 262144], P(None, 'band', 'dom'), as said below
- pair_tgt: int32 [2, 64], P(None, 'band'), may hold values from 0 to 31
- pair_src: int32 [2, 64], replicated, may hold values from 0 to 127, as said below
Outputs:
- target_exchange: bfloat16 [1024, 262144], P('band', 'dom')
- source_exchange: bfloat16 [2, 128, 262144], P(None, 'band', 'dom')
Inputs may be any that keep to these rules, and one draw needn't show every extreme that they name: `pair_src`: for each block, the 2 entries of one band group (entries g * 2 to g * 2 + 1) are distinct. `targets`: orbital values of order one. `sources`: orbital values of order one.
All inputs are finite; a program needn't handle non-finite values.
Results may differ from a plain program's by a relative error of at most 0.0039.
Values may be sent and summed in bfloat16 or wider, within the bound.
No kernel may reach another device: no remote copies, remote signals or barrier semaphores. Data moves between devices by JAX's collectives and lax.ppermute only.
A program may use at most 128 MiB of HBM per device.

v0:
```python
import jax
import jax.numpy as jnp
from jax import lax
from jax.sharding import PartitionSpec as P

NY = 64
NZ = 64
SWEEPS = 8


def with_halo(cells, sides, width):
    for axis, dim in sides:
        count = lax.axis_size(axis)
        ends = count - 1
        head = lax.slice_in_dim(cells, 0, width, axis=dim)
        tail = lax.slice_in_dim(cells, cells.shape[dim] - width, cells.shape[dim], axis=dim)
        cells = jnp.concatenate(
            [
                lax.ppermute(tail, axis, [(i, (i + 1) % count) for i in range(ends)]),
                cells,
                lax.ppermute(head, axis, [((i + 1) % count, i) for i in range(ends)]),
            ],
            axis=dim,
        )
    return cells


def operate(field):
    count, planes, flat = field.shape
    padded = with_halo(field, (("dom", 1),), 2)
    total = 90.0 * field
    near_x = padded[:, 3 : 3 + planes] + padded[:, 1 : 1 + planes]
    far_x = padded[:, 4 : 4 + planes] + padded[:, 0:planes]
    total = total - 16.0 * near_x + far_x
    margin = 2 * NZ + 2
    wide = jnp.pad(field, ((0, 0), (0, 0), (margin, margin)))
    z_pos = jnp.arange(flat, dtype=jnp.int32) % NZ

    def view(offset):
        return lax.slice_in_dim(wide, margin + offset, margin + offset + flat, axis=2)

    def z_mask(delta):
        inside = jnp.logical_and(z_pos + delta >= 0, z_pos + delta < NZ)
        return inside.astype(jnp.float32)[None, None, :]

    total = total - 16.0 * (view(NZ) + view(-NZ)) + (view(2 * NZ) + view(-2 * NZ))
    near_z = view(1) * z_mask(1) + view(-1) * z_mask(-1)
    far_z = view(2) * z_mask(2) + view(-2) * z_mask(-2)
    total = total - 16.0 * near_z + far_z
    return total / 12.0


def expand(vector):
    return vector[:, None, None]


def local_dot(left, right):
    return jnp.sum(left * right, axis=(1, 2))


def squares(residual):
    return lax.psum(local_dot(residual, residual), "dom")


def solve(density):
    solution = jnp.zeros_like(density)
    residual = density
    direction = density
    norm_now = squares(residual)
    for sweep in range(SWEEPS):
        applied = operate(direction)
        step_size = norm_now / lax.psum(local_dot(direction, applied), "dom")
        solution = solution + expand(step_size) * direction
        residual = residual - expand(step_size) * applied
        norm_next = squares(residual)
        direction = residual + expand(norm_next / norm_now) * direction
        norm_now = norm_next
    return solution


def per_device(targets, sources, pair_tgt, pair_src):
    orb_local, cell_count = targets.shape
    block_count, src_local = (sources.shape[0], sources.shape[1])
    pair_count = pair_tgt.shape[1]
    planes = cell_count // (NY * NZ)
    band_index = lax.axis_index("band")
    target_sum = jnp.zeros((orb_local, cell_count), jnp.float32)
    source_outs = []
    for block in range(block_count):
        block_rows = lax.all_gather(sources[block], "band", axis=0, tiled=True)
        source_ids = lax.dynamic_slice_in_dim(pair_src[block], band_index * pair_count, pair_count)
        target_ids = pair_tgt[block]
        source_vals = block_rows[source_ids].astype(jnp.float32)
        target_vals = targets[target_ids].astype(jnp.float32)
        density = (target_vals * source_vals).reshape(pair_count, planes, NY * NZ)
        potential = solve(density).reshape(pair_count, cell_count)
        selector = (target_ids[None, :] == jnp.arange(orb_local, dtype=jnp.int32)[:, None]).astype(
            jnp.float32
        )
        target_sum = target_sum + jnp.dot(
            selector,
            -potential * source_vals,
            precision=lax.Precision.HIGHEST,
            preferred_element_type=jnp.float32,
        )
        source_term = (-potential * target_vals).astype(jnp.bfloat16)
        every_row = lax.all_gather(source_term, "band", axis=0, tiled=True)
        first_owned = band_index * src_local
        owner_sel = (
            pair_src[block][None, :]
            == first_owned + jnp.arange(src_local, dtype=jnp.int32)[:, None]
        ).astype(jnp.bfloat16)
        owned = jnp.dot(owner_sel, every_row, preferred_element_type=jnp.float32)
        source_outs.append(owned.astype(jnp.bfloat16))
    return (target_sum.astype(jnp.bfloat16), jnp.stack(source_outs))


def solution(mesh):
    return jax.shard_map(
        per_device,
        mesh=mesh,
        in_specs=(P("band", "dom"), P(None, "band", "dom"), P(None, "band"), P()),
        out_specs=(P("band", "dom"), P(None, "band", "dom")),
        check_vma=False,
    )
```

profile of v0, /device:TPU:1, one launch (start us, length us, event | category | flops | bytes accessed | tf_op | source)
XLA Modules:
  0.0 1402.2 jit_solution(3203657927234137404)
XLA Ops:
  13.2 197.3 %all-gather.9.cloned.1.call-done = bf16[1,128,16384]{2,0,1:T(2,128)(2,1)} async-done(((bf16[1,4,16384]{2,0,1:T(2,128)(2,1)}), bf16[1,128,16384]{2,0,1:T(2,128)(2,1)}) %all-gather.9.cloned.1.call-update) | async-done | bytes 4194320 | tf_op jit(solution)/shard_map/all_gather | solution.py:90
  210.5 9.8 copy.19
  231.7 176.3 %all-gather.11.cloned.1.call-done = bf16[1,128,16384]{2,0,1:T(2,128)(2,1)} async-done(((bf16[1,4,16384]{2,0,1:T(2,128)(2,1)}), bf16[1,128,16384]{2,0,1:T(2,128)(2,1)}) %all-gather.11.cloned.1.call-update) | async-done | bytes 4194320 | tf_op jit(solution)/shard_map/all_gather | solution.py:90
  408.0 9.9 copy.18
  433.7 31.2 %all-reduce.30 = (f32[2]{0:T(128)S(1)}, f32[2]{0:T(128)S(1)}, f32[2]{0:T(128)S(1)}, f32[2]{0:T(128)S(1)}) all-reduce(f32[2]{0:T(128)S(1)} %get-tuple-element.144, f32[2]{0:T(128)S(1)} %get-tuple-element.108, f32[2]{0:T(128)S(1)} %get-tuple-element.143, f32[2]{0:T(128)S(1)} %get-tuple-element.106), channel_id=1, replica_groups=mesh['band'=32,'dom'=16] {'dom'}, use_global_device_ids=true, to_apply=%region_1.0 | all-reduce | flops 8 | bytes 64 | tf_op jit(solution)/shard_map/psum | solution.py:62
  465.3 35.7 %all-reduce.29 = (f32[2]{0:T(128)S(1)}, f32[2]{0:T(128)S(1)}) all-reduce(f32[2]{0:T(128)S(1)} %multiply_reduce_fusion.29, f32[2]{0:T(128)S(1)} %multiply_reduce_fusion.13), channel_id=1, replica_groups=mesh['band'=32,'dom'=16] {'dom'}, use_global_device_ids=true, to_apply=%region_5.6 | all-reduce | flops 4 | bytes 32 | tf_op jit(solution)/shard_map/psum | solution.py:62
  515.1 35.4 %all-reduce.28 = (f32[2]{0:T(128)S(1)}, f32[2]{0:T(128)S(1)}) all-reduce(f32[2]{0:T(128)S(1)} %get-tuple-element.100, f32[2]{0:T(128)S(1)} %get-tuple-element.98), channel_id=1, replica_groups=mesh['band'=32,'dom'=16] {'dom'}, use_global_device_ids=true, to_apply=%region_7.8 | all-reduce | flops 4 | bytes 32 | tf_op jit(solution)/shard_map/psum | solution.py:72
  552.0 33.6 %all-reduce.27 = (f32[2]{0:T(128)S(1)}, f32[2]{0:T(128)S(1)}) all-reduce(f32[2]{0:T(128)S(1)} %get-tuple-element.94, f32[2]{0:T(128)S(1)} %get-tuple-element.90), channel_id=1, replica_groups=mesh['band'=32,'dom'=16] {'dom'}, use_global_device_ids=true, to_apply=%region_9.10 | all-reduce | flops 4 | bytes 32 | tf_op jit(solution)/shard_map/psum | solution.py:62
  585.8 6.6 collective-permute-start.5
  600.7 5.6 collective-permute-done.20
  606.9 38.1 %all-reduce.26 = (f32[2]{0:T(128)S(1)}, f32[2]{0:T(128)S(1)}) all-reduce(f32[2]{0:T(128)S(1)} %get-tuple-element.88, f32[2]{0:T(128)S(1)} %get-tuple-element.86), channel_id=1, replica_groups=mesh['band'=32,'dom'=16] {'dom'}, use_global_device_ids=true, to_apply=%region_11.12 | all-reduce | flops 4 | bytes 32 | tf_op jit(solution)/shard_map/psum | solution.py:72
  646.4 33.5 %all-reduce.25 = (f32[2]{0:T(128)S(1)}, f32[2]{0:T(128)S(1)}) all-reduce(f32[2]{0:T(128)S(1)} %get-tuple-element.82, f32[2]{0:T(128)S(1)} %get-tuple-element.78), channel_id=1, replica_groups=mesh['band'=32,'dom'=16] {'dom'}, use_global_device_ids=true, to_apply=%region_13.14 | all-reduce | flops 4 | bytes 32 | tf_op jit(solution)/shard_map/psum | solution.py:62
  680.2 6.6 collective-permute-start.7
  701.2 38.1 %all-reduce.24 = (f32[2]{0:T(128)S(1)}, f32[2]{0:T(128)S(1)}) all-reduce(f32[2]{0:T(128)S(1)} %get-tuple-element.76, f32[2]{0:T(128)S(1)} %get-tuple-element.74), channel_id=1, replica_groups=mesh['band'=32,'dom'=16] {'dom'}, use_global_device_ids=true, to_apply=%region_15.16 | all-reduce | flops 4 | bytes 32 | tf_op jit(solution)/shard_map/psum | solution.py:72
  740.8 33.5 %all-reduce.23 = (f32[2]{0:T(128)S(1)}, f32[2]{0:T(128)S(1)}) all-reduce(f32[2]{0:T(128)S(1)} %get-tuple-element.70, f32[2]{0:T(128)S(1)} %get-tuple-element.66), channel_id=1, replica_groups=mesh['band'=32,'dom'=16] {'dom'}, use_global_device_ids=true, to_apply=%region_17.18 | all-reduce | flops 4 | bytes 32 | tf_op jit(solution)/shard_map/psum | solution.py:62
  774.5 6.6 collective-permute-start.9
  789.5 5.6 collective-permute-done.24
  795.6 38.1 %all-reduce.22 = (f32[2]{0:T(128)S(1)}, f32[2]{0:T(128)S(1)}) all-reduce(f32[2]{0:T(128)S(1)} %get-tuple-element.64, f32[2]{0:T(128)S(1)} %get-tuple-element.62), channel_id=1, replica_groups=mesh['band'=32,'dom'=16] {'dom'}, use_global_device_ids=true, to_apply=%region_19.20 | all-reduce | flops 4 | bytes 32 | tf_op jit(solution)/shard_map/psum | solution.py:72
  835.2 33.5 %all-reduce.21 = (f32[2]{0:T(128)S(1)}, f32[2]{0:T(128)S(1)}) all-reduce(f32[2]{0:T(128)S(1)} %get-tuple-element.58, f32[2]{0:T(128)S(1)} %get-tuple-element.54), channel_id=1, replica_groups=mesh['band'=32,'dom'=16] {'dom'}, use_global_device_ids=true, to_apply=%region_21.22 | all-reduce | flops 4 | bytes 32 | tf_op jit(solution)/shard_map/psum | solution.py:62
  868.9 6.6 collective-permute-start.11
  883.9 5.6 collective-permute-done.26
  890.0 38.1 %all-reduce.20 = (f32[2]{0:T(128)S(1)}, f32[2]{0:T(128)S(1)}) all-reduce(f32[2]{0:T(128)S(1)} %get-tuple-element.52, f32[2]{0:T(128)S(1)} %get-tuple-element.50), channel_id=1, replica_groups=mesh['band'=32,'dom'=16] {'dom'}, use_global_device_ids=true, to_apply=%region_23.24 | all-reduce | flops 4 | bytes 32 | tf_op jit(solution)/shard_map/psum | solution.py:72
  931.4 33.7 %all-reduce.19 = (f32[2]{0:T(128)S(1)}, f32[2]{0:T(128)S(1)}) all-reduce(f32[2]{0:T(128)} %get-tuple-element.46, f32[2]{0:T(128)S(1)} %get-tuple-element.42), channel_id=1, replica_groups=mesh['band'=32,'dom'=16] {'dom'}, use_global_device_ids=true, to_apply=%region_25.26 | all-reduce | flops 4 | bytes 32 | tf_op jit(solution)/shard_map/psum | solution.py:62
  965.9 6.6 collective-permute-start.13
  981.5 5.5 collective-permute-done.28
  988.1 38.7 %all-reduce.18 = (f32[2]{0:T(128)S(1)}, f32[2]{0:T(128)}) all-reduce(f32[2]{0:T(128)S(1)} %get-tuple-element.40, f32[2]{0:T(128)} %get-tuple-element.38), channel_id=1, replica_groups=mesh['band'=32,'dom'=16] {'dom'}, use_global_device_ids=true, to_apply=%region_27.28 | all-reduce | flops 4 | bytes 32 | tf_op jit(solution)/shard_map/psum | solution.py:72
  1030.7 34.2 %all-reduce.17 = (f32[2]{0:T(128)}, f32[2]{0:T(128)}) all-reduce(f32[2]{0:T(128)} %multiply_reduce_fusion.17, f32[2]{0:T(128)} %multiply_reduce_fusion.1), channel_id=1, replica_groups=mesh['band'=32,'dom'=16] {'dom'}, use_global_device_ids=true, to_apply=%region_29.30 | all-reduce | flops 4 | bytes 32 | tf_op jit(solution)/shard_map/psum | solution.py:62
  1066.7 6.6 collective-permute-start.15
  1082.3 5.6 collective-permute-done.30
  1089.0 38.2 %all-reduce.16 = (f32[2]{0:T(128)S(1)}, f32[2]{0:T(128)S(1)}) all-reduce(f32[2]{0:T(128)S(1)} %multiply_reduce_fusion.16, f32[2]{0:T(128)} %multiply_reduce_fusion), channel_id=1, replica_groups=mesh['band'=32,'dom'=16] {'dom'}, use_global_device_ids=true, to_apply=%region_31.32 | all-reduce | flops 4 | bytes 32 | tf_op jit(solution)/shard_map/psum | solution.py:72
  1135.2 122.1 %all-gather.15.cloned.1.call-done = bf16[32,2,16384]{2,1,0:T(2,128)(2,1)} async-done(((bf16[1,2,16384]{2,1,0:T(2,128)(2,1)}), bf16[32,2,16384]{2,1,0:T(2,128)(2,1)}) %all-gather.15.cloned.1.call-update) | async-done | bytes 2097168 | tf_op jit(solution)/shard_map/all_gather | solution.py:107
  1260.6 131.0 %all-gather.13.cloned.1.call-done = bf16[32,2,16384]{2,1,0:T(2,128)(2,1)} async-done(((bf16[1,2,16384]{2,1,0:T(2,128)(2,1)}), bf16[32,2,16384]{2,1,0:T(2,128)(2,1)}) %all-gather.13.cloned.1.call-update) | async-done | bytes 2097168 | tf_op jit(solution)/shard_map/all_gather | solution.py:107
  (219 shorter events, 139.7 us)
Async XLA Ops:
  7.2 203.3 %all-gather.9.cloned.1.call-start = ((), (), s32[]{:S(2)}) async-start(), calls=%async_computation | async-start | bytes 8650752 | tf_op jit(solution)/shard_map/all_gather | solution.py:90
  9.3 398.7 %all-gather.11.cloned.1.call-start = ((), (), s32[]{:S(2)}) async-start(), calls=%async_computation.1 | async-start | bytes 8650752 | tf_op jit(solution)/shard_map/all_gather | solution.py:90
  10.3 1247.1 %all-gather.15.cloned.1.call-start = ((), (), s32[]{:S(2)}) async-start(), calls=%async_computation.3 | async-start | bytes 2162688 | tf_op jit(solution)/shard_map/all_gather | solution.py:107
  224.2 205.2 %collective-permute-start.1 = (f32[2,2,4096]{2,1,0:T(2,128)S(1)}, f32[2,2,4096]{2,1,0:T(2,128)S(1)}, u32[]{:S(2)}, u32[]{:S(2)}) collective-permute-start(f32[2,2,4096]{2,1,0:T(2,128)S(1)} %get-tuple-element.147), channel_id=1, source_target_pairs={{0,1},{1,2},{2,3},{3,4},{4,5},{5,6},{6,7},{7,8},{8,9},{9,10},{10,1... | collective-permute-start | bytes 196616 | tf_op jit(solution)/shard_map/ppermute | solution.py:19
  229.6 199.9 %collective-permute-start = (f32[2,2,4096]{2,1,0:T(2,128)S(1)}, f32[2,2,4096]{2,1,0:T(2,128)S(1)}, u32[]{:S(2)}, u32[]{:S(2)}) collective-permute-start(f32[2,2,4096]{2,1,0:T(2,128)S(1)} %get-tuple-element.146), channel_id=1, source_target_pairs={{1,0},{2,1},{3,2},{4,3},{5,4},{6,5},{7,6},{8,7},{9,8},{10,9},{11,1... | collective-permute-start | bytes 196616 | tf_op jit(solution)/shard_map/ppermute | solution.py:21
  422.2 7.9 collective-permute-start.17
  501.2 9.6 collective-permute-start.3
  503.1 7.7 collective-permute-start.2
  585.8 14.3 %collective-permute-start.5 = (f32[2,2,4096]{2,1,0:T(2,128)S(1)}, f32[2,2,4096]{2,1,0:T(2,128)S(1)}, u32[]{:S(2)}, u32[]{:S(2)}) collective-permute-start(f32[2,2,4096]{2,1,0:T(2,128)S(1)} %get-tuple-element.135), channel_id=1, source_target_pairs={{0,1},{1,2},{2,3},{3,4},{4,5},{5,6},{6,7},{7,8},{8,9},{9,10},{10,1... | collective-permute-start | bytes 196616 | tf_op jit(solution)/shard_map/ppermute | solution.py:19
  592.4 7.7 collective-permute-start.4
  594.5 6.2 collective-permute-start.21
  598.2 8.1 collective-permute-start.20
  680.2 14.5 %collective-permute-start.7 = (f32[2,2,4096]{2,1,0:T(2,128)S(1)}, f32[2,2,4096]{2,1,0:T(2,128)S(1)}, u32[]{:S(2)}, u32[]{:S(2)}) collective-permute-start(f32[2,2,4096]{2,1,0:T(2,128)S(1)} %get-tuple-element.131), channel_id=1, source_target_pairs={{0,1},{1,2},{2,3},{3,4},{4,5},{5,6},{6,7},{7,8},{8,9},{9,10},{10,1... | collective-permute-start | bytes 196616 | tf_op jit(solution)/shard_map/ppermute | solution.py:19
  686.8 7.9 collective-permute-start.6
  688.9 6.4 collective-permute-start.23
  692.5 8.1 collective-permute-start.22
  774.5 14.3 %collective-permute-start.9 = (f32[2,2,4096]{2,1,0:T(2,128)S(1)}, f32[2,2,4096]{2,1,0:T(2,128)S(1)}, u32[]{:S(2)}, u32[]{:S(2)}) collective-permute-start(f32[2,2,4096]{2,1,0:T(2,128)S(1)} %get-tuple-element.127), channel_id=1, source_target_pairs={{0,1},{1,2},{2,3},{3,4},{4,5},{5,6},{6,7},{7,8},{8,9},{9,10},{10,1... | collective-permute-start | bytes 196616 | tf_op jit(solution)/shard_map/ppermute | solution.py:19
  781.2 7.7 collective-permute-start.8
  783.3 6.2 collective-permute-start.25
  786.9 8.1 collective-permute-start.24
  868.9 14.3 %collective-permute-start.11 = (f32[2,2,4096]{2,1,0:T(2,128)S(1)}, f32[2,2,4096]{2,1,0:T(2,128)S(1)}, u32[]{:S(2)}, u32[]{:S(2)}) collective-permute-start(f32[2,2,4096]{2,1,0:T(2,128)S(1)} %get-tuple-element.123), channel_id=1, source_target_pairs={{0,1},{1,2},{2,3},{3,4},{4,5},{5,6},{6,7},{7,8},{8,9},{9,10},{10,1... | collective-permute-start | bytes 196616 | tf_op jit(solution)/shard_map/ppermute | solution.py:19
  875.5 7.7 collective-permute-start.10
  881.3 8.1 collective-permute-start.26
  965.9 14.9 %collective-permute-start.13 = (f32[2,2,4096]{2,1,0:T(2,128)S(1)}, f32[2,2,4096]{2,1,0:T(2,128)S(1)}, u32[]{:S(2)}, u32[]{:S(2)}) collective-permute-start(f32[2,2,4096]{2,1,0:T(2,128)S(1)} %get-tuple-element.119), channel_id=1, source_target_pairs={{0,1},{1,2},{2,3},{3,4},{4,5},{5,6},{6,7},{7,8},{8,9},{9,10},{10,1... | collective-permute-start | bytes 196616 | tf_op jit(solution)/shard_map/ppermute | solution.py:19
  972.5 8.3 collective-permute-start.12
  975.2 6.2 collective-permute-start.29
  978.9 8.1 collective-permute-start.28
  1066.7 15.0 %collective-permute-start.15 = (f32[2,2,4096]{2,1,0:T(2,128)S(1)}, f32[2,2,4096]{2,1,0:T(2,128)S(1)}, u32[]{:S(2)}, u32[]{:S(2)}) collective-permute-start(f32[2,2,4096]{2,1,0:T(2,128)S(1)} %get-tuple-element.115), channel_id=1, source_target_pairs={{0,1},{1,2},{2,3},{3,4},{4,5},{5,6},{6,7},{7,8},{8,9},{9,10},{10,1... | collective-permute-start | bytes 196616 | tf_op jit(solution)/shard_map/ppermute | solution.py:19
  1073.3 8.4 collective-permute-start.14
  1076.1 6.2 collective-permute-start.31
  1079.8 8.1 collective-permute-start.30
  1130.2 261.3 %all-gather.13.cloned.1.call-start = ((), (), s32[]{:S(2)}) async-start(), calls=%async_computation.2 | async-start | bytes 2162688 | tf_op jit(solution)/shard_map/all_gather | solution.py:107
  (20 other events, 1209.5 us)
Sparse Core Ops, SparseCore 0:
  10.7 199.7 all-gather.8
  213.2 194.8 all-gather.10
  1130.3 127.0 all-gather.14
  1259.3 132.1 all-gather.12
where the time goes:
time: 1420 us; the launch traced here: 1400 us
  waiting for transfers between devices  666 us (47%)
  blocking collectives  534 us (38%)
  starting transfers between devices  109 us (8%)
  local copies, waits for them, and re-layouts  38.6 us (3%)
  other arithmetic  35.9 us (3%)
  between operations  14.8 us (1%)
    all_gather x2, waiting for transfers between devices, per_device(): block_rows = lax.all_gather(sources[block], 'band', axis=0, tiled=True)  374 us
    psum x8, blocking collectives, squares(): return lax.psum(local_dot(residual, residual), 'dom')  269 us
    psum x7, blocking collectives, solve(): step_size = norm_now / lax.psum(local_dot(direction, applied), 'dom')  265 us
    all_gather x2, waiting for transfers between devices, per_device(): every_row = lax.all_gather(source_term, 'band', axis=0, tiled=True)  253 us
    ppermute x16, starting transfers between devices, with_halo(): lax.ppermute(tail, axis, [(i, (i + 1) % count) for i in range(ends)])  77.4 us
    ppermute x16, waiting for transfers between devices, with_halo(): lax.ppermute(head, axis, [((i + 1) % count, i) for i in range(ends)])  39.3 us
    ppermute x16, starting transfers between devices, with_halo(): lax.ppermute(head, axis, [((i + 1) % count, i) for i in range(ends)])  31.6 us
  transfers between devices with their start and end apart: 36, of which 12 were waited for; matrix products, arithmetic and copies ran while one was open for 3% of the time, Pallas kernels for 0%

commit v1 on v0

v1 whole, which is shorter than its diff:
```python
import numpy as np
import jax
import jax.numpy as jnp
from jax import lax
from jax.experimental import pallas as pl
from jax.experimental.pallas import tpu as pltpu
from jax.sharding import PartitionSpec as P

SIDE = 64
SWEEPS = 8
RING = 16
ROW = 128
HALF = 64
VMEM_LIMIT = 48 * 1024 * 1024
F32 = jnp.float32
BF16 = jnp.bfloat16


def eigen_system():
    line = np.zeros((SIDE, SIDE))
    for delta, weight in ((0, 30.0), (1, -16.0), (2, 1.0)):
        for i in range(SIDE - delta):
            line[i, i + delta] = weight / 12.0
            line[i + delta, i] = weight / 12.0
    values, vectors = np.linalg.eigh(line)
    return values, vectors * np.where(vectors[0] < 0, -1.0, 1.0)[None, :]


def halves(matrix):
    high = np.asarray(matrix, np.float32).astype(jnp.bfloat16)
    low = (np.asarray(matrix, np.float64) - high.astype(np.float64)).astype(jnp.bfloat16)
    return np.stack([high, low])


def tables():
    values, v = eigen_system()
    along_z = np.kron(np.eye(2), v)
    even, odd = v[0::2], v[1::2]
    fwd = np.zeros((2, 32, 4, 2, 4, 32))
    bwd = np.zeros((2, 4, 32, 2, 32, 4))
    for x in range(4):
        fwd[0, :, x, 0, x, :] = even[:, 0::2].T
        fwd[0, :, x, 1, x, :] = odd[:, 0::2].T
        fwd[1, :, x, 0, x, :] = odd[:, 1::2].T
        fwd[1, :, x, 1, x, :] = even[:, 1::2].T
        bwd[0, x, :, 0, :, x] = even[:, 0::2]
        bwd[0, x, :, 1, :, x] = even[:, 1::2]
        bwd[1, x, :, 0, :, x] = odd[:, 1::2]
        bwd[1, x, :, 1, :, x] = odd[:, 0::2]
    along_x = np.zeros((2, SIDE, RING, 2, 4))
    for pick in range(2):
        along_x[pick, :, :, pick, :] = v.T.reshape(SIDE, RING, 4)
    rows = np.arange(SIDE).reshape(RING, 2, 1, 2, 1)
    spectrum = values[rows] + values.reshape(1, 1, SIDE, 1, 1) + values.reshape(1, 1, 1, 1, SIDE)
    return dict(
        z_fwd=halves(along_z),
        z_bwd=halves(along_z.T),
        y_fwd=halves(fwd.reshape(256, 256)),
        y_bwd=halves(bwd.reshape(256, 256)),
        x_fwd=halves(along_x.reshape(ROW, ROW)),
        x_bwd=halves(along_x.reshape(ROW, ROW).T),
        spectrum=spectrum.reshape(RING, ROW, ROW).astype(np.float32),
    )


def split(value):
    high = value.astype(BF16)
    return high, (value - high.astype(F32)).astype(BF16)


def mm(left, right):
    return jnp.dot(left, right, preferred_element_type=F32)


def left_mul(table, value):
    high, low = split(value)
    return mm(table[0], high) + mm(table[0], low) + mm(table[1], high)


def right_mul(value, table):
    high, low = split(value)
    return mm(high, table[0]) + mm(low, table[0]) + mm(high, table[1])


def mix_rows(table, value):
    swapped = jnp.concatenate([value[:, HALF:], value[:, :HALF]], axis=1)
    both = left_mul(table, jnp.concatenate([value, swapped], axis=0))
    lane = lax.broadcasted_iota(jnp.int32, (ROW, ROW), 1)
    return jnp.where(lane < HALF, both[:ROW], both[ROW:])


def vmem_call(kernel, outs, operands, scalars=0, scratch=()):
    whole = pl.BlockSpec(memory_space=pltpu.VMEM)
    smem = pl.BlockSpec(memory_space=pltpu.SMEM)
    return pl.pallas_call(
        kernel,
        out_shape=outs,
        in_specs=[smem] * scalars + [whole] * (len(operands) - scalars),
        out_specs=[whole] * len(outs),
        scratch_shapes=list(scratch),
        compiler_params=pltpu.CompilerParams(vmem_limit_bytes=VMEM_LIMIT),
    )(*operands)


def struct(shape, dtype):
    return jax.ShapeDtypeStruct(shape, dtype)


def owner_of(source):
    owner = lax.shift_right_logical(source, 2)
    return lax.shift_right_logical(owner, 1), lax.bitwise_and(owner, 1), lax.bitwise_and(source, 3)


def ring(value):
    return lax.bitwise_and(value, RING - 1)


def pick_kernel(place, pair_src, near0, near1, near2, near3, *outs):
    z, x, core = place[0], place[1], place[2]
    held = (
        (near0, 0),
        (near1, 1),
        (near2, RING - 1),
        (near3, jnp.where(core == 0, 2, RING - 2)),
    )
    for out, offset in zip(outs, (0, 4, -4, 8)):
        band = 2 * ring(z + offset) + x
        for slot in range(4):
            block, k = slot // 2, slot % 2
            z_own, x_own, row = owner_of(pair_src[block, 2 * band + k])
            index = 8 * lax.bitwise_xor(x_own, x) + 4 * block + row
            behind = ring(z - z_own)
            out[slot] = jnp.zeros((ROW, ROW), BF16)
            for rows, delta in held:

                @pl.when(behind == delta)
                def _():
                    out[slot] = rows[index]


def density_kernel(r0, r1, r2, r3, wanted, z_fwd, y_fwd, source_rows, spectra):
    for p in range(4):
        row = r0[p].astype(F32) + r1[p].astype(F32) + r2[p].astype(F32) + r3[p].astype(F32)
        source_rows[p] = row.astype(BF16)
        density = row * wanted[p].astype(F32)
        mixed = mix_rows(y_fwd, right_mul(density, z_fwd)).astype(spectra.dtype)
        for copy in range(4):
            spectra[4 * copy + p] = mixed


def solve_kernel(quarter, slabs, spectrum, x_fwd, x_bwd, out, residual, direction, total):
    def dot_of(value):
        return jnp.sum(value.reshape(RING, 8, ROW), axis=0)

    zero = jnp.zeros((8, ROW), F32)

    def start(j, carry):
        norm, power = carry
        rows = pl.ds(pl.multiple_of(8 * j, 8), 8)
        part = slabs[:, rows, :].astype(F32).reshape(ROW, ROW)
        value = left_mul(x_fwd, part)
        residual[j] = value
        direction[j] = value
        total[j] = jnp.zeros((ROW, ROW), F32)
        square = value * value
        return norm + dot_of(square), power + dot_of(square * spectrum[j])

    norm, power = lax.fori_loop(0, RING, start, (zero, zero))
    norm, power = jnp.sum(norm), jnp.sum(power)
    for sweep in range(SWEEPS):
        step = norm / power

        def advance(j, acc):
            d = direction[j]
            r = residual[j] - step * (spectrum[j] * d)
            total[j] = total[j] + step * d
            residual[j] = r
            return acc + dot_of(r * r)

        new = jnp.sum(lax.fori_loop(0, RING, advance, zero))
        if sweep < SWEEPS - 1:
            ratio = new / norm

            def turn(j, acc):
                d = residual[j] + ratio * direction[j]
                direction[j] = d
                return acc + dot_of(d * (spectrum[j] * d))

            power = jnp.sum(lax.fori_loop(0, RING, turn, zero))
            norm = new
    for jj in range(4):
        part = left_mul(x_bwd, total[4 * quarter[0] + jj])
        out[:, 8 * jj : 8 * jj + 8, :] = part.reshape(RING, 8, ROW).astype(out.dtype)


def term_kernel(pair_tgt, spectra, source_rows, wanted, z_bwd, y_bwd, target_rows, terms, held):
    for p in range(4):
        rows = jnp.concatenate([spectra[4 * q + p].astype(F32) for q in range(4)], axis=0)
        potential = right_mul(mix_rows(y_bwd, rows), z_bwd)
        terms[p] = (-potential * wanted[p].astype(F32)).astype(BF16)
        held[p] = -potential * source_rows[p].astype(F32)
    for p in range(4):
        same = jnp.zeros((ROW, ROW), F32)
        for other in range(4):
            hit = pair_tgt[p // 2, p % 2] == pair_tgt[other // 2, other % 2]
            same = same + jnp.where(hit, held[other], 0.0)
        target_rows[p] = same.astype(BF16)


def owner_kernel(place, pair_src, near0, near1, near2, near3, mine, partner, total):
    z, x, core = place[0], place[1], place[2]
    total[...] = jnp.zeros((16, ROW, ROW), F32)
    centres = (z, z - 1, z + 1, jnp.where(core == 0, z - 2, z + 2))
    for rows, centre in zip((near0, near1, near2, near3), centres):
        for m, offset in enumerate((0, -4, 4, 8)):
            band = 2 * ring(centre + offset) + x
            for slot in range(4):
                z_own, x_own, row = owner_of(pair_src[slot // 2, 2 * band + slot % 2])

                @pl.when(z_own == z)
                def _():
                    index = 8 * lax.bitwise_xor(x_own, x) + 4 * (slot // 2) + row
                    total[index] = total[index] + rows[4 * m + slot].astype(F32)

    mine[...] = total[0:8]
    partner[...] = total[8:16].astype(BF16)


AXES = ("band", "dom")


def shift(value, steps, mirror=False):
    pairs = []
    for z in range(RING):
        for x in range(2):
            for dom in range(16):
                go = -steps if mirror and dom % 2 else steps
                there = 2 * ((z + go) % RING) + x
                pairs.append(((2 * z + x) * 16 + dom, there * 16 + dom))
    return lax.ppermute(value, AXES, pairs)


def across(value):
    return lax.ppermute(value, "band", [(i, i ^ 1) for i in range(32)])


def neighbours(value):
    return value, shift(value, 1), shift(value, -1), shift(value, 2, True)


def per_device(targets, sources, pair_tgt, pair_src):
    table = {name: jnp.asarray(value) for name, value in tables().items()}
    band, dom = lax.axis_index("band"), lax.axis_index("dom")
    place = jnp.stack([band // 2, band % 2, dom % 2]).astype(jnp.int32)
    quarter = (dom // 4).astype(jnp.int32).reshape(1)

    own = sources.reshape(8, ROW, ROW)
    rows = jnp.concatenate([own, across(own)], axis=0)
    near = neighbours(rows)
    four = struct((4, ROW, ROW), BF16)
    picked = vmem_call(pick_kernel, [four] * 4, (place, pair_src) + near, scalars=2)
    reached = (picked[0], shift(picked[1], 4), shift(picked[2], -4), shift(picked[3], 8))

    ids = pair_tgt.reshape(4)
    wanted = targets[ids].reshape(4, ROW, ROW)
    source_rows, spectra = vmem_call(
        density_kernel,
        [four, struct((16, ROW, ROW), BF16)],
        reached + (wanted, table["z_fwd"], table["y_fwd"]),
    )
    slabs = lax.all_to_all(spectra, "dom", 0, 0, tiled=True)
    state = pltpu.VMEM((RING, ROW, ROW), F32)
    (solved,) = vmem_call(
        solve_kernel,
        [struct((16, 32, ROW), F32)],
        (quarter, slabs, table["spectrum"], table["x_fwd"], table["x_bwd"]),
        scalars=1,
        scratch=(state, state, state),
    )
    back = lax.all_to_all(solved, "dom", 0, 0, tiled=True)
    target_rows, terms = vmem_call(
        term_kernel,
        [four, four],
        (pair_tgt, back, source_rows, wanted, table["z_bwd"], table["y_bwd"]),
        scalars=1,
        scratch=(pltpu.VMEM((4, ROW, ROW), F32),),
    )

    gathered = jnp.concatenate([terms, shift(terms, 4), shift(terms, -4), shift(terms, 8)], axis=0)
    near = neighbours(gathered)
    mine, partner = vmem_call(
        owner_kernel,
        [struct((8, ROW, ROW), F32), struct((8, ROW, ROW), BF16)],
        (place, pair_src) + near,
        scalars=2,
        scratch=(pltpu.VMEM((16, ROW, ROW), F32),),
    )
    owned = (mine + across(partner).astype(F32)).astype(BF16).reshape(sources.shape)

    flat = target_rows.reshape(4, targets.shape[1])
    slots = jnp.arange(targets.shape[0], dtype=jnp.int32)[:, None]
    summed = jnp.zeros(targets.shape, BF16)
    for p in range(4):
        summed = jnp.where(slots == ids[p], flat[p][None, :], summed)
    return summed, owned


def solution(mesh):
    return jax.shard_map(
        per_device,
        mesh=mesh,
        in_specs=(P("band", "dom"), P(None, "band", "dom"), P(None, "band"), P()),
        out_specs=(P("band", "dom"), P(None, "band", "dom")),
        check_vma=False,
    )
```

time: 1420 us -> 207 us (0.15); the launches traced: 1400 us -> 206 us
  waiting for transfers between devices: 666 us -> 85.2 us
  blocking collectives: 534 us -> 0 us
  local copies, waits for them, and re-layouts: 38.6 us -> 4.47 us
  other arithmetic: 35.9 us -> 4.01 us
  Pallas kernels: 0 us -> 19.5 us
  starting transfers between devices: 109 us -> 91.6 us
    all_gather x4 -> x0, waiting for transfers between devices: 627 us -> none  [the longest x2 374 us: per_device(): block_rows = lax.all_gather(sources[block], 'band', axis=0, tiled=True)]
    psum x15 -> x0, blocking collectives: 534 us -> none  [the longest x8 269 us: squares(): return lax.psum(local_dot(residual, residual), 'dom')]
    ppermute x32 -> x14, starting transfers between devices: 109 us -> 79.8 us  [the longest x12 73.4 us: shift(): return lax.ppermute(value, AXES, pairs)]
    unnamed x40 -> x25, local copies, waits for them, and re-layouts: 27.7 us -> 0.81 us
    ppermute x32 -> x14, waiting for transfers between devices: 39.3 us -> 65.9 us  [the longest x12 57.7 us: shift(): return lax.ppermute(value, AXES, pairs)]
    pallas_call x0 -> x5, Pallas kernels: none -> 19.5 us  [vmem_call(): pl.pallas_call(kernel, out_shape=outs, in_specs=[smem] * scalars + [whole...]
    all_to_all x0 -> x2, waiting for transfers between devices: none -> 19.3 us  [the longest x1 11.3 us: per_device(): slabs = lax.all_to_all(spectra, 'dom', 0, 0, tiled=True)]
    reduce_sum x31 -> x0, other arithmetic: 15.2 us -> none  [local_dot(): return jnp.sum(left * right, axis=(1, 2))]
  transfers between devices with their start and end apart: 36 -> 16, of which waited for: 12 -> 13; matrix products, arithmetic and copies ran while one was open for 3% -> 3% of each run, Pallas kernels for 0% -> 0%
where the time goes in v1:
time: 207 us; the launch traced here: 206 us
  starting transfers between devices  91.6 us (44%)
  waiting for transfers between devices  85.2 us (41%)
  Pallas kernels  19.5 us (9%)
  local copies, waits for them, and re-layouts  4.47 us (2%)
  other arithmetic  4.01 us (2%)
    ppermute x12, starting transfers between devices, shift(): return lax.ppermute(value, AXES, pairs)  73.4 us
    ppermute x12, waiting for transfers between devices, shift(): return lax.ppermute(value, AXES, pairs)  57.7 us
    pallas_call x5, Pallas kernels, vmem_call(): pl.pallas_call(kernel, out_shape=outs, in_specs=[smem] * scalars + [whole...  19.5 us
    all_to_all x1, waiting for transfers between devices, per_device(): slabs = lax.all_to_all(spectra, 'dom', 0, 0, tiled=True)  11.3 us
    ppermute x2, waiting for transfers between devices, across(): return lax.ppermute(value, 'band', [(i, i ^ 1) for i in range(32)])  8.23 us
    all_to_all x1, waiting for transfers between devices, per_device(): back = lax.all_to_all(solved, 'dom', 0, 0, tiled=True)  8.01 us
    all_to_all x1, starting transfers between devices, per_device(): slabs = lax.all_to_all(spectra, 'dom', 0, 0, tiled=True)  7.19 us
    ppermute x2, starting transfers between devices, across(): return lax.ppermute(value, 'band', [(i, i ^ 1) for i in range(32)])  6.39 us
  transfers between devices with their start and end apart: 16, of which 13 were waited for; matrix products, arithmetic and copies ran while one was open for 3% of the time, Pallas kernels for 0%

profile of v1, /device:TPU:1, one launch (start us, length us, event | category | flops | bytes accessed | tf_op | source)
XLA Modules:
  0.0 205.7 jit_solution(2576730806603300873)
XLA Ops:
  2.0 3.9 %collective-permute-start = (bf16[8,128,128]{2,1,0:T(8,128)(2,1)S(1)}, bf16[8,128,128]{2,1,0:T(8,128)(2,1)S(1)}, u32[]{:S(2)}, u32[]{:S(2)}) collective-permute-start(bf16[8,128,128]{2,1,0:T(8,128)(2,1)S(1)} %reshape.80), channel_id=1, source_target_pairs={{0,16},{16,0},{32,48},{48,32},{64,80},{80,64},{96,112},{112,96},{1... | collective-permute-start | bytes 786440 | tf_op jit(solution)/shard_map/ppermute | solution.py:244
  6.0 3.7 %collective-permute-done = bf16[8,128,128]{2,1,0:T(8,128)(2,1)S(1)} collective-permute-done((bf16[8,128,128]{2,1,0:T(8,128)(2,1)S(1)}, bf16[8,128,128]{2,1,0:T(8,128)(2,1)S(1)}, u32[]{:S(2)}, u32[]{:S(2)}) %collective-permute-start) | collective-permute-done | bytes 262176 | tf_op jit(solution)/shard_map/ppermute | solution.py:244
  9.7 5.7 %collective-permute-start.1 = (bf16[16,128,128]{2,1,0:T(8,128)(2,1)S(1)}, bf16[16,128,128]{2,1,0:T(8,128)(2,1)S(1)}, u32[]{:S(2)}, u32[]{:S(2)}) collective-permute-start(bf16[16,128,128]{2,1,0:T(8,128)(2,1)S(1)} %constant_dynamic-update-slice_fusion.near0), channel_id=1, source_target_pairs={{0,32},{1,33},{2,34},{3,35},{4,36},{5,37},{6,38},{7,39},{8,40},{9,... | collective-permute-start | bytes 1572872 | tf_op jit(solution)/shard_map/ppermute | solution.py:240
  15.5 9.5 %collective-permute-start.2 = (bf16[16,128,128]{2,1,0:T(8,128)(2,1)S(1)}, bf16[16,128,128]{2,1,0:T(8,128)(2,1)S(1)}, u32[]{:S(2)}, u32[]{:S(2)}) collective-permute-start(bf16[16,128,128]{2,1,0:T(8,128)(2,1)S(1)} %constant_dynamic-update-slice_fusion.near0), channel_id=1, source_target_pairs={{0,480},{1,481},{2,482},{3,483},{4,484},{5,485},{6,486},{7,487},{8... | collective-permute-start | bytes 1572872 | tf_op jit(solution)/shard_map/ppermute | solution.py:240
  25.0 3.8 %collective-permute-start.3 = (bf16[16,128,128]{2,1,0:T(8,128)(2,1)S(1)}, bf16[16,128,128]{2,1,0:T(8,128)(2,1)S(1)}, u32[]{:S(2)}, u32[]{:S(2)}) collective-permute-start(bf16[16,128,128]{2,1,0:T(8,128)(2,1)S(1)} %constant_dynamic-update-slice_fusion.near0), channel_id=1, source_target_pairs={{0,64},{1,449},{2,66},{3,451},{4,68},{5,453},{6,70},{7,455},{8,72}... | collective-permute-start | bytes 1572872 | tf_op jit(solution)/shard_map/ppermute | solution.py:240
  29.6 4.1 %collective-permute-done.1.near1 = bf16[16,128,128]{2,1,0:T(8,128)(2,1)S(1)} collective-permute-done((bf16[16,128,128]{2,1,0:T(8,128)(2,1)S(1)}, bf16[16,128,128]{2,1,0:T(8,128)(2,1)S(1)}, u32[]{:S(2)}, u32[]{:S(2)}) %collective-permute-start.1) | collective-permute-done | bytes 524320 | tf_op jit(solution)/shard_map/ppermute | solution.py:240
  33.7 4.5 %collective-permute-done.2.near2 = bf16[16,128,128]{2,1,0:T(8,128)(2,1)S(1)} collective-permute-done((bf16[16,128,128]{2,1,0:T(8,128)(2,1)S(1)}, bf16[16,128,128]{2,1,0:T(8,128)(2,1)S(1)}, u32[]{:S(2)}, u32[]{:S(2)}) %collective-permute-start.2) | collective-permute-done | bytes 524320 | tf_op jit(solution)/shard_map/ppermute | solution.py:240
  38.2 9.7 %collective-permute-done.3.near3 = bf16[16,128,128]{2,1,0:T(8,128)(2,1)S(1)} collective-permute-done((bf16[16,128,128]{2,1,0:T(8,128)(2,1)S(1)}, bf16[16,128,128]{2,1,0:T(8,128)(2,1)S(1)}, u32[]{:S(2)}, u32[]{:S(2)}) %collective-permute-start.3) | collective-permute-done | bytes 524320 | tf_op jit(solution)/shard_map/ppermute | solution.py:240
  47.9 1.7 shard_map.122
  49.6 4.7 %collective-permute-start.4 = (bf16[4,128,128]{2,1,0:T(8,128)(2,1)}, bf16[4,128,128]{2,1,0:T(8,128)(2,1)S(1)}, u32[]{:S(2)}, u32[]{:S(2)}) collective-permute-start(bf16[4,128,128]{2,1,0:T(8,128)(2,1)} %get-tuple-element.13), channel_id=1, source_target_pairs={{0,128},{1,129},{2,130},{3,131},{4,132},{5,133},{6,134},{7,135},{8... | collective-permute-start | bytes 393224 | tf_op jit(solution)/shard_map/ppermute | solution.py:240
  54.3 4.5 %collective-permute-start.5 = (bf16[4,128,128]{2,1,0:T(8,128)(2,1)S(1)}, bf16[4,128,128]{2,1,0:T(8,128)(2,1)S(1)}, u32[]{:S(2)}, u32[]{:S(2)}) collective-permute-start(bf16[4,128,128]{2,1,0:T(8,128)(2,1)S(1)} %get-tuple-element.14), channel_id=1, source_target_pairs={{0,384},{1,385},{2,386},{3,387},{4,388},{5,389},{6,390},{7,391},{8... | collective-permute-start | bytes 393224 | tf_op jit(solution)/shard_map/ppermute | solution.py:240
  58.8 9.3 %collective-permute-start.6 = (bf16[4,128,128]{2,1,0:T(8,128)(2,1)S(1)}, bf16[4,128,128]{2,1,0:T(8,128)(2,1)S(1)}, u32[]{:S(2)}, u32[]{:S(2)}) collective-permute-start(bf16[4,128,128]{2,1,0:T(8,128)(2,1)S(1)} %get-tuple-element.15), channel_id=1, source_target_pairs={{0,256},{1,257},{2,258},{3,259},{4,260},{5,261},{6,262},{7,263},{8... | collective-permute-start | bytes 393224 | tf_op jit(solution)/shard_map/ppermute | solution.py:240
  69.5 11.1 %collective-permute-done.6.r3 = bf16[4,128,128]{2,1,0:T(8,128)(2,1)S(1)} collective-permute-done((bf16[4,128,128]{2,1,0:T(8,128)(2,1)S(1)}, bf16[4,128,128]{2,1,0:T(8,128)(2,1)S(1)}, u32[]{:S(2)}, u32[]{:S(2)}) %collective-permute-start.6) | collective-permute-done | bytes 131104 | tf_op jit(solution)/shard_map/ppermute | solution.py:240
  80.5 2.3 %shard_map.123 = (bf16[4,128,128]{2,1,0:T(8,128)(2,1)S(1)}, bf16[16,128,128]{2,1,0:T(8,128)(2,1)}) custom-call(bf16[4,128,128]{2,1,0:T(8,128)(2,1)S(1)} %get-tuple-element.12.r0, bf16[4,128,128]{2,1,0:T(8,128)(2,1)S(1)} %collective-permute-done.4.r1, bf16[4,128,128]{2,1,0:T(8,128)(2,1)S(1)} %collective-permute-done.5.r2, ...), custom_call_target="tpu_custom_call" | custom-call | tf_op jit(solution)/shard_map/pallas_call | solution.py:95
  82.8 7.2 %all-to-all-start = ((bf16[16,128,128]{2,1,0:T(8,128)(2,1)}), bf16[16,128,128]{2,1,0:T(8,128)(2,1)S(1)}, u32[]{:S(2)}, u32[]{:S(2)}) async-start(bf16[16,128,128]{2,1,0:T(8,128)(2,1)} %get-tuple-element.16), calls=%async_computation | async-start | bytes 1048576 | tf_op jit(solution)/shard_map/all_to_all | solution.py:271
  90.0 11.3 %all-to-all-done.slabs = bf16[16,128,128]{2,1,0:T(8,128)(2,1)S(1)} async-done(((bf16[16,128,128]{2,1,0:T(8,128)(2,1)}), bf16[16,128,128]{2,1,0:T(8,128)(2,1)S(1)}, u32[]{:S(2)}, u32[]{:S(2)}) %all-to-all-start) | async-done | bytes 524320 | tf_op jit(solution)/shard_map/all_to_all | solution.py:271
  101.3 12.1 %shard_map.124 = f32[16,32,128]{2,1,0:T(8,128)} custom-call(s32[1]{0:T(128)} %bitcast.1.quarter, bf16[16,128,128]{2,1,0:T(8,128)(2,1)S(1)} %all-to-all-done.slabs, f32[16,128,128]{2,1,0:T(8,128)S(1)} %copy-done.1, bf16[2,128,128]{2,1,0:T(8,128)(2,1)S(1)} %copy-done.4, bf16[2,128,128]{2,1,0:T(8,128)(2,1)S(1)} %copy-done.5), custom_call_target="tpu_custom_call" | custom-call | tf_op jit(solution)/shard_map/pallas_call | solution.py:95
  113.5 4.6 %all-to-all-start.1 = ((f32[16,32,128]{2,1,0:T(8,128)}), f32[16,32,128]{2,1,0:T(8,128)S(1)}, u32[]{:S(2)}, u32[]{:S(2)}) async-start(f32[16,32,128]{2,1,0:T(8,128)} %shard_map.124), calls=%async_computation.1 | async-start | bytes 524288 | tf_op jit(solution)/shard_map/all_to_all | solution.py:280
  118.8 8.0 %all-to-all-done.1.spectra = f32[16,32,128]{2,1,0:T(8,128)S(1)} async-done(((f32[16,32,128]{2,1,0:T(8,128)}), f32[16,32,128]{2,1,0:T(8,128)S(1)}, u32[]{:S(2)}, u32[]{:S(2)}) %all-to-all-start.1) | async-done | bytes 262176 | tf_op jit(solution)/shard_map/all_to_all | solution.py:280
  126.8 2.0 shard_map.125
  128.8 4.5 %collective-permute-start.7 = (bf16[4,128,128]{2,1,0:T(8,128)(2,1)S(1)}, bf16[4,128,128]{2,1,0:T(8,128)(2,1)S(1)}, u32[]{:S(2)}, u32[]{:S(2)}) collective-permute-start(bf16[4,128,128]{2,1,0:T(8,128)(2,1)S(1)} %get-tuple-element.19), channel_id=1, source_target_pairs={{0,128},{1,129},{2,130},{3,131},{4,132},{5,133},{6,134},{7,135},{8... | collective-permute-start | bytes 393224 | tf_op jit(solution)/shard_map/ppermute | solution.py:240
  134.6 4.7 %collective-permute-start.8 = (bf16[4,128,128]{2,1,0:T(8,128)(2,1)S(1)}, bf16[4,128,128]{2,1,0:T(8,128)(2,1)S(1)}, u32[]{:S(2)}, u32[]{:S(2)}) collective-permute-start(bf16[4,128,128]{2,1,0:T(8,128)(2,1)S(1)} %get-tuple-element.19), channel_id=1, source_target_pairs={{0,384},{1,385},{2,386},{3,387},{4,388},{5,389},{6,390},{7,391},{8... | collective-permute-start | bytes 393224 | tf_op jit(solution)/shard_map/ppermute | solution.py:240
  139.4 9.9 %collective-permute-start.9 = (bf16[4,128,128]{2,1,0:T(8,128)(2,1)S(1)}, bf16[4,128,128]{2,1,0:T(8,128)(2,1)S(1)}, u32[]{:S(2)}, u32[]{:S(2)}) collective-permute-start(bf16[4,128,128]{2,1,0:T(8,128)(2,1)S(1)} %get-tuple-element.19), channel_id=1, source_target_pairs={{0,256},{1,257},{2,258},{3,259},{4,260},{5,261},{6,262},{7,263},{8... | collective-permute-start | bytes 393224 | tf_op jit(solution)/shard_map/ppermute | solution.py:240
  149.6 12.1 %collective-permute-done.9 = bf16[4,128,128]{2,1,0:T(8,128)(2,1)S(1)} collective-permute-done((bf16[4,128,128]{2,1,0:T(8,128)(2,1)S(1)}, bf16[4,128,128]{2,1,0:T(8,128)(2,1)S(1)}, u32[]{:S(2)}, u32[]{:S(2)}) %collective-permute-start.9) | collective-permute-done | bytes 131104 | tf_op jit(solution)/shard_map/ppermute | solution.py:240
  161.7 1.9 collective-permute-start.10
  163.6 6.1 %collective-permute-start.11 = (bf16[16,128,128]{2,1,0:T(8,128)(2,1)S(1)}, bf16[16,128,128]{2,1,0:T(8,128)(2,1)S(1)}, u32[]{:S(2)}, u32[]{:S(2)}) collective-permute-start(bf16[16,128,128]{2,1,0:T(8,128)(2,1)S(1)} %constant_dynamic-update-slice_fusion.2.near0), channel_id=1, source_target_pairs={{0,480},{1,481},{2,482},{3,483},{4,484},{5,485},{6,486},{7,487},{8... | collective-permute-start | bytes 1572872 | tf_op jit(solution)/shard_map/ppermute | solution.py:240
  169.7 8.8 %collective-permute-start.12 = (bf16[16,128,128]{2,1,0:T(8,128)(2,1)S(1)}, bf16[16,128,128]{2,1,0:T(8,128)(2,1)S(1)}, u32[]{:S(2)}, u32[]{:S(2)}) collective-permute-start(bf16[16,128,128]{2,1,0:T(8,128)(2,1)S(1)} %constant_dynamic-update-slice_fusion.2.near0), channel_id=1, source_target_pairs={{0,64},{1,449},{2,66},{3,451},{4,68},{5,453},{6,70},{7,455},{8,72}... | collective-permute-start | bytes 1572872 | tf_op jit(solution)/shard_map/ppermute | solution.py:240
  179.8 2.4 %collective-permute-done.11.near2 = bf16[16,128,128]{2,1,0:T(8,128)(2,1)S(1)} collective-permute-done((bf16[16,128,128]{2,1,0:T(8,128)(2,1)S(1)}, bf16[16,128,128]{2,1,0:T(8,128)(2,1)S(1)}, u32[]{:S(2)}, u32[]{:S(2)}) %collective-permute-start.11) | collective-permute-done | bytes 524320 | tf_op jit(solution)/shard_map/ppermute | solution.py:240
  182.2 13.0 %collective-permute-done.12.near3 = bf16[16,128,128]{2,1,0:T(8,128)(2,1)S(1)} collective-permute-done((bf16[16,128,128]{2,1,0:T(8,128)(2,1)S(1)}, bf16[16,128,128]{2,1,0:T(8,128)(2,1)S(1)}, u32[]{:S(2)}, u32[]{:S(2)}) %collective-permute-start.12) | collective-permute-done | bytes 524320 | tf_op jit(solution)/shard_map/ppermute | solution.py:240
  195.2 1.4 shard_map.126
  196.6 2.4 %collective-permute-start.13 = (bf16[8,128,128]{2,1,0:T(8,128)(2,1)S(1)}, bf16[8,128,128]{2,1,0:T(8,128)(2,1)S(1)}, u32[]{:S(2)}, u32[]{:S(2)}) collective-permute-start(bf16[8,128,128]{2,1,0:T(8,128)(2,1)S(1)} %get-tuple-element.21), channel_id=1, source_target_pairs={{0,16},{16,0},{32,48},{48,32},{64,80},{80,64},{96,112},{112,96},{1... | collective-permute-start | bytes 786440 | tf_op jit(solution)/shard_map/ppermute | solution.py:244
  200.4 4.5 %collective-permute-done.13 = bf16[8,128,128]{2,1,0:T(8,128)(2,1)S(1)} collective-permute-done((bf16[8,128,128]{2,1,0:T(8,128)(2,1)S(1)}, bf16[8,128,128]{2,1,0:T(8,128)(2,1)S(1)}, u32[]{:S(2)}, u32[]{:S(2)}) %collective-permute-start.13) | collective-permute-done | bytes 262176 | tf_op jit(solution)/shard_map/ppermute | solution.py:244
  (46 shorter events, 9.3 us)
Async XLA Ops:
  0.6 67.5 %copy-start = (bf16[32,16384]{1,0:T(8,128)(2,1)S(1)}, bf16[32,16384]{1,0:T(8,128)(2,1)}, u32[]{:S(2)}) copy-start(bf16[32,16384]{1,0:T(8,128)(2,1)} %param.11) | copy-start | bytes 3145732
  2.0 7.7 %collective-permute-start = (bf16[8,128,128]{2,1,0:T(8,128)(2,1)S(1)}, bf16[8,128,128]{2,1,0:T(8,128)(2,1)S(1)}, u32[]{:S(2)}, u32[]{:S(2)}) collective-permute-start(bf16[8,128,128]{2,1,0:T(8,128)(2,1)S(1)} %reshape.80), channel_id=1, source_target_pairs={{0,16},{16,0},{32,48},{48,32},{64,80},{80,64},{96,112},{112,96},{1... | collective-permute-start | bytes 786440 | tf_op jit(solution)/shard_map/ppermute | solution.py:244
  9.7 24.0 %collective-permute-start.1 = (bf16[16,128,128]{2,1,0:T(8,128)(2,1)S(1)}, bf16[16,128,128]{2,1,0:T(8,128)(2,1)S(1)}, u32[]{:S(2)}, u32[]{:S(2)}) collective-permute-start(bf16[16,128,128]{2,1,0:T(8,128)(2,1)S(1)} %constant_dynamic-update-slice_fusion.near0), channel_id=1, source_target_pairs={{0,32},{1,33},{2,34},{3,35},{4,36},{5,37},{6,38},{7,39},{8,40},{9,... | collective-permute-start | bytes 1572872 | tf_op jit(solution)/shard_map/ppermute | solution.py:240
  15.5 22.7 %collective-permute-start.2 = (bf16[16,128,128]{2,1,0:T(8,128)(2,1)S(1)}, bf16[16,128,128]{2,1,0:T(8,128)(2,1)S(1)}, u32[]{:S(2)}, u32[]{:S(2)}) collective-permute-start(bf16[16,128,128]{2,1,0:T(8,128)(2,1)S(1)} %constant_dynamic-update-slice_fusion.near0), channel_id=1, source_target_pairs={{0,480},{1,481},{2,482},{3,483},{4,484},{5,485},{6,486},{7,487},{8... | collective-permute-start | bytes 1572872 | tf_op jit(solution)/shard_map/ppermute | solution.py:240
  25.0 23.0 %collective-permute-start.3 = (bf16[16,128,128]{2,1,0:T(8,128)(2,1)S(1)}, bf16[16,128,128]{2,1,0:T(8,128)(2,1)S(1)}, u32[]{:S(2)}, u32[]{:S(2)}) collective-permute-start(bf16[16,128,128]{2,1,0:T(8,128)(2,1)S(1)} %constant_dynamic-update-slice_fusion.near0), channel_id=1, source_target_pairs={{0,64},{1,449},{2,66},{3,451},{4,68},{5,453},{6,70},{7,455},{8,72}... | collective-permute-start | bytes 1572872 | tf_op jit(solution)/shard_map/ppermute | solution.py:240
  28.8 0.7 copy-start.9
  29.6 18.4 %copy-start.8 = (s32[2,64]{1,0:T(2,128)S(1)}, s32[2,64]{1,0:T(2,128)}, u32[]{:S(2)}) copy-start(s32[2,64]{1,0:T(2,128)} %pair_src.3) | copy-start | bytes 1540
  49.6 19.3 %collective-permute-start.4 = (bf16[4,128,128]{2,1,0:T(8,128)(2,1)}, bf16[4,128,128]{2,1,0:T(8,128)(2,1)S(1)}, u32[]{:S(2)}, u32[]{:S(2)}) collective-permute-start(bf16[4,128,128]{2,1,0:T(8,128)(2,1)} %get-tuple-element.13), channel_id=1, source_target_pairs={{0,128},{1,129},{2,130},{3,131},{4,132},{5,133},{6,134},{7,135},{8... | collective-permute-start | bytes 393224 | tf_op jit(solution)/shard_map/ppermute | solution.py:240
  54.3 15.2 %collective-permute-start.5 = (bf16[4,128,128]{2,1,0:T(8,128)(2,1)S(1)}, bf16[4,128,128]{2,1,0:T(8,128)(2,1)S(1)}, u32[]{:S(2)}, u32[]{:S(2)}) collective-permute-start(bf16[4,128,128]{2,1,0:T(8,128)(2,1)S(1)} %get-tuple-element.14), channel_id=1, source_target_pairs={{0,384},{1,385},{2,386},{3,387},{4,388},{5,389},{6,390},{7,391},{8... | collective-permute-start | bytes 393224 | tf_op jit(solution)/shard_map/ppermute | solution.py:240
  58.8 21.8 %collective-permute-start.6 = (bf16[4,128,128]{2,1,0:T(8,128)(2,1)S(1)}, bf16[4,128,128]{2,1,0:T(8,128)(2,1)S(1)}, u32[]{:S(2)}, u32[]{:S(2)}) collective-permute-start(bf16[4,128,128]{2,1,0:T(8,128)(2,1)S(1)} %get-tuple-element.15), channel_id=1, source_target_pairs={{0,256},{1,257},{2,258},{3,259},{4,260},{5,261},{6,262},{7,263},{8... | collective-permute-start | bytes 393224 | tf_op jit(solution)/shard_map/ppermute | solution.py:240
  68.1 12.4 %copy-start.7 = (bf16[2,128,128]{2,1,0:T(8,128)(2,1)S(1)}, bf16[2,128,128]{2,1,0:T(8,128)(2,1)}, u32[]{:S(2)}) copy-start(bf16[2,128,128]{2,1,0:T(8,128)(2,1)} %constant.66.clone.z_fwd) | copy-start | bytes 196612
  68.8 11.7 %copy-start.3 = (bf16[2,256,256]{2,1,0:T(8,128)(2,1)S(1)}, bf16[2,256,256]{2,1,0:T(8,128)(2,1)}, u32[]{:S(2)}) copy-start(bf16[2,256,256]{2,1,0:T(8,128)(2,1)} %constant.68.clone.y_fwd) | copy-start | bytes 786436
  68.9 32.4 %copy-start.1 = (f32[16,128,128]{2,1,0:T(8,128)S(1)}, f32[16,128,128]{2,1,0:T(8,128)}, u32[]{:S(2)}) copy-start(f32[16,128,128]{2,1,0:T(8,128)} %constant.72.clone.spectrum) | copy-start | bytes 3145732
  82.8 18.5 %copy-start.4 = (bf16[2,128,128]{2,1,0:T(8,128)(2,1)S(1)}, bf16[2,128,128]{2,1,0:T(8,128)(2,1)}, u32[]{:S(2)}) copy-start(bf16[2,128,128]{2,1,0:T(8,128)(2,1)} %constant.70.clone.x_fwd) | copy-start | bytes 196612
  82.8 18.5 %copy-start.5 = (bf16[2,128,128]{2,1,0:T(8,128)(2,1)S(1)}, bf16[2,128,128]{2,1,0:T(8,128)(2,1)}, u32[]{:S(2)}) copy-start(bf16[2,128,128]{2,1,0:T(8,128)(2,1)} %constant.71.clone.x_bwd) | copy-start | bytes 196612
  82.8 18.5 %all-to-all-start = ((bf16[16,128,128]{2,1,0:T(8,128)(2,1)}), bf16[16,128,128]{2,1,0:T(8,128)(2,1)S(1)}, u32[]{:S(2)}, u32[]{:S(2)}) async-start(bf16[16,128,128]{2,1,0:T(8,128)(2,1)} %get-tuple-element.16), calls=%async_computation | async-start | bytes 1048576 | tf_op jit(solution)/shard_map/all_to_all | solution.py:271
  113.4 13.4 %copy-start.2 = (bf16[2,256,256]{2,1,0:T(8,128)(2,1)S(1)}, bf16[2,256,256]{2,1,0:T(8,128)(2,1)}, u32[]{:S(2)}) copy-start(bf16[2,256,256]{2,1,0:T(8,128)(2,1)} %constant.69.clone.y_bwd) | copy-start | bytes 786436
  113.4 13.4 %copy-start.6 = (bf16[2,128,128]{2,1,0:T(8,128)(2,1)S(1)}, bf16[2,128,128]{2,1,0:T(8,128)(2,1)}, u32[]{:S(2)}) copy-start(bf16[2,128,128]{2,1,0:T(8,128)(2,1)} %constant.67.clone.z_bwd) | copy-start | bytes 196612
  113.5 13.4 %all-to-all-start.1 = ((f32[16,32,128]{2,1,0:T(8,128)}), f32[16,32,128]{2,1,0:T(8,128)S(1)}, u32[]{:S(2)}, u32[]{:S(2)}) async-start(f32[16,32,128]{2,1,0:T(8,128)} %shard_map.124), calls=%async_computation.1 | async-start | bytes 524288 | tf_op jit(solution)/shard_map/all_to_all | solution.py:280
  128.8 20.4 %collective-permute-start.7 = (bf16[4,128,128]{2,1,0:T(8,128)(2,1)S(1)}, bf16[4,128,128]{2,1,0:T(8,128)(2,1)S(1)}, u32[]{:S(2)}, u32[]{:S(2)}) collective-permute-start(bf16[4,128,128]{2,1,0:T(8,128)(2,1)S(1)} %get-tuple-element.19), channel_id=1, source_target_pairs={{0,128},{1,129},{2,130},{3,131},{4,132},{5,133},{6,134},{7,135},{8... | collective-permute-start | bytes 393224 | tf_op jit(solution)/shard_map/ppermute | solution.py:240
  134.6 14.9 %collective-permute-start.8 = (bf16[4,128,128]{2,1,0:T(8,128)(2,1)S(1)}, bf16[4,128,128]{2,1,0:T(8,128)(2,1)S(1)}, u32[]{:S(2)}, u32[]{:S(2)}) collective-permute-start(bf16[4,128,128]{2,1,0:T(8,128)(2,1)S(1)} %get-tuple-element.19), channel_id=1, source_target_pairs={{0,384},{1,385},{2,386},{3,387},{4,388},{5,389},{6,390},{7,391},{8... | collective-permute-start | bytes 393224 | tf_op jit(solution)/shard_map/ppermute | solution.py:240
  139.4 22.2 %collective-permute-start.9 = (bf16[4,128,128]{2,1,0:T(8,128)(2,1)S(1)}, bf16[4,128,128]{2,1,0:T(8,128)(2,1)S(1)}, u32[]{:S(2)}, u32[]{:S(2)}) collective-permute-start(bf16[4,128,128]{2,1,0:T(8,128)(2,1)S(1)} %get-tuple-element.19), channel_id=1, source_target_pairs={{0,256},{1,257},{2,258},{3,259},{4,260},{5,261},{6,262},{7,263},{8... | collective-permute-start | bytes 393224 | tf_op jit(solution)/shard_map/ppermute | solution.py:240
  161.7 18.1 %collective-permute-start.10 = (bf16[16,128,128]{2,1,0:T(8,128)(2,1)S(1)}, bf16[16,128,128]{2,1,0:T(8,128)(2,1)S(1)}, u32[]{:S(2)}, u32[]{:S(2)}) collective-permute-start(bf16[16,128,128]{2,1,0:T(8,128)(2,1)S(1)} %constant_dynamic-update-slice_fusion.2.near0), channel_id=1, source_target_pairs={{0,32},{1,33},{2,34},{3,35},{4,36},{5,37},{6,38},{7,39},{8,40},{9,... | collective-permute-start | bytes 1572872 | tf_op jit(solution)/shard_map/ppermute | solution.py:240
  163.6 18.6 %collective-permute-start.11 = (bf16[16,128,128]{2,1,0:T(8,128)(2,1)S(1)}, bf16[16,128,128]{2,1,0:T(8,128)(2,1)S(1)}, u32[]{:S(2)}, u32[]{:S(2)}) collective-permute-start(bf16[16,128,128]{2,1,0:T(8,128)(2,1)S(1)} %constant_dynamic-update-slice_fusion.2.near0), channel_id=1, source_target_pairs={{0,480},{1,481},{2,482},{3,483},{4,484},{5,485},{6,486},{7,487},{8... | collective-permute-start | bytes 1572872 | tf_op jit(solution)/shard_map/ppermute | solution.py:240
  169.7 25.5 %collective-permute-start.12 = (bf16[16,128,128]{2,1,0:T(8,128)(2,1)S(1)}, bf16[16,128,128]{2,1,0:T(8,128)(2,1)S(1)}, u32[]{:S(2)}, u32[]{:S(2)}) collective-permute-start(bf16[16,128,128]{2,1,0:T(8,128)(2,1)S(1)} %constant_dynamic-update-slice_fusion.2.near0), channel_id=1, source_target_pairs={{0,64},{1,449},{2,66},{3,451},{4,68},{5,453},{6,70},{7,455},{8,72}... | collective-permute-start | bytes 1572872 | tf_op jit(solution)/shard_map/ppermute | solution.py:240
  196.6 8.3 %collective-permute-start.13 = (bf16[8,128,128]{2,1,0:T(8,128)(2,1)S(1)}, bf16[8,128,128]{2,1,0:T(8,128)(2,1)S(1)}, u32[]{:S(2)}, u32[]{:S(2)}) collective-permute-start(bf16[8,128,128]{2,1,0:T(8,128)(2,1)S(1)} %get-tuple-element.21), channel_id=1, source_target_pairs={{0,16},{16,0},{32,48},{48,32},{64,80},{80,64},{96,112},{112,96},{1... | collective-permute-start | bytes 786440 | tf_op jit(solution)/shard_map/ppermute | solution.py:244

commit v2 on v1

v2 whole, which is shorter than its diff:
```python
import numpy as np
import jax
import jax.numpy as jnp
from jax import lax
from jax.experimental import pallas as pl
from jax.experimental.pallas import tpu as pltpu
from jax.sharding import PartitionSpec as P

SIDE = 64
SWEEPS = 8
RING = 16
CAP = 6
ROW = 128
HALF = 64
VMEM_LIMIT = 48 * 1024 * 1024
F32 = jnp.float32
BF16 = jnp.bfloat16


def eigen_system():
    line = np.zeros((SIDE, SIDE))
    for delta, weight in ((0, 30.0), (1, -16.0), (2, 1.0)):
        for i in range(SIDE - delta):
            line[i, i + delta] = weight / 12.0
            line[i + delta, i] = weight / 12.0
    values, vectors = np.linalg.eigh(line)
    return values, vectors * np.where(vectors[0] < 0, -1.0, 1.0)[None, :]


def halves(matrix):
    high = np.asarray(matrix, np.float32).astype(jnp.bfloat16)
    low = (np.asarray(matrix, np.float64) - high.astype(np.float64)).astype(jnp.bfloat16)
    return np.stack([high, low])


def tables():
    values, v = eigen_system()
    along_z = np.kron(np.eye(2), v)
    even, odd = v[0::2], v[1::2]
    fwd = np.zeros((2, 32, 4, 2, 4, 32))
    bwd = np.zeros((2, 4, 32, 2, 32, 4))
    for x in range(4):
        fwd[0, :, x, 0, x, :] = even[:, 0::2].T
        fwd[0, :, x, 1, x, :] = odd[:, 0::2].T
        fwd[1, :, x, 0, x, :] = odd[:, 1::2].T
        fwd[1, :, x, 1, x, :] = even[:, 1::2].T
        bwd[0, x, :, 0, :, x] = even[:, 0::2]
        bwd[0, x, :, 1, :, x] = even[:, 1::2]
        bwd[1, x, :, 0, :, x] = odd[:, 1::2]
        bwd[1, x, :, 1, :, x] = odd[:, 0::2]
    along_x = np.zeros((2, SIDE, RING, 2, 4))
    for pick in range(2):
        along_x[pick, :, :, pick, :] = v.T.reshape(SIDE, RING, 4)
    rows = np.arange(SIDE).reshape(RING, 2, 1, 2, 1)
    spectrum = values[rows] + values.reshape(1, 1, SIDE, 1, 1) + values.reshape(1, 1, 1, 1, SIDE)
    return dict(
        z_fwd=halves(along_z),
        z_bwd=halves(along_z.T),
        y_fwd=halves(fwd.reshape(256, 256)),
        y_bwd=halves(bwd.reshape(256, 256)),
        x_fwd=halves(along_x.reshape(ROW, ROW)),
        x_bwd=halves(along_x.reshape(ROW, ROW).T),
        spectrum=spectrum.reshape(RING, ROW, ROW).astype(np.float32),
    )


def split(value):
    high = value.astype(BF16)
    return high, (value - high.astype(F32)).astype(BF16)


def mm(left, right):
    return jnp.dot(left, right, preferred_element_type=F32)


def left_mul(table, value):
    high, low = split(value)
    return mm(table[0], high) + mm(table[0], low) + mm(table[1], high)


def right_mul(value, table):
    high, low = split(value)
    return mm(high, table[0]) + mm(low, table[0]) + mm(high, table[1])


def mix_rows(table, value):
    swapped = jnp.concatenate([value[:, HALF:], value[:, :HALF]], axis=1)
    both = left_mul(table, jnp.concatenate([value, swapped], axis=0))
    lane = lax.broadcasted_iota(jnp.int32, (ROW, ROW), 1)
    return jnp.where(lane < HALF, both[:ROW], both[ROW:])


def vmem_call(kernel, outs, operands, scalars=0, scratch=(), alias=None):
    whole = pl.BlockSpec(memory_space=pltpu.VMEM)
    smem = pl.BlockSpec(memory_space=pltpu.SMEM)
    return pl.pallas_call(
        kernel,
        out_shape=outs,
        in_specs=[smem] * scalars + [whole] * (len(operands) - scalars),
        out_specs=[whole] * len(outs),
        scratch_shapes=list(scratch),
        input_output_aliases=alias or {},
        compiler_params=pltpu.CompilerParams(vmem_limit_bytes=VMEM_LIMIT),
    )(*operands)


def struct(shape, dtype):
    return jax.ShapeDtypeStruct(shape, dtype)


def owner_of(source):
    owner = lax.shift_right_logical(source, 2)
    return lax.shift_right_logical(owner, 1), lax.bitwise_and(owner, 1), lax.bitwise_and(source, 3)


def ring(value):
    return lax.bitwise_and(value, RING - 1)


def each_want(pair_src, residue, x):
    for turn in range(4):
        band = 2 * (4 * turn + residue) + x
        for slot in range(4):
            block, k = slot // 2, slot % 2
            z_own, x_own, row = owner_of(pair_src[block, 2 * band + k])
            yield 4 * turn + slot, z_own, lax.bitwise_xor(x_own, x), 4 * block + row


def steps_of(core):
    return 1, -1, jnp.where(core == 0, 2, -2)


def pack_wanted_kernel(place, pair_src, own, other, *outs):
    z, x, core, first = place[0], place[1], place[2], place[3]
    for out, step in zip(outs, steps_of(core)):
        count = -first
        for _, z_own, side, row in each_want(pair_src, lax.bitwise_and(z + step, 3), x):
            mine = z_own == z
            fits = jnp.logical_and(mine, jnp.logical_and(count >= 0, count < CAP))
            for rows, where in ((own, 0), (other, 1)):

                @pl.when(jnp.logical_and(fits, side == where))
                def _():
                    out[count] = rows[row]

            count = count + mine.astype(jnp.int32)


def place_wanted_kernel(place, pair_src, own, other, near1, near2, near3, before, out):
    z, x, core, first = place[0], place[1], place[2], place[3]
    del before
    steps = steps_of(core)
    counts = [-first] * 3
    for index, z_own, side, row in each_want(pair_src, lax.bitwise_and(z, 3), x):
        for rows, where in ((own, 0), (other, 1)):

            @pl.when(jnp.logical_and(z_own == z, side == where))
            def _():
                out[index] = rows[row]

        for n, rows in enumerate((near1, near2, near3)):
            theirs = z_own == ring(z - steps[n])
            count = counts[n]

            @pl.when(jnp.logical_and(theirs, jnp.logical_and(count >= 0, count < CAP)))
            def _():
                out[index] = rows[count]

            counts[n] = count + theirs.astype(jnp.int32)


def density_kernel(reached, wanted, z_fwd, y_fwd, source_rows, spectra):
    for p in range(4):
        row = reached[p].astype(F32)
        for turn in range(1, 4):
            row = row + reached[4 * turn + p].astype(F32)
        source_rows[p] = row.astype(BF16)
        density = row * wanted[p].astype(F32)
        mixed = mix_rows(y_fwd, right_mul(density, z_fwd)).astype(spectra.dtype)
        for copy in range(4):
            spectra[4 * copy + p] = mixed


def solve_kernel(quarter, slabs, spectrum, x_fwd, x_bwd, out, first, residual, direction):
    def dot_of(value):
        return jnp.sum(value.reshape(RING, 8, ROW), axis=0)

    zero = jnp.zeros((8, ROW), F32)

    def start(j, carry):
        norm, power = carry
        part = slabs[:, pl.ds(pl.multiple_of(8 * j, 8), 8), :].reshape(ROW, ROW)
        value = mm(x_fwd[0], part) + mm(x_fwd[1], part)
        first[j] = value
        square = value * value
        return norm + dot_of(square), power + dot_of(square * spectrum[j])

    norm, power = lax.fori_loop(0, RING, start, (zero, zero), unroll=2)
    norm, power = jnp.sum(norm), jnp.sum(power)
    steps, ratios = [norm / power], [jnp.float32(0.0)]
    for sweep in range(SWEEPS - 1):
        step, ratio = steps[-1], ratios[-1]

        def advance(j, carry, sweep=sweep, step=step, ratio=ratio):
            new, power = carry
            lam = spectrum[j]
            if sweep == 0:
                d = first[j]
                r = d - step * (lam * d)
            else:
                d = residual[j] + ratio * (first[j] if sweep == 1 else direction[j])
                r = residual[j] - step * (lam * d)
            if sweep > 0:
                direction[j] = d
            residual[j] = r
            square = r * r
            return new + dot_of(square), power + dot_of(square * lam)

        new, power = lax.fori_loop(0, RING, advance, (zero, zero), unroll=2)
        new, power = jnp.sum(new), jnp.sum(power)
        ratio = new / norm
        steps.append(new / (power - ratio * new / step))
        ratios.append(ratio)
        norm = new

    for jj in range(4):
        j = 4 * quarter[0] + jj
        lam, r = spectrum[j], first[j]
        d, total = r, steps[0] * r
        for sweep in range(1, SWEEPS):
            r = r - steps[sweep - 1] * (lam * d)
            d = r + ratios[sweep] * d
            total = total + steps[sweep] * d
        part = left_mul(x_bwd, total)
        out[:, 8 * jj : 8 * jj + 8, :] = part.reshape(RING, 8, ROW).astype(out.dtype)


def term_kernel(pair_tgt, spectra, source_rows, wanted, z_bwd, y_bwd, target_rows, terms, held):
    for p in range(4):
        rows = jnp.concatenate([spectra[4 * q + p].astype(F32) for q in range(4)], axis=0)
        potential = right_mul(mix_rows(y_bwd, rows), z_bwd)
        term = (-potential * wanted[p].astype(F32)).astype(BF16)
        for turn in range(4):
            terms[4 * turn + p] = term
        held[p] = -potential * source_rows[p].astype(F32)
    for p in range(4):
        same = jnp.zeros((ROW, ROW), F32)
        for other in range(4):
            hit = pair_tgt[p // 2, p % 2] == pair_tgt[other // 2, other % 2]
            same = same + jnp.where(hit, held[other], 0.0)
        target_rows[p] = same.astype(BF16)


def pack_terms_kernel(place, pair_src, terms, *outs):
    z, x, core, first = place[0], place[1], place[2], place[3]
    for out, step in zip(outs, steps_of(core)):
        count = -first
        for index, z_own, _, _ in each_want(pair_src, lax.bitwise_and(z, 3), x):
            theirs = z_own == ring(z + step)

            @pl.when(jnp.logical_and(theirs, jnp.logical_and(count >= 0, count < CAP)))
            def _():
                out[count] = terms[index]

            count = count + theirs.astype(jnp.int32)


def add_terms_kernel(place, pair_src, terms, near1, near2, near3, before, total):
    z, x, core, first = place[0], place[1], place[2], place[3]
    total[...] = before[...]
    for index, z_own, side, row in each_want(pair_src, lax.bitwise_and(z, 3), x):

        @pl.when(jnp.logical_and(z_own == z, first == 0))
        def _():
            at = 8 * side + row
            total[at] = total[at] + terms[index].astype(F32)

    for rows, step in zip((near1, near2, near3), steps_of(core)):
        count = -first
        for _, z_own, side, row in each_want(pair_src, lax.bitwise_and(z - step, 3), x):
            mine = z_own == z

            @pl.when(jnp.logical_and(mine, jnp.logical_and(count >= 0, count < CAP)))
            def _():
                at = 8 * side + row
                total[at] = total[at] + rows[count].astype(F32)

            count = count + mine.astype(jnp.int32)


AXES = ("band", "dom")


def shift(value, steps, mirror=False):
    pairs = []
    for z in range(RING):
        for x in range(2):
            for dom in range(16):
                go = -steps if mirror and dom % 2 else steps
                there = 2 * ((z + go) % RING) + x
                pairs.append(((2 * z + x) * 16 + dom, there * 16 + dom))
    return lax.ppermute(value, AXES, pairs)


def across(value):
    return lax.ppermute(value, "band", [(i, i ^ 1) for i in range(32)])


def hand_over(values):
    plus, minus, two = values
    return shift(plus, 1), shift(minus, -1), shift(two, 2, True)


def along_ring(value):
    groups = [[2 * (4 * turn + rest) + x for turn in range(4)] for rest in range(4) for x in range(2)]
    return lax.all_to_all(value, "band", 0, 0, axis_index_groups=groups, tiled=True)


def rounds_of(pair_src):
    group = jnp.arange(pair_src.shape[1], dtype=jnp.int32) // 2
    z, x = group // 2, group % 2
    z_own = pair_src // 8
    key = (z_own * 8 + (z % 4) * 2 + x).reshape(-1)
    moves = ((z_own - z) % 4 != 0).astype(jnp.int32).reshape(-1)
    shared = moves * jnp.sum((key[:, None] == key[None, :]).astype(jnp.int32), axis=1)
    return jnp.maximum(1, (jnp.max(shared) + CAP - 1) // CAP)


def per_device(targets, sources, pair_tgt, pair_src):
    table = {name: jnp.asarray(value) for name, value in tables().items()}
    band, dom = lax.axis_index("band"), lax.axis_index("dom")
    quarter = (dom // 4).astype(jnp.int32).reshape(1)
    rounds = rounds_of(pair_src)
    packet = struct((CAP, ROW, ROW), BF16)
    sixteen = struct((16, ROW, ROW), BF16)

    def place_in(turn):
        return jnp.stack([band // 2, band % 2, dom % 2, CAP * turn]).astype(jnp.int32)

    own = sources.reshape(8, ROW, ROW)
    other = across(own)

    def deliver(turn, before):
        scalars = (place_in(turn), pair_src)
        packed = vmem_call(pack_wanted_kernel, [packet] * 3, scalars + (own, other), scalars=2)
        operands = scalars + (own, other) + hand_over(packed) + (before,)
        return vmem_call(place_wanted_kernel, [sixteen], operands, scalars=2, alias={7: 0})[0]

    picked = lax.fori_loop(0, rounds, deliver, jnp.zeros((16, ROW, ROW), BF16))
    reached = along_ring(picked)

    ids = pair_tgt.reshape(4)
    wanted = targets[ids].reshape(4, ROW, ROW)
    four = struct((4, ROW, ROW), BF16)
    source_rows, spectra = vmem_call(
        density_kernel,
        [four, sixteen],
        (reached, wanted, table["z_fwd"], table["y_fwd"]),
    )
    slabs = lax.all_to_all(spectra, "dom", 0, 0, tiled=True)
    state = pltpu.VMEM((RING, ROW, ROW), F32)
    (solved,) = vmem_call(
        solve_kernel,
        [struct((16, 32, ROW), F32)],
        (quarter, slabs, table["spectrum"], table["x_fwd"], table["x_bwd"]),
        scalars=1,
        scratch=(state, state, state),
    )
    back = lax.all_to_all(solved, "dom", 0, 0, tiled=True)
    target_rows, terms = vmem_call(
        term_kernel,
        [four, sixteen],
        (pair_tgt, back, source_rows, wanted, table["z_bwd"], table["y_bwd"]),
        scalars=1,
        scratch=(pltpu.VMEM((4, ROW, ROW), F32),),
    )

    gathered = along_ring(terms)

    def collect(turn, before):
        scalars = (place_in(turn), pair_src)
        packed = vmem_call(pack_terms_kernel, [packet] * 3, scalars + (gathered,), scalars=2)
        operands = scalars + (gathered,) + hand_over(packed) + (before,)
        outs = [struct((16, ROW, ROW), F32)]
        return vmem_call(add_terms_kernel, outs, operands, scalars=2, alias={6: 0})[0]

    total = lax.fori_loop(0, rounds, collect, jnp.zeros((16, ROW, ROW), F32))
    partner = across(total[8:].astype(BF16))
    owned = (total[:8] + partner.astype(F32)).astype(BF16).reshape(sources.shape)

    flat = target_rows.reshape(4, targets.shape[1])
    slots = jnp.arange(targets.shape[0], dtype=jnp.int32)[:, None]
    summed = jnp.zeros(targets.shape, BF16)
    for p in range(4):
        summed = jnp.where(slots == ids[p], flat[p][None, :], summed)
    return summed, owned


def solution(mesh):
    return jax.shard_map(
        per_device,
        mesh=mesh,
        in_specs=(P("band", "dom"), P(None, "band", "dom"), P(None, "band"), P()),
        out_specs=(P("band", "dom"), P(None, "band", "dom")),
        check_vma=False,
    )
```

time: 207 us -> 188 us (0.908); the launches traced: 206 us -> 184 us
  waiting for transfers between devices: 85.2 us -> 65.5 us
  starting transfers between devices: 91.6 us -> 74.3 us
  blocking collectives: 0 us -> 12.5 us
  local copies, waits for them, and re-layouts: 4.47 us -> 7.66 us
    ppermute x12 -> x6, waiting for transfers between devices: 57.7 us -> 9.79 us  [shift(): return lax.ppermute(value, AXES, pairs)]
    all_to_all x1 -> x2, waiting for transfers between devices: 8.01 us -> 39.5 us  [along_ring(): lax.all_to_all(value, 'band', 0, 0, axis_index_groups=groups, tiled=True)]
    ppermute x12 -> x6, starting transfers between devices: 73.4 us -> 43.7 us  [shift(): return lax.ppermute(value, AXES, pairs)]
    all_to_all x0 -> x1, blocking collectives: none -> 12.5 us  [per_device(): back = lax.all_to_all(solved, 'dom', 0, 0, tiled=True)]
    all_to_all x1 -> x2, starting transfers between devices: 4.62 us -> 16.9 us  [along_ring(): lax.all_to_all(value, 'band', 0, 0, axis_index_groups=groups, tiled=True)]
    ppermute x2, waiting for transfers between devices: 8.23 us -> 4.86 us  [across(): return lax.ppermute(value, 'band', [(i, i ^ 1) for i in range(32)])]
    pallas_call x5 -> x7, Pallas kernels: 19.5 us -> 18 us  [vmem_call(): pl.pallas_call(kernel, out_shape=outs, in_specs=[smem] * scalars + [whole...]
  transfers between devices with their start and end apart: 16 -> 11, of which waited for: 13 -> 8; matrix products, arithmetic and copies ran while one was open for 3% -> 3% of each run, Pallas kernels for 0% -> 0%
where the time goes in v2:
time: 188 us; the launch traced here: 184 us
  starting transfers between devices  74.3 us (40%)
  waiting for transfers between devices  65.5 us (35%)
  Pallas kernels  18 us (10%)
  blocking collectives  12.5 us (7%)
  local copies, waits for them, and re-layouts  7.66 us (4%)
  other arithmetic  4.85 us (3%)
    ppermute x6, starting transfers between devices, shift(): return lax.ppermute(value, AXES, pairs)  43.7 us
    all_to_all x2, waiting for transfers between devices, along_ring(): lax.all_to_all(value, 'band', 0, 0, axis_index_groups=groups, tiled=True)  39.5 us
    pallas_call x7, Pallas kernels, vmem_call(): pl.pallas_call(kernel, out_shape=outs, in_specs=[smem] * scalars + [whole...  18 us
    all_to_all x2, starting transfers between devices, along_ring(): lax.all_to_all(value, 'band', 0, 0, axis_index_groups=groups, tiled=True)  16.9 us
    all_to_all x1, blocking collectives, per_device(): back = lax.all_to_all(solved, 'dom', 0, 0, tiled=True)  12.5 us
    all_to_all x1, waiting for transfers between devices, per_device(): slabs = lax.all_to_all(spectra, 'dom', 0, 0, tiled=True)  11.3 us
    ppermute x6, waiting for transfers between devices, shift(): return lax.ppermute(value, AXES, pairs)  9.79 us
    all_to_all x1, starting transfers between devices, per_device(): slabs = lax.all_to_all(spectra, 'dom', 0, 0, tiled=True)  7.57 us
  transfers between devices with their start and end apart: 11, of which 8 were waited for; matrix products, arithmetic and copies ran while one was open for 3% of the time, Pallas kernels for 0%

profile of v2, /device:TPU:1, one launch (start us, length us, event | category | flops | bytes accessed | tf_op | source)
XLA Modules:
  0.0 184.5 jit_solution(15291295502530132205)
XLA Ops:
  0.6 1.3 reshape.139
  2.0 3.9 %collective-permute-start.6 = (bf16[8,128,128]{2,1,0:T(8,128)(2,1)S(1)}, bf16[8,128,128]{2,1,0:T(8,128)(2,1)S(1)}, u32[]{:S(2)}, u32[]{:S(2)}) collective-permute-start(bf16[8,128,128]{2,1,0:T(8,128)(2,1)S(1)} %reshape.139), channel_id=1, source_target_pairs={{0,16},{16,0},{32,48},{48,32},{64,80},{80,64},{96,112},{112,96},{1... | collective-permute-start | bytes 786440 | tf_op jit(solution)/shard_map/ppermute | solution.py:306
  8.4 1.3 collective-permute-done.6
  9.8 25.8 %while.28 = (s32[]{:T(128)}, bf16[16,128,128]{2,1,0:T(8,128)(2,1)S(1)}, s32[]{:T(128)}, s32[]{:T(128)}, s32[]{:T(128)}, /*index=5*/s32[]{:T(128)}, s32[2,64]{1,0...) while((s32[]{:T(128)}, ...), condition=%wide.region_3.4_spmd, body=%wide.region_2.3_spmd.sunk | while | flops 15 | bytes 2359569 | solution.py:349
  9.9 1.5 body.20
  11.4 5.7 %collective-permute-start = (bf16[6,128,128]{2,1,0:T(8,128)(2,1)S(1)}, bf16[6,128,128]{2,1,0:T(8,128)(2,1)S(1)}, u32[]{:S(2)}, u32[]{:S(2)}) collective-permute-start(bf16[6,128,128]{2,1,0:T(8,128)(2,1)S(1)} %get-tuple-element.752), channel_id=1, source_target_pairs={{0,32},{1,33},{2,34},{3,35},{4,36},{5,37},{6,38},{7,39},{8,40},{9,... | collective-permute-start | bytes 589832 | tf_op jit(solution)/shard_map/while/body/ppermute | solution.py:302
  17.1 9.5 %collective-permute-start.1 = (bf16[6,128,128]{2,1,0:T(8,128)(2,1)S(1)}, bf16[6,128,128]{2,1,0:T(8,128)(2,1)S(1)}, u32[]{:S(2)}, u32[]{:S(2)}) collective-permute-start(bf16[6,128,128]{2,1,0:T(8,128)(2,1)S(1)} %get-tuple-element.753), channel_id=1, source_target_pairs={{0,480},{1,481},{2,482},{3,483},{4,484},{5,485},{6,486},{7,487},{8... | collective-permute-start | bytes 589832 | tf_op jit(solution)/shard_map/while/body/ppermute | solution.py:302
  26.6 3.8 %collective-permute-start.2 = (bf16[6,128,128]{2,1,0:T(8,128)(2,1)S(1)}, bf16[6,128,128]{2,1,0:T(8,128)(2,1)S(1)}, u32[]{:S(2)}, u32[]{:S(2)}) collective-permute-start(bf16[6,128,128]{2,1,0:T(8,128)(2,1)S(1)} %get-tuple-element.754), channel_id=1, source_target_pairs={{0,64},{1,449},{2,66},{3,451},{4,68},{5,453},{6,70},{7,455},{8,72}... | collective-permute-start | bytes 589832 | tf_op jit(solution)/shard_map/while/body/ppermute | solution.py:302
  30.5 3.9 %collective-permute-done.2.near3 = bf16[6,128,128]{2,1,0:T(8,128)(2,1)S(1)} collective-permute-done((bf16[6,128,128]{2,1,0:T(8,128)(2,1)S(1)}, bf16[6,128,128]{2,1,0:T(8,128)(2,1)S(1)}, u32[]{:S(2)}, u32[]{:S(2)}) %collective-permute-start.2) | collective-permute-done | bytes 196640 | tf_op jit(solution)/shard_map/while/body/ppermute | solution.py:302
  34.3 1.2 body.21
  36.4 10.5 %all-to-all-start = ((bf16[16,128,128]{2,1,0:T(8,128)(2,1)}), bf16[16,128,128]{2,1,0:T(8,128)(2,1)S(1)}, u32[]{:S(2)}, u32[]{:S(2)}) async-start(bf16[16,128,128]{2,1,0:T(8,128)(2,1)} %copy-done.10), calls=%async_computation | async-start | bytes 1048576 | tf_op jit(solution)/shard_map/all_to_all | solution.py:316
  47.7 26.3 %all-to-all-done.reached = bf16[16,128,128]{2,1,0:T(8,128)(2,1)S(1)} async-done(((bf16[16,128,128]{2,1,0:T(8,128)(2,1)}), bf16[16,128,128]{2,1,0:T(8,128)(2,1)S(1)}, u32[]{:S(2)}, u32[]{:S(2)}) %all-to-all-start) | async-done | bytes 524320 | tf_op jit(solution)/shard_map/all_to_all | solution.py:316
  74.0 2.3 %shard_map.122 = (bf16[4,128,128]{2,1,0:T(8,128)(2,1)S(1)}, bf16[16,128,128]{2,1,0:T(8,128)(2,1)}) custom-call(bf16[16,128,128]{2,1,0:T(8,128)(2,1)S(1)} %all-to-all-done.reached, bf16[4,128,128]{2,1,0:T(8,128)(2,1)S(1)} %bitcast.43, bf16[2,128,128]{2,1,0:T(8,128)(2,1)S(1)} %copy-done.7, bf16[2,256,256]{2,1,0:T(8,128)(2,1)S(1)} %copy-done.3), custom_call_target="tpu_custom_call" | custom-call | tf_op jit(solution)/shard_map/pallas_call | solution.py:96
  76.3 7.6 %all-to-all-start.1 = ((bf16[16,128,128]{2,1,0:T(8,128)(2,1)}), bf16[16,128,128]{2,1,0:T(8,128)(2,1)S(1)}, u32[]{:S(2)}, u32[]{:S(2)}) async-start(bf16[16,128,128]{2,1,0:T(8,128)(2,1)} %get-tuple-element.593), calls=%async_computation.1 | async-start | bytes 1048576 | tf_op jit(solution)/shard_map/all_to_all | solution.py:360
  83.8 11.3 %all-to-all-done.1.slabs = bf16[16,128,128]{2,1,0:T(8,128)(2,1)S(1)} async-done(((bf16[16,128,128]{2,1,0:T(8,128)(2,1)}), bf16[16,128,128]{2,1,0:T(8,128)(2,1)S(1)}, u32[]{:S(2)}, u32[]{:S(2)}) %all-to-all-start.1) | async-done | bytes 524320 | tf_op jit(solution)/shard_map/all_to_all | solution.py:360
  95.2 6.1 %shard_map.123 = f32[16,32,128]{2,1,0:T(8,128)S(1)} custom-call(s32[1]{0:T(128)} %bitcast.9.quarter, bf16[16,128,128]{2,1,0:T(8,128)(2,1)S(1)} %all-to-all-done.1.slabs, f32[16,128,128]{2,1,0:T(8,128)S(1)} %copy-done.1, bf16[2,128,128]{2,1,0:T(8,128)(2,1)S(1)} %copy-done.4, bf16[2,128,128]{2,1,0:T(8,128)(2,1)S(1)} %copy-done.5), custom_call_target="tpu_custom_call" | custom-call | tf_op jit(solution)/shard_map/pallas_call | solution.py:96
  101.3 12.5 %all_to_all.20.spectra = f32[16,32,128]{2,1,0:T(8,128)S(1)} all-to-all(f32[16,32,128]{2,1,0:T(8,128)S(1)} %shard_map.123), channel_id=1, replica_groups=mesh['band'=32,'dom'=16] {'dom'}, dimensions={0} | all-to-all | bytes 524288 | tf_op jit(solution)/shard_map/all_to_all | solution.py:369
  113.8 2.8 %shard_map.124 = (bf16[4,128,128]{2,1,0:T(8,128)(2,1)S(1)}, bf16[16,128,128]{2,1,0:T(8,128)(2,1)}) custom-call(s32[2,2]{1,0:T(2,128)S(1)} %copy-done.8, f32[16,32,128]{2,1,0:T(8,128)S(1)} %all_to_all.20.spectra, bf16[4,128,128]{2,1,0:T(8,128)(2,1)S(1)} %get-tuple-element.594.source_rows, bf16[4,128,128]{2,1,0:T(8,128)(2,1)S(1)} %bitcast.44, ...), custom_call_target="tpu_custom_call" | custom-call | tf_op jit(solution)/shard_map/pallas_call | solution.py:96
  116.6 6.4 %all-to-all-start.3 = ((bf16[16,128,128]{2,1,0:T(8,128)(2,1)}), bf16[16,128,128]{2,1,0:T(8,128)(2,1)S(1)}, u32[]{:S(2)}, u32[]{:S(2)}) async-start(bf16[16,128,128]{2,1,0:T(8,128)(2,1)} %get-tuple-element.596), calls=%async_computation.3 | async-start | bytes 1048576 | tf_op jit(solution)/shard_map/all_to_all | solution.py:316
  123.7 1.3 iota_compare_fusion.2
  124.9 1.2 iota_compare_fusion
  126.2 13.2 %all-to-all-done.3 = bf16[16,128,128]{2,1,0:T(8,128)(2,1)S(1)} async-done(((bf16[16,128,128]{2,1,0:T(8,128)(2,1)}), bf16[16,128,128]{2,1,0:T(8,128)(2,1)S(1)}, u32[]{:S(2)}, u32[]{:S(2)}) %all-to-all-start.3) | async-done | bytes 524320 | tf_op jit(solution)/shard_map/all_to_all | solution.py:316
  140.5 34.8 %while.29 = (s32[]{:T(128)}, f32[16,128,128]{2,1,0:T(8,128)}, s32[]{:T(128)}, s32[]{:T(128)}, s32[]{:T(128)}, /*index=5*/s32[]{:T(128)}, s32[2,64]{1,0:T(2,128)S...) while((s32[]{:T(128)}, f32[16,128,128]{2,1,0:T(8,128)}, s32[]{:T(128)}, s32[]{:T(128)}, s32[]{:T(128)}, ...), condition=%wide.region_5.6_spmd, body=%wide.region_4.5_spmd.sunk | while | flops 15 | bytes 2359561 | solution.py:387
  141.7 15.7 %collective-permute-start.3 = (bf16[6,128,128]{2,1,0:T(8,128)(2,1)S(1)}, bf16[6,128,128]{2,1,0:T(8,128)(2,1)S(1)}, u32[]{:S(2)}, u32[]{:S(2)}) collective-permute-start(bf16[6,128,128]{2,1,0:T(8,128)(2,1)S(1)} %get-tuple-element.763), channel_id=1, source_target_pairs={{0,32},{1,33},{2,34},{3,35},{4,36},{5,37},{6,38},{7,39},{8,40},{9,... | collective-permute-start | bytes 589832 | tf_op jit(solution)/shard_map/while/body/ppermute | solution.py:302
  157.4 5.9 %collective-permute-start.4 = (bf16[6,128,128]{2,1,0:T(8,128)(2,1)S(1)}, bf16[6,128,128]{2,1,0:T(8,128)(2,1)S(1)}, u32[]{:S(2)}, u32[]{:S(2)}) collective-permute-start(bf16[6,128,128]{2,1,0:T(8,128)(2,1)S(1)} %get-tuple-element.764), channel_id=1, source_target_pairs={{0,480},{1,481},{2,482},{3,483},{4,484},{5,485},{6,486},{7,487},{8... | collective-permute-start | bytes 589832 | tf_op jit(solution)/shard_map/while/body/ppermute | solution.py:302
  163.3 3.1 %collective-permute-start.5 = (bf16[6,128,128]{2,1,0:T(8,128)(2,1)S(1)}, bf16[6,128,128]{2,1,0:T(8,128)(2,1)S(1)}, u32[]{:S(2)}, u32[]{:S(2)}) collective-permute-start(bf16[6,128,128]{2,1,0:T(8,128)(2,1)S(1)} %get-tuple-element.765), channel_id=1, source_target_pairs={{0,64},{1,449},{2,66},{3,451},{4,68},{5,453},{6,70},{7,455},{8,72}... | collective-permute-start | bytes 589832 | tf_op jit(solution)/shard_map/while/body/ppermute | solution.py:302
  167.0 5.3 %collective-permute-done.5.near3 = bf16[6,128,128]{2,1,0:T(8,128)(2,1)S(1)} collective-permute-done((bf16[6,128,128]{2,1,0:T(8,128)(2,1)S(1)}, bf16[6,128,128]{2,1,0:T(8,128)(2,1)S(1)}, u32[]{:S(2)}, u32[]{:S(2)}) %collective-permute-start.5) | collective-permute-done | bytes 196640 | tf_op jit(solution)/shard_map/while/body/ppermute | solution.py:302
  172.3 3.0 %body.23 = f32[16,128,128]{2,1,0:T(8,128)} custom-call(s32[4]{0:T(128)S(1)} %pad_add_fusion.5.place, s32[2,64]{1,0:T(2,128)S(1)} %get-tuple-element.825.pair_src, bf16[16,128,128]{2,1,0:T(8,128)(2,1)S(1)} %get-tuple-element.826.terms, bf16[6,128,128]{2,1,0:T(8,128)(2,1)S(1)} %collective-permute-done.3.near1, ...), custom_call_target="tpu_custom_call", output_to_operand_aliasing={{}: (6, {})} | custom-call | tf_op jit(solution)/shard_map/while/body/pallas_call | solution.py:96
  175.3 1.2 slice.54
  176.5 2.3 %collective-permute-start.7 = (bf16[8,128,128]{2,1,0:T(8,128)(2,1)S(1)}, bf16[8,128,128]{2,1,0:T(8,128)(2,1)S(1)}, u32[]{:S(2)}, u32[]{:S(2)}) collective-permute-start(bf16[8,128,128]{2,1,0:T(8,128)(2,1)S(1)} %slice.54), channel_id=1, source_target_pairs={{0,16},{16,0},{32,48},{48,32},{64,80},{80,64},{96,112},{112,96},{1... | collective-permute-start | bytes 786440 | tf_op jit(solution)/shard_map/ppermute | solution.py:306
  178.8 1.3 select_select_fusion
  180.1 3.5 %collective-permute-done.7 = bf16[8,128,128]{2,1,0:T(8,128)(2,1)S(1)} collective-permute-done((bf16[8,128,128]{2,1,0:T(8,128)(2,1)S(1)}, bf16[8,128,128]{2,1,0:T(8,128)(2,1)S(1)}, u32[]{:S(2)}, u32[]{:S(2)}) %collective-permute-start.7) | collective-permute-done | bytes 262176 | tf_op jit(solution)/shard_map/ppermute | solution.py:306
  (50 shorter events, 8.0 us)
Async XLA Ops:
  0.6 46.3 %copy-start = (bf16[32,16384]{1,0:T(8,128)(2,1)S(1)}, bf16[32,16384]{1,0:T(8,128)(2,1)}, u32[]{:S(2)}) copy-start(bf16[32,16384]{1,0:T(8,128)(2,1)} %param.15) | copy-start | bytes 3145732
  2.0 7.7 %collective-permute-start.6 = (bf16[8,128,128]{2,1,0:T(8,128)(2,1)S(1)}, bf16[8,128,128]{2,1,0:T(8,128)(2,1)S(1)}, u32[]{:S(2)}, u32[]{:S(2)}) collective-permute-start(bf16[8,128,128]{2,1,0:T(8,128)(2,1)S(1)} %reshape.139), channel_id=1, source_target_pairs={{0,16},{16,0},{32,48},{48,32},{64,80},{80,64},{96,112},{112,96},{1... | collective-permute-start | bytes 786440 | tf_op jit(solution)/shard_map/ppermute | solution.py:306
  5.9 0.7 copy-start.11
  11.4 19.1 %collective-permute-start = (bf16[6,128,128]{2,1,0:T(8,128)(2,1)S(1)}, bf16[6,128,128]{2,1,0:T(8,128)(2,1)S(1)}, u32[]{:S(2)}, u32[]{:S(2)}) collective-permute-start(bf16[6,128,128]{2,1,0:T(8,128)(2,1)S(1)} %get-tuple-element.752), channel_id=1, source_target_pairs={{0,32},{1,33},{2,34},{3,35},{4,36},{5,37},{6,38},{7,39},{8,40},{9,... | collective-permute-start | bytes 589832 | tf_op jit(solution)/shard_map/while/body/ppermute | solution.py:302
  17.1 13.3 %collective-permute-start.1 = (bf16[6,128,128]{2,1,0:T(8,128)(2,1)S(1)}, bf16[6,128,128]{2,1,0:T(8,128)(2,1)S(1)}, u32[]{:S(2)}, u32[]{:S(2)}) collective-permute-start(bf16[6,128,128]{2,1,0:T(8,128)(2,1)S(1)} %get-tuple-element.753), channel_id=1, source_target_pairs={{0,480},{1,481},{2,482},{3,483},{4,484},{5,485},{6,486},{7,487},{8... | collective-permute-start | bytes 589832 | tf_op jit(solution)/shard_map/while/body/ppermute | solution.py:302
  26.6 7.7 %collective-permute-start.2 = (bf16[6,128,128]{2,1,0:T(8,128)(2,1)S(1)}, bf16[6,128,128]{2,1,0:T(8,128)(2,1)S(1)}, u32[]{:S(2)}, u32[]{:S(2)}) collective-permute-start(bf16[6,128,128]{2,1,0:T(8,128)(2,1)S(1)} %get-tuple-element.754), channel_id=1, source_target_pairs={{0,64},{1,449},{2,66},{3,451},{4,68},{5,453},{6,70},{7,455},{8,72}... | collective-permute-start | bytes 589832 | tf_op jit(solution)/shard_map/while/body/ppermute | solution.py:302
  35.6 0.8 copy-start.10
  36.4 10.5 %copy-start.8 = (s32[2,2]{1,0:T(2,128)S(1)}, s32[2,2]{1,0:T(2,128)}, u32[]{:S(2)}) copy-start(s32[2,2]{1,0:T(2,128)} %pair_tgt.1) | copy-start | bytes 52
  36.4 37.6 %all-to-all-start = ((bf16[16,128,128]{2,1,0:T(8,128)(2,1)}), bf16[16,128,128]{2,1,0:T(8,128)(2,1)S(1)}, u32[]{:S(2)}, u32[]{:S(2)}) async-start(bf16[16,128,128]{2,1,0:T(8,128)(2,1)} %copy-done.10), calls=%async_computation | async-start | bytes 1048576 | tf_op jit(solution)/shard_map/all_to_all | solution.py:316
  47.0 27.1 %copy-start.7 = (bf16[2,128,128]{2,1,0:T(8,128)(2,1)S(1)}, bf16[2,128,128]{2,1,0:T(8,128)(2,1)}, u32[]{:S(2)}) copy-start(bf16[2,128,128]{2,1,0:T(8,128)(2,1)} %constant.221.clone.z_fwd) | copy-start | bytes 196612
  47.6 26.4 %copy-start.3 = (bf16[2,256,256]{2,1,0:T(8,128)(2,1)S(1)}, bf16[2,256,256]{2,1,0:T(8,128)(2,1)}, u32[]{:S(2)}) copy-start(bf16[2,256,256]{2,1,0:T(8,128)(2,1)} %constant.223.clone.y_fwd) | copy-start | bytes 786436
  47.7 47.5 %copy-start.1 = (f32[16,128,128]{2,1,0:T(8,128)S(1)}, f32[16,128,128]{2,1,0:T(8,128)}, u32[]{:S(2)}) copy-start(f32[16,128,128]{2,1,0:T(8,128)} %constant.227.clone.spectrum) | copy-start | bytes 3145732
  76.3 18.9 %copy-start.4 = (bf16[2,128,128]{2,1,0:T(8,128)(2,1)S(1)}, bf16[2,128,128]{2,1,0:T(8,128)(2,1)}, u32[]{:S(2)}) copy-start(bf16[2,128,128]{2,1,0:T(8,128)(2,1)} %constant.225.clone.x_fwd) | copy-start | bytes 196612
  76.3 18.9 %copy-start.5 = (bf16[2,128,128]{2,1,0:T(8,128)(2,1)S(1)}, bf16[2,128,128]{2,1,0:T(8,128)(2,1)}, u32[]{:S(2)}) copy-start(bf16[2,128,128]{2,1,0:T(8,128)(2,1)} %constant.226.clone.x_bwd) | copy-start | bytes 196612
  76.3 18.9 %all-to-all-start.1 = ((bf16[16,128,128]{2,1,0:T(8,128)(2,1)}), bf16[16,128,128]{2,1,0:T(8,128)(2,1)S(1)}, u32[]{:S(2)}, u32[]{:S(2)}) async-start(bf16[16,128,128]{2,1,0:T(8,128)(2,1)} %get-tuple-element.593), calls=%async_computation.1 | async-start | bytes 1048576 | tf_op jit(solution)/shard_map/all_to_all | solution.py:360
  101.3 12.5 %copy-start.2 = (bf16[2,256,256]{2,1,0:T(8,128)(2,1)S(1)}, bf16[2,256,256]{2,1,0:T(8,128)(2,1)}, u32[]{:S(2)}) copy-start(bf16[2,256,256]{2,1,0:T(8,128)(2,1)} %constant.224.clone.y_bwd) | copy-start | bytes 786436
  101.3 12.5 %copy-start.6 = (bf16[2,128,128]{2,1,0:T(8,128)(2,1)S(1)}, bf16[2,128,128]{2,1,0:T(8,128)(2,1)}, u32[]{:S(2)}) copy-start(bf16[2,128,128]{2,1,0:T(8,128)(2,1)} %constant.222.clone.z_bwd) | copy-start | bytes 196612
  116.6 22.8 %all-to-all-start.3 = ((bf16[16,128,128]{2,1,0:T(8,128)(2,1)}), bf16[16,128,128]{2,1,0:T(8,128)(2,1)S(1)}, u32[]{:S(2)}, u32[]{:S(2)}) async-start(bf16[16,128,128]{2,1,0:T(8,128)(2,1)} %get-tuple-element.596), calls=%async_computation.3 | async-start | bytes 1048576 | tf_op jit(solution)/shard_map/all_to_all | solution.py:316
  141.7 24.7 %collective-permute-start.3 = (bf16[6,128,128]{2,1,0:T(8,128)(2,1)S(1)}, bf16[6,128,128]{2,1,0:T(8,128)(2,1)S(1)}, u32[]{:S(2)}, u32[]{:S(2)}) collective-permute-start(bf16[6,128,128]{2,1,0:T(8,128)(2,1)S(1)} %get-tuple-element.763), channel_id=1, source_target_pairs={{0,32},{1,33},{2,34},{3,35},{4,36},{5,37},{6,38},{7,39},{8,40},{9,... | collective-permute-start | bytes 589832 | tf_op jit(solution)/shard_map/while/body/ppermute | solution.py:302
  157.4 9.6 %collective-permute-start.4 = (bf16[6,128,128]{2,1,0:T(8,128)(2,1)S(1)}, bf16[6,128,128]{2,1,0:T(8,128)(2,1)S(1)}, u32[]{:S(2)}, u32[]{:S(2)}) collective-permute-start(bf16[6,128,128]{2,1,0:T(8,128)(2,1)S(1)} %get-tuple-element.764), channel_id=1, source_target_pairs={{0,480},{1,481},{2,482},{3,483},{4,484},{5,485},{6,486},{7,487},{8... | collective-permute-start | bytes 589832 | tf_op jit(solution)/shard_map/while/body/ppermute | solution.py:302
  163.3 9.0 %collective-permute-start.5 = (bf16[6,128,128]{2,1,0:T(8,128)(2,1)S(1)}, bf16[6,128,128]{2,1,0:T(8,128)(2,1)S(1)}, u32[]{:S(2)}, u32[]{:S(2)}) collective-permute-start(bf16[6,128,128]{2,1,0:T(8,128)(2,1)S(1)} %get-tuple-element.765), channel_id=1, source_target_pairs={{0,64},{1,449},{2,66},{3,451},{4,68},{5,453},{6,70},{7,455},{8,72}... | collective-permute-start | bytes 589832 | tf_op jit(solution)/shard_map/while/body/ppermute | solution.py:302
  175.3 8.3 %copy-start.9 = (f32[16,128,128]{2,1,0:T(8,128)S(1)}, f32[16,128,128]{2,1,0:T(8,128)}, u32[]{:S(2)}) copy-start(f32[16,128,128]{2,1,0:T(8,128)} %get-tuple-element.597) | copy-start | bytes 3145732
  176.5 7.1 %collective-permute-start.7 = (bf16[8,128,128]{2,1,0:T(8,128)(2,1)S(1)}, bf16[8,128,128]{2,1,0:T(8,128)(2,1)S(1)}, u32[]{:S(2)}, u32[]{:S(2)}) collective-permute-start(bf16[8,128,128]{2,1,0:T(8,128)(2,1)S(1)} %slice.54), channel_id=1, source_target_pairs={{0,16},{16,0},{32,48},{48,32},{64,80},{80,64},{96,112},{112,96},{1... | collective-permute-start | bytes 786440 | tf_op jit(solution)/shard_map/ppermute | solution.py:306

commit v3 on v2

v3 whole, which is shorter than its diff:
```python
import numpy as np
import jax
import jax.numpy as jnp
from jax import lax
from jax.experimental import pallas as pl
from jax.experimental.pallas import tpu as pltpu
from jax.sharding import PartitionSpec as P

SIDE = 64
SWEEPS = 8
RING = 16
STEPS = (1, -1, 2, -2, 3)
CAPS = (5, 5, 5, 5, 3)
ROW = 128
HALF = 64
VMEM_LIMIT = 48 * 1024 * 1024
F32 = jnp.float32
BF16 = jnp.bfloat16


def eigen_system():
    line = np.zeros((SIDE, SIDE))
    for delta, weight in ((0, 30.0), (1, -16.0), (2, 1.0)):
        for i in range(SIDE - delta):
            line[i, i + delta] = weight / 12.0
            line[i + delta, i] = weight / 12.0
    values, vectors = np.linalg.eigh(line)
    return values, vectors * np.where(vectors[0] < 0, -1.0, 1.0)[None, :]


def halves(matrix):
    high = np.asarray(matrix, np.float32).astype(jnp.bfloat16)
    low = (np.asarray(matrix, np.float64) - high.astype(np.float64)).astype(jnp.bfloat16)
    return np.stack([high, low])


def tables():
    values, v = eigen_system()
    along_z = np.kron(np.eye(2), v)
    even, odd = v[0::2], v[1::2]
    fwd = np.zeros((2, 32, 4, 2, 4, 32))
    bwd = np.zeros((2, 4, 32, 2, 32, 4))
    for x in range(4):
        fwd[0, :, x, 0, x, :] = even[:, 0::2].T
        fwd[0, :, x, 1, x, :] = odd[:, 0::2].T
        fwd[1, :, x, 0, x, :] = odd[:, 1::2].T
        fwd[1, :, x, 1, x, :] = even[:, 1::2].T
        bwd[0, x, :, 0, :, x] = even[:, 0::2]
        bwd[0, x, :, 1, :, x] = even[:, 1::2]
        bwd[1, x, :, 0, :, x] = odd[:, 1::2]
        bwd[1, x, :, 1, :, x] = odd[:, 0::2]
    along_x = np.zeros((2, SIDE, RING, 2, 4))
    for pick in range(2):
        along_x[pick, :, :, pick, :] = v.T.reshape(SIDE, RING, 4)
    rows = np.arange(SIDE).reshape(RING, 2, 1, 2, 1)
    spectrum = values[rows] + values.reshape(1, 1, SIDE, 1, 1) + values.reshape(1, 1, 1, 1, SIDE)
    return dict(
        z_fwd=halves(along_z),
        z_bwd=halves(along_z.T),
        y_fwd=halves(fwd.reshape(256, 256)),
        y_bwd=halves(bwd.reshape(256, 256)),
        x_fwd=halves(along_x.reshape(ROW, ROW)),
        x_bwd=halves(along_x.reshape(ROW, ROW).T),
        spectrum=spectrum.reshape(RING, ROW, ROW).astype(np.float32),
    )


def split(value):
    high = value.astype(BF16)
    return high, (value - high.astype(F32)).astype(BF16)


def mm(left, right):
    return jnp.dot(left, right, preferred_element_type=F32)


def left_mul(table, value):
    high, low = split(value)
    return mm(table[0], high) + mm(table[0], low) + mm(table[1], high)


def right_mul(value, table):
    high, low = split(value)
    return mm(high, table[0]) + mm(low, table[0]) + mm(high, table[1])


def mix_rows(table, value):
    swapped = jnp.concatenate([value[:, HALF:], value[:, :HALF]], axis=1)
    both = left_mul(table, jnp.concatenate([value, swapped], axis=0))
    lane = lax.broadcasted_iota(jnp.int32, (ROW, ROW), 1)
    return jnp.where(lane < HALF, both[:ROW], both[ROW:])


def vmem_call(kernel, outs, operands, scalars=0, scratch=()):
    whole = pl.BlockSpec(memory_space=pltpu.VMEM)
    smem = pl.BlockSpec(memory_space=pltpu.SMEM)
    return pl.pallas_call(
        kernel,
        out_shape=outs,
        in_specs=[smem] * scalars + [whole] * (len(operands) - scalars),
        out_specs=[whole] * len(outs),
        scratch_shapes=list(scratch),
        compiler_params=pltpu.CompilerParams(vmem_limit_bytes=VMEM_LIMIT),
    )(*operands)


def struct(shape, dtype):
    return jax.ShapeDtypeStruct(shape, dtype)


def owner_of(source):
    owner = lax.shift_right_logical(source, 2)
    return lax.shift_right_logical(owner, 1), lax.bitwise_and(owner, 1), lax.bitwise_and(source, 3)


def ring(value):
    return lax.bitwise_and(value, RING - 1)


def each_want(pair_src, relay, x, way, kinds=3):
    for kind, offset in enumerate((0, -5, 5)[:kinds]):
        band = 2 * ring(relay + offset * way) + x
        for slot in range(4):
            z_own, x_own, row = owner_of(pair_src[slot // 2, 2 * band + slot % 2])
            yield kind, slot, z_own, lax.bitwise_xor(x_own, x), 4 * (slot // 2) + row


def lanes_of(place, sign):
    z, x, way, turn = place[0], place[1], place[2], place[3]
    for n, (step, cap) in enumerate(zip(STEPS, CAPS)):
        there = ring(z + sign * step * way)
        yield n, there, -cap * turn, cap, (way, 3) if step < 3 else (way, 2)


def wants_at(place, pair_src, relay, lane):
    way, kinds = lane
    for want in each_want(pair_src, relay, place[1], way, kinds):
        if kinds == 3 or want[0] == 1:
            yield want


def fits(hit, count, cap):
    return jnp.logical_and(hit, jnp.logical_and(count >= 0, count < cap))


def copy_row(out, at, own, other, side, row):
    for rows, where in ((own, 0), (other, 1)):

        @pl.when(side == where)
        def _():
            out[at] = rows[row]


def pack_wanted_kernel(place, pair_src, own, other, *outs):
    for n, relay, count, cap, lane in lanes_of(place, -1):
        for _, _, z_own, side, row in wants_at(place, pair_src, relay, lane):
            mine = z_own == place[0]

            @pl.when(fits(mine, count, cap))
            def _():
                copy_row(outs[n], count, own, other, side, row)

            count = count + mine.astype(jnp.int32)


def place_wanted_kernel(place, pair_src, own, other, *refs):
    near, before, outs = refs[:5], refs[5:-3], refs[-3:]
    z = place[0]
    for old, out in zip(before, outs):
        out[...] = old[...]
    if not before:
        for kind, slot, z_own, side, row in each_want(pair_src, z, place[1], place[2]):

            @pl.when(z_own == z)
            def _():
                copy_row(outs[kind], slot, own, other, side, row)

    for n, owner, count, cap, lane in lanes_of(place, 1):
        for kind, slot, z_own, _, _ in wants_at(place, pair_src, z, lane):
            theirs = z_own == owner

            @pl.when(fits(theirs, count, cap))
            def _():
                outs[kind][slot] = near[n][count]

            count = count + theirs.astype(jnp.int32)


def density_kernel(place, pair_src, here, ahead, behind, wanted, z_fwd, y_fwd, source_rows, spectra):
    z, x, way = place[0], place[1], place[2]
    for p in range(4):
        z_own, _, _ = owner_of(pair_src[p // 2, 2 * (2 * z + x) + p % 2])
        away = ring(way * (z_own - z) + 2)
        for rows, least, most in ((here, 0, 4), (ahead, 5, 10), (behind, 11, 15)):

            @pl.when(jnp.logical_and(away >= least, away <= most))
            def _():
                source_rows[p] = rows[p]

        density = source_rows[p].astype(F32) * wanted[p].astype(F32)
        mixed = mix_rows(y_fwd, right_mul(density, z_fwd)).astype(spectra.dtype)
        for copy in range(4):
            spectra[4 * copy + p] = mixed


def solve_kernel(quarter, slabs, spectrum, x_fwd, x_bwd, out, first, residual, direction):
    def dot_of(value):
        return jnp.sum(value.reshape(RING, 8, ROW), axis=0)

    zero = jnp.zeros((8, ROW), F32)

    def start(j, carry):
        norm, power = carry
        part = slabs[:, pl.ds(pl.multiple_of(8 * j, 8), 8), :].reshape(ROW, ROW)
        value = mm(x_fwd[0], part) + mm(x_fwd[1], part)
        first[j] = value
        square = value * value
        return norm + dot_of(square), power + dot_of(square * spectrum[j])

    norm, power = lax.fori_loop(0, RING, start, (zero, zero), unroll=2)
    norm, power = jnp.sum(norm), jnp.sum(power)
    steps, ratios = [norm / power], [jnp.float32(0.0)]
    for sweep in range(SWEEPS - 1):
        step, ratio = steps[-1], ratios[-1]

        def advance(j, carry, sweep=sweep, step=step, ratio=ratio):
            new, power = carry
            lam = spectrum[j]
            if sweep == 0:
                d = first[j]
                r = d - step * (lam * d)
            else:
                d = residual[j] + ratio * (first[j] if sweep == 1 else direction[j])
                r = residual[j] - step * (lam * d)
            if sweep > 0:
                direction[j] = d
            residual[j] = r
            square = r * r
            return new + dot_of(square), power + dot_of(square * lam)

        new, power = lax.fori_loop(0, RING, advance, (zero, zero), unroll=2)
        new, power = jnp.sum(new), jnp.sum(power)
        ratio = new / norm
        steps.append(new / (power - ratio * new / step))
        ratios.append(ratio)
        norm = new

    for jj in range(4):
        j = 4 * quarter[0] + jj
        lam, r = spectrum[j], first[j]
        d, total = r, steps[0] * r
        for sweep in range(1, SWEEPS):
            r = r - steps[sweep - 1] * (lam * d)
            d = r + ratios[sweep] * d
            total = total + steps[sweep] * d
        part = left_mul(x_bwd, total)
        out[:, 8 * jj : 8 * jj + 8, :] = part.reshape(RING, 8, ROW).astype(out.dtype)


def term_kernel(pair_tgt, spectra, source_rows, wanted, z_bwd, y_bwd, target_rows, terms, held):
    for p in range(4):
        rows = jnp.concatenate([spectra[4 * q + p].astype(F32) for q in range(4)], axis=0)
        potential = right_mul(mix_rows(y_bwd, rows), z_bwd)
        terms[p] = (-potential * wanted[p].astype(F32)).astype(BF16)
        held[p] = -potential * source_rows[p].astype(F32)
    for p in range(4):
        same = jnp.zeros((ROW, ROW), F32)
        for other in range(4):
            hit = pair_tgt[p // 2, p % 2] == pair_tgt[other // 2, other % 2]
            same = same + jnp.where(hit, held[other], 0.0)
        target_rows[p] = same.astype(BF16)


def pack_terms_kernel(place, pair_src, here, ahead, behind, *outs):
    terms = (here, ahead, behind)
    for n, owner, count, cap, lane in lanes_of(place, 1):
        for kind, slot, z_own, _, _ in wants_at(place, pair_src, place[0], lane):
            theirs = z_own == owner

            @pl.when(fits(theirs, count, cap))
            def _():
                outs[n][count] = terms[kind][slot]

            count = count + theirs.astype(jnp.int32)


def add_terms_kernel(place, pair_src, here, ahead, behind, *refs):
    near, before, totals = refs[:5], refs[5:-2], refs[-2:]
    terms = (here, ahead, behind)
    z = place[0]

    def add(side, row, term):
        for where, total in enumerate(totals):

            @pl.when(side == where)
            def _():
                total[row] = total[row] + term.astype(F32)

    for total in totals:
        total[...] = jnp.zeros((8, ROW, ROW), F32)
    for old, total in zip(before, totals):
        total[...] = old[...]
    if not before:
        for kind, slot, z_own, side, row in each_want(pair_src, z, place[1], place[2]):

            @pl.when(z_own == z)
            def _():
                add(side, row, terms[kind][slot])

    for n, relay, count, cap, lane in lanes_of(place, -1):
        for _, _, z_own, side, row in wants_at(place, pair_src, relay, lane):
            mine = z_own == z

            @pl.when(fits(mine, count, cap))
            def _():
                add(side, row, near[n][count])

            count = count + mine.astype(jnp.int32)


AXES = ("band", "dom")


def shift(value, steps):
    pairs = []
    for z in range(RING):
        for x in range(2):
            for dom in range(16):
                there = 2 * ((z + (-steps if dom % 2 else steps)) % RING) + x
                pairs.append(((2 * z + x) * 16 + dom, there * 16 + dom))
    return lax.ppermute(value, AXES, pairs)


def across(value):
    return lax.ppermute(value, "band", [(i, i ^ 1) for i in range(32)])


def rounds_of(pair_src):
    band = jnp.arange(pair_src.shape[1], dtype=jnp.int32) // 2
    z, x = band // 2, band % 2
    z_own = pair_src // 8
    away = (z_own - z + 2) % RING
    relay = jnp.where(away <= 4, z, jnp.where(away < 10, z + 5, z - 5)) % RING
    far = away == 10
    relay = jnp.where(far, RING, relay)
    key = ((z_own * 32 + relay) * 2 + x).reshape(-1)
    shared = jnp.sum((key[:, None] == key[None, :]).astype(jnp.int32), axis=1).reshape(pair_src.shape)
    turns = jnp.where(far, (shared + CAPS[4] - 1) // CAPS[4], (shared + CAPS[0] - 1) // CAPS[0])
    return jnp.max(jnp.where(relay == z_own, 1, turns))


def per_device(targets, sources, pair_tgt, pair_src):
    table = {name: jnp.asarray(value) for name, value in tables().items()}
    band, dom = lax.axis_index("band"), lax.axis_index("dom")
    quarter = (dom // 4).astype(jnp.int32).reshape(1)
    rounds = rounds_of(pair_src)
    packets = [struct((cap, ROW, ROW), BF16) for cap in CAPS]
    four = struct((4, ROW, ROW), BF16)
    eight = struct((8, ROW, ROW), F32)

    def scalars_of(turn):
        turn = jnp.asarray(turn, jnp.int32)
        return jnp.stack([band // 2, band % 2, 1 - 2 * (dom % 2), turn]).astype(jnp.int32), pair_src

    own = sources.reshape(8, ROW, ROW)
    other = across(own)

    def deliver(turn, before):
        scalars = scalars_of(turn)
        packed = vmem_call(pack_wanted_kernel, packets, scalars + (own, other), scalars=2)
        near = tuple(shift(packet, -step) for packet, step in zip(packed, STEPS))
        operands = scalars + (own, other) + near + tuple(before)
        return vmem_call(place_wanted_kernel, [four] * 3, operands, scalars=2)

    here, ahead, behind = lax.fori_loop(1, rounds, deliver, deliver(0, ()))
    reached = (here, shift(ahead, -5), shift(behind, 5))

    ids = pair_tgt.reshape(4)
    wanted = targets[ids].reshape(4, ROW, ROW)
    source_rows, spectra = vmem_call(
        density_kernel,
        [four, struct((16, ROW, ROW), BF16)],
        scalars_of(0) + reached + (wanted, table["z_fwd"], table["y_fwd"]),
        scalars=2,
    )
    slabs = lax.all_to_all(spectra, "dom", 0, 0, tiled=True)
    state = pltpu.VMEM((RING, ROW, ROW), F32)
    (solved,) = vmem_call(
        solve_kernel,
        [struct((16, 32, ROW), F32)],
        (quarter, slabs, table["spectrum"], table["x_fwd"], table["x_bwd"]),
        scalars=1,
        scratch=(state, state, state),
    )
    back = lax.all_to_all(solved, "dom", 0, 0, tiled=True)
    target_rows, terms = vmem_call(
        term_kernel,
        [four, four],
        (pair_tgt, back, source_rows, wanted, table["z_bwd"], table["y_bwd"]),
        scalars=1,
        scratch=(pltpu.VMEM((4, ROW, ROW), F32),),
    )
    held = (terms, shift(terms, 5), shift(terms, -5))

    def collect(turn, before):
        scalars = scalars_of(turn)
        packed = vmem_call(pack_terms_kernel, packets, scalars + held, scalars=2)
        near = tuple(shift(packet, step) for packet, step in zip(packed, STEPS))
        operands = scalars + held + near + tuple(before)
        return vmem_call(add_terms_kernel, [eight] * 2, operands, scalars=2)

    mine, partner = lax.fori_loop(1, rounds, collect, collect(0, ()))
    owned = (mine + across(partner.astype(BF16)).astype(F32)).astype(BF16).reshape(sources.shape)

    flat = target_rows.reshape(4, targets.shape[1])
    slots = jnp.arange(targets.shape[0], dtype=jnp.int32)[:, None]
    summed = jnp.zeros(targets.shape, BF16)
    for p in range(4):
        summed = jnp.where(slots == ids[p], flat[p][None, :], summed)
    return summed, owned


def solution(mesh):
    return jax.shard_map(
        per_device,
        mesh=mesh,
        in_specs=(P("band", "dom"), P(None, "band", "dom"), P(None, "band"), P()),
        out_specs=(P("band", "dom"), P(None, "band", "dom")),
        check_vma=False,
    )
```

time: 188 us -> 186 us (0.989)
  the two profiles are of different devices: /device:TPU:1 before, /device:TPU:2 now
where the time goes in v3:
time: 186 us; the launch traced here: 185 us
  starting transfers between devices  86.2 us (46%)
  waiting for transfers between devices  60.7 us (33%)
  Pallas kernels  21.4 us (12%)
  other arithmetic  7.53 us (4%)
  local copies, waits for them, and re-layouts  6.57 us (4%)
    ppermute x14, starting transfers between devices, shift(): return lax.ppermute(value, AXES, pairs)  63 us
    ppermute x14, waiting for transfers between devices, shift(): return lax.ppermute(value, AXES, pairs)  34 us
    pallas_call x7, Pallas kernels, vmem_call(): pl.pallas_call(kernel, out_shape=outs, in_specs=[smem] * scalars + [whole...  21.4 us
    ppermute x2, starting transfers between devices, across(): return lax.ppermute(value, 'band', [(i, i ^ 1) for i in range(32)])  13.3 us
    all_to_all x1, waiting for transfers between devices, per_device(): slabs = lax.all_to_all(spectra, 'dom', 0, 0, tiled=True)  12.4 us
    all_to_all x1, waiting for transfers between devices, per_device(): back = lax.all_to_all(solved, 'dom', 0, 0, tiled=True)  8.83 us
    all_to_all x1, starting transfers between devices, per_device(): slabs = lax.all_to_all(spectra, 'dom', 0, 0, tiled=True)  6.26 us
    ppermute x2, waiting for transfers between devices, across(): return lax.ppermute(value, 'band', [(i, i ^ 1) for i in range(32)])  5.52 us
  transfers between devices with their start and end apart: 18, of which 10 were waited for; matrix products, arithmetic and copies ran while one was open for 4% of the time, Pallas kernels for 0%

profile of v3, /device:TPU:2, one launch (start us, length us, event | category | flops | bytes accessed | tf_op | source)
XLA Modules:
  0.0 184.7 jit_solution(9006625787098143672)
XLA Ops:
  2.0 7.8 %collective-permute-start.10 = (bf16[8,128,128]{2,1,0:T(8,128)(2,1)S(1)}, bf16[8,128,128]{2,1,0:T(8,128)(2,1)S(1)}, u32[]{:S(2)}, u32[]{:S(2)}) collective-permute-start(bf16[8,128,128]{2,1,0:T(8,128)(2,1)S(1)} %reshape.148.own), channel_id=1, source_target_pairs={{0,16},{16,0},{32,48},{48,32},{64,80},{80,64},{96,112},{112,96},{1... | collective-permute-start | bytes 786440 | tf_op jit(solution)/shard_map/ppermute | solution.py:335
  11.0 3.2 %collective-permute-done.10.other = bf16[8,128,128]{2,1,0:T(8,128)(2,1)S(1)} collective-permute-done((bf16[8,128,128]{2,1,0:T(8,128)(2,1)S(1)}, bf16[8,128,128]{2,1,0:T(8,128)(2,1)S(1)}, u32[]{:S(2)}, u32[]{:S(2)}) %collective-permute-start.10) | collective-permute-done | bytes 262176 | tf_op jit(solution)/shard_map/ppermute | solution.py:335
  15.4 9.2 %collective-permute-start.11 = (bf16[5,128,128]{2,1,0:T(8,128)(2,1)S(1)}, bf16[5,128,128]{2,1,0:T(8,128)(2,1)S(1)}, u32[]{:S(2)}, u32[]{:S(2)}) collective-permute-start(bf16[5,128,128]{2,1,0:T(8,128)(2,1)S(1)} %get-tuple-element.724), channel_id=1, source_target_pairs={{0,480},{1,33},{2,482},{3,35},{4,484},{5,37},{6,486},{7,39},{8,488... | collective-permute-start | bytes 491528 | tf_op jit(solution)/shard_map/ppermute | solution.py:331
  24.6 1.9 %collective-permute-start.12 = (bf16[5,128,128]{2,1,0:T(8,128)(2,1)S(1)}, bf16[5,128,128]{2,1,0:T(8,128)(2,1)S(1)}, u32[]{:S(2)}, u32[]{:S(2)}) collective-permute-start(bf16[5,128,128]{2,1,0:T(8,128)(2,1)S(1)} %get-tuple-element.725), channel_id=1, source_target_pairs={{0,32},{1,481},{2,34},{3,483},{4,36},{5,485},{6,38},{7,487},{8,40}... | collective-permute-start | bytes 491528 | tf_op jit(solution)/shard_map/ppermute | solution.py:331
  26.5 4.4 %collective-permute-start.13 = (bf16[5,128,128]{2,1,0:T(8,128)(2,1)S(1)}, bf16[5,128,128]{2,1,0:T(8,128)(2,1)S(1)}, u32[]{:S(2)}, u32[]{:S(2)}) collective-permute-start(bf16[5,128,128]{2,1,0:T(8,128)(2,1)S(1)} %get-tuple-element.726), channel_id=1, source_target_pairs={{0,448},{1,65},{2,450},{3,67},{4,452},{5,69},{6,454},{7,71},{8,456... | collective-permute-start | bytes 491528 | tf_op jit(solution)/shard_map/ppermute | solution.py:331
  30.9 2.4 %collective-permute-start.14 = (bf16[5,128,128]{2,1,0:T(8,128)(2,1)S(1)}, bf16[5,128,128]{2,1,0:T(8,128)(2,1)S(1)}, u32[]{:S(2)}, u32[]{:S(2)}) collective-permute-start(bf16[5,128,128]{2,1,0:T(8,128)(2,1)S(1)} %get-tuple-element.727), channel_id=1, source_target_pairs={{0,64},{1,449},{2,66},{3,451},{4,68},{5,453},{6,70},{7,455},{8,72}... | collective-permute-start | bytes 491528 | tf_op jit(solution)/shard_map/ppermute | solution.py:331
  34.3 5.8 %collective-permute-start.15 = (bf16[3,128,128]{2,1,0:T(8,128)(2,1)S(1)}, bf16[3,128,128]{2,1,0:T(8,128)(2,1)S(1)}, u32[]{:S(2)}, u32[]{:S(2)}) collective-permute-start(bf16[3,128,128]{2,1,0:T(8,128)(2,1)S(1)} %get-tuple-element.728), channel_id=1, source_target_pairs={{0,416},{1,97},{2,418},{3,99},{4,420},{5,101},{6,422},{7,103},{8,4... | collective-permute-start | bytes 294920 | tf_op jit(solution)/shard_map/ppermute | solution.py:331
  40.7 2.6 %collective-permute-done.15.refs_4_ = bf16[3,128,128]{2,1,0:T(8,128)(2,1)S(1)} collective-permute-done((bf16[3,128,128]{2,1,0:T(8,128)(2,1)S(1)}, bf16[3,128,128]{2,1,0:T(8,128)(2,1)S(1)}, u32[]{:S(2)}, u32[]{:S(2)}) %collective-permute-start.15) | collective-permute-done | bytes 98336 | tf_op jit(solution)/shard_map/ppermute | solution.py:331
  45.1 2.1 %shard_map.123 = (bf16[4,128,128]{2,1,0:T(8,128)(2,1)}, bf16[4,128,128]{2,1,0:T(8,128)(2,1)}, bf16[4,128,128]{2,1,0:T(8,128)(2,1)}) custom-call(s32[4]{0:T(128)S(1)} %pad_add_fusion.2.place, s32[2,64]{1,0:T(2,128)S(1)} %copy-done.11, bf16[8,128,128]{2,1,0:T(8,128)(2,1)S(1)} %reshape.148.own, bf16[8,128,128]{2,1,0:T(8,128)(2,1)S(1)} %collective-permute-done.10.other, ...), custom_call_target="tpu_custom_call" | custom-call | tf_op jit(solution)/shard_map/pallas_call | solution.py:97
  47.7 8.3 %collective-permute-start.16 = (bf16[4,128,128]{2,1,0:T(8,128)(2,1)}, bf16[4,128,128]{2,1,0:T(8,128)(2,1)S(1)}, u32[]{:S(2)}, u32[]{:S(2)}) collective-permute-start(bf16[4,128,128]{2,1,0:T(8,128)(2,1)} %get-tuple-element.733), channel_id=1, source_target_pairs={{0,352},{1,161},{2,354},{3,163},{4,356},{5,165},{6,358},{7,167},{8... | collective-permute-start | bytes 393224 | tf_op jit(solution)/shard_map/ppermute | solution.py:331
  56.0 2.4 %collective-permute-start.17 = (bf16[4,128,128]{2,1,0:T(8,128)(2,1)}, bf16[4,128,128]{2,1,0:T(8,128)(2,1)S(1)}, u32[]{:S(2)}, u32[]{:S(2)}) collective-permute-start(bf16[4,128,128]{2,1,0:T(8,128)(2,1)} %get-tuple-element.734), channel_id=1, source_target_pairs={{0,160},{1,353},{2,162},{3,355},{4,164},{5,357},{6,166},{7,359},{8... | collective-permute-start | bytes 393224 | tf_op jit(solution)/shard_map/ppermute | solution.py:331
  59.2 7.7 %collective-permute-done.16.ahead = bf16[4,128,128]{2,1,0:T(8,128)(2,1)S(1)} collective-permute-done((bf16[4,128,128]{2,1,0:T(8,128)(2,1)}, bf16[4,128,128]{2,1,0:T(8,128)(2,1)S(1)}, u32[]{:S(2)}, u32[]{:S(2)}) %collective-permute-start.16) | collective-permute-done | bytes 131104 | tf_op jit(solution)/shard_map/ppermute | solution.py:331
  66.9 6.7 %collective-permute-done.17.behind = bf16[4,128,128]{2,1,0:T(8,128)(2,1)S(1)} collective-permute-done((bf16[4,128,128]{2,1,0:T(8,128)(2,1)}, bf16[4,128,128]{2,1,0:T(8,128)(2,1)S(1)}, u32[]{:S(2)}, u32[]{:S(2)}) %collective-permute-start.17) | collective-permute-done | bytes 131104 | tf_op jit(solution)/shard_map/ppermute | solution.py:331
  73.6 3.9 %shard_map.124 = (bf16[4,128,128]{2,1,0:T(8,128)(2,1)S(1)}, bf16[16,128,128]{2,1,0:T(8,128)(2,1)}) custom-call(s32[4]{0:T(128)S(1)} %pad_add_fusion.2.place, s32[2,64]{1,0:T(2,128)S(1)} %get-tuple-element.1097, bf16[4,128,128]{2,1,0:T(8,128)(2,1)} %get-tuple-element.732.here, bf16[4,128,128]{2,1,0:T(8,128)(2,1)S(1)} %collective-permute-done.16.ahead, ...), custom_call_target="tpu_custom_call" | custom-call | tf_op jit(solution)/shard_map/pallas_call | solution.py:97
  77.5 6.3 %all-to-all-start = ((bf16[16,128,128]{2,1,0:T(8,128)(2,1)}), bf16[16,128,128]{2,1,0:T(8,128)(2,1)S(1)}, u32[]{:S(2)}, u32[]{:S(2)}) async-start(bf16[16,128,128]{2,1,0:T(8,128)(2,1)} %get-tuple-element.735), calls=%async_computation | async-start | bytes 1048576 | tf_op jit(solution)/shard_map/all_to_all | solution.py:386
  83.8 12.4 %all-to-all-done.slabs = bf16[16,128,128]{2,1,0:T(8,128)(2,1)S(1)} async-done(((bf16[16,128,128]{2,1,0:T(8,128)(2,1)}), bf16[16,128,128]{2,1,0:T(8,128)(2,1)S(1)}, u32[]{:S(2)}, u32[]{:S(2)}) %all-to-all-start) | async-done | bytes 524320 | tf_op jit(solution)/shard_map/all_to_all | solution.py:386
  96.2 6.8 %shard_map.125 = f32[16,32,128]{2,1,0:T(8,128)} custom-call(s32[1]{0:T(128)} %bitcast.9.quarter, bf16[16,128,128]{2,1,0:T(8,128)(2,1)S(1)} %all-to-all-done.slabs, f32[16,128,128]{2,1,0:T(8,128)S(1)} %copy-done.1, bf16[2,128,128]{2,1,0:T(8,128)(2,1)S(1)} %copy-done.4, bf16[2,128,128]{2,1,0:T(8,128)(2,1)S(1)} %copy-done.5), custom_call_target="tpu_custom_call" | custom-call | tf_op jit(solution)/shard_map/pallas_call | solution.py:97
  103.0 3.7 %all-to-all-start.1 = ((f32[16,32,128]{2,1,0:T(8,128)}), f32[16,32,128]{2,1,0:T(8,128)S(1)}, u32[]{:S(2)}, u32[]{:S(2)}) async-start(f32[16,32,128]{2,1,0:T(8,128)} %shard_map.125), calls=%async_computation.1 | async-start | bytes 524288 | tf_op jit(solution)/shard_map/all_to_all | solution.py:395
  107.3 8.8 %all-to-all-done.1.spectra = f32[16,32,128]{2,1,0:T(8,128)S(1)} async-done(((f32[16,32,128]{2,1,0:T(8,128)}), f32[16,32,128]{2,1,0:T(8,128)S(1)}, u32[]{:S(2)}, u32[]{:S(2)}) %all-to-all-start.1) | async-done | bytes 262176 | tf_op jit(solution)/shard_map/all_to_all | solution.py:395
  116.2 2.7 %shard_map.126 = (bf16[4,128,128]{2,1,0:T(8,128)(2,1)S(1)}, bf16[4,128,128]{2,1,0:T(8,128)(2,1)}) custom-call(s32[2,2]{1,0:T(2,128)S(1)} %copy-done.8, f32[16,32,128]{2,1,0:T(8,128)S(1)} %all-to-all-done.1.spectra, bf16[4,128,128]{2,1,0:T(8,128)(2,1)S(1)} %get-tuple-element.736.source_rows, bf16[4,128,128]{2,1,0:T(8,128)(2,1)S(1)} %bitcast.47, ...), custom_call_target="tpu_custom_call" | custom-call | tf_op jit(solution)/shard_map/pallas_call | solution.py:97
  118.8 1.9 %collective-permute-start.18 = (bf16[4,128,128]{2,1,0:T(8,128)(2,1)}, bf16[4,128,128]{2,1,0:T(8,128)(2,1)}, u32[]{:S(2)}, u32[]{:S(2)}) collective-permute-start(bf16[4,128,128]{2,1,0:T(8,128)(2,1)} %get-tuple-element.1023.here), channel_id=1, source_target_pairs={{0,160},{1,353},{2,162},{3,355},{4,164},{5,357},{6,166},{7,359},{8... | collective-permute-start | bytes 393224 | tf_op jit(solution)/shard_map/ppermute | solution.py:331
  120.7 9.9 %collective-permute-start.19 = (bf16[4,128,128]{2,1,0:T(8,128)(2,1)}, bf16[4,128,128]{2,1,0:T(8,128)(2,1)}, u32[]{:S(2)}, u32[]{:S(2)}) collective-permute-start(bf16[4,128,128]{2,1,0:T(8,128)(2,1)} %get-tuple-element.1023.here), channel_id=1, source_target_pairs={{0,352},{1,161},{2,354},{3,163},{4,356},{5,165},{6,358},{7,167},{8... | collective-permute-start | bytes 393224 | tf_op jit(solution)/shard_map/ppermute | solution.py:331
  133.8 7.7 %collective-permute-done.18.ahead = bf16[4,128,128]{2,1,0:T(8,128)(2,1)} collective-permute-done((bf16[4,128,128]{2,1,0:T(8,128)(2,1)}, bf16[4,128,128]{2,1,0:T(8,128)(2,1)}, u32[]{:S(2)}, u32[]{:S(2)}) %collective-permute-start.18) | collective-permute-done | bytes 131104 | tf_op jit(solution)/shard_map/ppermute | solution.py:331
  143.2 1.9 %collective-permute-start.20 = (bf16[5,128,128]{2,1,0:T(8,128)(2,1)S(1)}, bf16[5,128,128]{2,1,0:T(8,128)(2,1)S(1)}, u32[]{:S(2)}, u32[]{:S(2)}) collective-permute-start(bf16[5,128,128]{2,1,0:T(8,128)(2,1)S(1)} %get-tuple-element.739), channel_id=1, source_target_pairs={{0,32},{1,481},{2,34},{3,483},{4,36},{5,485},{6,38},{7,487},{8,40}... | collective-permute-start | bytes 491528 | tf_op jit(solution)/shard_map/ppermute | solution.py:331
  145.1 5.1 %collective-permute-start.21 = (bf16[5,128,128]{2,1,0:T(8,128)(2,1)S(1)}, bf16[5,128,128]{2,1,0:T(8,128)(2,1)S(1)}, u32[]{:S(2)}, u32[]{:S(2)}) collective-permute-start(bf16[5,128,128]{2,1,0:T(8,128)(2,1)S(1)} %get-tuple-element.740), channel_id=1, source_target_pairs={{0,480},{1,33},{2,482},{3,35},{4,484},{5,37},{6,486},{7,39},{8,488... | collective-permute-start | bytes 491528 | tf_op jit(solution)/shard_map/ppermute | solution.py:331
  150.2 1.9 %collective-permute-start.22 = (bf16[5,128,128]{2,1,0:T(8,128)(2,1)S(1)}, bf16[5,128,128]{2,1,0:T(8,128)(2,1)S(1)}, u32[]{:S(2)}, u32[]{:S(2)}) collective-permute-start(bf16[5,128,128]{2,1,0:T(8,128)(2,1)S(1)} %get-tuple-element.741), channel_id=1, source_target_pairs={{0,64},{1,449},{2,66},{3,451},{4,68},{5,453},{6,70},{7,455},{8,72}... | collective-permute-start | bytes 491528 | tf_op jit(solution)/shard_map/ppermute | solution.py:331
  152.2 6.0 %collective-permute-start.23 = (bf16[5,128,128]{2,1,0:T(8,128)(2,1)S(1)}, bf16[5,128,128]{2,1,0:T(8,128)(2,1)S(1)}, u32[]{:S(2)}, u32[]{:S(2)}) collective-permute-start(bf16[5,128,128]{2,1,0:T(8,128)(2,1)S(1)} %get-tuple-element.742), channel_id=1, source_target_pairs={{0,448},{1,65},{2,450},{3,67},{4,452},{5,69},{6,454},{7,71},{8,456... | collective-permute-start | bytes 491528 | tf_op jit(solution)/shard_map/ppermute | solution.py:331
  158.2 1.9 %collective-permute-start.24 = (bf16[3,128,128]{2,1,0:T(8,128)(2,1)S(1)}, bf16[3,128,128]{2,1,0:T(8,128)(2,1)S(1)}, u32[]{:S(2)}, u32[]{:S(2)}) collective-permute-start(bf16[3,128,128]{2,1,0:T(8,128)(2,1)S(1)} %get-tuple-element.743), channel_id=1, source_target_pairs={{0,96},{1,417},{2,98},{3,419},{4,100},{5,421},{6,102},{7,423},{8,1... | collective-permute-start | bytes 294920 | tf_op jit(solution)/shard_map/ppermute | solution.py:331
  160.8 7.5 %collective-permute-done.24.refs_4_ = bf16[3,128,128]{2,1,0:T(8,128)(2,1)S(1)} collective-permute-done((bf16[3,128,128]{2,1,0:T(8,128)(2,1)S(1)}, bf16[3,128,128]{2,1,0:T(8,128)(2,1)S(1)}, u32[]{:S(2)}, u32[]{:S(2)}) %collective-permute-start.24) | collective-permute-done | bytes 98336 | tf_op jit(solution)/shard_map/ppermute | solution.py:331
  168.3 3.1 %shard_map.128 = (f32[8,128,128]{2,1,0:T(8,128)}, f32[8,128,128]{2,1,0:T(8,128)}) custom-call(s32[4]{0:T(128)S(1)} %pad_add_fusion.2.place, s32[2,64]{1,0:T(2,128)S(1)} %get-tuple-element.1097, bf16[4,128,128]{2,1,0:T(8,128)(2,1)} %get-tuple-element.1023.here, bf16[4,128,128]{2,1,0:T(8,128)(2,1)} %collective-permute-done.18.ahead, ...), custom_call_target="tpu_custom_call" | custom-call | tf_op jit(solution)/shard_map/pallas_call | solution.py:97
  173.0 5.4 %collective-permute-start.25 = (bf16[8,128,128]{2,1,0:T(8,128)(2,1)S(1)}, bf16[8,128,128]{2,1,0:T(8,128)(2,1)S(1)}, u32[]{:S(2)}, u32[]{:S(2)}) collective-permute-start(bf16[8,128,128]{2,1,0:T(8,128)(2,1)S(1)} %convert_element_type.13), channel_id=1, source_target_pairs={{0,16},{16,0},{32,48},{48,32},{64,80},{80,64},{96,112},{112,96},{1... | collective-permute-start | bytes 786440 | tf_op jit(solution)/shard_map/ppermute | solution.py:335
  180.5 2.3 %collective-permute-done.25 = bf16[8,128,128]{2,1,0:T(8,128)(2,1)S(1)} collective-permute-done((bf16[8,128,128]{2,1,0:T(8,128)(2,1)S(1)}, bf16[8,128,128]{2,1,0:T(8,128)(2,1)S(1)}, u32[]{:S(2)}, u32[]{:S(2)}) %collective-permute-start.25) | collective-permute-done | bytes 262176 | tf_op jit(solution)/shard_map/ppermute | solution.py:335
  (72 shorter events, 20.0 us)
Async XLA Ops:
  0.6 57.8 %copy-start = (bf16[32,16384]{1,0:T(8,128)(2,1)S(1)}, bf16[32,16384]{1,0:T(8,128)(2,1)}, u32[]{:S(2)}) copy-start(bf16[32,16384]{1,0:T(8,128)(2,1)} %param.15) | copy-start | bytes 3145732
  2.0 12.2 %collective-permute-start.10 = (bf16[8,128,128]{2,1,0:T(8,128)(2,1)S(1)}, bf16[8,128,128]{2,1,0:T(8,128)(2,1)S(1)}, u32[]{:S(2)}, u32[]{:S(2)}) collective-permute-start(bf16[8,128,128]{2,1,0:T(8,128)(2,1)S(1)} %reshape.148.own), channel_id=1, source_target_pairs={{0,16},{16,0},{32,48},{48,32},{64,80},{80,64},{96,112},{112,96},{1... | collective-permute-start | bytes 786440 | tf_op jit(solution)/shard_map/ppermute | solution.py:335
  9.9 0.7 copy-start.11
  15.4 27.9 %collective-permute-start.11 = (bf16[5,128,128]{2,1,0:T(8,128)(2,1)S(1)}, bf16[5,128,128]{2,1,0:T(8,128)(2,1)S(1)}, u32[]{:S(2)}, u32[]{:S(2)}) collective-permute-start(bf16[5,128,128]{2,1,0:T(8,128)(2,1)S(1)} %get-tuple-element.724), channel_id=1, source_target_pairs={{0,480},{1,33},{2,482},{3,35},{4,484},{5,37},{6,486},{7,39},{8,488... | collective-permute-start | bytes 491528 | tf_op jit(solution)/shard_map/ppermute | solution.py:331
  24.6 18.7 %collective-permute-start.12 = (bf16[5,128,128]{2,1,0:T(8,128)(2,1)S(1)}, bf16[5,128,128]{2,1,0:T(8,128)(2,1)S(1)}, u32[]{:S(2)}, u32[]{:S(2)}) collective-permute-start(bf16[5,128,128]{2,1,0:T(8,128)(2,1)S(1)} %get-tuple-element.725), channel_id=1, source_target_pairs={{0,32},{1,481},{2,34},{3,483},{4,36},{5,485},{6,38},{7,487},{8,40}... | collective-permute-start | bytes 491528 | tf_op jit(solution)/shard_map/ppermute | solution.py:331
  26.5 16.8 %collective-permute-start.13 = (bf16[5,128,128]{2,1,0:T(8,128)(2,1)S(1)}, bf16[5,128,128]{2,1,0:T(8,128)(2,1)S(1)}, u32[]{:S(2)}, u32[]{:S(2)}) collective-permute-start(bf16[5,128,128]{2,1,0:T(8,128)(2,1)S(1)} %get-tuple-element.726), channel_id=1, source_target_pairs={{0,448},{1,65},{2,450},{3,67},{4,452},{5,69},{6,454},{7,71},{8,456... | collective-permute-start | bytes 491528 | tf_op jit(solution)/shard_map/ppermute | solution.py:331
  30.9 14.2 %collective-permute-start.14 = (bf16[5,128,128]{2,1,0:T(8,128)(2,1)S(1)}, bf16[5,128,128]{2,1,0:T(8,128)(2,1)S(1)}, u32[]{:S(2)}, u32[]{:S(2)}) collective-permute-start(bf16[5,128,128]{2,1,0:T(8,128)(2,1)S(1)} %get-tuple-element.727), channel_id=1, source_target_pairs={{0,64},{1,449},{2,66},{3,451},{4,68},{5,453},{6,70},{7,455},{8,72}... | collective-permute-start | bytes 491528 | tf_op jit(solution)/shard_map/ppermute | solution.py:331
  33.5 0.7 copy-start.8
  34.3 9.0 %collective-permute-start.15 = (bf16[3,128,128]{2,1,0:T(8,128)(2,1)S(1)}, bf16[3,128,128]{2,1,0:T(8,128)(2,1)S(1)}, u32[]{:S(2)}, u32[]{:S(2)}) collective-permute-start(bf16[3,128,128]{2,1,0:T(8,128)(2,1)S(1)} %get-tuple-element.728), channel_id=1, source_target_pairs={{0,416},{1,97},{2,418},{3,99},{4,420},{5,101},{6,422},{7,103},{8,4... | collective-permute-start | bytes 294920 | tf_op jit(solution)/shard_map/ppermute | solution.py:331
  47.7 19.2 %collective-permute-start.16 = (bf16[4,128,128]{2,1,0:T(8,128)(2,1)}, bf16[4,128,128]{2,1,0:T(8,128)(2,1)S(1)}, u32[]{:S(2)}, u32[]{:S(2)}) collective-permute-start(bf16[4,128,128]{2,1,0:T(8,128)(2,1)} %get-tuple-element.733), channel_id=1, source_target_pairs={{0,352},{1,161},{2,354},{3,163},{4,356},{5,165},{6,358},{7,167},{8... | collective-permute-start | bytes 393224 | tf_op jit(solution)/shard_map/ppermute | solution.py:331
  56.0 17.6 %collective-permute-start.17 = (bf16[4,128,128]{2,1,0:T(8,128)(2,1)}, bf16[4,128,128]{2,1,0:T(8,128)(2,1)S(1)}, u32[]{:S(2)}, u32[]{:S(2)}) collective-permute-start(bf16[4,128,128]{2,1,0:T(8,128)(2,1)} %get-tuple-element.734), channel_id=1, source_target_pairs={{0,160},{1,353},{2,162},{3,355},{4,164},{5,357},{6,166},{7,359},{8... | collective-permute-start | bytes 393224 | tf_op jit(solution)/shard_map/ppermute | solution.py:331
  58.4 15.2 %copy-start.6 = (bf16[2,128,128]{2,1,0:T(8,128)(2,1)S(1)}, bf16[2,128,128]{2,1,0:T(8,128)(2,1)}, u32[]{:S(2)}) copy-start(bf16[2,128,128]{2,1,0:T(8,128)(2,1)} %constant.248.clone.z_fwd) | copy-start | bytes 196612
  59.1 14.5 %copy-start.2 = (bf16[2,256,256]{2,1,0:T(8,128)(2,1)S(1)}, bf16[2,256,256]{2,1,0:T(8,128)(2,1)}, u32[]{:S(2)}) copy-start(bf16[2,256,256]{2,1,0:T(8,128)(2,1)} %constant.250.clone.y_fwd) | copy-start | bytes 786436
  59.1 37.0 %copy-start.1 = (f32[16,128,128]{2,1,0:T(8,128)S(1)}, f32[16,128,128]{2,1,0:T(8,128)}, u32[]{:S(2)}) copy-start(f32[16,128,128]{2,1,0:T(8,128)} %constant.254.clone.spectrum) | copy-start | bytes 3145732
  77.5 18.7 %copy-start.4 = (bf16[2,128,128]{2,1,0:T(8,128)(2,1)S(1)}, bf16[2,128,128]{2,1,0:T(8,128)(2,1)}, u32[]{:S(2)}) copy-start(bf16[2,128,128]{2,1,0:T(8,128)(2,1)} %constant.252.clone.x_fwd) | copy-start | bytes 196612
  77.5 18.7 %copy-start.5 = (bf16[2,128,128]{2,1,0:T(8,128)(2,1)S(1)}, bf16[2,128,128]{2,1,0:T(8,128)(2,1)}, u32[]{:S(2)}) copy-start(bf16[2,128,128]{2,1,0:T(8,128)(2,1)} %constant.253.clone.x_bwd) | copy-start | bytes 196612
  77.5 18.6 %all-to-all-start = ((bf16[16,128,128]{2,1,0:T(8,128)(2,1)}), bf16[16,128,128]{2,1,0:T(8,128)(2,1)S(1)}, u32[]{:S(2)}, u32[]{:S(2)}) async-start(bf16[16,128,128]{2,1,0:T(8,128)(2,1)} %get-tuple-element.735), calls=%async_computation | async-start | bytes 1048576 | tf_op jit(solution)/shard_map/all_to_all | solution.py:386
  103.0 13.2 %copy-start.3 = (bf16[2,256,256]{2,1,0:T(8,128)(2,1)S(1)}, bf16[2,256,256]{2,1,0:T(8,128)(2,1)}, u32[]{:S(2)}) copy-start(bf16[2,256,256]{2,1,0:T(8,128)(2,1)} %constant.251.clone.y_bwd) | copy-start | bytes 786436
  103.0 13.2 %copy-start.7 = (bf16[2,128,128]{2,1,0:T(8,128)(2,1)S(1)}, bf16[2,128,128]{2,1,0:T(8,128)(2,1)}, u32[]{:S(2)}) copy-start(bf16[2,128,128]{2,1,0:T(8,128)(2,1)} %constant.249.clone.z_bwd) | copy-start | bytes 196612
  103.0 13.2 %all-to-all-start.1 = ((f32[16,32,128]{2,1,0:T(8,128)}), f32[16,32,128]{2,1,0:T(8,128)S(1)}, u32[]{:S(2)}, u32[]{:S(2)}) async-start(f32[16,32,128]{2,1,0:T(8,128)} %shard_map.125), calls=%async_computation.1 | async-start | bytes 524288 | tf_op jit(solution)/shard_map/all_to_all | solution.py:395
  118.8 22.6 %collective-permute-start.18 = (bf16[4,128,128]{2,1,0:T(8,128)(2,1)}, bf16[4,128,128]{2,1,0:T(8,128)(2,1)}, u32[]{:S(2)}, u32[]{:S(2)}) collective-permute-start(bf16[4,128,128]{2,1,0:T(8,128)(2,1)} %get-tuple-element.1023.here), channel_id=1, source_target_pairs={{0,160},{1,353},{2,162},{3,355},{4,164},{5,357},{6,166},{7,359},{8... | collective-permute-start | bytes 393224 | tf_op jit(solution)/shard_map/ppermute | solution.py:331
  120.7 20.7 %collective-permute-start.19 = (bf16[4,128,128]{2,1,0:T(8,128)(2,1)}, bf16[4,128,128]{2,1,0:T(8,128)(2,1)}, u32[]{:S(2)}, u32[]{:S(2)}) collective-permute-start(bf16[4,128,128]{2,1,0:T(8,128)(2,1)} %get-tuple-element.1023.here), channel_id=1, source_target_pairs={{0,352},{1,161},{2,354},{3,163},{4,356},{5,165},{6,358},{7,167},{8... | collective-permute-start | bytes 393224 | tf_op jit(solution)/shard_map/ppermute | solution.py:331
  143.2 25.1 %collective-permute-start.20 = (bf16[5,128,128]{2,1,0:T(8,128)(2,1)S(1)}, bf16[5,128,128]{2,1,0:T(8,128)(2,1)S(1)}, u32[]{:S(2)}, u32[]{:S(2)}) collective-permute-start(bf16[5,128,128]{2,1,0:T(8,128)(2,1)S(1)} %get-tuple-element.739), channel_id=1, source_target_pairs={{0,32},{1,481},{2,34},{3,483},{4,36},{5,485},{6,38},{7,487},{8,40}... | collective-permute-start | bytes 491528 | tf_op jit(solution)/shard_map/ppermute | solution.py:331
  145.1 23.1 %collective-permute-start.21 = (bf16[5,128,128]{2,1,0:T(8,128)(2,1)S(1)}, bf16[5,128,128]{2,1,0:T(8,128)(2,1)S(1)}, u32[]{:S(2)}, u32[]{:S(2)}) collective-permute-start(bf16[5,128,128]{2,1,0:T(8,128)(2,1)S(1)} %get-tuple-element.740), channel_id=1, source_target_pairs={{0,480},{1,33},{2,482},{3,35},{4,484},{5,37},{6,486},{7,39},{8,488... | collective-permute-start | bytes 491528 | tf_op jit(solution)/shard_map/ppermute | solution.py:331
  150.2 18.0 %collective-permute-start.22 = (bf16[5,128,128]{2,1,0:T(8,128)(2,1)S(1)}, bf16[5,128,128]{2,1,0:T(8,128)(2,1)S(1)}, u32[]{:S(2)}, u32[]{:S(2)}) collective-permute-start(bf16[5,128,128]{2,1,0:T(8,128)(2,1)S(1)} %get-tuple-element.741), channel_id=1, source_target_pairs={{0,64},{1,449},{2,66},{3,451},{4,68},{5,453},{6,70},{7,455},{8,72}... | collective-permute-start | bytes 491528 | tf_op jit(solution)/shard_map/ppermute | solution.py:331
  152.2 16.1 %collective-permute-start.23 = (bf16[5,128,128]{2,1,0:T(8,128)(2,1)S(1)}, bf16[5,128,128]{2,1,0:T(8,128)(2,1)S(1)}, u32[]{:S(2)}, u32[]{:S(2)}) collective-permute-start(bf16[5,128,128]{2,1,0:T(8,128)(2,1)S(1)} %get-tuple-element.742), channel_id=1, source_target_pairs={{0,448},{1,65},{2,450},{3,67},{4,452},{5,69},{6,454},{7,71},{8,456... | collective-permute-start | bytes 491528 | tf_op jit(solution)/shard_map/ppermute | solution.py:331
  158.2 10.0 %collective-permute-start.24 = (bf16[3,128,128]{2,1,0:T(8,128)(2,1)S(1)}, bf16[3,128,128]{2,1,0:T(8,128)(2,1)S(1)}, u32[]{:S(2)}, u32[]{:S(2)}) collective-permute-start(bf16[3,128,128]{2,1,0:T(8,128)(2,1)S(1)} %get-tuple-element.743), channel_id=1, source_target_pairs={{0,96},{1,417},{2,98},{3,419},{4,100},{5,421},{6,102},{7,423},{8,1... | collective-permute-start | bytes 294920 | tf_op jit(solution)/shard_map/ppermute | solution.py:331
  171.9 6.6 %copy-start.12 = (bf16[16384]{0:T(1024)(128)(2,1)S(1)}, bf16[16384]{0:T(1024)(128)(2,1)}, u32[]{:S(2)}) copy-start(bf16[16384]{0:T(1024)(128)(2,1)} %get-tuple-element.796) | copy-start | bytes 98308
  171.9 6.6 %copy-start.13 = (bf16[16384]{0:T(1024)(128)(2,1)S(1)}, bf16[16384]{0:T(1024)(128)(2,1)}, u32[]{:S(2)}) copy-start(bf16[16384]{0:T(1024)(128)(2,1)} %get-tuple-element.797) | copy-start | bytes 98308
  171.9 6.6 %copy-start.14 = (bf16[16384]{0:T(1024)(128)(2,1)S(1)}, bf16[16384]{0:T(1024)(128)(2,1)}, u32[]{:S(2)}) copy-start(bf16[16384]{0:T(1024)(128)(2,1)} %get-tuple-element.798) | copy-start | bytes 98308
  173.0 9.8 %collective-permute-start.25 = (bf16[8,128,128]{2,1,0:T(8,128)(2,1)S(1)}, bf16[8,128,128]{2,1,0:T(8,128)(2,1)S(1)}, u32[]{:S(2)}, u32[]{:S(2)}) collective-permute-start(bf16[8,128,128]{2,1,0:T(8,128)(2,1)S(1)} %convert_element_type.13), channel_id=1, source_target_pairs={{0,16},{16,0},{32,48},{48,32},{64,80},{80,64},{96,112},{112,96},{1... | collective-permute-start | bytes 786440 | tf_op jit(solution)/shard_map/ppermute | solution.py:335
  178.5 0.7 copy-start.15
  (1 other events, 0.7 us)

commit v4 on v2

v4 whole, which is shorter than its diff:
```python
import numpy as np
import jax
import jax.numpy as jnp
from jax import lax
from jax.experimental import pallas as pl
from jax.experimental.pallas import tpu as pltpu
from jax.sharding import PartitionSpec as P

SIDE = 64
SWEEPS = 8
RING = 16
CAP = 4
ROW = 128
HALF = 64
VMEM_LIMIT = 48 * 1024 * 1024
F32 = jnp.float32
BF16 = jnp.bfloat16


def eigen_system():
    line = np.zeros((SIDE, SIDE))
    for delta, weight in ((0, 30.0), (1, -16.0), (2, 1.0)):
        for i in range(SIDE - delta):
            line[i, i + delta] = weight / 12.0
            line[i + delta, i] = weight / 12.0
    values, vectors = np.linalg.eigh(line)
    return values, vectors * np.where(vectors[0] < 0, -1.0, 1.0)[None, :]


def halves(matrix):
    high = np.asarray(matrix, np.float32).astype(jnp.bfloat16)
    low = (np.asarray(matrix, np.float64) - high.astype(np.float64)).astype(jnp.bfloat16)
    return np.stack([high, low])


def tables():
    values, v = eigen_system()
    along_z = np.kron(np.eye(2), v)
    even, odd = v[0::2], v[1::2]
    fwd = np.zeros((2, 32, 4, 2, 4, 32))
    bwd = np.zeros((2, 4, 32, 2, 32, 4))
    for x in range(4):
        fwd[0, :, x, 0, x, :] = even[:, 0::2].T
        fwd[0, :, x, 1, x, :] = odd[:, 0::2].T
        fwd[1, :, x, 0, x, :] = odd[:, 1::2].T
        fwd[1, :, x, 1, x, :] = even[:, 1::2].T
        bwd[0, x, :, 0, :, x] = even[:, 0::2]
        bwd[0, x, :, 1, :, x] = even[:, 1::2]
        bwd[1, x, :, 0, :, x] = odd[:, 1::2]
        bwd[1, x, :, 1, :, x] = odd[:, 0::2]
    along_x = np.zeros((2, SIDE, RING, 2, 4))
    for pick in range(2):
        along_x[pick, :, :, pick, :] = v.T.reshape(SIDE, RING, 4)
    rows = np.arange(SIDE).reshape(RING, 2, 1, 2, 1)
    spectrum = values[rows] + values.reshape(1, 1, SIDE, 1, 1) + values.reshape(1, 1, 1, 1, SIDE)
    return dict(
        z_fwd=halves(along_z),
        z_bwd=halves(along_z.T),
        y_fwd=halves(fwd.reshape(256, 256)),
        y_bwd=halves(bwd.reshape(256, 256)),
        x_fwd=halves(along_x.reshape(ROW, ROW)),
        x_bwd=halves(along_x.reshape(ROW, ROW).T),
        spectrum=spectrum.reshape(RING, ROW, ROW).astype(np.float32),
    )


def split(value):
    high = value.astype(BF16)
    return high, (value - high.astype(F32)).astype(BF16)


def mm(left, right):
    return jnp.dot(left, right, preferred_element_type=F32)


def left_mul(table, value):
    high, low = split(value)
    return mm(table[0], high) + mm(table[0], low) + mm(table[1], high)


def right_mul(value, table):
    high, low = split(value)
    return mm(high, table[0]) + mm(low, table[0]) + mm(high, table[1])


def mix_rows(table, value):
    swapped = jnp.concatenate([value[:, HALF:], value[:, :HALF]], axis=1)
    both = left_mul(table, jnp.concatenate([value, swapped], axis=0))
    lane = lax.broadcasted_iota(jnp.int32, (ROW, ROW), 1)
    return jnp.where(lane < HALF, both[:ROW], both[ROW:])


def vmem_call(kernel, outs, operands, scalars=0, scratch=()):
    whole = pl.BlockSpec(memory_space=pltpu.VMEM)
    smem = pl.BlockSpec(memory_space=pltpu.SMEM)
    return pl.pallas_call(
        kernel,
        out_shape=outs,
        in_specs=[smem] * scalars + [whole] * (len(operands) - scalars),
        out_specs=[whole] * len(outs),
        scratch_shapes=list(scratch),
        compiler_params=pltpu.CompilerParams(vmem_limit_bytes=VMEM_LIMIT),
    )(*operands)


def smem_call(kernel, size, *operands):
    smem = pl.BlockSpec(memory_space=pltpu.SMEM)
    return pl.pallas_call(
        kernel,
        out_shape=struct((size,), jnp.int32),
        in_specs=[smem] * len(operands),
        out_specs=smem,
    )(*operands)


def struct(shape, dtype):
    return jax.ShapeDtypeStruct(shape, dtype)


def owner_of(source):
    return lax.shift_right_logical(source, 2), lax.bitwise_and(source, 3)


def wants_of(pair_src, member):
    for quad in range(4):
        for slot in range(4):
            owner, row = owner_of(pair_src[slot // 2, 2 * (8 * quad + member) + slot % 2])
            yield 4 * quad + slot, owner, 4 * (slot // 2) + row


def in_round(hit, count):
    return jnp.logical_and(hit, jnp.logical_and(count >= 0, count < CAP))


def sent_kernel(place, pair_src, sent):
    for member in range(8):
        for n in range(CAP):
            sent[member * CAP + n] = -1
        count = -CAP * place[1]
        for _, owner, row in wants_of(pair_src, member):
            hit = owner == place[0]

            @pl.when(in_round(hit, count))
            def _():
                sent[member * CAP + count] = row

            count = count + hit.astype(jnp.int32)


def found_kernel(place, pair_src, found):
    band = place[0]
    wants = list(wants_of(pair_src, lax.bitwise_and(band, 7)))
    for index, owner, _ in wants:
        count = -CAP * place[1]
        for _, other, _ in wants[:index]:
            count = count + (other == owner).astype(jnp.int32)
        near = lax.shift_right_logical(owner, 3) == lax.shift_right_logical(band, 3)
        at = lax.bitwise_and(owner, 7) * CAP + count
        found[index] = jnp.where(in_round(near, count), at, -1)


def pack_rows_kernel(sent, own, out):
    for n in range(8 * CAP):

        @pl.when(sent[n] >= 0)
        def _():
            out[n] = own[sent[n]]


def place_rows_kernel(found, near, *refs):
    out = refs[-1]
    for before in refs[:-1]:
        out[...] = before[...]
    for want in range(16):

        @pl.when(found[want] >= 0)
        def _():
            out[want] = near[found[want]]


def pack_terms_kernel(found, held, out):
    for want in range(16):

        @pl.when(found[want] >= 0)
        def _():
            out[found[want]] = held[want]


def add_terms_kernel(sent, near, *refs):
    total = refs[-1]
    total[...] = jnp.zeros((8, ROW, ROW), F32)
    for before in refs[:-1]:
        total[...] = before[...]
    for n in range(8 * CAP):

        @pl.when(sent[n] >= 0)
        def _():
            total[sent[n]] = total[sent[n]] + near[n].astype(F32)


def density_kernel(place, pair_src, reached, wanted, z_fwd, y_fwd, source_rows, spectra):
    for p in range(4):
        owner, _ = owner_of(pair_src[p // 2, 2 * place[0] + p % 2])
        source_rows[p] = reached[4 * lax.shift_right_logical(owner, 3) + p]
        density = source_rows[p].astype(F32) * wanted[p].astype(F32)
        mixed = mix_rows(y_fwd, right_mul(density, z_fwd)).astype(spectra.dtype)
        for copy in range(4):
            spectra[4 * copy + p] = mixed


def solve_kernel(quarter, slabs, spectrum, x_fwd, x_bwd, out, first, residual, direction):
    def dot_of(value):
        return jnp.sum(value.reshape(RING, 8, ROW), axis=0)

    zero = jnp.zeros((8, ROW), F32)

    def start(j, carry):
        norm, power = carry
        part = slabs[:, pl.ds(pl.multiple_of(8 * j, 8), 8), :].reshape(ROW, ROW)
        value = mm(x_fwd[0], part) + mm(x_fwd[1], part)
        first[j] = value
        square = value * value
        return norm + dot_of(square), power + dot_of(square * spectrum[j])

    norm, power = lax.fori_loop(0, RING, start, (zero, zero), unroll=2)
    norm, power = jnp.sum(norm), jnp.sum(power)
    steps, ratios = [norm / power], [jnp.float32(0.0)]
    for sweep in range(SWEEPS - 1):
        step, ratio = steps[-1], ratios[-1]

        def advance(j, carry, sweep=sweep, step=step, ratio=ratio):
            new, power = carry
            lam = spectrum[j]
            if sweep == 0:
                d = first[j]
                r = d - step * (lam * d)
            else:
                d = residual[j] + ratio * (first[j] if sweep == 1 else direction[j])
                r = residual[j] - step * (lam * d)
            if sweep > 0:
                direction[j] = d
            residual[j] = r
            square = r * r
            return new + dot_of(square), power + dot_of(square * lam)

        new, power = lax.fori_loop(0, RING, advance, (zero, zero), unroll=2)
        new, power = jnp.sum(new), jnp.sum(power)
        ratio = new / norm
        steps.append(new / (power - ratio * new / step))
        ratios.append(ratio)
        norm = new

    for jj in range(4):
        j = 4 * quarter[0] + jj
        lam, r = spectrum[j], first[j]
        d, total = r, steps[0] * r
        for sweep in range(1, SWEEPS):
            r = r - steps[sweep - 1] * (lam * d)
            d = r + ratios[sweep] * d
            total = total + steps[sweep] * d
        part = left_mul(x_bwd, total)
        out[:, 8 * jj : 8 * jj + 8, :] = part.reshape(RING, 8, ROW).astype(out.dtype)


def term_kernel(pair_tgt, spectra, source_rows, wanted, z_bwd, y_bwd, target_rows, terms, held):
    for p in range(4):
        rows = jnp.concatenate([spectra[4 * q + p].astype(F32) for q in range(4)], axis=0)
        potential = right_mul(mix_rows(y_bwd, rows), z_bwd)
        term = (-potential * wanted[p].astype(F32)).astype(BF16)
        for quad in range(4):
            terms[4 * quad + p] = term
        held[p] = -potential * source_rows[p].astype(F32)
    for p in range(4):
        same = jnp.zeros((ROW, ROW), F32)
        for other in range(4):
            hit = pair_tgt[p // 2, p % 2] == pair_tgt[other // 2, other % 2]
            same = same + jnp.where(hit, held[other], 0.0)
        target_rows[p] = same.astype(BF16)


def within_quad(value):
    groups = [[8 * quad + member for member in range(8)] for quad in range(4)]
    return lax.all_to_all(value, "band", 0, 0, axis_index_groups=groups, tiled=True)


def along_ring(value):
    groups = [[8 * quad + member for quad in range(4)] for member in range(8)]
    return lax.all_to_all(value, "band", 0, 0, axis_index_groups=groups, tiled=True)


def rounds_of(pair_src):
    band = jnp.arange(pair_src.shape[1], dtype=jnp.int32) // 2
    key = ((pair_src // 4) * 8 + band % 8).reshape(-1)
    shared = jnp.sum((key[:, None] == key[None, :]).astype(jnp.int32), axis=1)
    return (jnp.max(shared) + CAP - 1) // CAP


def per_device(targets, sources, pair_tgt, pair_src):
    table = {name: jnp.asarray(value) for name, value in tables().items()}
    band, dom = lax.axis_index("band"), lax.axis_index("dom")
    quarter = (dom // 4).astype(jnp.int32).reshape(1)
    rounds = rounds_of(pair_src)
    four = struct((4, ROW, ROW), BF16)
    sixteen = struct((16, ROW, ROW), BF16)
    packet = struct((8 * CAP, ROW, ROW), BF16)
    own = sources.reshape(8, ROW, ROW)

    def place_in(turn):
        return jnp.stack([band, jnp.asarray(turn, jnp.int32)]).astype(jnp.int32)

    def sent_in(turn):
        return smem_call(sent_kernel, 8 * CAP, place_in(turn), pair_src)

    def found_in(turn):
        return smem_call(found_kernel, 16, place_in(turn), pair_src)

    def deliver(sent, found, before):
        (packed,) = vmem_call(pack_rows_kernel, [packet], (sent, own), scalars=1)
        operands = (found, within_quad(packed)) + before
        return vmem_call(place_rows_kernel, [sixteen], operands, scalars=1)[0]

    sent, found = sent_in(0), found_in(0)
    picked = lax.fori_loop(
        1,
        rounds,
        lambda turn, before: deliver(sent_in(turn), found_in(turn), (before,)),
        deliver(sent, found, ()),
    )
    reached = along_ring(picked)

    ids = pair_tgt.reshape(4)
    wanted = targets[ids].reshape(4, ROW, ROW)
    source_rows, spectra = vmem_call(
        density_kernel,
        [four, sixteen],
        (place_in(0), pair_src, reached, wanted, table["z_fwd"], table["y_fwd"]),
        scalars=2,
    )
    slabs = lax.all_to_all(spectra, "dom", 0, 0, tiled=True)
    state = pltpu.VMEM((RING, ROW, ROW), F32)
    (solved,) = vmem_call(
        solve_kernel,
        [struct((16, 32, ROW), F32)],
        (quarter, slabs, table["spectrum"], table["x_fwd"], table["x_bwd"]),
        scalars=1,
        scratch=(state, state, state),
    )
    back = lax.all_to_all(solved, "dom", 0, 0, tiled=True)
    target_rows, terms = vmem_call(
        term_kernel,
        [four, sixteen],
        (pair_tgt, back, source_rows, wanted, table["z_bwd"], table["y_bwd"]),
        scalars=1,
        scratch=(pltpu.VMEM((4, ROW, ROW), F32),),
    )
    held = along_ring(terms)

    def collect(sent, found, before):
        (packed,) = vmem_call(pack_terms_kernel, [packet], (found, held), scalars=1)
        operands = (sent, within_quad(packed)) + before
        return vmem_call(add_terms_kernel, [struct((8, ROW, ROW), F32)], operands, scalars=1)[0]

    total = lax.fori_loop(
        1,
        rounds,
        lambda turn, before: collect(sent_in(turn), found_in(turn), (before,)),
        collect(sent, found, ()),
    )
    owned = total.astype(BF16).reshape(sources.shape)

    flat = target_rows.reshape(4, targets.shape[1])
    slots = jnp.arange(targets.shape[0], dtype=jnp.int32)[:, None]
    summed = jnp.zeros(targets.shape, BF16)
    for p in range(4):
        summed = jnp.where(slots == ids[p], flat[p][None, :], summed)
    return summed, owned


def solution(mesh):
    return jax.shard_map(
        per_device,
        mesh=mesh,
        in_specs=(P("band", "dom"), P(None, "band", "dom"), P(None, "band"), P()),
        out_specs=(P("band", "dom"), P(None, "band", "dom")),
        check_vma=False,
    )
```

time: 188 us -> 197 us (1.048)
  waiting for transfers between devices: 65.5 us -> 108 us
  starting transfers between devices: 74.3 us -> 38.2 us
  Pallas kernels: 18 us -> 20.8 us
  local copies, waits for them, and re-layouts: 7.66 us -> 5.21 us
    ppermute x8 -> x0, starting transfers between devices: 49.9 us -> none  [the longest x6 43.7 us: shift(): return lax.ppermute(value, AXES, pairs)]
    all_to_all x0 -> x2, waiting for transfers between devices: none -> 44.5 us  [within_quad(): lax.all_to_all(value, 'band', 0, 0, axis_index_groups=groups, tiled=True)]
    ppermute x8 -> x0, waiting for transfers between devices: 14.6 us -> none  [the longest x6 9.79 us: shift(): return lax.ppermute(value, AXES, pairs)]
    all_to_all x2, waiting for transfers between devices: 39.5 us -> 52.5 us  [along_ring(): lax.all_to_all(value, 'band', 0, 0, axis_index_groups=groups, tiled=True)]
    all_to_all x0 -> x2, starting transfers between devices: none -> 11 us  [within_quad(): lax.all_to_all(value, 'band', 0, 0, axis_index_groups=groups, tiled=True)]
    all_to_all x1, starting transfers between devices: 7.57 us -> 10.7 us  [per_device(): slabs = lax.all_to_all(spectra, 'dom', 0, 0, tiled=True)]
    pallas_call x0 -> x2, Pallas kernels: none -> 3.09 us  [smem_call(): pl.pallas_call(kernel, out_shape=struct((size,), jnp.int32), in_specs=[sm...]
  transfers between devices with their start and end apart: 11 -> 5, of which waited for: 8 -> 5; matrix products, arithmetic and copies ran while one was open for 3% -> 3% of each run, Pallas kernels for 0% -> 1%
where the time goes in v4:
time: 197 us; the launch traced here: 193 us
  waiting for transfers between devices  108 us (55%)
  starting transfers between devices  38.2 us (19%)
  Pallas kernels  20.8 us (11%)
  blocking collectives  12.5 us (6%)
  other arithmetic  6.5 us (3%)
  local copies, waits for them, and re-layouts  5.21 us (3%)
    all_to_all x2, waiting for transfers between devices, along_ring(): lax.all_to_all(value, 'band', 0, 0, axis_index_groups=groups, tiled=True)  52.5 us
    all_to_all x2, waiting for transfers between devices, within_quad(): lax.all_to_all(value, 'band', 0, 0, axis_index_groups=groups, tiled=True)  44.5 us
    pallas_call x7, Pallas kernels, vmem_call(): pl.pallas_call(kernel, out_shape=outs, in_specs=[smem] * scalars + [whole...  17.7 us
    all_to_all x2, starting transfers between devices, along_ring(): lax.all_to_all(value, 'band', 0, 0, axis_index_groups=groups, tiled=True)  16.5 us
    all_to_all x1, blocking collectives, per_device(): back = lax.all_to_all(solved, 'dom', 0, 0, tiled=True)  12.5 us
    all_to_all x1, waiting for transfers between devices, per_device(): slabs = lax.all_to_all(spectra, 'dom', 0, 0, tiled=True)  11.3 us
    all_to_all x2, starting transfers between devices, within_quad(): lax.all_to_all(value, 'band', 0, 0, axis_index_groups=groups, tiled=True)  11 us
    all_to_all x1, starting transfers between devices, per_device(): slabs = lax.all_to_all(spectra, 'dom', 0, 0, tiled=True)  10.7 us
  transfers between devices with their start and end apart: 5, of which 5 were waited for; matrix products, arithmetic and copies ran while one was open for 3% of the time, Pallas kernels for 1%

profile of v4, /device:TPU:1, one launch (start us, length us, event | category | flops | bytes accessed | tf_op | source)
XLA Modules:
  0.0 193.0 jit_solution(1077687563460951771)
XLA Ops:
  0.7 1.3 reshape.106.own
  2.0 0.6 pad_add_fusion.2.place
  2.7 1.7 shard_map.123.sent
  4.4 0.6 copy-done.12
  4.9 1.8 shard_map.124
  6.7 7.4 %all-to-all-start.2 = ((bf16[32,128,128]{2,1,0:T(8,128)(2,1)}), bf16[32,128,128]{2,1,0:T(8,128)(2,1)S(1)}, u32[]{:S(2)}, u32[]{:S(2)}) async-start(bf16[32,128,128]{2,1,0:T(8,128)(2,1)} %shard_map.124), calls=%async_computation.2 | async-start | bytes 2097152 | tf_op jit(solution)/shard_map/all_to_all | solution.py:283
  14.4 0.7 reduce_max.9
  15.8 1.4 shard_map.122.found
  17.2 20.7 %all-to-all-done.2.near = bf16[32,128,128]{2,1,0:T(8,128)(2,1)S(1)} async-done(((bf16[32,128,128]{2,1,0:T(8,128)(2,1)}), bf16[32,128,128]{2,1,0:T(8,128)(2,1)S(1)}, u32[]{:S(2)}, u32[]{:S(2)}) %all-to-all-start.2) | async-done | bytes 1048608 | tf_op jit(solution)/shard_map/all_to_all | solution.py:283
  38.0 0.7 shard_map.125
  38.7 0.8 copy-done.17
  39.5 13.0 %all-to-all-start.3 = ((bf16[16,128,128]{2,1,0:T(8,128)(2,1)}), bf16[16,128,128]{2,1,0:T(8,128)(2,1)S(1)}, u32[]{:S(2)}, u32[]{:S(2)}) async-start(bf16[16,128,128]{2,1,0:T(8,128)(2,1)} %copy-done.17), calls=%async_computation.3 | async-start | bytes 1048576 | tf_op jit(solution)/shard_map/all_to_all | solution.py:288
  52.6 0.7 gather_fusion
  53.3 27.7 %all-to-all-done.3.reached = bf16[16,128,128]{2,1,0:T(8,128)(2,1)S(1)} async-done(((bf16[16,128,128]{2,1,0:T(8,128)(2,1)}), bf16[16,128,128]{2,1,0:T(8,128)(2,1)S(1)}, u32[]{:S(2)}, u32[]{:S(2)}) %all-to-all-start.3) | async-done | bytes 524320 | tf_op jit(solution)/shard_map/all_to_all | solution.py:288
  81.0 2.8 %shard_map.126 = (bf16[4,128,128]{2,1,0:T(8,128)(2,1)S(1)}, bf16[16,128,128]{2,1,0:T(8,128)(2,1)}) custom-call(s32[2]{0:T(128)S(1)} %copy-done.15, s32[2,64]{1,0:T(2,128)S(1)} %get-tuple-element.241, bf16[16,128,128]{2,1,0:T(8,128)(2,1)S(1)} %all-to-all-done.3.reached, bf16[4,128,128]{2,1,0:T(8,128)(2,1)S(1)} %bitcast.32, ...), custom_call_target="tpu_custom_call" | custom-call | tf_op jit(solution)/shard_map/pallas_call | solution.py:96
  83.8 10.7 %all-to-all-start.4 = ((bf16[16,128,128]{2,1,0:T(8,128)(2,1)}), bf16[16,128,128]{2,1,0:T(8,128)(2,1)S(1)}, u32[]{:S(2)}, u32[]{:S(2)}) async-start(bf16[16,128,128]{2,1,0:T(8,128)(2,1)} %get-tuple-element.73), calls=%async_computation.4 | async-start | bytes 1048576 | tf_op jit(solution)/shard_map/all_to_all | solution.py:339
  94.6 11.3 %all-to-all-done.4.slabs = bf16[16,128,128]{2,1,0:T(8,128)(2,1)S(1)} async-done(((bf16[16,128,128]{2,1,0:T(8,128)(2,1)}), bf16[16,128,128]{2,1,0:T(8,128)(2,1)S(1)}, u32[]{:S(2)}, u32[]{:S(2)}) %all-to-all-start.4) | async-done | bytes 524320 | tf_op jit(solution)/shard_map/all_to_all | solution.py:339
  105.9 6.2 %shard_map.127 = f32[16,32,128]{2,1,0:T(8,128)S(1)} custom-call(s32[1]{0:T(128)} %bitcast.5.quarter, bf16[16,128,128]{2,1,0:T(8,128)(2,1)S(1)} %all-to-all-done.4.slabs, f32[16,128,128]{2,1,0:T(8,128)S(1)} %copy-done.1, bf16[2,128,128]{2,1,0:T(8,128)(2,1)S(1)} %copy-done.4, bf16[2,128,128]{2,1,0:T(8,128)(2,1)S(1)} %copy-done.5), custom_call_target="tpu_custom_call" | custom-call | tf_op jit(solution)/shard_map/pallas_call | solution.py:96
  112.1 12.5 %all_to_all.42.spectra = f32[16,32,128]{2,1,0:T(8,128)S(1)} all-to-all(f32[16,32,128]{2,1,0:T(8,128)S(1)} %shard_map.127), channel_id=1, replica_groups=mesh['band'=32,'dom'=16] {'dom'}, dimensions={0} | all-to-all | bytes 524288 | tf_op jit(solution)/shard_map/all_to_all | solution.py:348
  124.6 2.8 %shard_map.128 = (bf16[4,128,128]{2,1,0:T(8,128)(2,1)S(1)}, bf16[16,128,128]{2,1,0:T(8,128)(2,1)}) custom-call(s32[2,2]{1,0:T(2,128)S(1)} %copy-done.16, f32[16,32,128]{2,1,0:T(8,128)S(1)} %all_to_all.42.spectra, bf16[4,128,128]{2,1,0:T(8,128)(2,1)S(1)} %get-tuple-element.74.source_rows, bf16[4,128,128]{2,1,0:T(8,128)(2,1)S(1)} %bitcast.33, ...), custom_call_target="tpu_custom_call" | custom-call | tf_op jit(solution)/shard_map/pallas_call | solution.py:96
  127.4 3.5 %all-to-all-start.6 = ((bf16[16,128,128]{2,1,0:T(8,128)(2,1)}), bf16[16,128,128]{2,1,0:T(8,128)(2,1)S(1)}, u32[]{:S(2)}, u32[]{:S(2)}) async-start(bf16[16,128,128]{2,1,0:T(8,128)(2,1)} %get-tuple-element.76), calls=%async_computation.6 | async-start | bytes 1048576 | tf_op jit(solution)/shard_map/all_to_all | solution.py:288
  131.0 0.7 fusion.2
  131.6 1.3 iota_compare_fusion.2
  132.9 1.3 iota_compare_fusion
  134.2 24.8 %all-to-all-done.6.held = bf16[16,128,128]{2,1,0:T(8,128)(2,1)S(1)} async-done(((bf16[16,128,128]{2,1,0:T(8,128)(2,1)}), bf16[16,128,128]{2,1,0:T(8,128)(2,1)S(1)}, u32[]{:S(2)}, u32[]{:S(2)}) %all-to-all-start.6) | async-done | bytes 524320 | tf_op jit(solution)/shard_map/all_to_all | solution.py:288
  159.1 1.7 shard_map.129
  160.7 3.7 %all-to-all-start.7 = ((bf16[32,128,128]{2,1,0:T(8,128)(2,1)}), bf16[32,128,128]{2,1,0:T(8,128)(2,1)S(1)}, u32[]{:S(2)}, u32[]{:S(2)}) async-start(bf16[32,128,128]{2,1,0:T(8,128)(2,1)} %shard_map.129), calls=%async_computation.7 | async-start | bytes 2097152 | tf_op jit(solution)/shard_map/all_to_all | solution.py:283
  164.4 1.3 select_select_fusion
  165.7 23.8 %all-to-all-done.7.near = bf16[32,128,128]{2,1,0:T(8,128)(2,1)S(1)} async-done(((bf16[32,128,128]{2,1,0:T(8,128)(2,1)}), bf16[32,128,128]{2,1,0:T(8,128)(2,1)S(1)}, u32[]{:S(2)}, u32[]{:S(2)}) %all-to-all-start.7) | async-done | bytes 1048608 | tf_op jit(solution)/shard_map/all_to_all | solution.py:283
  189.5 1.7 shard_map.130
  191.1 1.1 convert_element_type.7
  192.2 0.8 reshape.109
  (40 shorter events, 0.7 us)
Async XLA Ops:
  0.6 51.9 %copy-start = (bf16[32,16384]{1,0:T(8,128)(2,1)S(1)}, bf16[32,16384]{1,0:T(8,128)(2,1)}, u32[]{:S(2)}) copy-start(bf16[32,16384]{1,0:T(8,128)(2,1)} %param.15) | copy-start | bytes 3145732
  2.0 0.7 copy-start.18
  4.4 0.6 copy-start.12
  6.7 31.2 %all-to-all-start.2 = ((bf16[32,128,128]{2,1,0:T(8,128)(2,1)}), bf16[32,128,128]{2,1,0:T(8,128)(2,1)S(1)}, u32[]{:S(2)}, u32[]{:S(2)}) async-start(bf16[32,128,128]{2,1,0:T(8,128)(2,1)} %shard_map.124), calls=%async_computation.2 | async-start | bytes 2097152 | tf_op jit(solution)/shard_map/all_to_all | solution.py:283
  17.2 20.7 %copy-start.14 = (s32[16]{0:T(128)S(1)}, s32[16]{0:T(128)}, u32[]{:S(2)}) copy-start(s32[16]{0:T(128)} %shard_map.122.found) | copy-start | bytes 196
  38.7 0.8 copy-start.17
  39.5 13.0 %copy-start.16 = (s32[2,2]{1,0:T(2,128)S(1)}, s32[2,2]{1,0:T(2,128)}, u32[]{:S(2)}) copy-start(s32[2,2]{1,0:T(2,128)} %pair_tgt.1) | copy-start | bytes 52
  39.5 41.5 %all-to-all-start.3 = ((bf16[16,128,128]{2,1,0:T(8,128)(2,1)}), bf16[16,128,128]{2,1,0:T(8,128)(2,1)S(1)}, u32[]{:S(2)}, u32[]{:S(2)}) async-start(bf16[16,128,128]{2,1,0:T(8,128)(2,1)} %copy-done.17), calls=%async_computation.3 | async-start | bytes 1048576 | tf_op jit(solution)/shard_map/all_to_all | solution.py:288
  52.6 28.4 %copy-start.6 = (bf16[2,128,128]{2,1,0:T(8,128)(2,1)S(1)}, bf16[2,128,128]{2,1,0:T(8,128)(2,1)}, u32[]{:S(2)}) copy-start(bf16[2,128,128]{2,1,0:T(8,128)(2,1)} %constant.100.clone.z_fwd) | copy-start | bytes 196612
  53.3 27.7 %copy-start.3 = (bf16[2,256,256]{2,1,0:T(8,128)(2,1)S(1)}, bf16[2,256,256]{2,1,0:T(8,128)(2,1)}, u32[]{:S(2)}) copy-start(bf16[2,256,256]{2,1,0:T(8,128)(2,1)} %constant.102.clone.y_fwd) | copy-start | bytes 786436
  53.3 27.7 %copy-start.15 = (s32[2]{0:T(128)S(1)}, s32[2]{0:T(128)}, u32[]{:S(2)}) copy-start(s32[2]{0:T(128)} %pad_add_fusion.2.place) | copy-start | bytes 28
  53.3 52.5 %copy-start.1 = (f32[16,128,128]{2,1,0:T(8,128)S(1)}, f32[16,128,128]{2,1,0:T(8,128)}, u32[]{:S(2)}) copy-start(f32[16,128,128]{2,1,0:T(8,128)} %constant.106.clone.spectrum) | copy-start | bytes 3145732
  83.8 22.0 %copy-start.4 = (bf16[2,128,128]{2,1,0:T(8,128)(2,1)S(1)}, bf16[2,128,128]{2,1,0:T(8,128)(2,1)}, u32[]{:S(2)}) copy-start(bf16[2,128,128]{2,1,0:T(8,128)(2,1)} %constant.104.clone.x_fwd) | copy-start | bytes 196612
  83.8 22.0 %copy-start.5 = (bf16[2,128,128]{2,1,0:T(8,128)(2,1)S(1)}, bf16[2,128,128]{2,1,0:T(8,128)(2,1)}, u32[]{:S(2)}) copy-start(bf16[2,128,128]{2,1,0:T(8,128)(2,1)} %constant.105.clone.x_bwd) | copy-start | bytes 196612
  83.8 22.0 %all-to-all-start.4 = ((bf16[16,128,128]{2,1,0:T(8,128)(2,1)}), bf16[16,128,128]{2,1,0:T(8,128)(2,1)S(1)}, u32[]{:S(2)}, u32[]{:S(2)}) async-start(bf16[16,128,128]{2,1,0:T(8,128)(2,1)} %get-tuple-element.73), calls=%async_computation.4 | async-start | bytes 1048576 | tf_op jit(solution)/shard_map/all_to_all | solution.py:339
  112.1 12.5 %copy-start.2 = (bf16[2,256,256]{2,1,0:T(8,128)(2,1)S(1)}, bf16[2,256,256]{2,1,0:T(8,128)(2,1)}, u32[]{:S(2)}) copy-start(bf16[2,256,256]{2,1,0:T(8,128)(2,1)} %constant.103.clone.y_bwd) | copy-start | bytes 786436
  112.1 12.5 %copy-start.7 = (bf16[2,128,128]{2,1,0:T(8,128)(2,1)S(1)}, bf16[2,128,128]{2,1,0:T(8,128)(2,1)}, u32[]{:S(2)}) copy-start(bf16[2,128,128]{2,1,0:T(8,128)(2,1)} %constant.101.clone.z_bwd) | copy-start | bytes 196612
  127.4 31.6 %all-to-all-start.6 = ((bf16[16,128,128]{2,1,0:T(8,128)(2,1)}), bf16[16,128,128]{2,1,0:T(8,128)(2,1)S(1)}, u32[]{:S(2)}, u32[]{:S(2)}) async-start(bf16[16,128,128]{2,1,0:T(8,128)(2,1)} %get-tuple-element.76), calls=%async_computation.6 | async-start | bytes 1048576 | tf_op jit(solution)/shard_map/all_to_all | solution.py:288
  160.7 28.8 %all-to-all-start.7 = ((bf16[32,128,128]{2,1,0:T(8,128)(2,1)}), bf16[32,128,128]{2,1,0:T(8,128)(2,1)S(1)}, u32[]{:S(2)}, u32[]{:S(2)}) async-start(bf16[32,128,128]{2,1,0:T(8,128)(2,1)} %shard_map.129), calls=%async_computation.7 | async-start | bytes 2097152 | tf_op jit(solution)/shard_map/all_to_all | solution.py:283
  164.4 25.1 %copy-start.13 = (s32[32]{0:T(128)S(1)}, s32[32]{0:T(128)}, u32[]{:S(2)}) copy-start(s32[32]{0:T(128)} %shard_map.123.sent) | copy-start | bytes 388

commit v5 on v4

v5 whole, which is shorter than its diff:
```python
import numpy as np
import jax
import jax.numpy as jnp
from jax import lax
from jax.experimental import pallas as pl
from jax.experimental.pallas import tpu as pltpu
from jax.sharding import PartitionSpec as P

SIDE = 64
SWEEPS = 8
RING = 16
CAP = 6
STEPS = (1, -1, 2)
ROW = 128
HALF = 64
VMEM_LIMIT = 48 * 1024 * 1024
F32 = jnp.float32
BF16 = jnp.bfloat16


def eigen_system():
    line = np.zeros((SIDE, SIDE))
    for delta, weight in ((0, 30.0), (1, -16.0), (2, 1.0)):
        for i in range(SIDE - delta):
            line[i, i + delta] = weight / 12.0
            line[i + delta, i] = weight / 12.0
    values, vectors = np.linalg.eigh(line)
    return values, vectors * np.where(vectors[0] < 0, -1.0, 1.0)[None, :]


def halves(matrix):
    high = np.asarray(matrix, np.float32).astype(jnp.bfloat16)
    low = (np.asarray(matrix, np.float64) - high.astype(np.float64)).astype(jnp.bfloat16)
    return np.stack([high, low])


def tables():
    values, v = eigen_system()
    along_z = np.kron(np.eye(2), v)
    even, odd = v[0::2], v[1::2]
    fwd = np.zeros((2, 32, 4, 2, 4, 32))
    bwd = np.zeros((2, 4, 32, 2, 32, 4))
    for x in range(4):
        fwd[0, :, x, 0, x, :] = even[:, 0::2].T
        fwd[0, :, x, 1, x, :] = odd[:, 0::2].T
        fwd[1, :, x, 0, x, :] = odd[:, 1::2].T
        fwd[1, :, x, 1, x, :] = even[:, 1::2].T
        bwd[0, x, :, 0, :, x] = even[:, 0::2]
        bwd[0, x, :, 1, :, x] = even[:, 1::2]
        bwd[1, x, :, 0, :, x] = odd[:, 1::2]
        bwd[1, x, :, 1, :, x] = odd[:, 0::2]
    along_x = np.zeros((4, SIDE, RING, 4, 4))
    for pick in range(4):
        along_x[pick, :, :, pick, :] = v.T.reshape(SIDE, RING, 4)
    rows = np.arange(SIDE).reshape(8, 4, 1, 2, 1)
    spectrum = values[rows] + values.reshape(1, 1, SIDE, 1, 1) + values.reshape(1, 1, 1, 1, SIDE)
    return dict(
        z_fwd=halves(along_z),
        z_bwd=halves(along_z.T),
        y_fwd=halves(fwd.reshape(256, 256)),
        y_bwd=halves(bwd.reshape(256, 256)),
        x_fwd=halves(along_x.reshape(256, 256)),
        x_bwd=halves(along_x.reshape(256, 256).T),
        spectrum=spectrum.reshape(8, 256, ROW).astype(np.float32),
    )


def split(value):
    high = value.astype(BF16)
    return high, (value - high.astype(F32)).astype(BF16)


def mm(left, right):
    return jnp.dot(left, right, preferred_element_type=F32)


def left_mul(table, value):
    high, low = split(value)
    return mm(table[0], high) + mm(table[0], low) + mm(table[1], high)


def right_mul(value, table):
    high, low = split(value)
    return mm(high, table[0]) + mm(low, table[0]) + mm(high, table[1])


def swap_halves(value):
    return jnp.concatenate([value[:, HALF:], value[:, :HALF]], axis=1)


def by_half(both):
    lane = lax.broadcasted_iota(jnp.int32, (ROW, ROW), 1)
    return jnp.where(lane < HALF, both[:ROW], both[ROW:])


def vmem_call(kernel, outs, operands, scalars=0, scratch=()):
    whole = pl.BlockSpec(memory_space=pltpu.VMEM)
    smem = pl.BlockSpec(memory_space=pltpu.SMEM)
    return pl.pallas_call(
        kernel,
        out_shape=outs,
        in_specs=[smem] * scalars + [whole] * (len(operands) - scalars),
        out_specs=[whole] * len(outs),
        scratch_shapes=list(scratch),
        compiler_params=pltpu.CompilerParams(vmem_limit_bytes=VMEM_LIMIT),
    )(*operands)


def smem_call(kernel, size, *operands):
    smem = pl.BlockSpec(memory_space=pltpu.SMEM)
    return pl.pallas_call(
        kernel,
        out_shape=struct((size,), jnp.int32),
        in_specs=[smem] * len(operands),
        out_specs=smem,
    )(*operands)


def struct(shape, dtype):
    return jax.ShapeDtypeStruct(shape, dtype)


def ring(value):
    return lax.bitwise_and(value, RING - 1)


def want_of(pair_src, z, x, want):
    quad, slot = lax.shift_right_logical(want, 2), lax.bitwise_and(want, 3)
    block = lax.shift_right_logical(slot, 1)
    band = 2 * (4 * quad + lax.bitwise_and(z, 3)) + x
    source = pair_src[block, 2 * band + lax.bitwise_and(slot, 1)]
    z_own = lax.shift_right_logical(source, 3)
    other = lax.bitwise_xor(lax.bitwise_and(lax.shift_right_logical(source, 2), 1), x)
    return z_own, 8 * other + 4 * block + lax.bitwise_and(source, 3)


def wants_of(pair_src, z, x):
    for want in range(16):
        yield (want,) + want_of(pair_src, z, x, jnp.int32(want))


def in_round(hit, count):
    return jnp.logical_and(hit, jnp.logical_and(count >= 0, count < CAP))


def sent_kernel(place, pair_src, sent):
    z, x = place[0], place[1]
    for lane, step in enumerate(STEPS):
        for n in range(CAP):
            sent[lane * CAP + n] = -1
        count = -CAP * place[2]
        for _, z_own, row in wants_of(pair_src, z + step, x):
            hit = z_own == z

            @pl.when(in_round(hit, count))
            def _():
                sent[lane * CAP + count] = row

            count = count + hit.astype(jnp.int32)


def found_kernel(place, pair_src, found):
    z, x, turn = place[0], place[1], place[2]
    counts = [-CAP * turn for _ in STEPS]
    for want, z_own, row in wants_of(pair_src, z, x):
        at = jnp.where(jnp.logical_and(z_own == z, turn == 0), row, -1)
        for lane, step in enumerate(STEPS):
            hit = z_own == ring(z - step)
            at = jnp.where(in_round(hit, counts[lane]), 16 + lane * CAP + counts[lane], at)
            counts[lane] = counts[lane] + hit.astype(jnp.int32)
        found[want] = at


def pack_rows_kernel(sent, own, other, *outs):
    for lane, out in enumerate(outs):
        for n in range(CAP):
            row = sent[lane * CAP + n]

            @pl.when(row >= 0)
            def _():
                @pl.when(row < 8)
                def _():
                    out[n] = own[row]

                @pl.when(row >= 8)
                def _():
                    out[n] = other[row - 8]


def place_rows_kernel(found, own, other, *refs):
    out = refs[-1]
    for before in refs[3:-1]:
        out[...] = before[...]
    spans = [(own, 0, 8), (other, 8, 16)]
    spans += [(near, 16 + lane * CAP, 16 + lane * CAP + CAP) for lane, near in enumerate(refs[:3])]
    for want in range(16):
        at = found[want]

        @pl.when(at >= 0)
        def _():
            for rows, first, last in spans:

                @pl.when(jnp.logical_and(at >= first, at < last))
                def _():
                    out[want] = rows[at - first]


def for_each_solved(place, pair_src, body):
    z, x = place[0], place[1]

    def step(want, carry):
        z_own, _ = want_of(pair_src, z, x, want)
        ahead = ring(z - z_own)

        @pl.when(jnp.logical_or(ahead <= 2, ahead == RING - 1))
        def _():
            body(want)

        return carry

    lax.fori_loop(0, 16, step, 0)


def density_kernel(place, pair_src, sources, wanted, z_fwd, y_fwd, spectra):
    def body(want):
        density = sources[want].astype(F32) * wanted[want].astype(F32)
        along = right_mul(density, z_fwd)
        mixed = left_mul(y_fwd, jnp.concatenate([along, swap_halves(along)], axis=0))
        spectra[want] = by_half(mixed).astype(BF16)

    for_each_solved(place, pair_src, body)


def solve_kernel(slabs, spectrum, x_fwd, x_bwd, out, residual, direction, total):
    def dot_of(value):
        return jnp.sum(value.reshape(32, 8, ROW), axis=0)

    zero = jnp.zeros((8, ROW), F32)

    def start(j, carry):
        norm, power = carry
        part = slabs[:, pl.ds(pl.multiple_of(16 * j, 16), 16), :].reshape(256, ROW)
        value = mm(x_fwd[0], part) + mm(x_fwd[1], part)
        direction[j] = value
        square = value * value
        return norm + dot_of(square), power + dot_of(square * spectrum[j])

    norm, power = lax.fori_loop(0, 8, start, (zero, zero))
    norm, power = jnp.sum(norm), jnp.sum(power)
    step, ratio = norm / power, jnp.float32(0.0)
    for sweep in range(SWEEPS - 1):

        def advance(j, carry, sweep=sweep, step=step, ratio=ratio):
            new, power = carry
            lam = spectrum[j]
            if sweep == 0:
                d = direction[j]
                r = d - step * (lam * d)
                total[j] = step * d
            else:
                r = residual[j]
                d = r + ratio * direction[j]
                r = r - step * (lam * d)
                direction[j] = d
                total[j] = total[j] + step * d
            residual[j] = r
            square = r * r
            return new + dot_of(square), power + dot_of(square * lam)

        new, power = lax.fori_loop(0, 8, advance, (zero, zero))
        new, power = jnp.sum(new), jnp.sum(power)
        ratio = new / norm
        step = new / (power - ratio * new / step)
        norm = new

    def finish(j, carry):
        value = total[j] + step * (residual[j] + ratio * direction[j])
        part = left_mul(x_bwd, value).reshape(RING, 16, ROW)
        out[:, pl.ds(pl.multiple_of(16 * j, 16), 16), :] = part.astype(out.dtype)
        return carry

    lax.fori_loop(0, 8, finish, 0)


def term_kernel(place, pair_src, spectra, sources, wanted, z_bwd, y_bwd, terms, shares):
    def body(want):
        rows = spectra[want]
        rows = jnp.concatenate([rows, swap_halves(rows)], axis=0)
        potential = right_mul(by_half(mm(y_bwd[0], rows) + mm(y_bwd[1], rows)), z_bwd)
        terms[want] = (-potential * wanted[want].astype(F32)).astype(BF16)
        shares[want] = (-potential * sources[want].astype(F32)).astype(BF16)

    for_each_solved(place, pair_src, body)


def pack_terms_kernel(found, terms, *outs):
    for want in range(16):
        at = found[want] - 16

        @pl.when(at >= 0)
        def _():
            for lane, out in enumerate(outs):

                @pl.when(jnp.logical_and(at >= lane * CAP, at < lane * CAP + CAP))
                def _():
                    out[at - lane * CAP] = terms[want]


def add_terms_kernel(sent, found, terms, *refs):
    near, before, (mine, partner, held) = refs[:3], refs[3:-3], refs[-3:]
    mine[...] = before[0][...] if before else jnp.zeros((8, ROW, ROW), F32)
    held[...] = before[1][...].astype(F32) if before else jnp.zeros((8, ROW, ROW), F32)

    def add(row, term):
        @pl.when(row < 8)
        def _():
            mine[row] = mine[row] + term[...].astype(F32)

        @pl.when(row >= 8)
        def _():
            held[row - 8] = held[row - 8] + term[...].astype(F32)

    for want in range(16):
        at = found[want]

        @pl.when(jnp.logical_and(at >= 0, at < 16))
        def _():
            add(at, terms.at[want])

    for lane in range(3):
        for n in range(CAP):
            row = sent[lane * CAP + n]

            @pl.when(row >= 0)
            def _():
                add(row, near[lane].at[n])

    partner[...] = held[...].astype(BF16)


def target_kernel(place, pair_src, pair_tgt, shares, rows, held):
    z, x = place[0], place[1]
    quad = lax.shift_right_logical(z, 2)
    for p in range(4):
        z_own, _ = want_of(pair_src, z, x, 4 * quad + p)
        ahead = lax.bitwise_and(z - z_own, 3)
        relay = ring(z_own + jnp.where(ahead == 3, -1, ahead))
        held[p] = shares[4 * lax.shift_right_logical(relay, 2) + p].astype(F32)
    for p in range(4):
        same = jnp.zeros((ROW, ROW), F32)
        for other in range(4):
            hit = pair_tgt[p // 2, p % 2] == pair_tgt[other // 2, other % 2]
            same = same + jnp.where(hit, held[other], 0.0)
        rows[p] = same.astype(BF16)


def shift(value, steps):
    pairs = [(2 * z + x, 2 * ((z + steps) % RING) + x) for z in range(RING) for x in range(2)]
    return lax.ppermute(value, "band", pairs)


def across(value):
    return lax.ppermute(value, "band", [(i, i ^ 1) for i in range(32)])


def along_ring(value):
    groups = [[8 * quad + member for quad in range(4)] for member in range(8)]
    return lax.all_to_all(value, "band", 0, 0, axis_index_groups=groups, tiled=True)


def rounds_of(pair_src):
    band = jnp.arange(pair_src.shape[1], dtype=jnp.int32) // 2
    z, x = band // 2, band % 2
    z_own = pair_src // 8
    key = (z_own * 8 + (z % 4) * 2 + x).reshape(-1)
    moves = ((z_own - z) % 4 != 0).astype(jnp.int32).reshape(-1)
    shared = moves * jnp.sum((key[:, None] == key[None, :]).astype(jnp.int32), axis=1)
    return jnp.maximum(1, (jnp.max(shared) + CAP - 1) // CAP)


def per_device(targets, sources, pair_tgt, pair_src):
    table = {name: jnp.asarray(value) for name, value in tables().items()}
    band = lax.axis_index("band")
    rounds = rounds_of(pair_src)
    sixteen = struct((16, ROW, ROW), BF16)
    packets = [struct((CAP, ROW, ROW), BF16)] * 3

    def place_in(turn):
        turn = jnp.asarray(turn, jnp.int32)
        return jnp.stack([band // 2, band % 2, turn]).astype(jnp.int32)

    def sent_in(turn):
        return smem_call(sent_kernel, 3 * CAP, place_in(turn), pair_src)

    def found_in(turn):
        return smem_call(found_kernel, 16, place_in(turn), pair_src)

    ids = pair_tgt.reshape(4)
    wanted = targets[ids].reshape(4, ROW, ROW)
    wanted = along_ring(jnp.concatenate([wanted] * 4, axis=0))

    own = sources.reshape(8, ROW, ROW)
    other = across(own)

    def deliver(sent, found, before):
        packed = vmem_call(pack_rows_kernel, packets, (sent, own, other), scalars=1)
        near = tuple(shift(packet, step) for packet, step in zip(packed, STEPS))
        operands = (found, own, other) + near + before
        return vmem_call(place_rows_kernel, [sixteen], operands, scalars=1)[0]

    sent, found = sent_in(0), found_in(0)
    rows = lax.fori_loop(
        1,
        rounds,
        lambda turn, before: deliver(sent_in(turn), found_in(turn), (before,)),
        deliver(sent, found, ()),
    )
    where = (place_in(0), pair_src)
    (spectra,) = vmem_call(
        density_kernel,
        [sixteen],
        where + (rows, wanted, table["z_fwd"], table["y_fwd"]),
        scalars=2,
    )
    slabs = lax.all_to_all(spectra, "dom", 0, 0, tiled=True)
    (solved,) = vmem_call(
        solve_kernel,
        [sixteen],
        (slabs, table["spectrum"], table["x_fwd"], table["x_bwd"]),
        scratch=[pltpu.VMEM((8, 256, ROW), F32)] * 3,
    )
    back = lax.all_to_all(solved, "dom", 0, 0, tiled=True)
    terms, shares = vmem_call(
        term_kernel,
        [sixteen, sixteen],
        where + (back, rows, wanted, table["z_bwd"], table["y_bwd"]),
        scalars=2,
    )
    shares = along_ring(shares)

    def collect(sent, found, before):
        packed = vmem_call(pack_terms_kernel, packets, (found, terms), scalars=1)
        near = tuple(shift(packet, -step) for packet, step in zip(packed, STEPS))
        outs = [struct((8, ROW, ROW), F32), struct((8, ROW, ROW), BF16)]
        operands = (sent, found, terms) + near + before
        scratch = [pltpu.VMEM((8, ROW, ROW), F32)]
        return vmem_call(add_terms_kernel, outs, operands, scalars=2, scratch=scratch)

    mine, partner = lax.fori_loop(
        1,
        rounds,
        lambda turn, before: collect(sent_in(turn), found_in(turn), tuple(before)),
        collect(sent, found, ()),
    )
    owned = (mine + across(partner).astype(F32)).astype(BF16).reshape(sources.shape)

    (target_rows,) = vmem_call(
        target_kernel,
        [struct((4, ROW, ROW), BF16)],
        where + (pair_tgt, shares),
        scalars=3,
        scratch=[pltpu.VMEM((4, ROW, ROW), F32)],
    )
    flat = target_rows.reshape(4, targets.shape[1])
    slots = jnp.arange(targets.shape[0], dtype=jnp.int32)[:, None]
    summed = jnp.zeros(targets.shape, BF16)
    for p in range(4):
        summed = jnp.where(slots == ids[p], flat[p][None, :], summed)
    return summed, owned


def solution(mesh):
    return jax.shard_map(
        per_device,
        mesh=mesh,
        in_specs=(P("band", "dom"), P(None, "band", "dom"), P(None, "band"), P()),
        out_specs=(P("band", "dom"), P(None, "band", "dom")),
        check_vma=False,
    )
```

time: 197 us -> 176 us (0.89)
  the two profiles are of different devices: /device:TPU:1 before, /device:TPU:64 now
where the time goes in v5:
time: 176 us; the launch traced here: 175 us
  starting transfers between devices  58.6 us (33%)
  waiting for transfers between devices  44.8 us (25%)
  blocking collectives  34.4 us (20%)
  Pallas kernels  23.1 us (13%)
  other arithmetic  7.23 us (4%)
  local copies, waits for them, and re-layouts  4.97 us (3%)
    ppermute x6, waiting for transfers between devices, shift(): return lax.ppermute(value, 'band', pairs)  37.2 us
    all_to_all x2, starting transfers between devices, along_ring(): lax.all_to_all(value, 'band', 0, 0, axis_index_groups=groups, tiled=True)  27.4 us
    ppermute x6, starting transfers between devices, shift(): return lax.ppermute(value, 'band', pairs)  25.9 us
    pallas_call x8, Pallas kernels, vmem_call(): pl.pallas_call(kernel, out_shape=outs, in_specs=[smem] * scalars + [whole...  20.2 us
    all_to_all x1, blocking collectives, per_device(): slabs = lax.all_to_all(spectra, 'dom', 0, 0, tiled=True)  19.3 us
    all_to_all x1, blocking collectives, per_device(): back = lax.all_to_all(solved, 'dom', 0, 0, tiled=True)  15.1 us
    ppermute x2, waiting for transfers between devices, across(): return lax.ppermute(value, 'band', [(i, i ^ 1) for i in range(32)])  7.59 us
    ppermute x2, starting transfers between devices, across(): return lax.ppermute(value, 'band', [(i, i ^ 1) for i in range(32)])  5.31 us
  transfers between devices with their start and end apart: 10, of which 7 were waited for; matrix products, arithmetic and copies ran while one was open for 4% of the time, Pallas kernels for 5%

profile of v5, /device:TPU:64, one launch (start us, length us, event | category | flops | bytes accessed | tf_op | source)
XLA Modules:
  0.0 174.8 jit_solution(1201667818379474728)
XLA Ops:
  3.4 13.4 %all-to-all-start = ((bf16[16,128,128]{2,1,0:T(8,128)(2,1)}), bf16[16,128,128]{2,1,0:T(8,128)(2,1)S(1)}, u32[]{:S(2)}, u32[]{:S(2)}) async-start(bf16[16,128,128]{2,1,0:T(8,128)(2,1)} %pad_maximum_fusion), calls=%async_computation | async-start | bytes 1048576 | tf_op jit(solution)/shard_map/all_to_all | solution.py:368
  17.1 3.4 %collective-permute-start.6 = (bf16[8,128,128]{2,1,0:T(8,128)(2,1)S(1)}, bf16[8,128,128]{2,1,0:T(8,128)(2,1)}, u32[]{:S(2)}, u32[]{:S(2)}) collective-permute-start(bf16[8,128,128]{2,1,0:T(8,128)(2,1)S(1)} %reshape.135.own), channel_id=1, source_target_pairs={{0,16},{16,0},{32,48},{48,32},{64,80},{80,64},{96,112},{112,96},{1... | collective-permute-start | bytes 786440 | tf_op jit(solution)/shard_map/ppermute | solution.py:363
  21.2 1.4 shard_map.122.found
  22.6 1.5 shard_map.123.sent
  24.5 2.4 %collective-permute-done.6.other = bf16[8,128,128]{2,1,0:T(8,128)(2,1)} collective-permute-done((bf16[8,128,128]{2,1,0:T(8,128)(2,1)S(1)}, bf16[8,128,128]{2,1,0:T(8,128)(2,1)}, u32[]{:S(2)}, u32[]{:S(2)}) %collective-permute-start.6) | collective-permute-done | bytes 262176 | tf_op jit(solution)/shard_map/ppermute | solution.py:363
  26.9 1.1 shard_map.124
  28.1 2.9 %collective-permute-start.7 = (bf16[6,128,128]{2,1,0:T(8,128)(2,1)S(1)}, bf16[6,128,128]{2,1,0:T(8,128)(2,1)S(1)}, u32[]{:S(2)}, u32[]{:S(2)}) collective-permute-start(bf16[6,128,128]{2,1,0:T(8,128)(2,1)S(1)} %get-tuple-element.529), channel_id=1, source_target_pairs={{0,32},{16,48},{32,64},{48,80},{64,96},{80,112},{96,128},{112,144}... | collective-permute-start | bytes 589832 | tf_op jit(solution)/shard_map/ppermute | solution.py:359
  31.0 2.9 %collective-permute-start.8 = (bf16[6,128,128]{2,1,0:T(8,128)(2,1)S(1)}, bf16[6,128,128]{2,1,0:T(8,128)(2,1)S(1)}, u32[]{:S(2)}, u32[]{:S(2)}) collective-permute-start(bf16[6,128,128]{2,1,0:T(8,128)(2,1)S(1)} %get-tuple-element.530), channel_id=1, source_target_pairs={{0,480},{16,496},{32,0},{48,16},{64,32},{80,48},{96,64},{112,80},{... | collective-permute-start | bytes 589832 | tf_op jit(solution)/shard_map/ppermute | solution.py:359
  33.9 7.8 %collective-permute-start.9 = (bf16[6,128,128]{2,1,0:T(8,128)(2,1)S(1)}, bf16[6,128,128]{2,1,0:T(8,128)(2,1)S(1)}, u32[]{:S(2)}, u32[]{:S(2)}) collective-permute-start(bf16[6,128,128]{2,1,0:T(8,128)(2,1)S(1)} %get-tuple-element.531), channel_id=1, source_target_pairs={{0,64},{16,80},{32,96},{48,112},{64,128},{80,144},{96,160},{112,17... | collective-permute-start | bytes 589832 | tf_op jit(solution)/shard_map/ppermute | solution.py:359
  43.1 2.1 %collective-permute-done.7.refs_0_ = bf16[6,128,128]{2,1,0:T(8,128)(2,1)S(1)} collective-permute-done((bf16[6,128,128]{2,1,0:T(8,128)(2,1)S(1)}, bf16[6,128,128]{2,1,0:T(8,128)(2,1)S(1)}, u32[]{:S(2)}, u32[]{:S(2)}) %collective-permute-start.7) | collective-permute-done | bytes 196640 | tf_op jit(solution)/shard_map/ppermute | solution.py:359
  45.2 2.8 %collective-permute-done.8.refs_1_ = bf16[6,128,128]{2,1,0:T(8,128)(2,1)S(1)} collective-permute-done((bf16[6,128,128]{2,1,0:T(8,128)(2,1)S(1)}, bf16[6,128,128]{2,1,0:T(8,128)(2,1)S(1)}, u32[]{:S(2)}, u32[]{:S(2)}) %collective-permute-start.8) | collective-permute-done | bytes 196640 | tf_op jit(solution)/shard_map/ppermute | solution.py:359
  48.0 5.4 %collective-permute-done.9.refs_2_ = bf16[6,128,128]{2,1,0:T(8,128)(2,1)S(1)} collective-permute-done((bf16[6,128,128]{2,1,0:T(8,128)(2,1)S(1)}, bf16[6,128,128]{2,1,0:T(8,128)(2,1)S(1)}, u32[]{:S(2)}, u32[]{:S(2)}) %collective-permute-start.9) | collective-permute-done | bytes 196640 | tf_op jit(solution)/shard_map/ppermute | solution.py:359
  53.4 1.9 %shard_map.125 = bf16[16,128,128]{2,1,0:T(8,128)(2,1)} custom-call(s32[16]{0:T(128)S(1)} %copy-done.13, bf16[8,128,128]{2,1,0:T(8,128)(2,1)S(1)} %reshape.135.own, bf16[8,128,128]{2,1,0:T(8,128)(2,1)} %collective-permute-done.6.other, bf16[6,128,128]{2,1,0:T(8,128)(2,1)S(1)} %collective-permute-done.7.refs_0_, ...), custom_call_target="tpu_custom_call" | custom-call | tf_op jit(solution)/shard_map/pallas_call | solution.py:99
  55.3 0.9 copy-done.5
  56.3 2.5 %shard_map.126 = bf16[16,128,128]{2,1,0:T(8,128)(2,1)S(1)} custom-call(s32[3]{0:T(128)S(1)} %copy-done.12, s32[2,64]{1,0:T(2,128)S(1)} %get-tuple-element.788, bf16[16,128,128]{2,1,0:T(8,128)(2,1)} %get-tuple-element.532.sources, bf16[16,128,128]{2,1,0:T(8,128)(2,1)S(1)} %all-to-all-done.wanted, bf16[2,128,128]{2,1,0:T(8,128)(2,1)S(1)} %copy-done.8, ...), custom_call_target="tpu_custom_call" | custom-call | tf_op jit(solution)/shard_map/pallas_call | solution.py:99
  58.8 19.3 %all_to_all.20.slabs = bf16[16,128,128]{2,1,0:T(8,128)(2,1)S(1)} all-to-all(bf16[16,128,128]{2,1,0:T(8,128)(2,1)S(1)} %shard_map.126), channel_id=1, replica_groups=mesh['band'=32,'dom'=16] {'dom'}, dimensions={0} | all-to-all | bytes 1048576 | tf_op jit(solution)/shard_map/all_to_all | solution.py:425
  78.2 8.8 %shard_map.127 = bf16[16,128,128]{2,1,0:T(8,128)(2,1)S(1)} custom-call(bf16[16,128,128]{2,1,0:T(8,128)(2,1)S(1)} %all_to_all.20.slabs, f32[8,256,128]{2,1,0:T(8,128)S(1)} %copy-done.1, bf16[2,256,256]{2,1,0:T(8,128)(2,1)S(1)} %copy-done.3, bf16[2,256,256]{2,1,0:T(8,128)(2,1)S(1)} %copy-done.2), custom_call_target="tpu_custom_call" | custom-call | tf_op jit(solution)/shard_map/pallas_call | solution.py:99
  87.0 15.1 %all_to_all.21.spectra = bf16[16,128,128]{2,1,0:T(8,128)(2,1)S(1)} all-to-all(bf16[16,128,128]{2,1,0:T(8,128)(2,1)S(1)} %shard_map.127), channel_id=1, replica_groups=mesh['band'=32,'dom'=16] {'dom'}, dimensions={0} | all-to-all | bytes 1048576 | tf_op jit(solution)/shard_map/all_to_all | solution.py:432
  102.1 2.6 %shard_map.128 = (bf16[16,128,128]{2,1,0:T(8,128)(2,1)S(1)}, bf16[16,128,128]{2,1,0:T(8,128)(2,1)}) custom-call(s32[3]{0:T(128)S(1)} %copy-done.12, s32[2,64]{1,0:T(2,128)S(1)} %get-tuple-element.788, bf16[16,128,128]{2,1,0:T(8,128)(2,1)S(1)} %all_to_all.21.spectra, bf16[16,128,128]{2,1,0:T(8,128)(2,1)S(1)} %copy-done.16, ...), custom_call_target="tpu_custom_call" | custom-call | tf_op jit(solution)/shard_map/pallas_call | solution.py:99
  104.8 14.0 %all-to-all-start.3 = ((bf16[16,128,128]{2,1,0:T(8,128)(2,1)}), bf16[16,128,128]{2,1,0:T(8,128)(2,1)S(1)}, u32[]{:S(2)}, u32[]{:S(2)}) async-start(bf16[16,128,128]{2,1,0:T(8,128)(2,1)} %get-tuple-element.533), calls=%async_computation.3 | async-start | bytes 1048576 | tf_op jit(solution)/shard_map/all_to_all | solution.py:368
  119.4 2.5 %collective-permute-start.10 = (bf16[6,128,128]{2,1,0:T(8,128)(2,1)S(1)}, bf16[6,128,128]{2,1,0:T(8,128)(2,1)S(1)}, u32[]{:S(2)}, u32[]{:S(2)}) collective-permute-start(bf16[6,128,128]{2,1,0:T(8,128)(2,1)S(1)} %get-tuple-element.535), channel_id=1, source_target_pairs={{0,480},{16,496},{32,0},{48,16},{64,32},{80,48},{96,64},{112,80},{... | collective-permute-start | bytes 589832 | tf_op jit(solution)/shard_map/ppermute | solution.py:359
  122.0 3.3 %collective-permute-start.11 = (bf16[6,128,128]{2,1,0:T(8,128)(2,1)S(1)}, bf16[6,128,128]{2,1,0:T(8,128)(2,1)S(1)}, u32[]{:S(2)}, u32[]{:S(2)}) collective-permute-start(bf16[6,128,128]{2,1,0:T(8,128)(2,1)S(1)} %get-tuple-element.536), channel_id=1, source_target_pairs={{0,32},{16,48},{32,64},{48,80},{64,96},{80,112},{96,128},{112,144}... | collective-permute-start | bytes 589832 | tf_op jit(solution)/shard_map/ppermute | solution.py:359
  125.3 6.4 %collective-permute-start.12 = (bf16[6,128,128]{2,1,0:T(8,128)(2,1)S(1)}, bf16[6,128,128]{2,1,0:T(8,128)(2,1)S(1)}, u32[]{:S(2)}, u32[]{:S(2)}) collective-permute-start(bf16[6,128,128]{2,1,0:T(8,128)(2,1)S(1)} %get-tuple-element.537), channel_id=1, source_target_pairs={{0,448},{16,464},{32,480},{48,496},{64,0},{80,16},{96,32},{112,48}... | collective-permute-start | bytes 589832 | tf_op jit(solution)/shard_map/ppermute | solution.py:359
  131.8 16.9 %collective-permute-done.10.refs_0_ = bf16[6,128,128]{2,1,0:T(8,128)(2,1)S(1)} collective-permute-done((bf16[6,128,128]{2,1,0:T(8,128)(2,1)S(1)}, bf16[6,128,128]{2,1,0:T(8,128)(2,1)S(1)}, u32[]{:S(2)}, u32[]{:S(2)}) %collective-permute-start.10) | collective-permute-done | bytes 196640 | tf_op jit(solution)/shard_map/ppermute | solution.py:359
  148.7 10.0 %collective-permute-done.12.refs_2_ = bf16[6,128,128]{2,1,0:T(8,128)(2,1)S(1)} collective-permute-done((bf16[6,128,128]{2,1,0:T(8,128)(2,1)S(1)}, bf16[6,128,128]{2,1,0:T(8,128)(2,1)S(1)}, u32[]{:S(2)}, u32[]{:S(2)}) %collective-permute-start.12) | collective-permute-done | bytes 196640 | tf_op jit(solution)/shard_map/ppermute | solution.py:359
  158.7 1.8 %shard_map.131 = (f32[8,128,128]{2,1,0:T(8,128)}, bf16[8,128,128]{2,1,0:T(8,128)(2,1)}) custom-call(s32[18]{0:T(128)S(1)} %copy-done.14, s32[16]{0:T(128)S(1)} %copy-done.13, bf16[16,128,128]{2,1,0:T(8,128)(2,1)S(1)} %get-tuple-element.740.terms, bf16[6,128,128]{2,1,0:T(8,128)(2,1)S(1)} %collective-permute-done.10.refs_0_, ...), custom_call_target="tpu_custom_call" | custom-call | tf_op jit(solution)/shard_map/pallas_call | solution.py:99
  160.6 1.9 %collective-permute-start.13 = (bf16[8,128,128]{2,1,0:T(8,128)(2,1)}, bf16[8,128,128]{2,1,0:T(8,128)(2,1)S(1)}, u32[]{:S(2)}, u32[]{:S(2)}) collective-permute-start(bf16[8,128,128]{2,1,0:T(8,128)(2,1)} %get-tuple-element.541), channel_id=1, source_target_pairs={{0,16},{16,0},{32,48},{48,32},{64,80},{80,64},{96,112},{112,96},{1... | collective-permute-start | bytes 786440 | tf_op jit(solution)/shard_map/ppermute | solution.py:363
  163.2 1.2 iota_compare_fusion.2
  164.4 1.3 iota_compare_fusion
  165.7 5.2 %collective-permute-done.13 = bf16[8,128,128]{2,1,0:T(8,128)(2,1)S(1)} collective-permute-done((bf16[8,128,128]{2,1,0:T(8,128)(2,1)}, bf16[8,128,128]{2,1,0:T(8,128)(2,1)S(1)}, u32[]{:S(2)}, u32[]{:S(2)}) %collective-permute-start.13) | collective-permute-done | bytes 262176 | tf_op jit(solution)/shard_map/ppermute | solution.py:363
  170.9 1.1 add_convert_fusion
  173.5 1.3 select_select_fusion
  (55 shorter events, 7.7 us)
Async XLA Ops:
  0.6 1.2 copy-start
  3.4 13.4 %copy-start.19 = (bf16[2,4,16384]{2,1,0:T(4,128)(2,1)S(1)}, bf16[2,4,16384]{2,1,0:T(4,128)(2,1)}, u32[]{:S(2)}) copy-start(bf16[2,4,16384]{2,1,0:T(4,128)(2,1)} %param.16) | copy-start | bytes 786436
  3.4 51.9 %all-to-all-start = ((bf16[16,128,128]{2,1,0:T(8,128)(2,1)}), bf16[16,128,128]{2,1,0:T(8,128)(2,1)S(1)}, u32[]{:S(2)}, u32[]{:S(2)}) async-start(bf16[16,128,128]{2,1,0:T(8,128)(2,1)} %pad_maximum_fusion), calls=%async_computation | async-start | bytes 1048576 | tf_op jit(solution)/shard_map/all_to_all | solution.py:368
  17.1 9.8 %collective-permute-start.6 = (bf16[8,128,128]{2,1,0:T(8,128)(2,1)S(1)}, bf16[8,128,128]{2,1,0:T(8,128)(2,1)}, u32[]{:S(2)}, u32[]{:S(2)}) collective-permute-start(bf16[8,128,128]{2,1,0:T(8,128)(2,1)S(1)} %reshape.135.own), channel_id=1, source_target_pairs={{0,16},{16,0},{32,48},{48,32},{64,80},{80,64},{96,112},{112,96},{1... | collective-permute-start | bytes 786440 | tf_op jit(solution)/shard_map/ppermute | solution.py:363
  20.6 0.7 copy-start.18
  24.4 2.5 %copy-start.14 = (s32[18]{0:T(128)S(1)}, s32[18]{0:T(128)}, u32[]{:S(2)}) copy-start(s32[18]{0:T(128)} %shard_map.123.sent) | copy-start | bytes 220
  28.1 17.1 %collective-permute-start.7 = (bf16[6,128,128]{2,1,0:T(8,128)(2,1)S(1)}, bf16[6,128,128]{2,1,0:T(8,128)(2,1)S(1)}, u32[]{:S(2)}, u32[]{:S(2)}) collective-permute-start(bf16[6,128,128]{2,1,0:T(8,128)(2,1)S(1)} %get-tuple-element.529), channel_id=1, source_target_pairs={{0,32},{16,48},{32,64},{48,80},{64,96},{80,112},{96,128},{112,144}... | collective-permute-start | bytes 589832 | tf_op jit(solution)/shard_map/ppermute | solution.py:359
  31.0 17.0 %collective-permute-start.8 = (bf16[6,128,128]{2,1,0:T(8,128)(2,1)S(1)}, bf16[6,128,128]{2,1,0:T(8,128)(2,1)S(1)}, u32[]{:S(2)}, u32[]{:S(2)}) collective-permute-start(bf16[6,128,128]{2,1,0:T(8,128)(2,1)S(1)} %get-tuple-element.530), channel_id=1, source_target_pairs={{0,480},{16,496},{32,0},{48,16},{64,32},{80,48},{96,64},{112,80},{... | collective-permute-start | bytes 589832 | tf_op jit(solution)/shard_map/ppermute | solution.py:359
  33.9 19.5 %collective-permute-start.9 = (bf16[6,128,128]{2,1,0:T(8,128)(2,1)S(1)}, bf16[6,128,128]{2,1,0:T(8,128)(2,1)S(1)}, u32[]{:S(2)}, u32[]{:S(2)}) collective-permute-start(bf16[6,128,128]{2,1,0:T(8,128)(2,1)S(1)} %get-tuple-element.531), channel_id=1, source_target_pairs={{0,64},{16,80},{32,96},{48,112},{64,128},{80,144},{96,160},{112,17... | collective-permute-start | bytes 589832 | tf_op jit(solution)/shard_map/ppermute | solution.py:359
  43.1 10.3 %copy-start.13 = (s32[16]{0:T(128)S(1)}, s32[16]{0:T(128)}, u32[]{:S(2)}) copy-start(s32[16]{0:T(128)} %shard_map.122.found) | copy-start | bytes 196
  55.3 0.9 copy-start.5
  55.3 1.0 copy-start.8
  55.3 0.9 copy-start.12
  56.3 21.9 %copy-start.1 = (f32[8,256,128]{2,1,0:T(8,128)S(1)}, f32[8,256,128]{2,1,0:T(8,128)}, u32[]{:S(2)}) copy-start(f32[8,256,128]{2,1,0:T(8,128)} %constant.224.clone.spectrum) | copy-start | bytes 3145732
  58.8 19.4 %copy-start.2 = (bf16[2,256,256]{2,1,0:T(8,128)(2,1)S(1)}, bf16[2,256,256]{2,1,0:T(8,128)(2,1)}, u32[]{:S(2)}) copy-start(bf16[2,256,256]{2,1,0:T(8,128)(2,1)} %constant.223.clone.x_bwd) | copy-start | bytes 786436
  58.8 19.4 %copy-start.3 = (bf16[2,256,256]{2,1,0:T(8,128)(2,1)S(1)}, bf16[2,256,256]{2,1,0:T(8,128)(2,1)}, u32[]{:S(2)}) copy-start(bf16[2,256,256]{2,1,0:T(8,128)(2,1)} %constant.222.clone.x_fwd) | copy-start | bytes 786436
  87.0 15.2 %copy-start.4 = (bf16[2,256,256]{2,1,0:T(8,128)(2,1)S(1)}, bf16[2,256,256]{2,1,0:T(8,128)(2,1)}, u32[]{:S(2)}) copy-start(bf16[2,256,256]{2,1,0:T(8,128)(2,1)} %constant.221.clone.y_bwd) | copy-start | bytes 786436
  87.0 15.1 %copy-start.7 = (bf16[2,128,128]{2,1,0:T(8,128)(2,1)S(1)}, bf16[2,128,128]{2,1,0:T(8,128)(2,1)}, u32[]{:S(2)}) copy-start(bf16[2,128,128]{2,1,0:T(8,128)(2,1)} %constant.219.clone.z_bwd) | copy-start | bytes 196612
  87.0 15.1 %copy-start.16 = (bf16[16,128,128]{2,1,0:T(8,128)(2,1)S(1)}, bf16[16,128,128]{2,1,0:T(8,128)(2,1)}, u32[]{:S(2)}) copy-start(bf16[16,128,128]{2,1,0:T(8,128)(2,1)} %get-tuple-element.532.sources) | copy-start | bytes 1572868
  104.8 68.0 %all-to-all-start.3 = ((bf16[16,128,128]{2,1,0:T(8,128)(2,1)}), bf16[16,128,128]{2,1,0:T(8,128)(2,1)S(1)}, u32[]{:S(2)}, u32[]{:S(2)}) async-start(bf16[16,128,128]{2,1,0:T(8,128)(2,1)} %get-tuple-element.533), calls=%async_computation.3 | async-start | bytes 1048576 | tf_op jit(solution)/shard_map/all_to_all | solution.py:368
  119.4 29.3 %collective-permute-start.10 = (bf16[6,128,128]{2,1,0:T(8,128)(2,1)S(1)}, bf16[6,128,128]{2,1,0:T(8,128)(2,1)S(1)}, u32[]{:S(2)}, u32[]{:S(2)}) collective-permute-start(bf16[6,128,128]{2,1,0:T(8,128)(2,1)S(1)} %get-tuple-element.535), channel_id=1, source_target_pairs={{0,480},{16,496},{32,0},{48,16},{64,32},{80,48},{96,64},{112,80},{... | collective-permute-start | bytes 589832 | tf_op jit(solution)/shard_map/ppermute | solution.py:359
  122.0 26.7 %collective-permute-start.11 = (bf16[6,128,128]{2,1,0:T(8,128)(2,1)S(1)}, bf16[6,128,128]{2,1,0:T(8,128)(2,1)S(1)}, u32[]{:S(2)}, u32[]{:S(2)}) collective-permute-start(bf16[6,128,128]{2,1,0:T(8,128)(2,1)S(1)} %get-tuple-element.536), channel_id=1, source_target_pairs={{0,32},{16,48},{32,64},{48,80},{64,96},{80,112},{96,128},{112,144}... | collective-permute-start | bytes 589832 | tf_op jit(solution)/shard_map/ppermute | solution.py:359
  125.3 6.4 %copy-start.15 = (s32[2,2]{1,0:T(2,128)S(1)}, s32[2,2]{1,0:T(2,128)}, u32[]{:S(2)}) copy-start(s32[2,2]{1,0:T(2,128)} %pair_tgt.1) | copy-start | bytes 52
  125.3 33.4 %collective-permute-start.12 = (bf16[6,128,128]{2,1,0:T(8,128)(2,1)S(1)}, bf16[6,128,128]{2,1,0:T(8,128)(2,1)S(1)}, u32[]{:S(2)}, u32[]{:S(2)}) collective-permute-start(bf16[6,128,128]{2,1,0:T(8,128)(2,1)S(1)} %get-tuple-element.537), channel_id=1, source_target_pairs={{0,448},{16,464},{32,480},{48,496},{64,0},{80,16},{96,32},{112,48}... | collective-permute-start | bytes 589832 | tf_op jit(solution)/shard_map/ppermute | solution.py:359
  160.6 10.3 %collective-permute-start.13 = (bf16[8,128,128]{2,1,0:T(8,128)(2,1)}, bf16[8,128,128]{2,1,0:T(8,128)(2,1)S(1)}, u32[]{:S(2)}, u32[]{:S(2)}) collective-permute-start(bf16[8,128,128]{2,1,0:T(8,128)(2,1)} %get-tuple-element.541), channel_id=1, source_target_pairs={{0,16},{16,0},{32,48},{48,32},{64,80},{80,64},{96,112},{112,96},{1... | collective-permute-start | bytes 786440 | tf_op jit(solution)/shard_map/ppermute | solution.py:363

commit v6 on v5

--- a/solution.py
+++ b/solution.py
@@ -10,7 +10,7 @@
 SWEEPS = 8
 RING = 16
 CAP = 6
-STEPS = (1, -1, 2)
+LANES = 3
 ROW = 128
 HALF = 64
 VMEM_LIMIT = 48 * 1024 * 1024
@@ -49,18 +49,18 @@
         bwd[0, x, :, 1, :, x] = even[:, 1::2]
         bwd[1, x, :, 0, :, x] = odd[:, 1::2]
         bwd[1, x, :, 1, :, x] = odd[:, 0::2]
-    along_x = np.zeros((4, SIDE, RING, 4, 4))
-    for pick in range(4):
+    along_x = np.zeros((2, SIDE, RING, 2, 4))
+    for pick in range(2):
         along_x[pick, :, :, pick, :] = v.T.reshape(SIDE, RING, 4)
-    rows = np.arange(SIDE).reshape(8, 4, 1, 2, 1)
+    rows = np.arange(SIDE).reshape(16, 2, 1, 2, 1)
     spectrum = values[rows] + values.reshape(1, 1, SIDE, 1, 1) + values.reshape(1, 1, 1, 1, SIDE)
     return dict(
         z_fwd=halves(along_z),
         z_bwd=halves(along_z.T),
         y_fwd=halves(fwd.reshape(256, 256)),
         y_bwd=halves(bwd.reshape(256, 256)),
-        x_fwd=halves(along_x.reshape(256, 256)),
-        x_bwd=halves(along_x.reshape(256, 256).T),
+        x_fwd=halves(along_x.reshape(ROW, ROW)),
+        x_bwd=halves(along_x.reshape(ROW, ROW).T),
         spectrum=spectrum.reshape(8, 256, ROW).astype(np.float32),
     )
 
@@ -124,6 +124,14 @@
     return lax.bitwise_and(value, RING - 1)
 
 
+def far_step(z):
+    return 2 - 4 * lax.bitwise_and(z, 1)
+
+
+def steps_of(z):
+    return 1, -1, far_step(z)
+
+
 def want_of(pair_src, z, x, want):
     quad, slot = lax.shift_right_logical(want, 2), lax.bitwise_and(want, 3)
     block = lax.shift_right_logical(slot, 1)
@@ -145,7 +153,7 @@
 
 def sent_kernel(place, pair_src, sent):
     z, x = place[0], place[1]
-    for lane, step in enumerate(STEPS):
+    for lane, step in enumerate(steps_of(z)):
         for n in range(CAP):
             sent[lane * CAP + n] = -1
         count = -CAP * place[2]
@@ -161,10 +169,10 @@
 
 def found_kernel(place, pair_src, found):
     z, x, turn = place[0], place[1], place[2]
-    counts = [-CAP * turn for _ in STEPS]
+    counts = [-CAP * turn] * LANES
     for want, z_own, row in wants_of(pair_src, z, x):
         at = jnp.where(jnp.logical_and(z_own == z, turn == 0), row, -1)
-        for lane, step in enumerate(STEPS):
+        for lane, step in enumerate(steps_of(z)):
             hit = z_own == ring(z - step)
             at = jnp.where(in_round(hit, counts[lane]), 16 + lane * CAP + counts[lane], at)
             counts[lane] = counts[lane] + hit.astype(jnp.int32)
@@ -210,9 +218,9 @@
 
     def step(want, carry):
         z_own, _ = want_of(pair_src, z, x, want)
-        ahead = ring(z - z_own)
-
-        @pl.when(jnp.logical_or(ahead <= 2, ahead == RING - 1))
+        near = jnp.logical_or(ring(z - z_own + 1) <= 2, ring(z - z_own) == ring(far_step(z)))
+
+        @pl.when(near)
         def _():
             body(want)
 
@@ -239,8 +247,11 @@
 
     def start(j, carry):
         norm, power = carry
-        part = slabs[:, pl.ds(pl.multiple_of(16 * j, 16), 16), :].reshape(256, ROW)
+        part = slabs[:, pl.ds(pl.multiple_of(16 * j, 16), 16), :].astype(F32)
+        part = [part[:, :8].reshape(ROW, ROW), part[:, 8:].reshape(ROW, ROW)]
+        part = jnp.concatenate(part, axis=1).astype(BF16)
         value = mm(x_fwd[0], part) + mm(x_fwd[1], part)
+        value = jnp.concatenate([value[:, :ROW], value[:, ROW:]], axis=0)
         direction[j] = value
         square = value * value
         return norm + dot_of(square), power + dot_of(square * spectrum[j])
@@ -275,7 +286,9 @@
 
     def finish(j, carry):
         value = total[j] + step * (residual[j] + ratio * direction[j])
-        part = left_mul(x_bwd, value).reshape(RING, 16, ROW)
+        part = left_mul(x_bwd, jnp.concatenate([value[:ROW], value[ROW:]], axis=1))
+        part = [part[:, :ROW].reshape(RING, 8, ROW), part[:, ROW:].reshape(RING, 8, ROW)]
+        part = jnp.concatenate(part, axis=1)
         out[:, pl.ds(pl.multiple_of(16 * j, 16), 16), :] = part.astype(out.dtype)
         return carry
 
@@ -344,7 +357,7 @@
     for p in range(4):
         z_own, _ = want_of(pair_src, z, x, 4 * quad + p)
         ahead = lax.bitwise_and(z - z_own, 3)
-        relay = ring(z_own + jnp.where(ahead == 3, -1, ahead))
+        relay = ring(z_own + jnp.where(ahead == 3, -1, jnp.where(ahead == 2, far_step(z_own), ahead)))
         held[p] = shares[4 * lax.shift_right_logical(relay, 2) + p].astype(F32)
     for p in range(4):
         same = jnp.zeros((ROW, ROW), F32)
@@ -354,9 +367,20 @@
         rows[p] = same.astype(BF16)
 
 
-def shift(value, steps):
-    pairs = [(2 * z + x, 2 * ((z + steps) % RING) + x) for z in range(RING) for x in range(2)]
-    return lax.ppermute(value, "band", pairs)
+def hand_over(packets, sign):
+    moves = (lambda z: 1, lambda z: -1, far_step_of)
+    return tuple(
+        lax.ppermute(
+            packet,
+            "band",
+            [(2 * z + x, 2 * ((z + sign * move(z)) % RING) + x) for z in range(RING) for x in range(2)],
+        )
+        for packet, move in zip(packets, moves)
+    )
+
+
+def far_step_of(z):
+    return -2 if z % 2 else 2
 
 
 def across(value):
@@ -395,16 +419,14 @@
     def found_in(turn):
         return smem_call(found_kernel, 16, place_in(turn), pair_src)
 
-    ids = pair_tgt.reshape(4)
+    own, ids = lax.optimization_barrier((sources.reshape(8, ROW, ROW), pair_tgt.reshape(4)))
+    other = across(own)
     wanted = targets[ids].reshape(4, ROW, ROW)
     wanted = along_ring(jnp.concatenate([wanted] * 4, axis=0))
 
-    own = sources.reshape(8, ROW, ROW)
-    other = across(own)
-
     def deliver(sent, found, before):
         packed = vmem_call(pack_rows_kernel, packets, (sent, own, other), scalars=1)
-        near = tuple(shift(packet, step) for packet, step in zip(packed, STEPS))
+        near = hand_over(packed, 1)
         operands = (found, own, other) + near + before
         return vmem_call(place_rows_kernel, [sixteen], operands, scalars=1)[0]
 
@@ -436,22 +458,24 @@
         where + (back, rows, wanted, table["z_bwd"], table["y_bwd"]),
         scalars=2,
     )
-    shares = along_ring(shares)
-
-    def collect(sent, found, before):
-        packed = vmem_call(pack_terms_kernel, packets, (found, terms), scalars=1)
-        near = tuple(shift(packet, -step) for packet, step in zip(packed, STEPS))
+
+    def give_back(found):
+        return hand_over(vmem_call(pack_terms_kernel, packets, (found, terms), scalars=1), -1)
+
+    def collect(sent, found, near, before):
         outs = [struct((8, ROW, ROW), F32), struct((8, ROW, ROW), BF16)]
         operands = (sent, found, terms) + near + before
         scratch = [pltpu.VMEM((8, ROW, ROW), F32)]
         return vmem_call(add_terms_kernel, outs, operands, scalars=2, scratch=scratch)
 
-    mine, partner = lax.fori_loop(
-        1,
-        rounds,
-        lambda turn, before: collect(sent_in(turn), found_in(turn), tuple(before)),
-        collect(sent, found, ()),
-    )
+    def collect_in(turn, before):
+        found = found_in(turn)
+        return collect(sent_in(turn), found, give_back(found), tuple(before))
+
+    near = give_back(found)
+    near, shares = lax.optimization_barrier((near, shares))
+    shares = along_ring(shares)
+    mine, partner = lax.fori_loop(1, rounds, collect_in, collect(sent, found, near, ()))
     owned = (mine + across(partner).astype(F32)).astype(BF16).reshape(sources.shape)
 
     (target_rows,) = vmem_call(

time: 176 us -> 167 us (0.949)
  the two profiles are of different devices: /device:TPU:64 before, /device:TPU:2 now
where the time goes in v6:
time: 167 us; the launch traced here: 166 us
  starting transfers between devices  49.8 us (30%)
  waiting for transfers between devices  41.7 us (25%)
  blocking collectives  33.6 us (20%)
  Pallas kernels  26.5 us (16%)
  other arithmetic  7.35 us (4%)
  local copies, waits for them, and re-layouts  5.49 us (3%)
    all_to_all x2, starting transfers between devices, along_ring(): lax.all_to_all(value, 'band', 0, 0, axis_index_groups=groups, tiled=True)  25.8 us
    pallas_call x8, Pallas kernels, vmem_call(): pl.pallas_call(kernel, out_shape=outs, in_specs=[smem] * scalars + [whole...  23.7 us
    ppermute x6, starting transfers between devices, hand_over(): lax.ppermute(packet, 'band', [(2 * z + x, 2 * ((z + sign * move(z)) % RIN...  19.7 us
    ppermute x6, waiting for transfers between devices, hand_over(): lax.ppermute(packet, 'band', [(2 * z + x, 2 * ((z + sign * move(z)) % RIN...  18.7 us
    all_to_all x1, blocking collectives, per_device(): slabs = lax.all_to_all(spectra, 'dom', 0, 0, tiled=True)  18.4 us
    all_to_all x2, waiting for transfers between devices, along_ring(): lax.all_to_all(value, 'band', 0, 0, axis_index_groups=groups, tiled=True)  16.5 us
    all_to_all x1, blocking collectives, per_device(): back = lax.all_to_all(solved, 'dom', 0, 0, tiled=True)  15.1 us
    ppermute x2, waiting for transfers between devices, across(): return lax.ppermute(value, 'band', [(i, i ^ 1) for i in range(32)])  6.56 us
  transfers between devices with their start and end apart: 10, of which 7 were waited for; matrix products, arithmetic and copies ran while one was open for 4% of the time, Pallas kernels for 5%

profile of v6, /device:TPU:2, one launch (start us, length us, event | category | flops | bytes accessed | tf_op | source)
XLA Modules:
  0.0 166.1 jit_solution(4899546223664153421)
XLA Ops:
  1.5 1.2 reshape.104.own
  4.3 15.1 %all-to-all-start = ((bf16[16,128,128]{2,1,0:T(8,128)(2,1)}), bf16[16,128,128]{2,1,0:T(8,128)(2,1)S(1)}, u32[]{:S(2)}, u32[]{:S(2)}) async-start(bf16[16,128,128]{2,1,0:T(8,128)(2,1)} %pad_maximum_fusion), calls=%async_computation | async-start | bytes 1048576 | tf_op jit(solution)/shard_map/all_to_all | solution.py:392
  19.4 2.4 %collective-permute-start.6 = (bf16[8,128,128]{2,1,0:T(8,128)(2,1)S(1)}, bf16[8,128,128]{2,1,0:T(8,128)(2,1)}, u32[]{:S(2)}, u32[]{:S(2)}) collective-permute-start(bf16[8,128,128]{2,1,0:T(8,128)(2,1)S(1)} %reshape.104.own), channel_id=1, source_target_pairs={{0,16},{16,0},{32,48},{48,32},{64,80},{80,64},{96,112},{112,96},{1... | collective-permute-start | bytes 786440 | tf_op jit(solution)/shard_map/ppermute | solution.py:387
  22.5 1.4 shard_map.122.found
  23.9 1.5 shard_map.123.sent
  25.8 3.3 %collective-permute-done.6.other = bf16[8,128,128]{2,1,0:T(8,128)(2,1)} collective-permute-done((bf16[8,128,128]{2,1,0:T(8,128)(2,1)S(1)}, bf16[8,128,128]{2,1,0:T(8,128)(2,1)}, u32[]{:S(2)}, u32[]{:S(2)}) %collective-permute-start.6) | collective-permute-done | bytes 262176 | tf_op jit(solution)/shard_map/ppermute | solution.py:387
  29.2 1.1 shard_map.124
  30.3 2.9 %collective-permute-start.7 = (bf16[6,128,128]{2,1,0:T(8,128)(2,1)S(1)}, bf16[6,128,128]{2,1,0:T(8,128)(2,1)S(1)}, u32[]{:S(2)}, u32[]{:S(2)}) collective-permute-start(bf16[6,128,128]{2,1,0:T(8,128)(2,1)S(1)} %get-tuple-element.537), channel_id=1, source_target_pairs={{0,32},{16,48},{32,64},{48,80},{64,96},{80,112},{96,128},{112,144}... | collective-permute-start | bytes 589832 | tf_op jit(solution)/shard_map/ppermute | solution.py:373
  33.2 5.3 %collective-permute-start.8 = (bf16[6,128,128]{2,1,0:T(8,128)(2,1)S(1)}, bf16[6,128,128]{2,1,0:T(8,128)(2,1)S(1)}, u32[]{:S(2)}, u32[]{:S(2)}) collective-permute-start(bf16[6,128,128]{2,1,0:T(8,128)(2,1)S(1)} %get-tuple-element.538), channel_id=1, source_target_pairs={{0,480},{16,496},{32,0},{48,16},{64,32},{80,48},{96,64},{112,80},{... | collective-permute-start | bytes 589832 | tf_op jit(solution)/shard_map/ppermute | solution.py:373
  38.5 1.9 %collective-permute-start.9 = (bf16[6,128,128]{2,1,0:T(8,128)(2,1)S(1)}, bf16[6,128,128]{2,1,0:T(8,128)(2,1)S(1)}, u32[]{:S(2)}, u32[]{:S(2)}) collective-permute-start(bf16[6,128,128]{2,1,0:T(8,128)(2,1)S(1)} %get-tuple-element.539), channel_id=1, source_target_pairs={{0,64},{16,80},{32,480},{48,496},{64,128},{80,144},{96,32},{112,48... | collective-permute-start | bytes 589832 | tf_op jit(solution)/shard_map/ppermute | solution.py:373
  41.8 9.5 %collective-permute-done.7.refs_0_ = bf16[6,128,128]{2,1,0:T(8,128)(2,1)S(1)} collective-permute-done((bf16[6,128,128]{2,1,0:T(8,128)(2,1)S(1)}, bf16[6,128,128]{2,1,0:T(8,128)(2,1)S(1)}, u32[]{:S(2)}, u32[]{:S(2)}) %collective-permute-start.7) | collective-permute-done | bytes 196640 | tf_op jit(solution)/shard_map/ppermute | solution.py:373
  51.2 4.5 %collective-permute-done.9.refs_2_ = bf16[6,128,128]{2,1,0:T(8,128)(2,1)S(1)} collective-permute-done((bf16[6,128,128]{2,1,0:T(8,128)(2,1)S(1)}, bf16[6,128,128]{2,1,0:T(8,128)(2,1)S(1)}, u32[]{:S(2)}, u32[]{:S(2)}) %collective-permute-start.9) | collective-permute-done | bytes 196640 | tf_op jit(solution)/shard_map/ppermute | solution.py:373
  55.7 2.0 %shard_map.125 = bf16[16,128,128]{2,1,0:T(8,128)(2,1)} custom-call(s32[16]{0:T(128)S(1)} %copy-done.13, bf16[8,128,128]{2,1,0:T(8,128)(2,1)S(1)} %reshape.104.own, bf16[8,128,128]{2,1,0:T(8,128)(2,1)} %collective-permute-done.6.other, bf16[6,128,128]{2,1,0:T(8,128)(2,1)S(1)} %collective-permute-done.7.refs_0_, ...), custom_call_target="tpu_custom_call" | custom-call | tf_op jit(solution)/shard_map/pallas_call | solution.py:99
  58.7 4.6 %shard_map.126 = bf16[16,128,128]{2,1,0:T(8,128)(2,1)S(1)} custom-call(s32[3]{0:T(128)S(1)} %copy-done.12, s32[2,64]{1,0:T(2,128)S(1)} %get-tuple-element.800, bf16[16,128,128]{2,1,0:T(8,128)(2,1)} %get-tuple-element.540.sources, bf16[16,128,128]{2,1,0:T(8,128)(2,1)S(1)} %all-to-all-done.wanted, bf16[2,128,128]{2,1,0:T(8,128)(2,1)S(1)} %copy-done.8, ...), custom_call_target="tpu_custom_call" | custom-call | tf_op jit(solution)/shard_map/pallas_call | solution.py:99
  63.3 18.4 %all_to_all.20.slabs = bf16[16,128,128]{2,1,0:T(8,128)(2,1)S(1)} all-to-all(bf16[16,128,128]{2,1,0:T(8,128)(2,1)S(1)} %shard_map.126), channel_id=1, replica_groups=mesh['band'=32,'dom'=16] {'dom'}, dimensions={0} | all-to-all | bytes 1048576 | tf_op jit(solution)/shard_map/all_to_all | solution.py:447
  81.8 8.2 %shard_map.127 = bf16[16,128,128]{2,1,0:T(8,128)(2,1)S(1)} custom-call(bf16[16,128,128]{2,1,0:T(8,128)(2,1)S(1)} %all_to_all.20.slabs, f32[8,256,128]{2,1,0:T(8,128)S(1)} %copy-done.1, bf16[2,128,128]{2,1,0:T(8,128)(2,1)S(1)} %copy-done.7, bf16[2,128,128]{2,1,0:T(8,128)(2,1)S(1)} %copy-done.6), custom_call_target="tpu_custom_call" | custom-call | tf_op jit(solution)/shard_map/pallas_call | solution.py:99
  90.0 15.1 %all_to_all.21.spectra = bf16[16,128,128]{2,1,0:T(8,128)(2,1)S(1)} all-to-all(bf16[16,128,128]{2,1,0:T(8,128)(2,1)S(1)} %shard_map.127), channel_id=1, replica_groups=mesh['band'=32,'dom'=16] {'dom'}, dimensions={0} | all-to-all | bytes 1048576 | tf_op jit(solution)/shard_map/all_to_all | solution.py:454
  105.1 4.5 %shard_map.128 = (bf16[16,128,128]{2,1,0:T(8,128)(2,1)S(1)}, bf16[16,128,128]{2,1,0:T(8,128)(2,1)}) custom-call(s32[3]{0:T(128)S(1)} %copy-done.12, s32[2,64]{1,0:T(2,128)S(1)} %get-tuple-element.800, bf16[16,128,128]{2,1,0:T(8,128)(2,1)S(1)} %all_to_all.21.spectra, bf16[16,128,128]{2,1,0:T(8,128)(2,1)S(1)} %copy-done.16, ...), custom_call_target="tpu_custom_call" | custom-call | tf_op jit(solution)/shard_map/pallas_call | solution.py:99
  110.4 1.9 %collective-permute-start.10 = (bf16[6,128,128]{2,1,0:T(8,128)(2,1)S(1)}, bf16[6,128,128]{2,1,0:T(8,128)(2,1)S(1)}, u32[]{:S(2)}, u32[]{:S(2)}) collective-permute-start(bf16[6,128,128]{2,1,0:T(8,128)(2,1)S(1)} %get-tuple-element.542), channel_id=1, source_target_pairs={{0,480},{16,496},{32,0},{48,16},{64,32},{80,48},{96,64},{112,80},{... | collective-permute-start | bytes 589832 | tf_op jit(solution)/shard_map/ppermute | solution.py:373
  112.3 3.9 %collective-permute-start.11 = (bf16[6,128,128]{2,1,0:T(8,128)(2,1)S(1)}, bf16[6,128,128]{2,1,0:T(8,128)(2,1)S(1)}, u32[]{:S(2)}, u32[]{:S(2)}) collective-permute-start(bf16[6,128,128]{2,1,0:T(8,128)(2,1)S(1)} %get-tuple-element.543), channel_id=1, source_target_pairs={{0,32},{16,48},{32,64},{48,80},{64,96},{80,112},{96,128},{112,144}... | collective-permute-start | bytes 589832 | tf_op jit(solution)/shard_map/ppermute | solution.py:373
  116.2 3.7 %collective-permute-start.12 = (bf16[6,128,128]{2,1,0:T(8,128)(2,1)S(1)}, bf16[6,128,128]{2,1,0:T(8,128)(2,1)S(1)}, u32[]{:S(2)}, u32[]{:S(2)}) collective-permute-start(bf16[6,128,128]{2,1,0:T(8,128)(2,1)S(1)} %get-tuple-element.544), channel_id=1, source_target_pairs={{0,448},{16,464},{32,96},{48,112},{64,0},{80,16},{96,160},{112,176... | collective-permute-start | bytes 589832 | tf_op jit(solution)/shard_map/ppermute | solution.py:373
  120.0 2.6 %collective-permute-done.11.refs_1_ = bf16[6,128,128]{2,1,0:T(8,128)(2,1)S(1)} collective-permute-done((bf16[6,128,128]{2,1,0:T(8,128)(2,1)S(1)}, bf16[6,128,128]{2,1,0:T(8,128)(2,1)S(1)}, u32[]{:S(2)}, u32[]{:S(2)}) %collective-permute-start.11) | collective-permute-done | bytes 196640 | tf_op jit(solution)/shard_map/ppermute | solution.py:373
  122.6 2.1 %collective-permute-done.12.refs_2_ = bf16[6,128,128]{2,1,0:T(8,128)(2,1)S(1)} collective-permute-done((bf16[6,128,128]{2,1,0:T(8,128)(2,1)S(1)}, bf16[6,128,128]{2,1,0:T(8,128)(2,1)S(1)}, u32[]{:S(2)}, u32[]{:S(2)}) %collective-permute-start.12) | collective-permute-done | bytes 196640 | tf_op jit(solution)/shard_map/ppermute | solution.py:373
  124.7 10.7 %all-to-all-start.3 = ((bf16[16,128,128]{2,1,0:T(8,128)(2,1)}), bf16[16,128,128]{2,1,0:T(8,128)(2,1)S(1)}, u32[]{:S(2)}, u32[]{:S(2)}) async-start(bf16[16,128,128]{2,1,0:T(8,128)(2,1)} %get-tuple-element.546), calls=%async_computation.3 | async-start | bytes 1048576 | tf_op jit(solution)/shard_map/all_to_all | solution.py:392
  135.4 1.8 %shard_map.131 = (f32[8,128,128]{2,1,0:T(8,128)}, bf16[8,128,128]{2,1,0:T(8,128)(2,1)}) custom-call(s32[18]{0:T(128)S(1)} %copy-done.14, s32[16]{0:T(128)S(1)} %copy-done.13, bf16[16,128,128]{2,1,0:T(8,128)(2,1)S(1)} %get-tuple-element.752.terms, bf16[6,128,128]{2,1,0:T(8,128)(2,1)S(1)} %collective-permute-done.10.refs_0_, ...), custom_call_target="tpu_custom_call" | custom-call | tf_op jit(solution)/shard_map/pallas_call | solution.py:99
  137.2 1.9 %collective-permute-start.13 = (bf16[8,128,128]{2,1,0:T(8,128)(2,1)}, bf16[8,128,128]{2,1,0:T(8,128)(2,1)S(1)}, u32[]{:S(2)}, u32[]{:S(2)}) collective-permute-start(bf16[8,128,128]{2,1,0:T(8,128)(2,1)} %get-tuple-element.553), channel_id=1, source_target_pairs={{0,16},{16,0},{32,48},{48,32},{64,80},{80,64},{96,112},{112,96},{1... | collective-permute-start | bytes 786440 | tf_op jit(solution)/shard_map/ppermute | solution.py:387
  139.8 1.3 iota_compare_fusion.2
  141.1 1.3 iota_compare_fusion
  142.4 3.2 %collective-permute-done.13 = bf16[8,128,128]{2,1,0:T(8,128)(2,1)S(1)} collective-permute-done((bf16[8,128,128]{2,1,0:T(8,128)(2,1)}, bf16[8,128,128]{2,1,0:T(8,128)(2,1)S(1)}, u32[]{:S(2)}, u32[]{:S(2)}) %collective-permute-start.13) | collective-permute-done | bytes 262176 | tf_op jit(solution)/shard_map/ppermute | solution.py:387
  145.7 1.1 add_convert_fusion
  147.6 16.5 %all-to-all-done.3.shares = bf16[16,128,128]{2,1,0:T(8,128)(2,1)S(1)} async-done(((bf16[16,128,128]{2,1,0:T(8,128)(2,1)}), bf16[16,128,128]{2,1,0:T(8,128)(2,1)S(1)}, u32[]{:S(2)}, u32[]{:S(2)}) %all-to-all-start.3) | async-done | bytes 524320 | tf_op jit(solution)/shard_map/all_to_all | solution.py:392
  164.8 1.3 select_select_fusion
  (52 shorter events, 8.0 us)
Async XLA Ops:
  0.6 2.1 %copy-start = (bf16[32,16384]{1,0:T(8,128)(2,1)S(1)}, bf16[32,16384]{1,0:T(8,128)(2,1)}, u32[]{:S(2)}) copy-start(bf16[32,16384]{1,0:T(8,128)(2,1)} %param.15) | copy-start | bytes 3145732
  4.3 53.4 %all-to-all-start = ((bf16[16,128,128]{2,1,0:T(8,128)(2,1)}), bf16[16,128,128]{2,1,0:T(8,128)(2,1)S(1)}, u32[]{:S(2)}, u32[]{:S(2)}) async-start(bf16[16,128,128]{2,1,0:T(8,128)(2,1)} %pad_maximum_fusion), calls=%async_computation | async-start | bytes 1048576 | tf_op jit(solution)/shard_map/all_to_all | solution.py:392
  19.4 9.8 %collective-permute-start.6 = (bf16[8,128,128]{2,1,0:T(8,128)(2,1)S(1)}, bf16[8,128,128]{2,1,0:T(8,128)(2,1)}, u32[]{:S(2)}, u32[]{:S(2)}) collective-permute-start(bf16[8,128,128]{2,1,0:T(8,128)(2,1)S(1)} %reshape.104.own), channel_id=1, source_target_pairs={{0,16},{16,0},{32,48},{48,32},{64,80},{80,64},{96,112},{112,96},{1... | collective-permute-start | bytes 786440 | tf_op jit(solution)/shard_map/ppermute | solution.py:387
  21.9 0.7 copy-start.18
  25.7 3.4 %copy-start.14 = (s32[18]{0:T(128)S(1)}, s32[18]{0:T(128)}, u32[]{:S(2)}) copy-start(s32[18]{0:T(128)} %shard_map.123.sent) | copy-start | bytes 220
  30.3 20.9 %collective-permute-start.7 = (bf16[6,128,128]{2,1,0:T(8,128)(2,1)S(1)}, bf16[6,128,128]{2,1,0:T(8,128)(2,1)S(1)}, u32[]{:S(2)}, u32[]{:S(2)}) collective-permute-start(bf16[6,128,128]{2,1,0:T(8,128)(2,1)S(1)} %get-tuple-element.537), channel_id=1, source_target_pairs={{0,32},{16,48},{32,64},{48,80},{64,96},{80,112},{96,128},{112,144}... | collective-permute-start | bytes 589832 | tf_op jit(solution)/shard_map/ppermute | solution.py:373
  33.2 18.0 %collective-permute-start.8 = (bf16[6,128,128]{2,1,0:T(8,128)(2,1)S(1)}, bf16[6,128,128]{2,1,0:T(8,128)(2,1)S(1)}, u32[]{:S(2)}, u32[]{:S(2)}) collective-permute-start(bf16[6,128,128]{2,1,0:T(8,128)(2,1)S(1)} %get-tuple-element.538), channel_id=1, source_target_pairs={{0,480},{16,496},{32,0},{48,16},{64,32},{80,48},{96,64},{112,80},{... | collective-permute-start | bytes 589832 | tf_op jit(solution)/shard_map/ppermute | solution.py:373
  38.5 17.2 %collective-permute-start.9 = (bf16[6,128,128]{2,1,0:T(8,128)(2,1)S(1)}, bf16[6,128,128]{2,1,0:T(8,128)(2,1)S(1)}, u32[]{:S(2)}, u32[]{:S(2)}) collective-permute-start(bf16[6,128,128]{2,1,0:T(8,128)(2,1)S(1)} %get-tuple-element.539), channel_id=1, source_target_pairs={{0,64},{16,80},{32,480},{48,496},{64,128},{80,144},{96,32},{112,48... | collective-permute-start | bytes 589832 | tf_op jit(solution)/shard_map/ppermute | solution.py:373
  41.7 14.0 %copy-start.13 = (s32[16]{0:T(128)S(1)}, s32[16]{0:T(128)}, u32[]{:S(2)}) copy-start(s32[16]{0:T(128)} %shard_map.122.found) | copy-start | bytes 196
  57.8 0.9 copy-start.3
  57.8 1.0 copy-start.8
  57.8 0.9 copy-start.12
  58.7 23.0 %copy-start.1 = (f32[8,256,128]{2,1,0:T(8,128)S(1)}, f32[8,256,128]{2,1,0:T(8,128)}, u32[]{:S(2)}) copy-start(f32[8,256,128]{2,1,0:T(8,128)} %constant.224.clone.spectrum) | copy-start | bytes 3145732
  63.3 18.5 %copy-start.6 = (bf16[2,128,128]{2,1,0:T(8,128)(2,1)S(1)}, bf16[2,128,128]{2,1,0:T(8,128)(2,1)}, u32[]{:S(2)}) copy-start(bf16[2,128,128]{2,1,0:T(8,128)(2,1)} %constant.223.clone.x_bwd) | copy-start | bytes 196612
  63.3 18.5 %copy-start.7 = (bf16[2,128,128]{2,1,0:T(8,128)(2,1)S(1)}, bf16[2,128,128]{2,1,0:T(8,128)(2,1)}, u32[]{:S(2)}) copy-start(bf16[2,128,128]{2,1,0:T(8,128)(2,1)} %constant.222.clone.x_fwd) | copy-start | bytes 196612
  90.0 15.2 %copy-start.2 = (bf16[2,256,256]{2,1,0:T(8,128)(2,1)S(1)}, bf16[2,256,256]{2,1,0:T(8,128)(2,1)}, u32[]{:S(2)}) copy-start(bf16[2,256,256]{2,1,0:T(8,128)(2,1)} %constant.221.clone.y_bwd) | copy-start | bytes 786436
  90.0 15.2 %copy-start.5 = (bf16[2,128,128]{2,1,0:T(8,128)(2,1)S(1)}, bf16[2,128,128]{2,1,0:T(8,128)(2,1)}, u32[]{:S(2)}) copy-start(bf16[2,128,128]{2,1,0:T(8,128)(2,1)} %constant.219.clone.z_bwd) | copy-start | bytes 196612
  90.0 15.1 %copy-start.16 = (bf16[16,128,128]{2,1,0:T(8,128)(2,1)S(1)}, bf16[16,128,128]{2,1,0:T(8,128)(2,1)}, u32[]{:S(2)}) copy-start(bf16[16,128,128]{2,1,0:T(8,128)(2,1)} %get-tuple-element.540.sources) | copy-start | bytes 1572868
  110.4 9.6 %collective-permute-start.10 = (bf16[6,128,128]{2,1,0:T(8,128)(2,1)S(1)}, bf16[6,128,128]{2,1,0:T(8,128)(2,1)S(1)}, u32[]{:S(2)}, u32[]{:S(2)}) collective-permute-start(bf16[6,128,128]{2,1,0:T(8,128)(2,1)S(1)} %get-tuple-element.542), channel_id=1, source_target_pairs={{0,480},{16,496},{32,0},{48,16},{64,32},{80,48},{96,64},{112,80},{... | collective-permute-start | bytes 589832 | tf_op jit(solution)/shard_map/ppermute | solution.py:373
  112.3 10.3 %collective-permute-start.11 = (bf16[6,128,128]{2,1,0:T(8,128)(2,1)S(1)}, bf16[6,128,128]{2,1,0:T(8,128)(2,1)S(1)}, u32[]{:S(2)}, u32[]{:S(2)}) collective-permute-start(bf16[6,128,128]{2,1,0:T(8,128)(2,1)S(1)} %get-tuple-element.543), channel_id=1, source_target_pairs={{0,32},{16,48},{32,64},{48,80},{64,96},{80,112},{96,128},{112,144}... | collective-permute-start | bytes 589832 | tf_op jit(solution)/shard_map/ppermute | solution.py:373
  116.2 8.5 %collective-permute-start.12 = (bf16[6,128,128]{2,1,0:T(8,128)(2,1)S(1)}, bf16[6,128,128]{2,1,0:T(8,128)(2,1)S(1)}, u32[]{:S(2)}, u32[]{:S(2)}) collective-permute-start(bf16[6,128,128]{2,1,0:T(8,128)(2,1)S(1)} %get-tuple-element.544), channel_id=1, source_target_pairs={{0,448},{16,464},{32,96},{48,112},{64,0},{80,16},{96,160},{112,176... | collective-permute-start | bytes 589832 | tf_op jit(solution)/shard_map/ppermute | solution.py:373
  124.7 39.4 %all-to-all-start.3 = ((bf16[16,128,128]{2,1,0:T(8,128)(2,1)}), bf16[16,128,128]{2,1,0:T(8,128)(2,1)S(1)}, u32[]{:S(2)}, u32[]{:S(2)}) async-start(bf16[16,128,128]{2,1,0:T(8,128)(2,1)} %get-tuple-element.546), calls=%async_computation.3 | async-start | bytes 1048576 | tf_op jit(solution)/shard_map/all_to_all | solution.py:392
  137.2 8.5 %collective-permute-start.13 = (bf16[8,128,128]{2,1,0:T(8,128)(2,1)}, bf16[8,128,128]{2,1,0:T(8,128)(2,1)S(1)}, u32[]{:S(2)}, u32[]{:S(2)}) collective-permute-start(bf16[8,128,128]{2,1,0:T(8,128)(2,1)} %get-tuple-element.553), channel_id=1, source_target_pairs={{0,16},{16,0},{32,48},{48,32},{64,80},{80,64},{96,112},{112,96},{1... | collective-permute-start | bytes 786440 | tf_op jit(solution)/shard_map/ppermute | solution.py:387
  146.8 17.3 %copy-start.15 = (s32[2,2]{1,0:T(2,128)S(1)}, s32[2,2]{1,0:T(2,128)}, u32[]{:S(2)}) copy-start(s32[2,2]{1,0:T(2,128)} %pair_tgt.1) | copy-start | bytes 52

commit v7 on v6

--- a/solution.py
+++ b/solution.py
@@ -9,8 +9,10 @@
 SIDE = 64
 SWEEPS = 8
 RING = 16
-CAP = 6
-LANES = 3
+HOP = 5
+CAPS = (5, 5, 5, 5, 3)
+STARTS = (0, 5, 10, 15, 20)
+WANTS = 12
 ROW = 128
 HALF = 64
 VMEM_LIMIT = 48 * 1024 * 1024
@@ -125,17 +127,21 @@
 
 
 def far_step(z):
-    return 2 - 4 * lax.bitwise_and(z, 1)
+    return 6 * lax.bitwise_and(z, 1) - 3
 
 
 def steps_of(z):
-    return 1, -1, far_step(z)
+    return 1, -1, 2, -2, far_step(z)
+
+
+def far_kind(relay):
+    return 2 - lax.bitwise_and(relay, 1)
 
 
 def want_of(pair_src, z, x, want):
-    quad, slot = lax.shift_right_logical(want, 2), lax.bitwise_and(want, 3)
+    kind, slot = lax.shift_right_logical(want, 2), lax.bitwise_and(want, 3)
     block = lax.shift_right_logical(slot, 1)
-    band = 2 * (4 * quad + lax.bitwise_and(z, 3)) + x
+    band = 2 * ring(z + HOP * (jnp.where(kind == 2, 1, 0) - jnp.where(kind == 1, 1, 0))) + x
     source = pair_src[block, 2 * band + lax.bitwise_and(slot, 1)]
     z_own = lax.shift_right_logical(source, 3)
     other = lax.bitwise_xor(lax.bitwise_and(lax.shift_right_logical(source, 2), 1), x)
@@ -143,46 +149,51 @@
 
 
 def wants_of(pair_src, z, x):
-    for want in range(16):
+    for want in range(WANTS):
         yield (want,) + want_of(pair_src, z, x, jnp.int32(want))
 
 
-def in_round(hit, count):
-    return jnp.logical_and(hit, jnp.logical_and(count >= 0, count < CAP))
+def on_lane(lane, relay, want, hit):
+    return hit if lane < 4 else jnp.logical_and(hit, far_kind(relay) == want // 4)
+
+
+def in_round(lane, hit, count):
+    return jnp.logical_and(hit, jnp.logical_and(count >= 0, count < CAPS[lane]))
 
 
 def sent_kernel(place, pair_src, sent):
     z, x = place[0], place[1]
     for lane, step in enumerate(steps_of(z)):
-        for n in range(CAP):
-            sent[lane * CAP + n] = -1
-        count = -CAP * place[2]
-        for _, z_own, row in wants_of(pair_src, z + step, x):
-            hit = z_own == z
-
-            @pl.when(in_round(hit, count))
+        for n in range(CAPS[lane]):
+            sent[STARTS[lane] + n] = -1
+        count = -CAPS[lane] * place[2]
+        for want, z_own, row in wants_of(pair_src, z + step, x):
+            hit = on_lane(lane, z + step, want, z_own == z)
+
+            @pl.when(in_round(lane, hit, count))
             def _():
-                sent[lane * CAP + count] = row
+                sent[STARTS[lane] + count] = row
 
             count = count + hit.astype(jnp.int32)
 
 
 def found_kernel(place, pair_src, found):
     z, x, turn = place[0], place[1], place[2]
-    counts = [-CAP * turn] * LANES
+    counts = [-cap * turn for cap in CAPS]
     for want, z_own, row in wants_of(pair_src, z, x):
         at = jnp.where(jnp.logical_and(z_own == z, turn == 0), row, -1)
         for lane, step in enumerate(steps_of(z)):
-            hit = z_own == ring(z - step)
-            at = jnp.where(in_round(hit, counts[lane]), 16 + lane * CAP + counts[lane], at)
+            owner = ring(z - step if lane < 4 else z + step)
+            hit = on_lane(lane, z, want, z_own == owner)
+            at = jnp.where(in_round(lane, hit, counts[lane]), 16 + STARTS[lane] + counts[lane], at)
             counts[lane] = counts[lane] + hit.astype(jnp.int32)
         found[want] = at
 
 
 def pack_rows_kernel(sent, own, other, *outs):
     for lane, out in enumerate(outs):
-        for n in range(CAP):
-            row = sent[lane * CAP + n]
+        for n in range(CAPS[lane]):
+            row = sent[STARTS[lane] + n]
 
             @pl.when(row >= 0)
             def _():
@@ -197,11 +208,11 @@
 
 def place_rows_kernel(found, own, other, *refs):
     out = refs[-1]
-    for before in refs[3:-1]:
+    for before in refs[5:-1]:
         out[...] = before[...]
     spans = [(own, 0, 8), (other, 8, 16)]
-    spans += [(near, 16 + lane * CAP, 16 + lane * CAP + CAP) for lane, near in enumerate(refs[:3])]
-    for want in range(16):
+    spans += [(near, 16 + first, 16 + first + cap) for near, first, cap in zip(refs, STARTS, CAPS)]
+    for want in range(WANTS):
         at = found[want]
 
         @pl.when(at >= 0)
@@ -215,23 +226,30 @@
 
 def for_each_solved(place, pair_src, body):
     z, x = place[0], place[1]
-
-    def step(want, carry):
-        z_own, _ = want_of(pair_src, z, x, want)
-        near = jnp.logical_or(ring(z - z_own + 1) <= 2, ring(z - z_own) == ring(far_step(z)))
-
-        @pl.when(near)
-        def _():
-            body(want)
-
-        return carry
-
-    lax.fori_loop(0, 16, step, 0)
-
-
-def density_kernel(place, pair_src, sources, wanted, z_fwd, y_fwd, spectra):
-    def body(want):
-        density = sources[want].astype(F32) * wanted[want].astype(F32)
+    for kind in range(3):
+
+        def step(slot, carry, kind=kind):
+            want = 4 * kind + slot
+            z_own, _ = want_of(pair_src, z, x, want)
+            here = ring(z_own - z + 2) <= 4
+            if kind:
+                far = ring(z_own - z) == ring(far_step(z))
+                here = jnp.logical_or(here, jnp.logical_and(far, far_kind(z) == kind))
+
+            @pl.when(here)
+            def _():
+                body(kind, slot, want)
+
+            return carry
+
+        lax.fori_loop(0, 4, step, 0)
+
+
+def density_kernel(place, pair_src, sources, here, below, above, z_fwd, y_fwd, spectra):
+    wanted = (here, below, above)
+
+    def body(kind, slot, want):
+        density = sources[want].astype(F32) * wanted[kind][slot].astype(F32)
         along = right_mul(density, z_fwd)
         mixed = left_mul(y_fwd, jnp.concatenate([along, swap_halves(along)], axis=0))
         spectra[want] = by_half(mixed).astype(BF16)
@@ -295,32 +313,41 @@
     lax.fori_loop(0, 8, finish, 0)
 
 
-def term_kernel(place, pair_src, spectra, sources, wanted, z_bwd, y_bwd, terms, shares):
-    def body(want):
+def term_kernel(place, pair_src, spectra, here, below, above, z_bwd, y_bwd, terms, potentials):
+    wanted = (here, below, above)
+
+    def body(kind, slot, want):
         rows = spectra[want]
         rows = jnp.concatenate([rows, swap_halves(rows)], axis=0)
         potential = right_mul(by_half(mm(y_bwd[0], rows) + mm(y_bwd[1], rows)), z_bwd)
-        terms[want] = (-potential * wanted[want].astype(F32)).astype(BF16)
-        shares[want] = (-potential * sources[want].astype(F32)).astype(BF16)
+        terms[want] = (-potential * wanted[kind][slot].astype(F32)).astype(BF16)
+        potentials[want] = potential
 
     for_each_solved(place, pair_src, body)
 
 
+def share_kernel(place, pair_src, potentials, sources, *shares):
+    def body(kind, slot, want):
+        shares[kind][slot] = (-potentials[want] * sources[want].astype(F32)).astype(BF16)
+
+    for_each_solved(place, pair_src, body)
+
+
 def pack_terms_kernel(found, terms, *outs):
-    for want in range(16):
+    for want in range(WANTS):
         at = found[want] - 16
 
         @pl.when(at >= 0)
         def _():
-            for lane, out in enumerate(outs):
-
-                @pl.when(jnp.logical_and(at >= lane * CAP, at < lane * CAP + CAP))
+            for out, first, cap in zip(outs, STARTS, CAPS):
+
+                @pl.when(jnp.logical_and(at >= first, at < first + cap))
                 def _():
-                    out[at - lane * CAP] = terms[want]
+                    out[at - first] = terms[want]
 
 
 def add_terms_kernel(sent, found, terms, *refs):
-    near, before, (mine, partner, held) = refs[:3], refs[3:-3], refs[-3:]
+    near, before, (mine, partner, held) = refs[:5], refs[5:-3], refs[-3:]
     mine[...] = before[0][...] if before else jnp.zeros((8, ROW, ROW), F32)
     held[...] = before[1][...].astype(F32) if before else jnp.zeros((8, ROW, ROW), F32)
 
@@ -333,16 +360,16 @@
         def _():
             held[row - 8] = held[row - 8] + term[...].astype(F32)
 
-    for want in range(16):
+    for want in range(WANTS):
         at = found[want]
 
         @pl.when(jnp.logical_and(at >= 0, at < 16))
         def _():
             add(at, terms.at[want])
 
-    for lane in range(3):
-        for n in range(CAP):
-            row = sent[lane * CAP + n]
+    for lane in range(5):
+        for n in range(CAPS[lane]):
+            row = sent[STARTS[lane] + n]
 
             @pl.when(row >= 0)
             def _():
@@ -351,14 +378,26 @@
     partner[...] = held[...].astype(BF16)
 
 
-def target_kernel(place, pair_src, pair_tgt, shares, rows, held):
+def target_kernel(place, pair_src, pair_tgt, here, above, below, rows, held):
     z, x = place[0], place[1]
-    quad = lax.shift_right_logical(z, 2)
     for p in range(4):
-        z_own, _ = want_of(pair_src, z, x, 4 * quad + p)
-        ahead = lax.bitwise_and(z - z_own, 3)
-        relay = ring(z_own + jnp.where(ahead == 3, -1, jnp.where(ahead == 2, far_step(z_own), ahead)))
-        held[p] = shares[4 * lax.shift_right_logical(relay, 2) + p].astype(F32)
+        z_own, _ = want_of(pair_src, z, x, jnp.int32(p))
+        away = ring(z_own - z + 2)
+        up = jnp.logical_or(away < 10, jnp.logical_and(away == 10, lax.bitwise_and(z_own, 1) == 0))
+        close = away <= 4
+
+        @pl.when(close)
+        def _():
+            held[p] = here[p].astype(F32)
+
+        @pl.when(jnp.logical_and(jnp.logical_not(close), up))
+        def _():
+            held[p] = above[p].astype(F32)
+
+        @pl.when(jnp.logical_not(up))
+        def _():
+            held[p] = below[p].astype(F32)
+
     for p in range(4):
         same = jnp.zeros((ROW, ROW), F32)
         for other in range(4):
@@ -367,39 +406,33 @@
         rows[p] = same.astype(BF16)
 
 
+def shift(value, move):
+    pairs = [(2 * z + x, 2 * ((z + move(z)) % RING) + x) for z in range(RING) for x in range(2)]
+    return lax.ppermute(value, "band", pairs)
+
+
 def hand_over(packets, sign):
-    moves = (lambda z: 1, lambda z: -1, far_step_of)
-    return tuple(
-        lax.ppermute(
-            packet,
-            "band",
-            [(2 * z + x, 2 * ((z + sign * move(z)) % RING) + x) for z in range(RING) for x in range(2)],
-        )
-        for packet, move in zip(packets, moves)
-    )
-
-
-def far_step_of(z):
-    return -2 if z % 2 else 2
+    moves = [lambda z, step=step: sign * step for step in (1, -1, 2, -2)]
+    moves.append(lambda z: 3 if z % 2 else -3)
+    return tuple(shift(packet, move) for packet, move in zip(packets, moves))
 
 
 def across(value):
     return lax.ppermute(value, "band", [(i, i ^ 1) for i in range(32)])
-
-
-def along_ring(value):
-    groups = [[8 * quad + member for quad in range(4)] for member in range(8)]
-    return lax.all_to_all(value, "band", 0, 0, axis_index_groups=groups, tiled=True)
 
 
 def rounds_of(pair_src):
     band = jnp.arange(pair_src.shape[1], dtype=jnp.int32) // 2
     z, x = band // 2, band % 2
     z_own = pair_src // 8
-    key = (z_own * 8 + (z % 4) * 2 + x).reshape(-1)
-    moves = ((z_own - z) % 4 != 0).astype(jnp.int32).reshape(-1)
-    shared = moves * jnp.sum((key[:, None] == key[None, :]).astype(jnp.int32), axis=1)
-    return jnp.maximum(1, (jnp.max(shared) + CAP - 1) // CAP)
+    away = (z_own - z + 2) % RING
+    relay = jnp.where(away <= 4, z, jnp.where(away < 10, z + HOP, z - HOP)) % RING
+    far = away == 10
+    relay = jnp.where(far, RING, relay)
+    key = ((z_own * 32 + relay) * 2 + x).reshape(-1)
+    shared = jnp.sum((key[:, None] == key[None, :]).astype(jnp.int32), axis=1).reshape(pair_src.shape)
+    turns = jnp.where(far, (shared + CAPS[4] - 1) // CAPS[4], (shared + CAPS[0] - 1) // CAPS[0])
+    return jnp.max(jnp.where(relay == z_own, 1, turns))
 
 
 def per_device(targets, sources, pair_tgt, pair_src):
@@ -407,14 +440,15 @@
     band = lax.axis_index("band")
     rounds = rounds_of(pair_src)
     sixteen = struct((16, ROW, ROW), BF16)
-    packets = [struct((CAP, ROW, ROW), BF16)] * 3
+    four = struct((4, ROW, ROW), BF16)
+    packets = [struct((cap, ROW, ROW), BF16) for cap in CAPS]
 
     def place_in(turn):
         turn = jnp.asarray(turn, jnp.int32)
         return jnp.stack([band // 2, band % 2, turn]).astype(jnp.int32)
 
     def sent_in(turn):
-        return smem_call(sent_kernel, 3 * CAP, place_in(turn), pair_src)
+        return smem_call(sent_kernel, sum(CAPS), place_in(turn), pair_src)
 
     def found_in(turn):
         return smem_call(found_kernel, 16, place_in(turn), pair_src)
@@ -422,7 +456,8 @@
     own, ids = lax.optimization_barrier((sources.reshape(8, ROW, ROW), pair_tgt.reshape(4)))
     other = across(own)
     wanted = targets[ids].reshape(4, ROW, ROW)
-    wanted = along_ring(jnp.concatenate([wanted] * 4, axis=0))
+    other, wanted = lax.optimization_barrier((other, wanted))
+    wanted = (wanted, shift(wanted, lambda z: HOP), shift(wanted, lambda z: -HOP))
 
     def deliver(sent, found, before):
         packed = vmem_call(pack_rows_kernel, packets, (sent, own, other), scalars=1)
@@ -441,7 +476,7 @@
     (spectra,) = vmem_call(
         density_kernel,
         [sixteen],
-        where + (rows, wanted, table["z_fwd"], table["y_fwd"]),
+        where + (rows,) + wanted + (table["z_fwd"], table["y_fwd"]),
         scalars=2,
     )
     slabs = lax.all_to_all(spectra, "dom", 0, 0, tiled=True)
@@ -452,15 +487,15 @@
         scratch=[pltpu.VMEM((8, 256, ROW), F32)] * 3,
     )
     back = lax.all_to_all(solved, "dom", 0, 0, tiled=True)
-    terms, shares = vmem_call(
+    terms, potentials = vmem_call(
         term_kernel,
-        [sixteen, sixteen],
-        where + (back, rows, wanted, table["z_bwd"], table["y_bwd"]),
+        [sixteen, struct((16, ROW, ROW), F32)],
+        where + (back,) + wanted + (table["z_bwd"], table["y_bwd"]),
         scalars=2,
     )
 
-    def give_back(found):
-        return hand_over(vmem_call(pack_terms_kernel, packets, (found, terms), scalars=1), -1)
+    def pack_in(found):
+        return vmem_call(pack_terms_kernel, packets, (found, terms), scalars=1)
 
     def collect(sent, found, near, before):
         outs = [struct((8, ROW, ROW), F32), struct((8, ROW, ROW), BF16)]
@@ -470,18 +505,20 @@
 
     def collect_in(turn, before):
         found = found_in(turn)
-        return collect(sent_in(turn), found, give_back(found), tuple(before))
-
-    near = give_back(found)
-    near, shares = lax.optimization_barrier((near, shares))
-    shares = along_ring(shares)
+        return collect(sent_in(turn), found, hand_over(pack_in(found), -1), tuple(before))
+
+    near = hand_over(pack_in(found), -1)
+    last, potentials = lax.optimization_barrier((near[4], potentials))
+    near = near[:4] + (last,)
+    shares = vmem_call(share_kernel, [four] * 3, where + (potentials, rows), scalars=2)
+    above, below = shift(shares[1], lambda z: -HOP), shift(shares[2], lambda z: HOP)
     mine, partner = lax.fori_loop(1, rounds, collect_in, collect(sent, found, near, ()))
     owned = (mine + across(partner).astype(F32)).astype(BF16).reshape(sources.shape)
 
     (target_rows,) = vmem_call(
         target_kernel,
-        [struct((4, ROW, ROW), BF16)],
-        where + (pair_tgt, shares),
+        [four],
+        where + (pair_tgt, shares[0], above, below),
         scalars=3,
         scratch=[pltpu.VMEM((4, ROW, ROW), F32)],
     )

time: 167 us -> 177 us (1.060)
  the two profiles are of different devices: /device:TPU:2 before, /device:TPU:24 now
where the time goes in v7:
time: 177 us; the launch traced here: 176 us
  starting transfers between devices  73 us (41%)
  blocking collectives  32.4 us (18%)
  waiting for transfers between devices  29 us (16%)
  Pallas kernels  27.7 us (16%)
  local copies, waits for them, and re-layouts  6.03 us (3%)
  other arithmetic  5.26 us (3%)
    ppermute x14, starting transfers between devices, shift(): return lax.ppermute(value, 'band', pairs)  67.7 us
    ppermute x14, waiting for transfers between devices, shift(): return lax.ppermute(value, 'band', pairs)  26.4 us
    pallas_call x9, Pallas kernels, vmem_call(): pl.pallas_call(kernel, out_shape=outs, in_specs=[smem] * scalars + [whole...  24.7 us
    all_to_all x1, blocking collectives, per_device(): slabs = lax.all_to_all(spectra, 'dom', 0, 0, tiled=True)  17.3 us
    all_to_all x1, blocking collectives, per_device(): back = lax.all_to_all(solved, 'dom', 0, 0, tiled=True)  15.1 us
    ppermute x2, starting transfers between devices, across(): return lax.ppermute(value, 'band', [(i, i ^ 1) for i in range(32)])  5.32 us
  transfers between devices with their start and end apart: 16, of which 5 were waited for; matrix products, arithmetic and copies ran while one was open for 4% of the time, Pallas kernels for 4%

profile of v7, /device:TPU:24, one launch (start us, length us, event | category | flops | bytes accessed | tf_op | source)
XLA Modules:
  0.0 175.7 jit_solution(7457358975190620460)
XLA Ops:
  2.7 3.4 %collective-permute-start.10 = (bf16[8,128,128]{2,1,0:T(8,128)(2,1)S(1)}, bf16[8,128,128]{2,1,0:T(8,128)(2,1)}, u32[]{:S(2)}, u32[]{:S(2)}) collective-permute-start(bf16[8,128,128]{2,1,0:T(8,128)(2,1)S(1)} %reshape.113.own), channel_id=1, source_target_pairs={{0,16},{16,0},{32,48},{48,32},{64,80},{80,64},{96,112},{112,96},{1... | collective-permute-start | bytes 786440 | tf_op jit(solution)/shard_map/ppermute | solution.py:421
  7.5 1.6 shard_map.123.sent
  10.1 2.7 %collective-permute-done.10.other = bf16[8,128,128]{2,1,0:T(8,128)(2,1)} collective-permute-done((bf16[8,128,128]{2,1,0:T(8,128)(2,1)S(1)}, bf16[8,128,128]{2,1,0:T(8,128)(2,1)}, u32[]{:S(2)}, u32[]{:S(2)}) %collective-permute-start.10) | collective-permute-done | bytes 262176 | tf_op jit(solution)/shard_map/ppermute | solution.py:421
  14.0 12.3 %collective-permute-start.15 = (bf16[3,128,128]{2,1,0:T(8,128)(2,1)S(1)}, bf16[3,128,128]{2,1,0:T(8,128)(2,1)S(1)}, u32[]{:S(2)}, u32[]{:S(2)}) collective-permute-start(bf16[3,128,128]{2,1,0:T(8,128)(2,1)S(1)} %get-tuple-element.553), channel_id=1, source_target_pairs={{0,416},{16,432},{32,128},{48,144},{64,480},{80,496},{96,192},{112... | collective-permute-start | bytes 294920 | tf_op jit(solution)/shard_map/ppermute | solution.py:411
  26.3 1.9 %collective-permute-start.11 = (bf16[5,128,128]{2,1,0:T(8,128)(2,1)S(1)}, bf16[5,128,128]{2,1,0:T(8,128)(2,1)S(1)}, u32[]{:S(2)}, u32[]{:S(2)}) collective-permute-start(bf16[5,128,128]{2,1,0:T(8,128)(2,1)S(1)} %get-tuple-element.549), channel_id=1, source_target_pairs={{0,32},{16,48},{32,64},{48,80},{64,96},{80,112},{96,128},{112,144}... | collective-permute-start | bytes 491528 | tf_op jit(solution)/shard_map/ppermute | solution.py:411
  28.2 8.1 %collective-permute-start.17 = (bf16[4,128,128]{2,1,0:T(8,128)(2,1)S(1)}, bf16[4,128,128]{2,1,0:T(8,128)(2,1)S(1)}, u32[]{:S(2)}, u32[]{:S(2)}) collective-permute-start(bf16[4,128,128]{2,1,0:T(8,128)(2,1)S(1)} %bitcast.36), channel_id=1, source_target_pairs={{0,352},{16,368},{32,384},{48,400},{64,416},{80,432},{96,448},{112... | collective-permute-start | bytes 393224 | tf_op jit(solution)/shard_map/ppermute | solution.py:411
  36.3 2.5 %collective-permute-start.16 = (bf16[4,128,128]{2,1,0:T(8,128)(2,1)S(1)}, bf16[4,128,128]{2,1,0:T(8,128)(2,1)S(1)}, u32[]{:S(2)}, u32[]{:S(2)}) collective-permute-start(bf16[4,128,128]{2,1,0:T(8,128)(2,1)S(1)} %bitcast.37), channel_id=1, source_target_pairs={{0,160},{16,176},{32,192},{48,208},{64,224},{80,240},{96,256},{112... | collective-permute-start | bytes 393224 | tf_op jit(solution)/shard_map/ppermute | solution.py:411
  38.9 6.3 %collective-permute-start.12 = (bf16[5,128,128]{2,1,0:T(8,128)(2,1)S(1)}, bf16[5,128,128]{2,1,0:T(8,128)(2,1)S(1)}, u32[]{:S(2)}, u32[]{:S(2)}) collective-permute-start(bf16[5,128,128]{2,1,0:T(8,128)(2,1)S(1)} %get-tuple-element.550), channel_id=1, source_target_pairs={{0,480},{16,496},{32,0},{48,16},{64,32},{80,48},{96,64},{112,80},{... | collective-permute-start | bytes 491528 | tf_op jit(solution)/shard_map/ppermute | solution.py:411
  45.2 1.9 %collective-permute-start.13 = (bf16[5,128,128]{2,1,0:T(8,128)(2,1)S(1)}, bf16[5,128,128]{2,1,0:T(8,128)(2,1)S(1)}, u32[]{:S(2)}, u32[]{:S(2)}) collective-permute-start(bf16[5,128,128]{2,1,0:T(8,128)(2,1)S(1)} %get-tuple-element.551), channel_id=1, source_target_pairs={{0,64},{16,80},{32,96},{48,112},{64,128},{80,144},{96,160},{112,17... | collective-permute-start | bytes 491528 | tf_op jit(solution)/shard_map/ppermute | solution.py:411
  47.2 6.0 %collective-permute-start.14 = (bf16[5,128,128]{2,1,0:T(8,128)(2,1)S(1)}, bf16[5,128,128]{2,1,0:T(8,128)(2,1)S(1)}, u32[]{:S(2)}, u32[]{:S(2)}) collective-permute-start(bf16[5,128,128]{2,1,0:T(8,128)(2,1)S(1)} %get-tuple-element.552), channel_id=1, source_target_pairs={{0,448},{16,464},{32,480},{48,496},{64,0},{80,16},{96,32},{112,48}... | collective-permute-start | bytes 491528 | tf_op jit(solution)/shard_map/ppermute | solution.py:411
  53.2 1.4 shard_map.122.found
  55.6 5.4 %collective-permute-done.13.refs_2_ = bf16[5,128,128]{2,1,0:T(8,128)(2,1)S(1)} collective-permute-done((bf16[5,128,128]{2,1,0:T(8,128)(2,1)S(1)}, bf16[5,128,128]{2,1,0:T(8,128)(2,1)S(1)}, u32[]{:S(2)}, u32[]{:S(2)}) %collective-permute-start.13) | collective-permute-done | bytes 163872 | tf_op jit(solution)/shard_map/ppermute | solution.py:411
  61.1 2.0 %shard_map.125 = bf16[16,128,128]{2,1,0:T(8,128)(2,1)} custom-call(s32[16]{0:T(128)S(1)} %copy-done.13, bf16[8,128,128]{2,1,0:T(8,128)(2,1)S(1)} %reshape.113.own, bf16[8,128,128]{2,1,0:T(8,128)(2,1)} %collective-permute-done.10.other, bf16[5,128,128]{2,1,0:T(8,128)(2,1)S(1)} %collective-permute-done.11.refs_0_, ...), custom_call_target="tpu_custom_call" | custom-call | tf_op jit(solution)/shard_map/pallas_call | solution.py:101
  64.4 3.5 %shard_map.126 = bf16[16,128,128]{2,1,0:T(8,128)(2,1)S(1)} custom-call(s32[3]{0:T(128)S(1)} %copy-done.12, s32[2,64]{1,0:T(2,128)S(1)} %get-tuple-element.851, bf16[16,128,128]{2,1,0:T(8,128)(2,1)} %get-tuple-element.554.sources, bf16[4,128,128]{2,1,0:T(8,128)(2,1)S(1)} %bitcast.38, bf16[4,128,128]{2,1,0:T(8,128)(2,1)S(1)} %collective-permute-done.16.below, ...), custom_call_target="tpu_custom_call" | custom-call | tf_op jit(solution)/shard_map/pallas_call | solution.py:101
  67.9 17.3 %all_to_all.10.slabs = bf16[16,128,128]{2,1,0:T(8,128)(2,1)S(1)} all-to-all(bf16[16,128,128]{2,1,0:T(8,128)(2,1)S(1)} %shard_map.126), channel_id=1, replica_groups=mesh['band'=32,'dom'=16] {'dom'}, dimensions={0} | all-to-all | bytes 1048576 | tf_op jit(solution)/shard_map/all_to_all | solution.py:482
  85.2 8.1 %shard_map.127 = bf16[16,128,128]{2,1,0:T(8,128)(2,1)S(1)} custom-call(bf16[16,128,128]{2,1,0:T(8,128)(2,1)S(1)} %all_to_all.10.slabs, f32[8,256,128]{2,1,0:T(8,128)S(1)} %copy-done.1, bf16[2,128,128]{2,1,0:T(8,128)(2,1)S(1)} %copy-done.7, bf16[2,128,128]{2,1,0:T(8,128)(2,1)S(1)} %copy-done.6), custom_call_target="tpu_custom_call" | custom-call | tf_op jit(solution)/shard_map/pallas_call | solution.py:101
  93.4 15.1 %all_to_all.11.spectra = bf16[16,128,128]{2,1,0:T(8,128)(2,1)S(1)} all-to-all(bf16[16,128,128]{2,1,0:T(8,128)(2,1)S(1)} %shard_map.127), channel_id=1, replica_groups=mesh['band'=32,'dom'=16] {'dom'}, dimensions={0} | all-to-all | bytes 1048576 | tf_op jit(solution)/shard_map/all_to_all | solution.py:489
  108.5 3.5 %shard_map.128 = (bf16[16,128,128]{2,1,0:T(8,128)(2,1)}, f32[16,128,128]{2,1,0:T(8,128)S(1)}) custom-call(s32[3]{0:T(128)S(1)} %copy-done.12, s32[2,64]{1,0:T(2,128)S(1)} %get-tuple-element.851, bf16[16,128,128]{2,1,0:T(8,128)(2,1)S(1)} %all_to_all.11.spectra, bf16[4,128,128]{2,1,0:T(8,128)(2,1)S(1)} %bitcast.39, ...), custom_call_target="tpu_custom_call" | custom-call | tf_op jit(solution)/shard_map/pallas_call | solution.py:101
  112.0 1.9 %shard_map.129 = (bf16[5,128,128]{2,1,0:T(8,128)(2,1)}, bf16[5,128,128]{2,1,0:T(8,128)(2,1)}, bf16[5,128,128]{2,1,0:T(8,128)(2,1)S(1)}, bf16[5,128,128]{2,1,0:T(8,128)(2,1)S(1)}, bf16[3,128,128]{2,1,0:T(8,128)(2,1)S(1)}) custom-call(s32[16]{0:T(128)S(1)} %copy-done.13, bf16[16,128,128]{2,1,0:T(8,128)(2,1)} %get-tuple-element.783.terms), custom_call_target="tpu_custom_call" | custom-call | tf_op jit(solution)/shard_map/pallas_call | solution.py:101
  113.9 1.9 %collective-permute-start.21 = (bf16[5,128,128]{2,1,0:T(8,128)(2,1)}, bf16[5,128,128]{2,1,0:T(8,128)(2,1)S(1)}, u32[]{:S(2)}, u32[]{:S(2)}) collective-permute-start(bf16[5,128,128]{2,1,0:T(8,128)(2,1)} %get-tuple-element.563), channel_id=1, source_target_pairs={{0,480},{16,496},{32,0},{48,16},{64,32},{80,48},{96,64},{112,80},{... | collective-permute-start | bytes 491528 | tf_op jit(solution)/shard_map/ppermute | solution.py:411
  115.9 3.9 %collective-permute-start.22 = (bf16[5,128,128]{2,1,0:T(8,128)(2,1)}, bf16[5,128,128]{2,1,0:T(8,128)(2,1)S(1)}, u32[]{:S(2)}, u32[]{:S(2)}) collective-permute-start(bf16[5,128,128]{2,1,0:T(8,128)(2,1)} %get-tuple-element.564), channel_id=1, source_target_pairs={{0,32},{16,48},{32,64},{48,80},{64,96},{80,112},{96,128},{112,144}... | collective-permute-start | bytes 491528 | tf_op jit(solution)/shard_map/ppermute | solution.py:411
  119.8 3.8 %collective-permute-start.23 = (bf16[5,128,128]{2,1,0:T(8,128)(2,1)S(1)}, bf16[5,128,128]{2,1,0:T(8,128)(2,1)S(1)}, u32[]{:S(2)}, u32[]{:S(2)}) collective-permute-start(bf16[5,128,128]{2,1,0:T(8,128)(2,1)S(1)} %get-tuple-element.565), channel_id=1, source_target_pairs={{0,448},{16,464},{32,480},{48,496},{64,0},{80,16},{96,32},{112,48}... | collective-permute-start | bytes 491528 | tf_op jit(solution)/shard_map/ppermute | solution.py:411
  123.6 3.4 %collective-permute-start.24 = (bf16[5,128,128]{2,1,0:T(8,128)(2,1)S(1)}, bf16[5,128,128]{2,1,0:T(8,128)(2,1)S(1)}, u32[]{:S(2)}, u32[]{:S(2)}) collective-permute-start(bf16[5,128,128]{2,1,0:T(8,128)(2,1)S(1)} %get-tuple-element.566), channel_id=1, source_target_pairs={{0,64},{16,80},{32,96},{48,112},{64,128},{80,144},{96,160},{112,17... | collective-permute-start | bytes 491528 | tf_op jit(solution)/shard_map/ppermute | solution.py:411
  127.0 4.8 %collective-permute-start.18 = (bf16[3,128,128]{2,1,0:T(8,128)(2,1)S(1)}, bf16[3,128,128]{2,1,0:T(8,128)(2,1)S(1)}, u32[]{:S(2)}, u32[]{:S(2)}) collective-permute-start(bf16[3,128,128]{2,1,0:T(8,128)(2,1)S(1)} %get-tuple-element.557), channel_id=1, source_target_pairs={{0,416},{16,432},{32,128},{48,144},{64,480},{80,496},{96,192},{112... | collective-permute-start | bytes 294920 | tf_op jit(solution)/shard_map/ppermute | solution.py:411
  132.5 7.8 %collective-permute-done.18.refs_4_ = bf16[3,128,128]{2,1,0:T(8,128)(2,1)S(1)} collective-permute-done((bf16[3,128,128]{2,1,0:T(8,128)(2,1)S(1)}, bf16[3,128,128]{2,1,0:T(8,128)(2,1)S(1)}, u32[]{:S(2)}, u32[]{:S(2)}) %collective-permute-start.18) | collective-permute-done | bytes 98336 | tf_op jit(solution)/shard_map/ppermute | solution.py:411
  140.3 1.4 shard_map.130
  141.8 2.3 %shard_map.132 = (f32[8,128,128]{2,1,0:T(8,128)}, bf16[8,128,128]{2,1,0:T(8,128)(2,1)}) custom-call(s32[23]{0:T(128)S(1)} %copy-done.14, s32[16]{0:T(128)S(1)} %copy-done.13, bf16[16,128,128]{2,1,0:T(8,128)(2,1)} %get-tuple-element.783.terms, bf16[5,128,128]{2,1,0:T(8,128)(2,1)S(1)} %collective-permute-done.21.refs_0_, ...), custom_call_target="tpu_custom_call" | custom-call | tf_op jit(solution)/shard_map/pallas_call | solution.py:101
  144.7 4.4 %collective-permute-start.19 = (bf16[4,128,128]{2,1,0:T(8,128)(2,1)}, bf16[4,128,128]{2,1,0:T(8,128)(2,1)S(1)}, u32[]{:S(2)}, u32[]{:S(2)}) collective-permute-start(bf16[4,128,128]{2,1,0:T(8,128)(2,1)} %copy-done.16), channel_id=1, source_target_pairs={{0,352},{16,368},{32,384},{48,400},{64,416},{80,432},{96,448},{112... | collective-permute-start | bytes 393224 | tf_op jit(solution)/shard_map/ppermute | solution.py:411
  149.1 6.3 %collective-permute-start.20 = (bf16[4,128,128]{2,1,0:T(8,128)(2,1)S(1)}, bf16[4,128,128]{2,1,0:T(8,128)(2,1)S(1)}, u32[]{:S(2)}, u32[]{:S(2)}) collective-permute-start(bf16[4,128,128]{2,1,0:T(8,128)(2,1)S(1)} %get-tuple-element.562), channel_id=1, source_target_pairs={{0,160},{16,176},{32,192},{48,208},{64,224},{80,240},{96,256},{112... | collective-permute-start | bytes 393224 | tf_op jit(solution)/shard_map/ppermute | solution.py:411
  157.8 1.9 %collective-permute-start.25 = (bf16[8,128,128]{2,1,0:T(8,128)(2,1)}, bf16[8,128,128]{2,1,0:T(8,128)(2,1)S(1)}, u32[]{:S(2)}, u32[]{:S(2)}) collective-permute-start(bf16[8,128,128]{2,1,0:T(8,128)(2,1)} %get-tuple-element.571), channel_id=1, source_target_pairs={{0,16},{16,0},{32,48},{48,32},{64,80},{80,64},{96,112},{112,96},{1... | collective-permute-start | bytes 786440 | tf_op jit(solution)/shard_map/ppermute | solution.py:421
  159.7 4.7 %collective-permute-done.19.above = bf16[4,128,128]{2,1,0:T(8,128)(2,1)S(1)} collective-permute-done((bf16[4,128,128]{2,1,0:T(8,128)(2,1)}, bf16[4,128,128]{2,1,0:T(8,128)(2,1)S(1)}, u32[]{:S(2)}, u32[]{:S(2)}) %collective-permute-start.19) | collective-permute-done | bytes 131104 | tf_op jit(solution)/shard_map/ppermute | solution.py:411
  164.4 8.4 %collective-permute-done.20.below = bf16[4,128,128]{2,1,0:T(8,128)(2,1)S(1)} collective-permute-done((bf16[4,128,128]{2,1,0:T(8,128)(2,1)S(1)}, bf16[4,128,128]{2,1,0:T(8,128)(2,1)S(1)}, u32[]{:S(2)}, u32[]{:S(2)}) %collective-permute-start.20) | collective-permute-done | bytes 131104 | tf_op jit(solution)/shard_map/ppermute | solution.py:411
  (76 shorter events, 14.4 us)
Async XLA Ops:
  0.6 8.6 %copy-start = (bf16[32,16384]{1,0:T(8,128)(2,1)S(1)}, bf16[32,16384]{1,0:T(8,128)(2,1)}, u32[]{:S(2)}) copy-start(bf16[32,16384]{1,0:T(8,128)(2,1)} %param.15) | copy-start | bytes 3145732
  1.5 4.7 %copy-start.20 = (s32[4]{0:T(128)}, s32[4]{0:T(128)S(1)}, u32[]{:S(2)}) copy-start(s32[4]{0:T(128)S(1)} %reshape.114) | copy-start | bytes 52
  2.7 10.0 %collective-permute-start.10 = (bf16[8,128,128]{2,1,0:T(8,128)(2,1)S(1)}, bf16[8,128,128]{2,1,0:T(8,128)(2,1)}, u32[]{:S(2)}, u32[]{:S(2)}) collective-permute-start(bf16[8,128,128]{2,1,0:T(8,128)(2,1)S(1)} %reshape.113.own), channel_id=1, source_target_pairs={{0,16},{16,0},{32,48},{48,32},{64,80},{80,64},{96,112},{112,96},{1... | collective-permute-start | bytes 786440 | tf_op jit(solution)/shard_map/ppermute | solution.py:421
  10.1 2.7 %copy-start.14 = (s32[23]{0:T(128)S(1)}, s32[23]{0:T(128)}, u32[]{:S(2)}) copy-start(s32[23]{0:T(128)} %shard_map.123.sent) | copy-start | bytes 280
  14.0 31.3 %collective-permute-start.15 = (bf16[3,128,128]{2,1,0:T(8,128)(2,1)S(1)}, bf16[3,128,128]{2,1,0:T(8,128)(2,1)S(1)}, u32[]{:S(2)}, u32[]{:S(2)}) collective-permute-start(bf16[3,128,128]{2,1,0:T(8,128)(2,1)S(1)} %get-tuple-element.553), channel_id=1, source_target_pairs={{0,416},{16,432},{32,128},{48,144},{64,480},{80,496},{96,192},{112... | collective-permute-start | bytes 294920 | tf_op jit(solution)/shard_map/ppermute | solution.py:411
  26.3 20.9 %collective-permute-start.11 = (bf16[5,128,128]{2,1,0:T(8,128)(2,1)S(1)}, bf16[5,128,128]{2,1,0:T(8,128)(2,1)S(1)}, u32[]{:S(2)}, u32[]{:S(2)}) collective-permute-start(bf16[5,128,128]{2,1,0:T(8,128)(2,1)S(1)} %get-tuple-element.549), channel_id=1, source_target_pairs={{0,32},{16,48},{32,64},{48,80},{64,96},{80,112},{96,128},{112,144}... | collective-permute-start | bytes 491528 | tf_op jit(solution)/shard_map/ppermute | solution.py:411
  28.2 34.9 %collective-permute-start.17 = (bf16[4,128,128]{2,1,0:T(8,128)(2,1)S(1)}, bf16[4,128,128]{2,1,0:T(8,128)(2,1)S(1)}, u32[]{:S(2)}, u32[]{:S(2)}) collective-permute-start(bf16[4,128,128]{2,1,0:T(8,128)(2,1)S(1)} %bitcast.36), channel_id=1, source_target_pairs={{0,352},{16,368},{32,384},{48,400},{64,416},{80,432},{96,448},{112... | collective-permute-start | bytes 393224 | tf_op jit(solution)/shard_map/ppermute | solution.py:411
  36.3 26.8 %collective-permute-start.16 = (bf16[4,128,128]{2,1,0:T(8,128)(2,1)S(1)}, bf16[4,128,128]{2,1,0:T(8,128)(2,1)S(1)}, u32[]{:S(2)}, u32[]{:S(2)}) collective-permute-start(bf16[4,128,128]{2,1,0:T(8,128)(2,1)S(1)} %bitcast.37), channel_id=1, source_target_pairs={{0,160},{16,176},{32,192},{48,208},{64,224},{80,240},{96,256},{112... | collective-permute-start | bytes 393224 | tf_op jit(solution)/shard_map/ppermute | solution.py:411
  38.9 16.8 %collective-permute-start.12 = (bf16[5,128,128]{2,1,0:T(8,128)(2,1)S(1)}, bf16[5,128,128]{2,1,0:T(8,128)(2,1)S(1)}, u32[]{:S(2)}, u32[]{:S(2)}) collective-permute-start(bf16[5,128,128]{2,1,0:T(8,128)(2,1)S(1)} %get-tuple-element.550), channel_id=1, source_target_pairs={{0,480},{16,496},{32,0},{48,16},{64,32},{80,48},{96,64},{112,80},{... | collective-permute-start | bytes 491528 | tf_op jit(solution)/shard_map/ppermute | solution.py:411
  45.2 15.8 %collective-permute-start.13 = (bf16[5,128,128]{2,1,0:T(8,128)(2,1)S(1)}, bf16[5,128,128]{2,1,0:T(8,128)(2,1)S(1)}, u32[]{:S(2)}, u32[]{:S(2)}) collective-permute-start(bf16[5,128,128]{2,1,0:T(8,128)(2,1)S(1)} %get-tuple-element.551), channel_id=1, source_target_pairs={{0,64},{16,80},{32,96},{48,112},{64,128},{80,144},{96,160},{112,17... | collective-permute-start | bytes 491528 | tf_op jit(solution)/shard_map/ppermute | solution.py:411
  47.2 13.9 %collective-permute-start.14 = (bf16[5,128,128]{2,1,0:T(8,128)(2,1)S(1)}, bf16[5,128,128]{2,1,0:T(8,128)(2,1)S(1)}, u32[]{:S(2)}, u32[]{:S(2)}) collective-permute-start(bf16[5,128,128]{2,1,0:T(8,128)(2,1)S(1)} %get-tuple-element.552), channel_id=1, source_target_pairs={{0,448},{16,464},{32,480},{48,496},{64,0},{80,16},{96,32},{112,48}... | collective-permute-start | bytes 491528 | tf_op jit(solution)/shard_map/ppermute | solution.py:411
  55.0 6.1 %copy-start.13 = (s32[16]{0:T(128)S(1)}, s32[16]{0:T(128)}, u32[]{:S(2)}) copy-start(s32[16]{0:T(128)} %shard_map.122.found) | copy-start | bytes 196
  63.1 1.0 copy-start.2
  63.1 1.0 copy-start.5
  63.7 0.7 copy-start.12
  64.4 20.8 %copy-start.1 = (f32[8,256,128]{2,1,0:T(8,128)S(1)}, f32[8,256,128]{2,1,0:T(8,128)}, u32[]{:S(2)}) copy-start(f32[8,256,128]{2,1,0:T(8,128)} %constant.238.clone.spectrum) | copy-start | bytes 3145732
  67.9 17.3 %copy-start.6 = (bf16[2,128,128]{2,1,0:T(8,128)(2,1)S(1)}, bf16[2,128,128]{2,1,0:T(8,128)(2,1)}, u32[]{:S(2)}) copy-start(bf16[2,128,128]{2,1,0:T(8,128)(2,1)} %constant.237.clone.x_bwd) | copy-start | bytes 196612
  67.9 17.3 %copy-start.7 = (bf16[2,128,128]{2,1,0:T(8,128)(2,1)S(1)}, bf16[2,128,128]{2,1,0:T(8,128)(2,1)}, u32[]{:S(2)}) copy-start(bf16[2,128,128]{2,1,0:T(8,128)(2,1)} %constant.236.clone.x_fwd) | copy-start | bytes 196612
  93.4 15.1 %copy-start.3 = (bf16[2,256,256]{2,1,0:T(8,128)(2,1)S(1)}, bf16[2,256,256]{2,1,0:T(8,128)(2,1)}, u32[]{:S(2)}) copy-start(bf16[2,256,256]{2,1,0:T(8,128)(2,1)} %constant.235.clone.y_bwd) | copy-start | bytes 786436
  93.4 15.1 %copy-start.8 = (bf16[2,128,128]{2,1,0:T(8,128)(2,1)S(1)}, bf16[2,128,128]{2,1,0:T(8,128)(2,1)}, u32[]{:S(2)}) copy-start(bf16[2,128,128]{2,1,0:T(8,128)(2,1)} %constant.233.clone.z_bwd) | copy-start | bytes 196612
  113.9 27.8 %collective-permute-start.21 = (bf16[5,128,128]{2,1,0:T(8,128)(2,1)}, bf16[5,128,128]{2,1,0:T(8,128)(2,1)S(1)}, u32[]{:S(2)}, u32[]{:S(2)}) collective-permute-start(bf16[5,128,128]{2,1,0:T(8,128)(2,1)} %get-tuple-element.563), channel_id=1, source_target_pairs={{0,480},{16,496},{32,0},{48,16},{64,32},{80,48},{96,64},{112,80},{... | collective-permute-start | bytes 491528 | tf_op jit(solution)/shard_map/ppermute | solution.py:411
  115.9 25.9 %collective-permute-start.22 = (bf16[5,128,128]{2,1,0:T(8,128)(2,1)}, bf16[5,128,128]{2,1,0:T(8,128)(2,1)S(1)}, u32[]{:S(2)}, u32[]{:S(2)}) collective-permute-start(bf16[5,128,128]{2,1,0:T(8,128)(2,1)} %get-tuple-element.564), channel_id=1, source_target_pairs={{0,32},{16,48},{32,64},{48,80},{64,96},{80,112},{96,128},{112,144}... | collective-permute-start | bytes 491528 | tf_op jit(solution)/shard_map/ppermute | solution.py:411
  119.8 22.0 %collective-permute-start.23 = (bf16[5,128,128]{2,1,0:T(8,128)(2,1)S(1)}, bf16[5,128,128]{2,1,0:T(8,128)(2,1)S(1)}, u32[]{:S(2)}, u32[]{:S(2)}) collective-permute-start(bf16[5,128,128]{2,1,0:T(8,128)(2,1)S(1)} %get-tuple-element.565), channel_id=1, source_target_pairs={{0,448},{16,464},{32,480},{48,496},{64,0},{80,16},{96,32},{112,48}... | collective-permute-start | bytes 491528 | tf_op jit(solution)/shard_map/ppermute | solution.py:411
  123.6 18.1 %collective-permute-start.24 = (bf16[5,128,128]{2,1,0:T(8,128)(2,1)S(1)}, bf16[5,128,128]{2,1,0:T(8,128)(2,1)S(1)}, u32[]{:S(2)}, u32[]{:S(2)}) collective-permute-start(bf16[5,128,128]{2,1,0:T(8,128)(2,1)S(1)} %get-tuple-element.566), channel_id=1, source_target_pairs={{0,64},{16,80},{32,96},{48,112},{64,128},{80,144},{96,160},{112,17... | collective-permute-start | bytes 491528 | tf_op jit(solution)/shard_map/ppermute | solution.py:411
  127.0 4.8 %copy-start.21 = (s32[4]{0:T(128)S(1)}, s32[4]{0:T(128)}, u32[]{:S(2)}) copy-start(s32[4]{0:T(128)} %copy-done.20) | copy-start | bytes 52
  127.0 13.2 %collective-permute-start.18 = (bf16[3,128,128]{2,1,0:T(8,128)(2,1)S(1)}, bf16[3,128,128]{2,1,0:T(8,128)(2,1)S(1)}, u32[]{:S(2)}, u32[]{:S(2)}) collective-permute-start(bf16[3,128,128]{2,1,0:T(8,128)(2,1)S(1)} %get-tuple-element.557), channel_id=1, source_target_pairs={{0,416},{16,432},{32,128},{48,144},{64,480},{80,496},{96,192},{112... | collective-permute-start | bytes 294920 | tf_op jit(solution)/shard_map/ppermute | solution.py:411
  141.7 2.4 %copy-start.16 = (bf16[4,128,128]{2,1,0:T(8,128)(2,1)}, bf16[4,128,128]{2,1,0:T(8,128)(2,1)S(1)}, u32[]{:S(2)}) copy-start(bf16[4,128,128]{2,1,0:T(8,128)(2,1)S(1)} %get-tuple-element.561) | copy-start | bytes 393220
  144.7 19.7 %collective-permute-start.19 = (bf16[4,128,128]{2,1,0:T(8,128)(2,1)}, bf16[4,128,128]{2,1,0:T(8,128)(2,1)S(1)}, u32[]{:S(2)}, u32[]{:S(2)}) collective-permute-start(bf16[4,128,128]{2,1,0:T(8,128)(2,1)} %copy-done.16), channel_id=1, source_target_pairs={{0,352},{16,368},{32,384},{48,400},{64,416},{80,432},{96,448},{112... | collective-permute-start | bytes 393224 | tf_op jit(solution)/shard_map/ppermute | solution.py:411
  149.1 23.7 %collective-permute-start.20 = (bf16[4,128,128]{2,1,0:T(8,128)(2,1)S(1)}, bf16[4,128,128]{2,1,0:T(8,128)(2,1)S(1)}, u32[]{:S(2)}, u32[]{:S(2)}) collective-permute-start(bf16[4,128,128]{2,1,0:T(8,128)(2,1)S(1)} %get-tuple-element.562), channel_id=1, source_target_pairs={{0,160},{16,176},{32,192},{48,208},{64,224},{80,240},{96,256},{112... | collective-permute-start | bytes 393224 | tf_op jit(solution)/shard_map/ppermute | solution.py:411
  157.8 15.0 %copy-start.15 = (s32[2,2]{1,0:T(2,128)S(1)}, s32[2,2]{1,0:T(2,128)}, u32[]{:S(2)}) copy-start(s32[2,2]{1,0:T(2,128)} %pair_tgt.1) | copy-start | bytes 52
  157.8 17.1 %collective-permute-start.25 = (bf16[8,128,128]{2,1,0:T(8,128)(2,1)}, bf16[8,128,128]{2,1,0:T(8,128)(2,1)S(1)}, u32[]{:S(2)}, u32[]{:S(2)}) collective-permute-start(bf16[8,128,128]{2,1,0:T(8,128)(2,1)} %get-tuple-element.571), channel_id=1, source_target_pairs={{0,16},{16,0},{32,48},{48,32},{64,80},{80,64},{96,112},{112,96},{1... | collective-permute-start | bytes 786440 | tf_op jit(solution)/shard_map/ppermute | solution.py:421
  173.5 1.3 copy-start.18
  (1 other events, 0.7 us)

commit v8 on v6

--- a/solution.py
+++ b/solution.py
@@ -296,6 +296,8 @@
 
 
 def term_kernel(place, pair_src, spectra, sources, wanted, z_bwd, y_bwd, terms, shares):
+    shares[...] = jnp.zeros((16, ROW, ROW), BF16)
+
     def body(want):
         rows = spectra[want]
         rows = jnp.concatenate([rows, swap_halves(rows)], axis=0)
@@ -349,22 +351,6 @@
                 add(row, near[lane].at[n])
 
     partner[...] = held[...].astype(BF16)
-
-
-def target_kernel(place, pair_src, pair_tgt, shares, rows, held):
-    z, x = place[0], place[1]
-    quad = lax.shift_right_logical(z, 2)
-    for p in range(4):
-        z_own, _ = want_of(pair_src, z, x, 4 * quad + p)
-        ahead = lax.bitwise_and(z - z_own, 3)
-        relay = ring(z_own + jnp.where(ahead == 3, -1, jnp.where(ahead == 2, far_step(z_own), ahead)))
-        held[p] = shares[4 * lax.shift_right_logical(relay, 2) + p].astype(F32)
-    for p in range(4):
-        same = jnp.zeros((ROW, ROW), F32)
-        for other in range(4):
-            hit = pair_tgt[p // 2, p % 2] == pair_tgt[other // 2, other % 2]
-            same = same + jnp.where(hit, held[other], 0.0)
-        rows[p] = same.astype(BF16)
 
 
 def hand_over(packets, sign):
@@ -387,9 +373,15 @@
     return lax.ppermute(value, "band", [(i, i ^ 1) for i in range(32)])
 
 
-def along_ring(value):
-    groups = [[8 * quad + member for quad in range(4)] for member in range(8)]
-    return lax.all_to_all(value, "band", 0, 0, axis_index_groups=groups, tiled=True)
+RING_GROUPS = [[8 * quad + member for quad in range(4)] for member in range(8)]
+
+
+def to_relays(value):
+    return lax.all_gather(value, "band", axis_index_groups=RING_GROUPS, tiled=True)
+
+
+def from_relays(value):
+    return lax.psum_scatter(value, "band", axis_index_groups=RING_GROUPS, tiled=True)
 
 
 def rounds_of(pair_src):
@@ -422,21 +414,22 @@
     own, ids = lax.optimization_barrier((sources.reshape(8, ROW, ROW), pair_tgt.reshape(4)))
     other = across(own)
     wanted = targets[ids].reshape(4, ROW, ROW)
-    wanted = along_ring(jnp.concatenate([wanted] * 4, axis=0))
-
-    def deliver(sent, found, before):
-        packed = vmem_call(pack_rows_kernel, packets, (sent, own, other), scalars=1)
+
+    def pack_rows_in(sent):
+        return vmem_call(pack_rows_kernel, packets, (sent, own, other), scalars=1)
+
+    def deliver(packed, found, before):
         near = hand_over(packed, 1)
         operands = (found, own, other) + near + before
         return vmem_call(place_rows_kernel, [sixteen], operands, scalars=1)[0]
 
+    def deliver_in(turn, before):
+        return deliver(pack_rows_in(sent_in(turn)), found_in(turn), (before,))
+
     sent, found = sent_in(0), found_in(0)
-    rows = lax.fori_loop(
-        1,
-        rounds,
-        lambda turn, before: deliver(sent_in(turn), found_in(turn), (before,)),
-        deliver(sent, found, ()),
-    )
+    packed, wanted = lax.optimization_barrier((pack_rows_in(sent), wanted))
+    wanted = to_relays(wanted)
+    rows = lax.fori_loop(1, rounds, deliver_in, deliver(packed, found, ()))
     where = (place_in(0), pair_src)
     (spectra,) = vmem_call(
         density_kernel,
@@ -473,24 +466,16 @@
         return collect(sent_in(turn), found, give_back(found), tuple(before))
 
     near = give_back(found)
-    near, shares = lax.optimization_barrier((near, shares))
-    shares = along_ring(shares)
+    shares = from_relays(shares)
     mine, partner = lax.fori_loop(1, rounds, collect_in, collect(sent, found, near, ()))
     owned = (mine + across(partner).astype(F32)).astype(BF16).reshape(sources.shape)
 
-    (target_rows,) = vmem_call(
-        target_kernel,
-        [struct((4, ROW, ROW), BF16)],
-        where + (pair_tgt, shares),
-        scalars=3,
-        scratch=[pltpu.VMEM((4, ROW, ROW), F32)],
-    )
-    flat = target_rows.reshape(4, targets.shape[1])
+    flat = shares.reshape(4, targets.shape[1]).astype(F32)
     slots = jnp.arange(targets.shape[0], dtype=jnp.int32)[:, None]
-    summed = jnp.zeros(targets.shape, BF16)
+    summed = jnp.zeros(targets.shape, F32)
     for p in range(4):
-        summed = jnp.where(slots == ids[p], flat[p][None, :], summed)
-    return summed, owned
+        summed = summed + jnp.where(slots == ids[p], flat[p][None, :], 0.0)
+    return summed.astype(BF16), owned
 
 
 def solution(mesh):

time: 167 us -> 180 us (1.078)
  the two profiles are of different devices: /device:TPU:2 before, /device:TPU:1 now
where the time goes in v8:
time: 180 us; the launch traced here: 179 us
  blocking collectives  65.4 us (36%)
  waiting for transfers between devices  32.1 us (18%)
  starting transfers between devices  30.4 us (17%)
  Pallas kernels  23.8 us (13%)
  between operations  15.1 us (8%)
  other arithmetic  7.27 us (4%)
  local copies, waits for them, and re-layouts  5.37 us (3%)
    all_gather x1, blocking collectives, to_relays(): lax.all_gather(value, 'band', axis_index_groups=RING_GROUPS, tiled=True)  31.6 us
    ppermute x6, starting transfers between devices, hand_over(): lax.ppermute(packet, 'band', [(2 * z + x, 2 * ((z + sign * move(z)) % RIN...  24.5 us
    reduce_scatter x1, waiting for transfers between devices, from_relays(): lax.psum_scatter(value, 'band', axis_index_groups=RING_GROUPS, tiled=True)  24.5 us
    pallas_call x7, Pallas kernels, vmem_call(): pl.pallas_call(kernel, out_shape=outs, in_specs=[smem] * scalars + [whole...  20.8 us
    all_to_all x1, blocking collectives, per_device(): slabs = lax.all_to_all(spectra, 'dom', 0, 0, tiled=True)  18.7 us
    all_to_all x1, blocking collectives, per_device(): back = lax.all_to_all(solved, 'dom', 0, 0, tiled=True)  15.1 us
    ppermute x2, starting transfers between devices, across(): return lax.ppermute(value, 'band', [(i, i ^ 1) for i in range(32)])  5.86 us
    ppermute x6, waiting for transfers between devices, hand_over(): lax.ppermute(packet, 'band', [(2 * z + x, 2 * ((z + sign * move(z)) % RIN...  5.37 us
  transfers between devices with their start and end apart: 9, of which 4 were waited for; matrix products, arithmetic and copies ran while one was open for 4% of the time, Pallas kernels for 3%

profile of v8, /device:TPU:1, one launch (start us, length us, event | category | flops | bytes accessed | tf_op | source)
XLA Modules:
  0.0 179.4 jit_solution(2397735219040263976)
XLA Ops:
  7.2 0.8 reshape.106
  8.1 1.2 reshape.105.own
  9.3 4.0 %collective-permute-start.6 = (bf16[8,128,128]{2,1,0:T(8,128)(2,1)S(1)}, bf16[8,128,128]{2,1,0:T(8,128)(2,1)}, u32[]{:S(2)}, u32[]{:S(2)}) collective-permute-start(bf16[8,128,128]{2,1,0:T(8,128)(2,1)S(1)} %reshape.105.own), channel_id=1, source_target_pairs={{0,16},{16,0},{32,48},{48,32},{64,80},{80,64},{96,112},{112,96},{1... | collective-permute-start | bytes 786440 | tf_op jit(solution)/shard_map/ppermute | solution.py:373
  13.9 1.4 shard_map.122.found
  15.3 1.5 shard_map.123.sent
  17.9 0.7 fusion.1
  20.1 1.1 shard_map.124
  21.3 3.5 %collective-permute-start.7 = (bf16[6,128,128]{2,1,0:T(8,128)(2,1)S(1)}, bf16[6,128,128]{2,1,0:T(8,128)(2,1)S(1)}, u32[]{:S(2)}, u32[]{:S(2)}) collective-permute-start(bf16[6,128,128]{2,1,0:T(8,128)(2,1)S(1)} %get-tuple-element.540), channel_id=1, source_target_pairs={{0,32},{16,48},{32,64},{48,80},{64,96},{80,112},{96,128},{112,144}... | collective-permute-start | bytes 589832 | tf_op jit(solution)/shard_map/ppermute | solution.py:359
  24.8 9.5 %collective-permute-start.8 = (bf16[6,128,128]{2,1,0:T(8,128)(2,1)S(1)}, bf16[6,128,128]{2,1,0:T(8,128)(2,1)S(1)}, u32[]{:S(2)}, u32[]{:S(2)}) collective-permute-start(bf16[6,128,128]{2,1,0:T(8,128)(2,1)S(1)} %get-tuple-element.541), channel_id=1, source_target_pairs={{0,480},{16,496},{32,0},{48,16},{64,32},{80,48},{96,64},{112,80},{... | collective-permute-start | bytes 589832 | tf_op jit(solution)/shard_map/ppermute | solution.py:359
  34.3 1.9 %collective-permute-start.9 = (bf16[6,128,128]{2,1,0:T(8,128)(2,1)S(1)}, bf16[6,128,128]{2,1,0:T(8,128)(2,1)S(1)}, u32[]{:S(2)}, u32[]{:S(2)}) collective-permute-start(bf16[6,128,128]{2,1,0:T(8,128)(2,1)S(1)} %get-tuple-element.542), channel_id=1, source_target_pairs={{0,64},{16,80},{32,480},{48,496},{64,128},{80,144},{96,32},{112,48... | collective-permute-start | bytes 589832 | tf_op jit(solution)/shard_map/ppermute | solution.py:359
  36.2 31.6 %all_gather.3.wanted = bf16[16,128,128]{2,1,0:T(8,128)(2,1)S(1)} all-gather(bf16[4,128,128]{2,1,0:T(8,128)(2,1)S(1)} %bitcast.36), channel_id=1, replica_groups={{0,128,256,384},{16,144,272,400},{32,160,288,416},{48,176,304,432},{64,..., dimensions={0}, use_global_device_ids=true | all-gather | bytes 655360 | tf_op jit(solution)/shard_map/all_gather | solution.py:380
  67.9 2.0 %shard_map.125 = bf16[16,128,128]{2,1,0:T(8,128)(2,1)} custom-call(s32[16]{0:T(128)S(1)} %copy-done.14, bf16[8,128,128]{2,1,0:T(8,128)(2,1)S(1)} %reshape.105.own, bf16[8,128,128]{2,1,0:T(8,128)(2,1)} %collective-permute-done.6.other, bf16[6,128,128]{2,1,0:T(8,128)(2,1)S(1)} %collective-permute-done.7.refs_0_, ...), custom_call_target="tpu_custom_call" | custom-call | tf_op jit(solution)/shard_map/pallas_call | solution.py:99
  69.9 0.9 copy-done.3
  70.8 3.5 %shard_map.126 = bf16[16,128,128]{2,1,0:T(8,128)(2,1)S(1)} custom-call(s32[3]{0:T(128)S(1)} %copy-done.13, s32[2,64]{1,0:T(2,128)S(1)} %get-tuple-element.799, bf16[16,128,128]{2,1,0:T(8,128)(2,1)} %get-tuple-element.543.sources, bf16[16,128,128]{2,1,0:T(8,128)(2,1)S(1)} %all_gather.3.wanted, bf16[2,128,128]{2,1,0:T(8,128)(2,1)S(1)} %copy-done.9, ...), custom_call_target="tpu_custom_call" | custom-call | tf_op jit(solution)/shard_map/pallas_call | solution.py:99
  74.4 18.7 %all_to_all.10.slabs = bf16[16,128,128]{2,1,0:T(8,128)(2,1)S(1)} all-to-all(bf16[16,128,128]{2,1,0:T(8,128)(2,1)S(1)} %shard_map.126), channel_id=1, replica_groups=mesh['band'=32,'dom'=16] {'dom'}, dimensions={0} | all-to-all | bytes 1048576 | tf_op jit(solution)/shard_map/all_to_all | solution.py:440
  93.1 8.1 %shard_map.127 = bf16[16,128,128]{2,1,0:T(8,128)(2,1)S(1)} custom-call(bf16[16,128,128]{2,1,0:T(8,128)(2,1)S(1)} %all_to_all.10.slabs, f32[8,256,128]{2,1,0:T(8,128)S(1)} %copy-done.1, bf16[2,128,128]{2,1,0:T(8,128)(2,1)S(1)} %copy-done.8, bf16[2,128,128]{2,1,0:T(8,128)(2,1)S(1)} %copy-done.7), custom_call_target="tpu_custom_call" | custom-call | tf_op jit(solution)/shard_map/pallas_call | solution.py:99
  101.3 15.1 %all_to_all.11.spectra = bf16[16,128,128]{2,1,0:T(8,128)(2,1)S(1)} all-to-all(bf16[16,128,128]{2,1,0:T(8,128)(2,1)S(1)} %shard_map.127), channel_id=1, replica_groups=mesh['band'=32,'dom'=16] {'dom'}, dimensions={0} | all-to-all | bytes 1048576 | tf_op jit(solution)/shard_map/all_to_all | solution.py:447
  116.4 3.6 %shard_map.128 = (bf16[16,128,128]{2,1,0:T(8,128)(2,1)S(1)}, bf16[16,128,128]{2,1,0:T(8,128)(2,1)}) custom-call(s32[3]{0:T(128)S(1)} %copy-done.13, s32[2,64]{1,0:T(2,128)S(1)} %get-tuple-element.799, bf16[16,128,128]{2,1,0:T(8,128)(2,1)S(1)} %all_to_all.11.spectra, bf16[16,128,128]{2,1,0:T(8,128)(2,1)S(1)} %copy-done.16, ...), custom_call_target="tpu_custom_call" | custom-call | tf_op jit(solution)/shard_map/pallas_call | solution.py:99
  120.8 4.5 %collective-permute-start.10 = (bf16[6,128,128]{2,1,0:T(8,128)(2,1)S(1)}, bf16[6,128,128]{2,1,0:T(8,128)(2,1)S(1)}, u32[]{:S(2)}, u32[]{:S(2)}) collective-permute-start(bf16[6,128,128]{2,1,0:T(8,128)(2,1)S(1)} %get-tuple-element.547), channel_id=1, source_target_pairs={{0,480},{16,496},{32,0},{48,16},{64,32},{80,48},{96,64},{112,80},{... | collective-permute-start | bytes 589832 | tf_op jit(solution)/shard_map/ppermute | solution.py:359
  125.3 1.9 %collective-permute-start.11 = (bf16[6,128,128]{2,1,0:T(8,128)(2,1)S(1)}, bf16[6,128,128]{2,1,0:T(8,128)(2,1)S(1)}, u32[]{:S(2)}, u32[]{:S(2)}) collective-permute-start(bf16[6,128,128]{2,1,0:T(8,128)(2,1)S(1)} %get-tuple-element.548), channel_id=1, source_target_pairs={{0,32},{16,48},{32,64},{48,80},{64,96},{80,112},{96,128},{112,144}... | collective-permute-start | bytes 589832 | tf_op jit(solution)/shard_map/ppermute | solution.py:359
  127.2 3.1 %collective-permute-start.12 = (bf16[6,128,128]{2,1,0:T(8,128)(2,1)S(1)}, bf16[6,128,128]{2,1,0:T(8,128)(2,1)S(1)}, u32[]{:S(2)}, u32[]{:S(2)}) collective-permute-start(bf16[6,128,128]{2,1,0:T(8,128)(2,1)S(1)} %get-tuple-element.549), channel_id=1, source_target_pairs={{0,448},{16,464},{32,96},{48,112},{64,0},{80,16},{96,160},{112,176... | collective-permute-start | bytes 589832 | tf_op jit(solution)/shard_map/ppermute | solution.py:359
  130.3 3.0 %collective-permute-done.11.refs_1_ = bf16[6,128,128]{2,1,0:T(8,128)(2,1)S(1)} collective-permute-done((bf16[6,128,128]{2,1,0:T(8,128)(2,1)S(1)}, bf16[6,128,128]{2,1,0:T(8,128)(2,1)S(1)}, u32[]{:S(2)}, u32[]{:S(2)}) %collective-permute-start.11) | collective-permute-done | bytes 196640 | tf_op jit(solution)/shard_map/ppermute | solution.py:359
  133.3 2.4 %collective-permute-done.12.refs_2_ = bf16[6,128,128]{2,1,0:T(8,128)(2,1)S(1)} collective-permute-done((bf16[6,128,128]{2,1,0:T(8,128)(2,1)S(1)}, bf16[6,128,128]{2,1,0:T(8,128)(2,1)S(1)}, u32[]{:S(2)}, u32[]{:S(2)}) %collective-permute-start.12) | collective-permute-done | bytes 196640 | tf_op jit(solution)/shard_map/ppermute | solution.py:359
  135.7 1.7 shard_map.130
  137.4 1.9 %collective-permute-start.13 = (bf16[8,128,128]{2,1,0:T(8,128)(2,1)}, bf16[8,128,128]{2,1,0:T(8,128)(2,1)S(1)}, u32[]{:S(2)}, u32[]{:S(2)}) collective-permute-start(bf16[8,128,128]{2,1,0:T(8,128)(2,1)} %get-tuple-element.553), channel_id=1, source_target_pairs={{0,16},{16,0},{32,48},{48,32},{64,80},{80,64},{96,112},{112,96},{1... | collective-permute-start | bytes 786440 | tf_op jit(solution)/shard_map/ppermute | solution.py:373
  140.0 1.3 iota_compare_fusion.2
  141.2 1.3 iota_compare_fusion
  142.5 2.2 %collective-permute-done.13 = bf16[8,128,128]{2,1,0:T(8,128)(2,1)S(1)} collective-permute-done((bf16[8,128,128]{2,1,0:T(8,128)(2,1)}, bf16[8,128,128]{2,1,0:T(8,128)(2,1)S(1)}, u32[]{:S(2)}, u32[]{:S(2)}) %collective-permute-start.13) | collective-permute-done | bytes 262176 | tf_op jit(solution)/shard_map/ppermute | solution.py:373
  144.8 0.8 reshape.108
  145.6 24.5 %reduce-scatter.2.cloned.1.call-done = bf16[4,128,128]{2,1,0:T(8,128)(2,1)} async-done(((bf16[16,128,128]{2,1,0:T(8,128)(2,1)}), bf16[4,128,128]{2,1,0:T(8,128)(2,1)}) %reduce-scatter.2.cloned.1.call-update) | async-done | bytes 131088 | tf_op jit(solution)/shard_map/reduce_scatter | solution.py:384
  170.0 0.9 convert_element_type.18
  171.0 1.6 add_convert_fusion
  (49 shorter events, 3.9 us)
Async XLA Ops:
  7.2 12.2 %copy-start = (bf16[32,16384]{1,0:T(8,128)(2,1)S(1)}, bf16[32,16384]{1,0:T(8,128)(2,1)}, u32[]{:S(2)}) copy-start(bf16[32,16384]{1,0:T(8,128)(2,1)} %param.15) | copy-start | bytes 3145732
  7.2 162.8 %reduce-scatter.2.cloned.1.call-start = ((), (), s32[]{:S(2)}) async-start(), calls=%async_computation.3 | async-start | bytes 655360 | tf_op jit(solution)/shard_map/reduce_scatter | solution.py:384
  9.3 10.8 %collective-permute-start.6 = (bf16[8,128,128]{2,1,0:T(8,128)(2,1)S(1)}, bf16[8,128,128]{2,1,0:T(8,128)(2,1)}, u32[]{:S(2)}, u32[]{:S(2)}) collective-permute-start(bf16[8,128,128]{2,1,0:T(8,128)(2,1)S(1)} %reshape.105.own), channel_id=1, source_target_pairs={{0,16},{16,0},{32,48},{48,32},{64,80},{80,64},{96,112},{112,96},{1... | collective-permute-start | bytes 786440 | tf_op jit(solution)/shard_map/ppermute | solution.py:373
  16.8 3.3 %copy-start.15 = (s32[18]{0:T(128)S(1)}, s32[18]{0:T(128)}, u32[]{:S(2)}) copy-start(s32[18]{0:T(128)} %shard_map.123.sent) | copy-start | bytes 220
  19.4 48.5 %copy-start.14 = (s32[16]{0:T(128)S(1)}, s32[16]{0:T(128)}, u32[]{:S(2)}) copy-start(s32[16]{0:T(128)} %shard_map.122.found) | copy-start | bytes 196
  21.2 48.6 %copy-start.17 = (s32[2,64]{1,0:T(2,128)S(1)}, s32[2,64]{1,0:T(2,128)}, u32[]{:S(2)}) copy-start(s32[2,64]{1,0:T(2,128)} %pair_src.7) | copy-start | bytes 1540
  21.3 46.6 %collective-permute-start.7 = (bf16[6,128,128]{2,1,0:T(8,128)(2,1)S(1)}, bf16[6,128,128]{2,1,0:T(8,128)(2,1)S(1)}, u32[]{:S(2)}, u32[]{:S(2)}) collective-permute-start(bf16[6,128,128]{2,1,0:T(8,128)(2,1)S(1)} %get-tuple-element.540), channel_id=1, source_target_pairs={{0,32},{16,48},{32,64},{48,80},{64,96},{80,112},{96,128},{112,144}... | collective-permute-start | bytes 589832 | tf_op jit(solution)/shard_map/ppermute | solution.py:359
  24.8 43.0 %collective-permute-start.8 = (bf16[6,128,128]{2,1,0:T(8,128)(2,1)S(1)}, bf16[6,128,128]{2,1,0:T(8,128)(2,1)S(1)}, u32[]{:S(2)}, u32[]{:S(2)}) collective-permute-start(bf16[6,128,128]{2,1,0:T(8,128)(2,1)S(1)} %get-tuple-element.541), channel_id=1, source_target_pairs={{0,480},{16,496},{32,0},{48,16},{64,32},{80,48},{96,64},{112,80},{... | collective-permute-start | bytes 589832 | tf_op jit(solution)/shard_map/ppermute | solution.py:359
  34.3 33.5 %collective-permute-start.9 = (bf16[6,128,128]{2,1,0:T(8,128)(2,1)S(1)}, bf16[6,128,128]{2,1,0:T(8,128)(2,1)S(1)}, u32[]{:S(2)}, u32[]{:S(2)}) collective-permute-start(bf16[6,128,128]{2,1,0:T(8,128)(2,1)S(1)} %get-tuple-element.542), channel_id=1, source_target_pairs={{0,64},{16,80},{32,480},{48,496},{64,128},{80,144},{96,32},{112,48... | collective-permute-start | bytes 589832 | tf_op jit(solution)/shard_map/ppermute | solution.py:359
  67.9 2.0 %copy-start.13 = (s32[3]{0:T(128)S(1)}, s32[3]{0:T(128)}, u32[]{:S(2)}) copy-start(s32[3]{0:T(128)} %pad_add_fusion.2.place) | copy-start | bytes 40
  69.9 1.0 copy-start.3
  69.9 1.0 copy-start.9
  70.8 22.3 %copy-start.1 = (f32[8,256,128]{2,1,0:T(8,128)S(1)}, f32[8,256,128]{2,1,0:T(8,128)}, u32[]{:S(2)}) copy-start(f32[8,256,128]{2,1,0:T(8,128)} %constant.224.clone.spectrum) | copy-start | bytes 3145732
  70.8 22.3 %copy-start.7 = (bf16[2,128,128]{2,1,0:T(8,128)(2,1)S(1)}, bf16[2,128,128]{2,1,0:T(8,128)(2,1)}, u32[]{:S(2)}) copy-start(bf16[2,128,128]{2,1,0:T(8,128)(2,1)} %constant.223.clone.x_bwd) | copy-start | bytes 196612
  70.8 22.3 %copy-start.8 = (bf16[2,128,128]{2,1,0:T(8,128)(2,1)S(1)}, bf16[2,128,128]{2,1,0:T(8,128)(2,1)}, u32[]{:S(2)}) copy-start(bf16[2,128,128]{2,1,0:T(8,128)(2,1)} %constant.222.clone.x_fwd) | copy-start | bytes 196612
  101.3 15.2 %copy-start.2 = (bf16[2,256,256]{2,1,0:T(8,128)(2,1)S(1)}, bf16[2,256,256]{2,1,0:T(8,128)(2,1)}, u32[]{:S(2)}) copy-start(bf16[2,256,256]{2,1,0:T(8,128)(2,1)} %constant.221.clone.y_bwd) | copy-start | bytes 786436
  101.3 15.1 %copy-start.6 = (bf16[2,128,128]{2,1,0:T(8,128)(2,1)S(1)}, bf16[2,128,128]{2,1,0:T(8,128)(2,1)}, u32[]{:S(2)}) copy-start(bf16[2,128,128]{2,1,0:T(8,128)(2,1)} %constant.219.clone.z_bwd) | copy-start | bytes 196612
  101.3 15.1 %copy-start.16 = (bf16[16,128,128]{2,1,0:T(8,128)(2,1)S(1)}, bf16[16,128,128]{2,1,0:T(8,128)(2,1)}, u32[]{:S(2)}) copy-start(bf16[16,128,128]{2,1,0:T(8,128)(2,1)} %get-tuple-element.543.sources) | copy-start | bytes 1572868
  120.8 9.6 %collective-permute-start.10 = (bf16[6,128,128]{2,1,0:T(8,128)(2,1)S(1)}, bf16[6,128,128]{2,1,0:T(8,128)(2,1)S(1)}, u32[]{:S(2)}, u32[]{:S(2)}) collective-permute-start(bf16[6,128,128]{2,1,0:T(8,128)(2,1)S(1)} %get-tuple-element.547), channel_id=1, source_target_pairs={{0,480},{16,496},{32,0},{48,16},{64,32},{80,48},{96,64},{112,80},{... | collective-permute-start | bytes 589832 | tf_op jit(solution)/shard_map/ppermute | solution.py:359
  125.3 8.0 %collective-permute-start.11 = (bf16[6,128,128]{2,1,0:T(8,128)(2,1)S(1)}, bf16[6,128,128]{2,1,0:T(8,128)(2,1)S(1)}, u32[]{:S(2)}, u32[]{:S(2)}) collective-permute-start(bf16[6,128,128]{2,1,0:T(8,128)(2,1)S(1)} %get-tuple-element.548), channel_id=1, source_target_pairs={{0,32},{16,48},{32,64},{48,80},{64,96},{80,112},{96,128},{112,144}... | collective-permute-start | bytes 589832 | tf_op jit(solution)/shard_map/ppermute | solution.py:359
  127.2 8.5 %collective-permute-start.12 = (bf16[6,128,128]{2,1,0:T(8,128)(2,1)S(1)}, bf16[6,128,128]{2,1,0:T(8,128)(2,1)S(1)}, u32[]{:S(2)}, u32[]{:S(2)}) collective-permute-start(bf16[6,128,128]{2,1,0:T(8,128)(2,1)S(1)} %get-tuple-element.549), channel_id=1, source_target_pairs={{0,448},{16,464},{32,96},{48,112},{64,0},{80,16},{96,160},{112,176... | collective-permute-start | bytes 589832 | tf_op jit(solution)/shard_map/ppermute | solution.py:359
  137.4 7.3 %collective-permute-start.13 = (bf16[8,128,128]{2,1,0:T(8,128)(2,1)}, bf16[8,128,128]{2,1,0:T(8,128)(2,1)S(1)}, u32[]{:S(2)}, u32[]{:S(2)}) collective-permute-start(bf16[8,128,128]{2,1,0:T(8,128)(2,1)} %get-tuple-element.553), channel_id=1, source_target_pairs={{0,16},{16,0},{32,48},{48,32},{64,80},{80,64},{96,112},{112,96},{1... | collective-permute-start | bytes 786440 | tf_op jit(solution)/shard_map/ppermute | solution.py:373
Sparse Core Ops, SparseCore 0:
  130.4 39.5 reduce-scatter.1

commit v9 on v6

--- a/solution.py
+++ b/solution.py
@@ -213,33 +213,41 @@
                     out[want] = rows[at - first]
 
 
-def for_each_solved(place, pair_src, body):
+def for_each_solved(place, pair_src, queue, body):
     z, x = place[0], place[1]
 
-    def step(want, carry):
+    def note(want, count):
         z_own, _ = want_of(pair_src, z, x, want)
         near = jnp.logical_or(ring(z - z_own + 1) <= 2, ring(z - z_own) == ring(far_step(z)))
 
         @pl.when(near)
         def _():
-            body(want)
-
+            queue[count] = want
+
+        return count + near.astype(jnp.int32)
+
+    count = lax.fori_loop(0, 16, note, jnp.int32(0))
+
+    def step(turn, carry):
+        body((queue[2 * turn], queue[jnp.minimum(2 * turn + 1, count - 1)]))
         return carry
 
-    lax.fori_loop(0, 16, step, 0)
-
-
-def density_kernel(place, pair_src, sources, wanted, z_fwd, y_fwd, spectra):
-    def body(want):
-        density = sources[want].astype(F32) * wanted[want].astype(F32)
-        along = right_mul(density, z_fwd)
-        mixed = left_mul(y_fwd, jnp.concatenate([along, swap_halves(along)], axis=0))
-        spectra[want] = by_half(mixed).astype(BF16)
-
-    for_each_solved(place, pair_src, body)
-
-
-def solve_kernel(slabs, spectrum, x_fwd, x_bwd, out, residual, direction, total):
+    lax.fori_loop(0, lax.shift_right_logical(count + 1, 1), step, 0)
+
+
+def density_kernel(place, pair_src, sources, wanted, z_fwd, y_fwd, spectra, queue):
+    def body(wants):
+        pairs = [sources[want].astype(F32) * wanted[want].astype(F32) for want in wants]
+        pairs = [right_mul(pair, z_fwd) for pair in pairs]
+        pairs = [jnp.concatenate([pair, swap_halves(pair)], axis=0) for pair in pairs]
+        pairs = [by_half(left_mul(y_fwd, pair)).astype(BF16) for pair in pairs]
+        for want, pair in zip(wants, pairs):
+            spectra[want] = pair
+
+    for_each_solved(place, pair_src, queue, body)
+
+
+def solve_kernel(slabs, spectrum, x_fwd, x_bwd, out, residual, directions):
     def dot_of(value):
         return jnp.sum(value.reshape(32, 8, ROW), axis=0)
 
@@ -252,28 +260,26 @@
         part = jnp.concatenate(part, axis=1).astype(BF16)
         value = mm(x_fwd[0], part) + mm(x_fwd[1], part)
         value = jnp.concatenate([value[:, :ROW], value[:, ROW:]], axis=0)
-        direction[j] = value
+        directions[0, j] = value
         square = value * value
         return norm + dot_of(square), power + dot_of(square * spectrum[j])
 
     norm, power = lax.fori_loop(0, 8, start, (zero, zero))
     norm, power = jnp.sum(norm), jnp.sum(power)
-    step, ratio = norm / power, jnp.float32(0.0)
+    steps, ratio = [norm / power], jnp.float32(0.0)
     for sweep in range(SWEEPS - 1):
+        step = steps[-1]
 
         def advance(j, carry, sweep=sweep, step=step, ratio=ratio):
             new, power = carry
             lam = spectrum[j]
             if sweep == 0:
-                d = direction[j]
-                r = d - step * (lam * d)
-                total[j] = step * d
+                r = d = directions[0, j]
             else:
                 r = residual[j]
-                d = r + ratio * direction[j]
-                r = r - step * (lam * d)
-                direction[j] = d
-                total[j] = total[j] + step * d
+                d = r + ratio * directions[sweep - 1, j]
+                directions[sweep, j] = d
+            r = r - step * (lam * d)
             residual[j] = r
             square = r * r
             return new + dot_of(square), power + dot_of(square * lam)
@@ -281,11 +287,13 @@
         new, power = lax.fori_loop(0, 8, advance, (zero, zero))
         new, power = jnp.sum(new), jnp.sum(power)
         ratio = new / norm
-        step = new / (power - ratio * new / step)
+        steps.append(new / (power - ratio * new / step))
         norm = new
 
     def finish(j, carry):
-        value = total[j] + step * (residual[j] + ratio * direction[j])
+        value = steps[-1] * (residual[j] + ratio * directions[SWEEPS - 2, j])
+        for sweep in range(SWEEPS - 1):
+            value = value + steps[sweep] * directions[sweep, j]
         part = left_mul(x_bwd, jnp.concatenate([value[:ROW], value[ROW:]], axis=1))
         part = [part[:, :ROW].reshape(RING, 8, ROW), part[:, ROW:].reshape(RING, 8, ROW)]
         part = jnp.concatenate(part, axis=1)
@@ -295,15 +303,17 @@
     lax.fori_loop(0, 8, finish, 0)
 
 
-def term_kernel(place, pair_src, spectra, sources, wanted, z_bwd, y_bwd, terms, shares):
-    def body(want):
-        rows = spectra[want]
-        rows = jnp.concatenate([rows, swap_halves(rows)], axis=0)
-        potential = right_mul(by_half(mm(y_bwd[0], rows) + mm(y_bwd[1], rows)), z_bwd)
-        terms[want] = (-potential * wanted[want].astype(F32)).astype(BF16)
-        shares[want] = (-potential * sources[want].astype(F32)).astype(BF16)
-
-    for_each_solved(place, pair_src, body)
+def term_kernel(place, pair_src, spectra, sources, wanted, z_bwd, y_bwd, terms, shares, queue):
+    def body(wants):
+        pairs = [spectra[want] for want in wants]
+        pairs = [jnp.concatenate([pair, swap_halves(pair)], axis=0) for pair in pairs]
+        pairs = [by_half(mm(y_bwd[0], pair) + mm(y_bwd[1], pair)) for pair in pairs]
+        pairs = [-right_mul(pair, z_bwd) for pair in pairs]
+        for want, pair in zip(wants, pairs):
+            terms[want] = (pair * wanted[want].astype(F32)).astype(BF16)
+            shares[want] = (pair * sources[want].astype(F32)).astype(BF16)
+
+    for_each_solved(place, pair_src, queue, body)
 
 
 def pack_terms_kernel(found, terms, *outs):
@@ -405,7 +415,6 @@
 def per_device(targets, sources, pair_tgt, pair_src):
     table = {name: jnp.asarray(value) for name, value in tables().items()}
     band = lax.axis_index("band")
-    rounds = rounds_of(pair_src)
     sixteen = struct((16, ROW, ROW), BF16)
     packets = [struct((CAP, ROW, ROW), BF16)] * 3
 
@@ -422,34 +431,38 @@
     own, ids = lax.optimization_barrier((sources.reshape(8, ROW, ROW), pair_tgt.reshape(4)))
     other = across(own)
     wanted = targets[ids].reshape(4, ROW, ROW)
-    wanted = along_ring(jnp.concatenate([wanted] * 4, axis=0))
-
-    def deliver(sent, found, before):
-        packed = vmem_call(pack_rows_kernel, packets, (sent, own, other), scalars=1)
-        near = hand_over(packed, 1)
+
+    def pack_rows_in(sent):
+        return vmem_call(pack_rows_kernel, packets, (sent, own, other), scalars=1)
+
+    def deliver(near, found, before):
         operands = (found, own, other) + near + before
         return vmem_call(place_rows_kernel, [sixteen], operands, scalars=1)[0]
 
+    def deliver_in(turn, before):
+        return deliver(hand_over(pack_rows_in(sent_in(turn)), 1), found_in(turn), (before,))
+
     sent, found = sent_in(0), found_in(0)
-    rows = lax.fori_loop(
-        1,
-        rounds,
-        lambda turn, before: deliver(sent_in(turn), found_in(turn), (before,)),
-        deliver(sent, found, ()),
-    )
+    packed, found, wanted = lax.optimization_barrier((pack_rows_in(sent), found, wanted))
+    wanted = along_ring(jnp.concatenate([wanted] * 4, axis=0))
+    near = hand_over(packed, 1)
+    first, wants = lax.optimization_barrier((near[0], pair_src))
+    rounds = rounds_of(wants)
+    rows = lax.fori_loop(1, rounds, deliver_in, deliver((first,) + near[1:], found, ()))
     where = (place_in(0), pair_src)
     (spectra,) = vmem_call(
         density_kernel,
         [sixteen],
         where + (rows, wanted, table["z_fwd"], table["y_fwd"]),
         scalars=2,
+        scratch=[pltpu.SMEM((16,), jnp.int32)],
     )
     slabs = lax.all_to_all(spectra, "dom", 0, 0, tiled=True)
     (solved,) = vmem_call(
         solve_kernel,
         [sixteen],
         (slabs, table["spectrum"], table["x_fwd"], table["x_bwd"]),
-        scratch=[pltpu.VMEM((8, 256, ROW), F32)] * 3,
+        scratch=[pltpu.VMEM((8, 256, ROW), F32), pltpu.VMEM((SWEEPS - 1, 8, 256, ROW), F32)],
     )
     back = lax.all_to_all(solved, "dom", 0, 0, tiled=True)
     terms, shares = vmem_call(
@@ -457,6 +470,7 @@
         [sixteen, sixteen],
         where + (back, rows, wanted, table["z_bwd"], table["y_bwd"]),
         scalars=2,
+        scratch=[pltpu.SMEM((16,), jnp.int32)],
     )
 
     def give_back(found):

time: 167 us -> 173 us (1.036)
  the two profiles are of different devices: /device:TPU:2 before, /device:TPU:33 now
where the time goes in v9:
time: 173 us; the launch traced here: 172 us
  starting transfers between devices  53.9 us (31%)
  waiting for transfers between devices  46.9 us (27%)
  blocking collectives  34.2 us (20%)
  Pallas kernels  22.8 us (13%)
  other arithmetic  7.36 us (4%)
  local copies, waits for them, and re-layouts  5.49 us (3%)
    ppermute x6, starting transfers between devices, hand_over(): lax.ppermute(packet, 'band', [(2 * z + x, 2 * ((z + sign * move(z)) % RIN...  25.5 us
    ppermute x6, waiting for transfers between devices, hand_over(): lax.ppermute(packet, 'band', [(2 * z + x, 2 * ((z + sign * move(z)) % RIN...  24.6 us
    all_to_all x2, starting transfers between devices, along_ring(): lax.all_to_all(value, 'band', 0, 0, axis_index_groups=groups, tiled=True)  22.6 us
    pallas_call x8, Pallas kernels, vmem_call(): pl.pallas_call(kernel, out_shape=outs, in_specs=[smem] * scalars + [whole...  19.9 us
    all_to_all x2, waiting for transfers between devices, along_ring(): lax.all_to_all(value, 'band', 0, 0, axis_index_groups=groups, tiled=True)  19.3 us
    all_to_all x1, blocking collectives, per_device(): slabs = lax.all_to_all(spectra, 'dom', 0, 0, tiled=True)  19.1 us
    all_to_all x1, blocking collectives, per_device(): back = lax.all_to_all(solved, 'dom', 0, 0, tiled=True)  15.1 us
    ppermute x2, starting transfers between devices, across(): return lax.ppermute(value, 'band', [(i, i ^ 1) for i in range(32)])  5.78 us
  transfers between devices with their start and end apart: 10, of which 6 were waited for; matrix products, arithmetic and copies ran while one was open for 4% of the time, Pallas kernels for 4%

profile of v9, /device:TPU:33, one launch (start us, length us, event | category | flops | bytes accessed | tf_op | source)
XLA Modules:
  0.0 172.3 jit_solution(8000570683898635076)
XLA Ops:
  1.5 1.2 reshape.104.own
  2.7 3.1 %collective-permute-start.6 = (bf16[8,128,128]{2,1,0:T(8,128)(2,1)S(1)}, bf16[8,128,128]{2,1,0:T(8,128)(2,1)}, u32[]{:S(2)}, u32[]{:S(2)}) collective-permute-start(bf16[8,128,128]{2,1,0:T(8,128)(2,1)S(1)} %reshape.104.own), channel_id=1, source_target_pairs={{0,16},{16,0},{32,48},{48,32},{64,80},{80,64},{96,112},{112,96},{1... | collective-permute-start | bytes 786440 | tf_op jit(solution)/shard_map/ppermute | solution.py:397
  6.6 1.5 shard_map.122.sent
  8.1 1.4 shard_map.124.found
  10.2 1.7 collective-permute-done.6.other
  11.9 1.1 shard_map.123
  13.9 13.9 %all-to-all-start = ((bf16[16,128,128]{2,1,0:T(8,128)(2,1)}), bf16[16,128,128]{2,1,0:T(8,128)(2,1)S(1)}, u32[]{:S(2)}, u32[]{:S(2)}) async-start(bf16[16,128,128]{2,1,0:T(8,128)(2,1)} %pad_maximum_fusion), calls=%async_computation | async-start | bytes 1048576 | tf_op jit(solution)/shard_map/all_to_all | solution.py:402
  27.8 2.6 %collective-permute-start.7 = (bf16[6,128,128]{2,1,0:T(8,128)(2,1)S(1)}, bf16[6,128,128]{2,1,0:T(8,128)(2,1)S(1)}, u32[]{:S(2)}, u32[]{:S(2)}) collective-permute-start(bf16[6,128,128]{2,1,0:T(8,128)(2,1)S(1)} %get-tuple-element.548), channel_id=1, source_target_pairs={{0,32},{16,48},{32,64},{48,80},{64,96},{80,112},{96,128},{112,144}... | collective-permute-start | bytes 589832 | tf_op jit(solution)/shard_map/ppermute | solution.py:383
  30.5 2.6 %collective-permute-start.8 = (bf16[6,128,128]{2,1,0:T(8,128)(2,1)S(1)}, bf16[6,128,128]{2,1,0:T(8,128)(2,1)S(1)}, u32[]{:S(2)}, u32[]{:S(2)}) collective-permute-start(bf16[6,128,128]{2,1,0:T(8,128)(2,1)S(1)} %get-tuple-element.550), channel_id=1, source_target_pairs={{0,480},{16,496},{32,0},{48,16},{64,32},{80,48},{96,64},{112,80},{... | collective-permute-start | bytes 589832 | tf_op jit(solution)/shard_map/ppermute | solution.py:383
  33.1 6.4 %collective-permute-start.9 = (bf16[6,128,128]{2,1,0:T(8,128)(2,1)S(1)}, bf16[6,128,128]{2,1,0:T(8,128)(2,1)S(1)}, u32[]{:S(2)}, u32[]{:S(2)}) collective-permute-start(bf16[6,128,128]{2,1,0:T(8,128)(2,1)S(1)} %get-tuple-element.551), channel_id=1, source_target_pairs={{0,64},{16,80},{32,480},{48,496},{64,128},{80,144},{96,32},{112,48... | collective-permute-start | bytes 589832 | tf_op jit(solution)/shard_map/ppermute | solution.py:383
  39.5 14.8 %collective-permute-done.7.refs_0_ = bf16[6,128,128]{2,1,0:T(8,128)(2,1)S(1)} collective-permute-done((bf16[6,128,128]{2,1,0:T(8,128)(2,1)S(1)}, bf16[6,128,128]{2,1,0:T(8,128)(2,1)S(1)}, u32[]{:S(2)}, u32[]{:S(2)}) %collective-permute-start.7) | collective-permute-done | bytes 196640 | tf_op jit(solution)/shard_map/ppermute | solution.py:383
  56.0 5.1 %collective-permute-done.9.refs_2_ = bf16[6,128,128]{2,1,0:T(8,128)(2,1)S(1)} collective-permute-done((bf16[6,128,128]{2,1,0:T(8,128)(2,1)S(1)}, bf16[6,128,128]{2,1,0:T(8,128)(2,1)S(1)}, u32[]{:S(2)}, u32[]{:S(2)}) %collective-permute-start.9) | collective-permute-done | bytes 196640 | tf_op jit(solution)/shard_map/ppermute | solution.py:383
  61.1 2.0 %shard_map.125 = bf16[16,128,128]{2,1,0:T(8,128)(2,1)} custom-call(s32[16]{0:T(128)S(1)} %copy-done.13, bf16[8,128,128]{2,1,0:T(8,128)(2,1)S(1)} %reshape.104.own, bf16[8,128,128]{2,1,0:T(8,128)(2,1)} %collective-permute-done.6.other, bf16[6,128,128]{2,1,0:T(8,128)(2,1)S(1)} %collective-permute-done.7.refs_0_, ...), custom_call_target="tpu_custom_call" | custom-call | tf_op jit(solution)/shard_map/pallas_call | solution.py:99
  63.1 0.9 copy-done.3
  64.0 2.7 %shard_map.126 = bf16[16,128,128]{2,1,0:T(8,128)(2,1)S(1)} custom-call(s32[3]{0:T(128)S(1)} %copy-done.12, s32[2,64]{1,0:T(2,128)S(1)} %get-tuple-element.814, bf16[16,128,128]{2,1,0:T(8,128)(2,1)} %get-tuple-element.553.sources, bf16[16,128,128]{2,1,0:T(8,128)(2,1)S(1)} %all-to-all-done.wanted, bf16[2,128,128]{2,1,0:T(8,128)(2,1)S(1)} %copy-done.8, ...), custom_call_target="tpu_custom_call" | custom-call | tf_op jit(solution)/shard_map/pallas_call | solution.py:99
  66.7 19.1 %all_to_all.20.slabs = bf16[16,128,128]{2,1,0:T(8,128)(2,1)S(1)} all-to-all(bf16[16,128,128]{2,1,0:T(8,128)(2,1)S(1)} %shard_map.126), channel_id=1, replica_groups=mesh['band'=32,'dom'=16] {'dom'}, dimensions={0} | all-to-all | bytes 1048576 | tf_op jit(solution)/shard_map/all_to_all | solution.py:460
  85.8 8.2 %shard_map.127 = bf16[16,128,128]{2,1,0:T(8,128)(2,1)S(1)} custom-call(bf16[16,128,128]{2,1,0:T(8,128)(2,1)S(1)} %all_to_all.20.slabs, f32[8,256,128]{2,1,0:T(8,128)S(1)} %copy-done.1, bf16[2,128,128]{2,1,0:T(8,128)(2,1)S(1)} %copy-done.7, bf16[2,128,128]{2,1,0:T(8,128)(2,1)S(1)} %copy-done.6), custom_call_target="tpu_custom_call" | custom-call | tf_op jit(solution)/shard_map/pallas_call | solution.py:99
  94.1 15.1 %all_to_all.21.spectra = bf16[16,128,128]{2,1,0:T(8,128)(2,1)S(1)} all-to-all(bf16[16,128,128]{2,1,0:T(8,128)(2,1)S(1)} %shard_map.127), channel_id=1, replica_groups=mesh['band'=32,'dom'=16] {'dom'}, dimensions={0} | all-to-all | bytes 1048576 | tf_op jit(solution)/shard_map/all_to_all | solution.py:467
  109.2 2.7 %shard_map.128 = (bf16[16,128,128]{2,1,0:T(8,128)(2,1)S(1)}, bf16[16,128,128]{2,1,0:T(8,128)(2,1)}) custom-call(s32[3]{0:T(128)S(1)} %copy-done.12, s32[2,64]{1,0:T(2,128)S(1)} %get-tuple-element.814, bf16[16,128,128]{2,1,0:T(8,128)(2,1)S(1)} %all_to_all.21.spectra, bf16[16,128,128]{2,1,0:T(8,128)(2,1)S(1)} %copy-done.16, ...), custom_call_target="tpu_custom_call" | custom-call | tf_op jit(solution)/shard_map/pallas_call | solution.py:99
  112.6 5.7 %collective-permute-start.10 = (bf16[6,128,128]{2,1,0:T(8,128)(2,1)S(1)}, bf16[6,128,128]{2,1,0:T(8,128)(2,1)S(1)}, u32[]{:S(2)}, u32[]{:S(2)}) collective-permute-start(bf16[6,128,128]{2,1,0:T(8,128)(2,1)S(1)} %get-tuple-element.556), channel_id=1, source_target_pairs={{0,480},{16,496},{32,0},{48,16},{64,32},{80,48},{96,64},{112,80},{... | collective-permute-start | bytes 589832 | tf_op jit(solution)/shard_map/ppermute | solution.py:383
  118.4 1.9 %collective-permute-start.11 = (bf16[6,128,128]{2,1,0:T(8,128)(2,1)S(1)}, bf16[6,128,128]{2,1,0:T(8,128)(2,1)S(1)}, u32[]{:S(2)}, u32[]{:S(2)}) collective-permute-start(bf16[6,128,128]{2,1,0:T(8,128)(2,1)S(1)} %get-tuple-element.557), channel_id=1, source_target_pairs={{0,32},{16,48},{32,64},{48,80},{64,96},{80,112},{96,128},{112,144}... | collective-permute-start | bytes 589832 | tf_op jit(solution)/shard_map/ppermute | solution.py:383
  120.3 6.2 %collective-permute-start.12 = (bf16[6,128,128]{2,1,0:T(8,128)(2,1)S(1)}, bf16[6,128,128]{2,1,0:T(8,128)(2,1)S(1)}, u32[]{:S(2)}, u32[]{:S(2)}) collective-permute-start(bf16[6,128,128]{2,1,0:T(8,128)(2,1)S(1)} %get-tuple-element.558), channel_id=1, source_target_pairs={{0,448},{16,464},{32,96},{48,112},{64,0},{80,16},{96,160},{112,176... | collective-permute-start | bytes 589832 | tf_op jit(solution)/shard_map/ppermute | solution.py:383
  126.5 4.8 %collective-permute-done.12.refs_2_ = bf16[6,128,128]{2,1,0:T(8,128)(2,1)S(1)} collective-permute-done((bf16[6,128,128]{2,1,0:T(8,128)(2,1)S(1)}, bf16[6,128,128]{2,1,0:T(8,128)(2,1)S(1)}, u32[]{:S(2)}, u32[]{:S(2)}) %collective-permute-start.12) | collective-permute-done | bytes 196640 | tf_op jit(solution)/shard_map/ppermute | solution.py:383
  131.3 8.7 %all-to-all-start.3 = ((bf16[16,128,128]{2,1,0:T(8,128)(2,1)}), bf16[16,128,128]{2,1,0:T(8,128)(2,1)S(1)}, u32[]{:S(2)}, u32[]{:S(2)}) async-start(bf16[16,128,128]{2,1,0:T(8,128)(2,1)} %get-tuple-element.560), calls=%async_computation.3 | async-start | bytes 1048576 | tf_op jit(solution)/shard_map/all_to_all | solution.py:402
  140.0 1.8 %shard_map.131 = (f32[8,128,128]{2,1,0:T(8,128)}, bf16[8,128,128]{2,1,0:T(8,128)(2,1)}) custom-call(s32[18]{0:T(128)S(1)} %copy-done.14, s32[16]{0:T(128)S(1)} %copy-done.13, bf16[16,128,128]{2,1,0:T(8,128)(2,1)S(1)} %get-tuple-element.766.terms, bf16[6,128,128]{2,1,0:T(8,128)(2,1)S(1)} %collective-permute-done.10.refs_0_, ...), custom_call_target="tpu_custom_call" | custom-call | tf_op jit(solution)/shard_map/pallas_call | solution.py:99
  141.8 2.7 %collective-permute-start.13 = (bf16[8,128,128]{2,1,0:T(8,128)(2,1)}, bf16[8,128,128]{2,1,0:T(8,128)(2,1)S(1)}, u32[]{:S(2)}, u32[]{:S(2)}) collective-permute-start(bf16[8,128,128]{2,1,0:T(8,128)(2,1)} %get-tuple-element.567), channel_id=1, source_target_pairs={{0,16},{16,0},{32,48},{48,32},{64,80},{80,64},{96,112},{112,96},{1... | collective-permute-start | bytes 786440 | tf_op jit(solution)/shard_map/ppermute | solution.py:397
  145.1 1.3 iota_compare_fusion.2
  146.5 1.3 iota_compare_fusion
  147.8 1.3 collective-permute-done.13
  149.1 1.1 add_convert_fusion
  151.0 19.3 %all-to-all-done.3.shares = bf16[16,128,128]{2,1,0:T(8,128)(2,1)S(1)} async-done(((bf16[16,128,128]{2,1,0:T(8,128)(2,1)}), bf16[16,128,128]{2,1,0:T(8,128)(2,1)S(1)}, u32[]{:S(2)}, u32[]{:S(2)}) %all-to-all-start.3) | async-done | bytes 524320 | tf_op jit(solution)/shard_map/all_to_all | solution.py:402
  171.0 1.3 select_select_fusion
  (52 shorter events, 7.0 us)
Async XLA Ops:
  0.6 8.9 %copy-start = (bf16[32,16384]{1,0:T(8,128)(2,1)S(1)}, bf16[32,16384]{1,0:T(8,128)(2,1)}, u32[]{:S(2)}) copy-start(bf16[32,16384]{1,0:T(8,128)(2,1)} %param.15) | copy-start | bytes 3145732
  2.7 9.2 %collective-permute-start.6 = (bf16[8,128,128]{2,1,0:T(8,128)(2,1)S(1)}, bf16[8,128,128]{2,1,0:T(8,128)(2,1)}, u32[]{:S(2)}, u32[]{:S(2)}) collective-permute-start(bf16[8,128,128]{2,1,0:T(8,128)(2,1)S(1)} %reshape.104.own), channel_id=1, source_target_pairs={{0,16},{16,0},{32,48},{48,32},{64,80},{80,64},{96,112},{112,96},{1... | collective-permute-start | bytes 786440 | tf_op jit(solution)/shard_map/ppermute | solution.py:397
  5.9 0.7 copy-start.18
  10.2 1.7 %copy-start.14 = (s32[18]{0:T(128)S(1)}, s32[18]{0:T(128)}, u32[]{:S(2)}) copy-start(s32[18]{0:T(128)} %shard_map.122.sent) | copy-start | bytes 220
  13.9 49.2 %all-to-all-start = ((bf16[16,128,128]{2,1,0:T(8,128)(2,1)}), bf16[16,128,128]{2,1,0:T(8,128)(2,1)S(1)}, u32[]{:S(2)}, u32[]{:S(2)}) async-start(bf16[16,128,128]{2,1,0:T(8,128)(2,1)} %pad_maximum_fusion), calls=%async_computation | async-start | bytes 1048576 | tf_op jit(solution)/shard_map/all_to_all | solution.py:402
  27.8 26.5 %collective-permute-start.7 = (bf16[6,128,128]{2,1,0:T(8,128)(2,1)S(1)}, bf16[6,128,128]{2,1,0:T(8,128)(2,1)S(1)}, u32[]{:S(2)}, u32[]{:S(2)}) collective-permute-start(bf16[6,128,128]{2,1,0:T(8,128)(2,1)S(1)} %get-tuple-element.548), channel_id=1, source_target_pairs={{0,32},{16,48},{32,64},{48,80},{64,96},{80,112},{96,128},{112,144}... | collective-permute-start | bytes 589832 | tf_op jit(solution)/shard_map/ppermute | solution.py:383
  30.5 25.5 %collective-permute-start.8 = (bf16[6,128,128]{2,1,0:T(8,128)(2,1)S(1)}, bf16[6,128,128]{2,1,0:T(8,128)(2,1)S(1)}, u32[]{:S(2)}, u32[]{:S(2)}) collective-permute-start(bf16[6,128,128]{2,1,0:T(8,128)(2,1)S(1)} %get-tuple-element.550), channel_id=1, source_target_pairs={{0,480},{16,496},{32,0},{48,16},{64,32},{80,48},{96,64},{112,80},{... | collective-permute-start | bytes 589832 | tf_op jit(solution)/shard_map/ppermute | solution.py:383
  33.1 28.0 %collective-permute-start.9 = (bf16[6,128,128]{2,1,0:T(8,128)(2,1)S(1)}, bf16[6,128,128]{2,1,0:T(8,128)(2,1)S(1)}, u32[]{:S(2)}, u32[]{:S(2)}) collective-permute-start(bf16[6,128,128]{2,1,0:T(8,128)(2,1)S(1)} %get-tuple-element.551), channel_id=1, source_target_pairs={{0,64},{16,80},{32,480},{48,496},{64,128},{80,144},{96,32},{112,48... | collective-permute-start | bytes 589832 | tf_op jit(solution)/shard_map/ppermute | solution.py:383
  56.0 5.1 %copy-start.13 = (s32[16]{0:T(128)S(1)}, s32[16]{0:T(128)}, u32[]{:S(2)}) copy-start(s32[16]{0:T(128)} %shard_map.124.found) | copy-start | bytes 196
  63.0 0.9 copy-start.3
  63.1 1.0 copy-start.8
  63.1 0.9 copy-start.12
  64.0 21.8 %copy-start.1 = (f32[8,256,128]{2,1,0:T(8,128)S(1)}, f32[8,256,128]{2,1,0:T(8,128)}, u32[]{:S(2)}) copy-start(f32[8,256,128]{2,1,0:T(8,128)} %constant.224.clone.spectrum) | copy-start | bytes 3145732
  66.7 19.1 %copy-start.6 = (bf16[2,128,128]{2,1,0:T(8,128)(2,1)S(1)}, bf16[2,128,128]{2,1,0:T(8,128)(2,1)}, u32[]{:S(2)}) copy-start(bf16[2,128,128]{2,1,0:T(8,128)(2,1)} %constant.223.clone.x_bwd) | copy-start | bytes 196612
  66.7 19.1 %copy-start.7 = (bf16[2,128,128]{2,1,0:T(8,128)(2,1)S(1)}, bf16[2,128,128]{2,1,0:T(8,128)(2,1)}, u32[]{:S(2)}) copy-start(bf16[2,128,128]{2,1,0:T(8,128)(2,1)} %constant.222.clone.x_fwd) | copy-start | bytes 196612
  94.1 15.2 %copy-start.2 = (bf16[2,256,256]{2,1,0:T(8,128)(2,1)S(1)}, bf16[2,256,256]{2,1,0:T(8,128)(2,1)}, u32[]{:S(2)}) copy-start(bf16[2,256,256]{2,1,0:T(8,128)(2,1)} %constant.221.clone.y_bwd) | copy-start | bytes 786436
  94.1 15.1 %copy-start.5 = (bf16[2,128,128]{2,1,0:T(8,128)(2,1)S(1)}, bf16[2,128,128]{2,1,0:T(8,128)(2,1)}, u32[]{:S(2)}) copy-start(bf16[2,128,128]{2,1,0:T(8,128)(2,1)} %constant.219.clone.z_bwd) | copy-start | bytes 196612
  94.1 15.1 %copy-start.16 = (bf16[16,128,128]{2,1,0:T(8,128)(2,1)S(1)}, bf16[16,128,128]{2,1,0:T(8,128)(2,1)}, u32[]{:S(2)}) copy-start(bf16[16,128,128]{2,1,0:T(8,128)(2,1)} %get-tuple-element.553.sources) | copy-start | bytes 1572868
  112.6 13.9 %collective-permute-start.10 = (bf16[6,128,128]{2,1,0:T(8,128)(2,1)S(1)}, bf16[6,128,128]{2,1,0:T(8,128)(2,1)S(1)}, u32[]{:S(2)}, u32[]{:S(2)}) collective-permute-start(bf16[6,128,128]{2,1,0:T(8,128)(2,1)S(1)} %get-tuple-element.556), channel_id=1, source_target_pairs={{0,480},{16,496},{32,0},{48,16},{64,32},{80,48},{96,64},{112,80},{... | collective-permute-start | bytes 589832 | tf_op jit(solution)/shard_map/ppermute | solution.py:383
  118.4 8.1 %collective-permute-start.11 = (bf16[6,128,128]{2,1,0:T(8,128)(2,1)S(1)}, bf16[6,128,128]{2,1,0:T(8,128)(2,1)S(1)}, u32[]{:S(2)}, u32[]{:S(2)}) collective-permute-start(bf16[6,128,128]{2,1,0:T(8,128)(2,1)S(1)} %get-tuple-element.557), channel_id=1, source_target_pairs={{0,32},{16,48},{32,64},{48,80},{64,96},{80,112},{96,128},{112,144}... | collective-permute-start | bytes 589832 | tf_op jit(solution)/shard_map/ppermute | solution.py:383
  120.3 11.0 %collective-permute-start.12 = (bf16[6,128,128]{2,1,0:T(8,128)(2,1)S(1)}, bf16[6,128,128]{2,1,0:T(8,128)(2,1)S(1)}, u32[]{:S(2)}, u32[]{:S(2)}) collective-permute-start(bf16[6,128,128]{2,1,0:T(8,128)(2,1)S(1)} %get-tuple-element.558), channel_id=1, source_target_pairs={{0,448},{16,464},{32,96},{48,112},{64,0},{80,16},{96,160},{112,176... | collective-permute-start | bytes 589832 | tf_op jit(solution)/shard_map/ppermute | solution.py:383
  131.3 39.0 %all-to-all-start.3 = ((bf16[16,128,128]{2,1,0:T(8,128)(2,1)}), bf16[16,128,128]{2,1,0:T(8,128)(2,1)S(1)}, u32[]{:S(2)}, u32[]{:S(2)}) async-start(bf16[16,128,128]{2,1,0:T(8,128)(2,1)} %get-tuple-element.560), calls=%async_computation.3 | async-start | bytes 1048576 | tf_op jit(solution)/shard_map/all_to_all | solution.py:402
  141.8 7.3 %collective-permute-start.13 = (bf16[8,128,128]{2,1,0:T(8,128)(2,1)}, bf16[8,128,128]{2,1,0:T(8,128)(2,1)S(1)}, u32[]{:S(2)}, u32[]{:S(2)}) collective-permute-start(bf16[8,128,128]{2,1,0:T(8,128)(2,1)} %get-tuple-element.567), channel_id=1, source_target_pairs={{0,16},{16,0},{32,48},{48,32},{64,80},{80,64},{96,112},{112,96},{1... | collective-permute-start | bytes 786440 | tf_op jit(solution)/shard_map/ppermute | solution.py:397
  150.2 20.1 %copy-start.15 = (s32[2,2]{1,0:T(2,128)S(1)}, s32[2,2]{1,0:T(2,128)}, u32[]{:S(2)}) copy-start(s32[2,2]{1,0:T(2,128)} %pair_tgt.1) | copy-start | bytes 52

commit v10 on v9

--- a/solution.py
+++ b/solution.py
@@ -397,9 +397,15 @@
     return lax.ppermute(value, "band", [(i, i ^ 1) for i in range(32)])
 
 
-def along_ring(value):
-    groups = [[8 * quad + member for quad in range(4)] for member in range(8)]
-    return lax.all_to_all(value, "band", 0, 0, axis_index_groups=groups, tiled=True)
+RING_GROUPS = [[8 * quad + member for quad in range(4)] for member in range(8)]
+
+
+def to_relays(value):
+    return lax.all_gather(value, "band", axis_index_groups=RING_GROUPS, tiled=True)
+
+
+def from_relays(value):
+    return lax.all_to_all(value, "band", 0, 0, axis_index_groups=RING_GROUPS, tiled=True)
 
 
 def rounds_of(pair_src):
@@ -430,7 +436,8 @@
 
     own, ids = lax.optimization_barrier((sources.reshape(8, ROW, ROW), pair_tgt.reshape(4)))
     other = across(own)
-    wanted = targets[ids].reshape(4, ROW, ROW)
+    wanted = to_relays(targets[ids].reshape(4, ROW, ROW))
+    other, wanted = lax.optimization_barrier((other, wanted))
 
     def pack_rows_in(sent):
         return vmem_call(pack_rows_kernel, packets, (sent, own, other), scalars=1)
@@ -443,9 +450,7 @@
         return deliver(hand_over(pack_rows_in(sent_in(turn)), 1), found_in(turn), (before,))
 
     sent, found = sent_in(0), found_in(0)
-    packed, found, wanted = lax.optimization_barrier((pack_rows_in(sent), found, wanted))
-    wanted = along_ring(jnp.concatenate([wanted] * 4, axis=0))
-    near = hand_over(packed, 1)
+    near = hand_over(pack_rows_in(sent), 1)
     first, wants = lax.optimization_barrier((near[0], pair_src))
     rounds = rounds_of(wants)
     rows = lax.fori_loop(1, rounds, deliver_in, deliver((first,) + near[1:], found, ()))
@@ -488,7 +493,7 @@
 
     near = give_back(found)
     near, shares = lax.optimization_barrier((near, shares))
-    shares = along_ring(shares)
+    shares = from_relays(shares)
     mine, partner = lax.fori_loop(1, rounds, collect_in, collect(sent, found, near, ()))
     owned = (mine + across(partner).astype(F32)).astype(BF16).reshape(sources.shape)
 

time: 173 us -> 167 us (0.965)
  the two profiles are of different devices: /device:TPU:33 before, /device:TPU:38 now
where the time goes in v10:
time: 167 us; the launch traced here: 166 us
  blocking collectives  64.8 us (39%)
  starting transfers between devices  37.4 us (22%)
  waiting for transfers between devices  28.6 us (17%)
  Pallas kernels  21.6 us (13%)
  other arithmetic  6.46 us (4%)
  local copies, waits for them, and re-layouts  5.5 us (3%)
    all_gather x1, blocking collectives, to_relays(): lax.all_gather(value, 'band', axis_index_groups=RING_GROUPS, tiled=True)  32.8 us
    ppermute x6, starting transfers between devices, hand_over(): lax.ppermute(packet, 'band', [(2 * z + x, 2 * ((z + sign * move(z)) % RIN...  23.2 us
    pallas_call x8, Pallas kernels, vmem_call(): pl.pallas_call(kernel, out_shape=outs, in_specs=[smem] * scalars + [whole...  18.7 us
    all_to_all x1, blocking collectives, per_device(): slabs = lax.all_to_all(spectra, 'dom', 0, 0, tiled=True)  16.9 us
    all_to_all x1, blocking collectives, per_device(): back = lax.all_to_all(solved, 'dom', 0, 0, tiled=True)  15.1 us
    all_to_all x1, waiting for transfers between devices, from_relays(): lax.all_to_all(value, 'band', 0, 0, axis_index_groups=RING_GROUPS, tiled=...  14.5 us
    ppermute x6, waiting for transfers between devices, hand_over(): lax.ppermute(packet, 'band', [(2 * z + x, 2 * ((z + sign * move(z)) % RIN...  10.1 us
    all_to_all x1, starting transfers between devices, from_relays(): lax.all_to_all(value, 'band', 0, 0, axis_index_groups=RING_GROUPS, tiled=...  9.52 us
  transfers between devices with their start and end apart: 9, of which 5 were waited for; matrix products, arithmetic and copies ran while one was open for 4% of the time, Pallas kernels for 3%

profile of v10, /device:TPU:38, one launch (start us, length us, event | category | flops | bytes accessed | tf_op | source)
XLA Modules:
  0.0 166.0 jit_solution(14154621406983406490)
XLA Ops:
  0.6 0.8 reshape.105
  1.5 1.2 reshape.104.own
  2.7 2.7 %collective-permute-start.6 = (bf16[8,128,128]{2,1,0:T(8,128)(2,1)S(1)}, bf16[8,128,128]{2,1,0:T(8,128)(2,1)}, u32[]{:S(2)}, u32[]{:S(2)}) collective-permute-start(bf16[8,128,128]{2,1,0:T(8,128)(2,1)S(1)} %reshape.104.own), channel_id=1, source_target_pairs={{0,16},{16,0},{32,48},{48,32},{64,80},{80,64},{96,112},{112,96},{1... | collective-permute-start | bytes 786440 | tf_op jit(solution)/shard_map/ppermute | solution.py:397
  6.2 1.4 shard_map.122.found
  7.6 1.5 shard_map.123.sent
  9.8 32.8 %all_gather.3.wanted = bf16[16,128,128]{2,1,0:T(8,128)(2,1)S(1)} all-gather(bf16[4,128,128]{2,1,0:T(8,128)(2,1)S(1)} %bitcast.37), channel_id=1, replica_groups={{0,128,256,384},{16,144,272,400},{32,160,288,416},{48,176,304,432},{64,..., dimensions={0}, use_global_device_ids=true | all-gather | bytes 655360 | tf_op jit(solution)/shard_map/all_gather | solution.py:404
  42.6 1.1 shard_map.124
  43.7 3.0 %collective-permute-start.7 = (bf16[6,128,128]{2,1,0:T(8,128)(2,1)S(1)}, bf16[6,128,128]{2,1,0:T(8,128)(2,1)S(1)}, u32[]{:S(2)}, u32[]{:S(2)}) collective-permute-start(bf16[6,128,128]{2,1,0:T(8,128)(2,1)S(1)} %get-tuple-element.542), channel_id=1, source_target_pairs={{0,32},{16,48},{32,64},{48,80},{64,96},{80,112},{96,128},{112,144}... | collective-permute-start | bytes 589832 | tf_op jit(solution)/shard_map/ppermute | solution.py:383
  46.8 2.9 %collective-permute-start.8 = (bf16[6,128,128]{2,1,0:T(8,128)(2,1)S(1)}, bf16[6,128,128]{2,1,0:T(8,128)(2,1)S(1)}, u32[]{:S(2)}, u32[]{:S(2)}) collective-permute-start(bf16[6,128,128]{2,1,0:T(8,128)(2,1)S(1)} %get-tuple-element.544), channel_id=1, source_target_pairs={{0,480},{16,496},{32,0},{48,16},{64,32},{80,48},{96,64},{112,80},{... | collective-permute-start | bytes 589832 | tf_op jit(solution)/shard_map/ppermute | solution.py:383
  49.6 4.4 %collective-permute-start.9 = (bf16[6,128,128]{2,1,0:T(8,128)(2,1)S(1)}, bf16[6,128,128]{2,1,0:T(8,128)(2,1)S(1)}, u32[]{:S(2)}, u32[]{:S(2)}) collective-permute-start(bf16[6,128,128]{2,1,0:T(8,128)(2,1)S(1)} %get-tuple-element.545), channel_id=1, source_target_pairs={{0,64},{16,80},{32,480},{48,496},{64,128},{80,144},{96,32},{112,48... | collective-permute-start | bytes 589832 | tf_op jit(solution)/shard_map/ppermute | solution.py:383
  55.8 2.3 %collective-permute-done.9.refs_2_ = bf16[6,128,128]{2,1,0:T(8,128)(2,1)S(1)} collective-permute-done((bf16[6,128,128]{2,1,0:T(8,128)(2,1)S(1)}, bf16[6,128,128]{2,1,0:T(8,128)(2,1)S(1)}, u32[]{:S(2)}, u32[]{:S(2)}) %collective-permute-start.9) | collective-permute-done | bytes 196640 | tf_op jit(solution)/shard_map/ppermute | solution.py:383
  58.1 1.9 %shard_map.125 = bf16[16,128,128]{2,1,0:T(8,128)(2,1)} custom-call(s32[16]{0:T(128)S(1)} %copy-done.13, bf16[8,128,128]{2,1,0:T(8,128)(2,1)S(1)} %reshape.104.own, bf16[8,128,128]{2,1,0:T(8,128)(2,1)} %collective-permute-done.6.other, bf16[6,128,128]{2,1,0:T(8,128)(2,1)S(1)} %collective-permute-done.7.refs_0_, ...), custom_call_target="tpu_custom_call" | custom-call | tf_op jit(solution)/shard_map/pallas_call | solution.py:99
  60.0 0.9 copy-done.3
  61.0 2.1 %shard_map.126 = bf16[16,128,128]{2,1,0:T(8,128)(2,1)S(1)} custom-call(s32[3]{0:T(128)S(1)} %copy-done.12, s32[2,64]{1,0:T(2,128)S(1)} %get-tuple-element.807, bf16[16,128,128]{2,1,0:T(8,128)(2,1)} %get-tuple-element.547.sources, bf16[16,128,128]{2,1,0:T(8,128)(2,1)S(1)} %all_gather.3.wanted, bf16[2,128,128]{2,1,0:T(8,128)(2,1)S(1)} %copy-done.8, ...), custom_call_target="tpu_custom_call" | custom-call | tf_op jit(solution)/shard_map/pallas_call | solution.py:99
  63.1 16.9 %all_to_all.15.slabs = bf16[16,128,128]{2,1,0:T(8,128)(2,1)S(1)} all-to-all(bf16[16,128,128]{2,1,0:T(8,128)(2,1)S(1)} %shard_map.126), channel_id=1, replica_groups=mesh['band'=32,'dom'=16] {'dom'}, dimensions={0} | all-to-all | bytes 1048576 | tf_op jit(solution)/shard_map/all_to_all | solution.py:465
  80.0 8.2 %shard_map.127 = bf16[16,128,128]{2,1,0:T(8,128)(2,1)S(1)} custom-call(bf16[16,128,128]{2,1,0:T(8,128)(2,1)S(1)} %all_to_all.15.slabs, f32[8,256,128]{2,1,0:T(8,128)S(1)} %copy-done.1, bf16[2,128,128]{2,1,0:T(8,128)(2,1)S(1)} %copy-done.7, bf16[2,128,128]{2,1,0:T(8,128)(2,1)S(1)} %copy-done.6), custom_call_target="tpu_custom_call" | custom-call | tf_op jit(solution)/shard_map/pallas_call | solution.py:99
  88.2 15.1 %all_to_all.16.spectra = bf16[16,128,128]{2,1,0:T(8,128)(2,1)S(1)} all-to-all(bf16[16,128,128]{2,1,0:T(8,128)(2,1)S(1)} %shard_map.127), channel_id=1, replica_groups=mesh['band'=32,'dom'=16] {'dom'}, dimensions={0} | all-to-all | bytes 1048576 | tf_op jit(solution)/shard_map/all_to_all | solution.py:472
  103.4 2.2 %shard_map.128 = (bf16[16,128,128]{2,1,0:T(8,128)(2,1)S(1)}, bf16[16,128,128]{2,1,0:T(8,128)(2,1)}) custom-call(s32[3]{0:T(128)S(1)} %copy-done.12, s32[2,64]{1,0:T(2,128)S(1)} %get-tuple-element.807, bf16[16,128,128]{2,1,0:T(8,128)(2,1)S(1)} %all_to_all.16.spectra, bf16[16,128,128]{2,1,0:T(8,128)(2,1)S(1)} %copy-done.16, ...), custom_call_target="tpu_custom_call" | custom-call | tf_op jit(solution)/shard_map/pallas_call | solution.py:99
  106.2 6.1 %collective-permute-start.10 = (bf16[6,128,128]{2,1,0:T(8,128)(2,1)S(1)}, bf16[6,128,128]{2,1,0:T(8,128)(2,1)S(1)}, u32[]{:S(2)}, u32[]{:S(2)}) collective-permute-start(bf16[6,128,128]{2,1,0:T(8,128)(2,1)S(1)} %get-tuple-element.550), channel_id=1, source_target_pairs={{0,480},{16,496},{32,0},{48,16},{64,32},{80,48},{96,64},{112,80},{... | collective-permute-start | bytes 589832 | tf_op jit(solution)/shard_map/ppermute | solution.py:383
  112.4 1.9 %collective-permute-start.11 = (bf16[6,128,128]{2,1,0:T(8,128)(2,1)S(1)}, bf16[6,128,128]{2,1,0:T(8,128)(2,1)S(1)}, u32[]{:S(2)}, u32[]{:S(2)}) collective-permute-start(bf16[6,128,128]{2,1,0:T(8,128)(2,1)S(1)} %get-tuple-element.551), channel_id=1, source_target_pairs={{0,32},{16,48},{32,64},{48,80},{64,96},{80,112},{96,128},{112,144}... | collective-permute-start | bytes 589832 | tf_op jit(solution)/shard_map/ppermute | solution.py:383
  114.3 4.9 %collective-permute-start.12 = (bf16[6,128,128]{2,1,0:T(8,128)(2,1)S(1)}, bf16[6,128,128]{2,1,0:T(8,128)(2,1)S(1)}, u32[]{:S(2)}, u32[]{:S(2)}) collective-permute-start(bf16[6,128,128]{2,1,0:T(8,128)(2,1)S(1)} %get-tuple-element.552), channel_id=1, source_target_pairs={{0,448},{16,464},{32,96},{48,112},{64,0},{80,16},{96,160},{112,176... | collective-permute-start | bytes 589832 | tf_op jit(solution)/shard_map/ppermute | solution.py:383
  119.3 1.6 collective-permute-done.11.refs_1_
  120.9 6.1 %collective-permute-done.12.refs_2_ = bf16[6,128,128]{2,1,0:T(8,128)(2,1)S(1)} collective-permute-done((bf16[6,128,128]{2,1,0:T(8,128)(2,1)S(1)}, bf16[6,128,128]{2,1,0:T(8,128)(2,1)S(1)}, u32[]{:S(2)}, u32[]{:S(2)}) %collective-permute-start.12) | collective-permute-done | bytes 196640 | tf_op jit(solution)/shard_map/ppermute | solution.py:383
  127.0 9.5 %all-to-all-start.2 = ((bf16[16,128,128]{2,1,0:T(8,128)(2,1)}), bf16[16,128,128]{2,1,0:T(8,128)(2,1)S(1)}, u32[]{:S(2)}, u32[]{:S(2)}) async-start(bf16[16,128,128]{2,1,0:T(8,128)(2,1)} %get-tuple-element.554), calls=%async_computation.2 | async-start | bytes 1048576 | tf_op jit(solution)/shard_map/all_to_all | solution.py:408
  136.5 1.8 %shard_map.131 = (f32[8,128,128]{2,1,0:T(8,128)}, bf16[8,128,128]{2,1,0:T(8,128)(2,1)}) custom-call(s32[18]{0:T(128)S(1)} %copy-done.14, s32[16]{0:T(128)S(1)} %copy-done.13, bf16[16,128,128]{2,1,0:T(8,128)(2,1)S(1)} %get-tuple-element.760.terms, bf16[6,128,128]{2,1,0:T(8,128)(2,1)S(1)} %collective-permute-done.10.refs_0_, ...), custom_call_target="tpu_custom_call" | custom-call | tf_op jit(solution)/shard_map/pallas_call | solution.py:99
  138.3 1.9 %collective-permute-start.13 = (bf16[8,128,128]{2,1,0:T(8,128)(2,1)}, bf16[8,128,128]{2,1,0:T(8,128)(2,1)S(1)}, u32[]{:S(2)}, u32[]{:S(2)}) collective-permute-start(bf16[8,128,128]{2,1,0:T(8,128)(2,1)} %get-tuple-element.561), channel_id=1, source_target_pairs={{0,16},{16,0},{32,48},{48,32},{64,80},{80,64},{96,112},{112,96},{1... | collective-permute-start | bytes 786440 | tf_op jit(solution)/shard_map/ppermute | solution.py:397
  140.9 1.3 iota_compare_fusion.2
  142.2 1.3 iota_compare_fusion
  143.5 4.1 %collective-permute-done.13 = bf16[8,128,128]{2,1,0:T(8,128)(2,1)S(1)} collective-permute-done((bf16[8,128,128]{2,1,0:T(8,128)(2,1)}, bf16[8,128,128]{2,1,0:T(8,128)(2,1)S(1)}, u32[]{:S(2)}, u32[]{:S(2)}) %collective-permute-start.13) | collective-permute-done | bytes 262176 | tf_op jit(solution)/shard_map/ppermute | solution.py:397
  147.6 1.1 add_convert_fusion
  149.5 14.5 %all-to-all-done.2.shares = bf16[16,128,128]{2,1,0:T(8,128)(2,1)S(1)} async-done(((bf16[16,128,128]{2,1,0:T(8,128)(2,1)}), bf16[16,128,128]{2,1,0:T(8,128)(2,1)S(1)}, u32[]{:S(2)}, u32[]{:S(2)}) %all-to-all-start.2) | async-done | bytes 524320 | tf_op jit(solution)/shard_map/all_to_all | solution.py:408
  164.7 1.3 select_select_fusion
  (50 shorter events, 5.3 us)
Async XLA Ops:
  0.6 8.5 %copy-start = (bf16[32,16384]{1,0:T(8,128)(2,1)S(1)}, bf16[32,16384]{1,0:T(8,128)(2,1)}, u32[]{:S(2)}) copy-start(bf16[32,16384]{1,0:T(8,128)(2,1)} %param.15) | copy-start | bytes 3145732
  2.7 39.9 %collective-permute-start.6 = (bf16[8,128,128]{2,1,0:T(8,128)(2,1)S(1)}, bf16[8,128,128]{2,1,0:T(8,128)(2,1)}, u32[]{:S(2)}, u32[]{:S(2)}) collective-permute-start(bf16[8,128,128]{2,1,0:T(8,128)(2,1)S(1)} %reshape.104.own), channel_id=1, source_target_pairs={{0,16},{16,0},{32,48},{48,32},{64,80},{80,64},{96,112},{112,96},{1... | collective-permute-start | bytes 786440 | tf_op jit(solution)/shard_map/ppermute | solution.py:397
  5.5 0.7 copy-start.18
  9.8 32.8 %copy-start.14 = (s32[18]{0:T(128)S(1)}, s32[18]{0:T(128)}, u32[]{:S(2)}) copy-start(s32[18]{0:T(128)} %shard_map.123.sent) | copy-start | bytes 220
  43.7 10.3 %collective-permute-start.7 = (bf16[6,128,128]{2,1,0:T(8,128)(2,1)S(1)}, bf16[6,128,128]{2,1,0:T(8,128)(2,1)S(1)}, u32[]{:S(2)}, u32[]{:S(2)}) collective-permute-start(bf16[6,128,128]{2,1,0:T(8,128)(2,1)S(1)} %get-tuple-element.542), channel_id=1, source_target_pairs={{0,32},{16,48},{32,64},{48,80},{64,96},{80,112},{96,128},{112,144}... | collective-permute-start | bytes 589832 | tf_op jit(solution)/shard_map/ppermute | solution.py:383
  46.8 9.0 %collective-permute-start.8 = (bf16[6,128,128]{2,1,0:T(8,128)(2,1)S(1)}, bf16[6,128,128]{2,1,0:T(8,128)(2,1)S(1)}, u32[]{:S(2)}, u32[]{:S(2)}) collective-permute-start(bf16[6,128,128]{2,1,0:T(8,128)(2,1)S(1)} %get-tuple-element.544), channel_id=1, source_target_pairs={{0,480},{16,496},{32,0},{48,16},{64,32},{80,48},{96,64},{112,80},{... | collective-permute-start | bytes 589832 | tf_op jit(solution)/shard_map/ppermute | solution.py:383
  49.6 8.5 %collective-permute-start.9 = (bf16[6,128,128]{2,1,0:T(8,128)(2,1)S(1)}, bf16[6,128,128]{2,1,0:T(8,128)(2,1)S(1)}, u32[]{:S(2)}, u32[]{:S(2)}) collective-permute-start(bf16[6,128,128]{2,1,0:T(8,128)(2,1)S(1)} %get-tuple-element.545), channel_id=1, source_target_pairs={{0,64},{16,80},{32,480},{48,496},{64,128},{80,144},{96,32},{112,48... | collective-permute-start | bytes 589832 | tf_op jit(solution)/shard_map/ppermute | solution.py:383
  55.7 2.4 %copy-start.13 = (s32[16]{0:T(128)S(1)}, s32[16]{0:T(128)}, u32[]{:S(2)}) copy-start(s32[16]{0:T(128)} %shard_map.122.found) | copy-start | bytes 196
  60.0 0.9 copy-start.3
  60.0 1.0 copy-start.8
  60.0 0.9 copy-start.12
  61.0 19.0 %copy-start.1 = (f32[8,256,128]{2,1,0:T(8,128)S(1)}, f32[8,256,128]{2,1,0:T(8,128)}, u32[]{:S(2)}) copy-start(f32[8,256,128]{2,1,0:T(8,128)} %constant.224.clone.spectrum) | copy-start | bytes 3145732
  63.0 16.9 %copy-start.6 = (bf16[2,128,128]{2,1,0:T(8,128)(2,1)S(1)}, bf16[2,128,128]{2,1,0:T(8,128)(2,1)}, u32[]{:S(2)}) copy-start(bf16[2,128,128]{2,1,0:T(8,128)(2,1)} %constant.223.clone.x_bwd) | copy-start | bytes 196612
  63.1 16.9 %copy-start.7 = (bf16[2,128,128]{2,1,0:T(8,128)(2,1)S(1)}, bf16[2,128,128]{2,1,0:T(8,128)(2,1)}, u32[]{:S(2)}) copy-start(bf16[2,128,128]{2,1,0:T(8,128)(2,1)} %constant.222.clone.x_fwd) | copy-start | bytes 196612
  88.2 15.2 %copy-start.2 = (bf16[2,256,256]{2,1,0:T(8,128)(2,1)S(1)}, bf16[2,256,256]{2,1,0:T(8,128)(2,1)}, u32[]{:S(2)}) copy-start(bf16[2,256,256]{2,1,0:T(8,128)(2,1)} %constant.221.clone.y_bwd) | copy-start | bytes 786436
  88.2 15.2 %copy-start.5 = (bf16[2,128,128]{2,1,0:T(8,128)(2,1)S(1)}, bf16[2,128,128]{2,1,0:T(8,128)(2,1)}, u32[]{:S(2)}) copy-start(bf16[2,128,128]{2,1,0:T(8,128)(2,1)} %constant.219.clone.z_bwd) | copy-start | bytes 196612
  88.2 15.1 %copy-start.16 = (bf16[16,128,128]{2,1,0:T(8,128)(2,1)S(1)}, bf16[16,128,128]{2,1,0:T(8,128)(2,1)}, u32[]{:S(2)}) copy-start(bf16[16,128,128]{2,1,0:T(8,128)(2,1)} %get-tuple-element.547.sources) | copy-start | bytes 1572868
  106.2 13.0 %collective-permute-start.10 = (bf16[6,128,128]{2,1,0:T(8,128)(2,1)S(1)}, bf16[6,128,128]{2,1,0:T(8,128)(2,1)S(1)}, u32[]{:S(2)}, u32[]{:S(2)}) collective-permute-start(bf16[6,128,128]{2,1,0:T(8,128)(2,1)S(1)} %get-tuple-element.550), channel_id=1, source_target_pairs={{0,480},{16,496},{32,0},{48,16},{64,32},{80,48},{96,64},{112,80},{... | collective-permute-start | bytes 589832 | tf_op jit(solution)/shard_map/ppermute | solution.py:383
  112.4 8.5 %collective-permute-start.11 = (bf16[6,128,128]{2,1,0:T(8,128)(2,1)S(1)}, bf16[6,128,128]{2,1,0:T(8,128)(2,1)S(1)}, u32[]{:S(2)}, u32[]{:S(2)}) collective-permute-start(bf16[6,128,128]{2,1,0:T(8,128)(2,1)S(1)} %get-tuple-element.551), channel_id=1, source_target_pairs={{0,32},{16,48},{32,64},{48,80},{64,96},{80,112},{96,128},{112,144}... | collective-permute-start | bytes 589832 | tf_op jit(solution)/shard_map/ppermute | solution.py:383
  114.3 12.7 %collective-permute-start.12 = (bf16[6,128,128]{2,1,0:T(8,128)(2,1)S(1)}, bf16[6,128,128]{2,1,0:T(8,128)(2,1)S(1)}, u32[]{:S(2)}, u32[]{:S(2)}) collective-permute-start(bf16[6,128,128]{2,1,0:T(8,128)(2,1)S(1)} %get-tuple-element.552), channel_id=1, source_target_pairs={{0,448},{16,464},{32,96},{48,112},{64,0},{80,16},{96,160},{112,176... | collective-permute-start | bytes 589832 | tf_op jit(solution)/shard_map/ppermute | solution.py:383
  127.0 37.0 %all-to-all-start.2 = ((bf16[16,128,128]{2,1,0:T(8,128)(2,1)}), bf16[16,128,128]{2,1,0:T(8,128)(2,1)S(1)}, u32[]{:S(2)}, u32[]{:S(2)}) async-start(bf16[16,128,128]{2,1,0:T(8,128)(2,1)} %get-tuple-element.554), calls=%async_computation.2 | async-start | bytes 1048576 | tf_op jit(solution)/shard_map/all_to_all | solution.py:408
  138.3 9.3 %collective-permute-start.13 = (bf16[8,128,128]{2,1,0:T(8,128)(2,1)}, bf16[8,128,128]{2,1,0:T(8,128)(2,1)S(1)}, u32[]{:S(2)}, u32[]{:S(2)}) collective-permute-start(bf16[8,128,128]{2,1,0:T(8,128)(2,1)} %get-tuple-element.561), channel_id=1, source_target_pairs={{0,16},{16,0},{32,48},{48,32},{64,80},{80,64},{96,112},{112,96},{1... | collective-permute-start | bytes 786440 | tf_op jit(solution)/shard_map/ppermute | solution.py:397
  148.7 15.3 %copy-start.15 = (s32[2,2]{1,0:T(2,128)S(1)}, s32[2,2]{1,0:T(2,128)}, u32[]{:S(2)}) copy-start(s32[2,2]{1,0:T(2,128)} %pair_tgt.1) | copy-start | bytes 52

commit v11 on v9

--- a/solution.py
+++ b/solution.py
@@ -431,6 +431,7 @@
     own, ids = lax.optimization_barrier((sources.reshape(8, ROW, ROW), pair_tgt.reshape(4)))
     other = across(own)
     wanted = targets[ids].reshape(4, ROW, ROW)
+    wanted = along_ring(jnp.concatenate([wanted] * 4, axis=0))
 
     def pack_rows_in(sent):
         return vmem_call(pack_rows_kernel, packets, (sent, own, other), scalars=1)
@@ -443,9 +444,7 @@
         return deliver(hand_over(pack_rows_in(sent_in(turn)), 1), found_in(turn), (before,))
 
     sent, found = sent_in(0), found_in(0)
-    packed, found, wanted = lax.optimization_barrier((pack_rows_in(sent), found, wanted))
-    wanted = along_ring(jnp.concatenate([wanted] * 4, axis=0))
-    near = hand_over(packed, 1)
+    near = hand_over(pack_rows_in(sent), 1)
     first, wants = lax.optimization_barrier((near[0], pair_src))
     rounds = rounds_of(wants)
     rows = lax.fori_loop(1, rounds, deliver_in, deliver((first,) + near[1:], found, ()))
@@ -487,7 +486,6 @@
         return collect(sent_in(turn), found, give_back(found), tuple(before))
 
     near = give_back(found)
-    near, shares = lax.optimization_barrier((near, shares))
     shares = along_ring(shares)
     mine, partner = lax.fori_loop(1, rounds, collect_in, collect(sent, found, near, ()))
     owned = (mine + across(partner).astype(F32)).astype(BF16).reshape(sources.shape)

time: 173 us -> 165 us (0.954)
  the two profiles are of different devices: /device:TPU:33 before, /device:TPU:64 now
where the time goes in v11:
time: 165 us; the launch traced here: 164 us
  starting transfers between devices  51.8 us (31%)
  waiting for transfers between devices  38.8 us (24%)
  blocking collectives  34.5 us (21%)
  Pallas kernels  24 us (15%)
  other arithmetic  7.26 us (4%)
  local copies, waits for them, and re-layouts  6.14 us (4%)
    ppermute x6, waiting for transfers between devices, hand_over(): lax.ppermute(packet, 'band', [(2 * z + x, 2 * ((z + sign * move(z)) % RIN...  31.6 us
    ppermute x6, starting transfers between devices, hand_over(): lax.ppermute(packet, 'band', [(2 * z + x, 2 * ((z + sign * move(z)) % RIN...  25.2 us
    pallas_call x8, Pallas kernels, vmem_call(): pl.pallas_call(kernel, out_shape=outs, in_specs=[smem] * scalars + [whole...  21.2 us
    all_to_all x2, starting transfers between devices, along_ring(): lax.all_to_all(value, 'band', 0, 0, axis_index_groups=groups, tiled=True)  20.5 us
    all_to_all x1, blocking collectives, per_device(): slabs = lax.all_to_all(spectra, 'dom', 0, 0, tiled=True)  19.3 us
    all_to_all x1, blocking collectives, per_device(): back = lax.all_to_all(solved, 'dom', 0, 0, tiled=True)  15.1 us
    ppermute x2, waiting for transfers between devices, across(): return lax.ppermute(value, 'band', [(i, i ^ 1) for i in range(32)])  7.17 us
    ppermute x2, starting transfers between devices, across(): return lax.ppermute(value, 'band', [(i, i ^ 1) for i in range(32)])  6.11 us
  transfers between devices with their start and end apart: 10, of which 8 were waited for; matrix products, arithmetic and copies ran while one was open for 4% of the time, Pallas kernels for 5%

profile of v11, /device:TPU:64, one launch (start us, length us, event | category | flops | bytes accessed | tf_op | source)
XLA Modules:
  0.0 164.1 jit_solution(13975467421530185792)
XLA Ops:
  1.5 1.2 reshape.104.own
  4.3 13.3 %all-to-all-start = ((bf16[16,128,128]{2,1,0:T(8,128)(2,1)}), bf16[16,128,128]{2,1,0:T(8,128)(2,1)S(1)}, u32[]{:S(2)}, u32[]{:S(2)}) async-start(bf16[16,128,128]{2,1,0:T(8,128)(2,1)} %pad_maximum_fusion), calls=%async_computation | async-start | bytes 1048576 | tf_op jit(solution)/shard_map/all_to_all | solution.py:402
  17.6 3.4 %collective-permute-start.6 = (bf16[8,128,128]{2,1,0:T(8,128)(2,1)S(1)}, bf16[8,128,128]{2,1,0:T(8,128)(2,1)}, u32[]{:S(2)}, u32[]{:S(2)}) collective-permute-start(bf16[8,128,128]{2,1,0:T(8,128)(2,1)S(1)} %reshape.104.own), channel_id=1, source_target_pairs={{0,16},{16,0},{32,48},{48,32},{64,80},{80,64},{96,112},{112,96},{1... | collective-permute-start | bytes 786440 | tf_op jit(solution)/shard_map/ppermute | solution.py:397
  21.7 1.4 shard_map.122.found
  23.1 1.5 shard_map.123.sent
  24.6 2.8 %collective-permute-done.6.other = bf16[8,128,128]{2,1,0:T(8,128)(2,1)} collective-permute-done((bf16[8,128,128]{2,1,0:T(8,128)(2,1)S(1)}, bf16[8,128,128]{2,1,0:T(8,128)(2,1)}, u32[]{:S(2)}, u32[]{:S(2)}) %collective-permute-start.6) | collective-permute-done | bytes 262176 | tf_op jit(solution)/shard_map/ppermute | solution.py:397
  28.0 1.1 shard_map.124
  29.2 3.0 %collective-permute-start.7 = (bf16[6,128,128]{2,1,0:T(8,128)(2,1)S(1)}, bf16[6,128,128]{2,1,0:T(8,128)(2,1)S(1)}, u32[]{:S(2)}, u32[]{:S(2)}) collective-permute-start(bf16[6,128,128]{2,1,0:T(8,128)(2,1)S(1)} %get-tuple-element.535), channel_id=1, source_target_pairs={{0,32},{16,48},{32,64},{48,80},{64,96},{80,112},{96,128},{112,144}... | collective-permute-start | bytes 589832 | tf_op jit(solution)/shard_map/ppermute | solution.py:383
  32.2 2.9 %collective-permute-start.8 = (bf16[6,128,128]{2,1,0:T(8,128)(2,1)S(1)}, bf16[6,128,128]{2,1,0:T(8,128)(2,1)S(1)}, u32[]{:S(2)}, u32[]{:S(2)}) collective-permute-start(bf16[6,128,128]{2,1,0:T(8,128)(2,1)S(1)} %get-tuple-element.537), channel_id=1, source_target_pairs={{0,480},{16,496},{32,0},{48,16},{64,32},{80,48},{96,64},{112,80},{... | collective-permute-start | bytes 589832 | tf_op jit(solution)/shard_map/ppermute | solution.py:383
  35.1 7.9 %collective-permute-start.9 = (bf16[6,128,128]{2,1,0:T(8,128)(2,1)S(1)}, bf16[6,128,128]{2,1,0:T(8,128)(2,1)S(1)}, u32[]{:S(2)}, u32[]{:S(2)}) collective-permute-start(bf16[6,128,128]{2,1,0:T(8,128)(2,1)S(1)} %get-tuple-element.538), channel_id=1, source_target_pairs={{0,64},{16,80},{32,480},{48,496},{64,128},{80,144},{96,32},{112,48... | collective-permute-start | bytes 589832 | tf_op jit(solution)/shard_map/ppermute | solution.py:383
  42.9 2.1 %collective-permute-done.7.refs_0_ = bf16[6,128,128]{2,1,0:T(8,128)(2,1)S(1)} collective-permute-done((bf16[6,128,128]{2,1,0:T(8,128)(2,1)S(1)}, bf16[6,128,128]{2,1,0:T(8,128)(2,1)S(1)}, u32[]{:S(2)}, u32[]{:S(2)}) %collective-permute-start.7) | collective-permute-done | bytes 196640 | tf_op jit(solution)/shard_map/ppermute | solution.py:383
  46.7 2.6 %collective-permute-done.8.refs_1_ = bf16[6,128,128]{2,1,0:T(8,128)(2,1)S(1)} collective-permute-done((bf16[6,128,128]{2,1,0:T(8,128)(2,1)S(1)}, bf16[6,128,128]{2,1,0:T(8,128)(2,1)S(1)}, u32[]{:S(2)}, u32[]{:S(2)}) %collective-permute-start.8) | collective-permute-done | bytes 196640 | tf_op jit(solution)/shard_map/ppermute | solution.py:383
  49.4 2.5 %collective-permute-done.9.refs_2_ = bf16[6,128,128]{2,1,0:T(8,128)(2,1)S(1)} collective-permute-done((bf16[6,128,128]{2,1,0:T(8,128)(2,1)S(1)}, bf16[6,128,128]{2,1,0:T(8,128)(2,1)S(1)}, u32[]{:S(2)}, u32[]{:S(2)}) %collective-permute-start.9) | collective-permute-done | bytes 196640 | tf_op jit(solution)/shard_map/ppermute | solution.py:383
  51.9 2.0 %shard_map.125 = bf16[16,128,128]{2,1,0:T(8,128)(2,1)} custom-call(s32[16]{0:T(128)S(1)} %copy-done.13, bf16[8,128,128]{2,1,0:T(8,128)(2,1)S(1)} %reshape.104.own, bf16[8,128,128]{2,1,0:T(8,128)(2,1)} %collective-permute-done.6.other, bf16[6,128,128]{2,1,0:T(8,128)(2,1)S(1)} %collective-permute-done.7.refs_0_, ...), custom_call_target="tpu_custom_call" | custom-call | tf_op jit(solution)/shard_map/pallas_call | solution.py:99
  54.9 3.3 %shard_map.126 = bf16[16,128,128]{2,1,0:T(8,128)(2,1)S(1)} custom-call(s32[3]{0:T(128)S(1)} %copy-done.12, s32[2,64]{1,0:T(2,128)S(1)} %get-tuple-element.796, bf16[16,128,128]{2,1,0:T(8,128)(2,1)} %get-tuple-element.540.sources, bf16[16,128,128]{2,1,0:T(8,128)(2,1)S(1)} %all-to-all-done.wanted, bf16[2,128,128]{2,1,0:T(8,128)(2,1)S(1)} %copy-done.8, ...), custom_call_target="tpu_custom_call" | custom-call | tf_op jit(solution)/shard_map/pallas_call | solution.py:99
  58.2 19.3 %all_to_all.20.slabs = bf16[16,128,128]{2,1,0:T(8,128)(2,1)S(1)} all-to-all(bf16[16,128,128]{2,1,0:T(8,128)(2,1)S(1)} %shard_map.126), channel_id=1, replica_groups=mesh['band'=32,'dom'=16] {'dom'}, dimensions={0} | all-to-all | bytes 1048576 | tf_op jit(solution)/shard_map/all_to_all | solution.py:459
  77.6 8.3 %shard_map.127 = bf16[16,128,128]{2,1,0:T(8,128)(2,1)S(1)} custom-call(bf16[16,128,128]{2,1,0:T(8,128)(2,1)S(1)} %all_to_all.20.slabs, f32[8,256,128]{2,1,0:T(8,128)S(1)} %copy-done.1, bf16[2,128,128]{2,1,0:T(8,128)(2,1)S(1)} %copy-done.7, bf16[2,128,128]{2,1,0:T(8,128)(2,1)S(1)} %copy-done.6), custom_call_target="tpu_custom_call" | custom-call | tf_op jit(solution)/shard_map/pallas_call | solution.py:99
  85.9 15.1 %all_to_all.21.spectra = bf16[16,128,128]{2,1,0:T(8,128)(2,1)S(1)} all-to-all(bf16[16,128,128]{2,1,0:T(8,128)(2,1)S(1)} %shard_map.127), channel_id=1, replica_groups=mesh['band'=32,'dom'=16] {'dom'}, dimensions={0} | all-to-all | bytes 1048576 | tf_op jit(solution)/shard_map/all_to_all | solution.py:466
  101.0 3.2 %shard_map.128 = (bf16[16,128,128]{2,1,0:T(8,128)(2,1)S(1)}, bf16[16,128,128]{2,1,0:T(8,128)(2,1)}) custom-call(s32[3]{0:T(128)S(1)} %copy-done.12, s32[2,64]{1,0:T(2,128)S(1)} %get-tuple-element.796, bf16[16,128,128]{2,1,0:T(8,128)(2,1)S(1)} %all_to_all.21.spectra, bf16[16,128,128]{2,1,0:T(8,128)(2,1)S(1)} %copy-done.17, ...), custom_call_target="tpu_custom_call" | custom-call | tf_op jit(solution)/shard_map/pallas_call | solution.py:99
  104.2 7.2 %all-to-all-start.3 = ((bf16[16,128,128]{2,1,0:T(8,128)(2,1)}), bf16[16,128,128]{2,1,0:T(8,128)(2,1)S(1)}, u32[]{:S(2)}, u32[]{:S(2)}) async-start(bf16[16,128,128]{2,1,0:T(8,128)(2,1)} %get-tuple-element.541), calls=%async_computation.3 | async-start | bytes 1048576 | tf_op jit(solution)/shard_map/all_to_all | solution.py:402
  112.2 3.5 %collective-permute-start.10 = (bf16[6,128,128]{2,1,0:T(8,128)(2,1)S(1)}, bf16[6,128,128]{2,1,0:T(8,128)(2,1)S(1)}, u32[]{:S(2)}, u32[]{:S(2)}) collective-permute-start(bf16[6,128,128]{2,1,0:T(8,128)(2,1)S(1)} %get-tuple-element.543), channel_id=1, source_target_pairs={{0,480},{16,496},{32,0},{48,16},{64,32},{80,48},{96,64},{112,80},{... | collective-permute-start | bytes 589832 | tf_op jit(solution)/shard_map/ppermute | solution.py:383
  115.7 2.3 %collective-permute-start.11 = (bf16[6,128,128]{2,1,0:T(8,128)(2,1)S(1)}, bf16[6,128,128]{2,1,0:T(8,128)(2,1)S(1)}, u32[]{:S(2)}, u32[]{:S(2)}) collective-permute-start(bf16[6,128,128]{2,1,0:T(8,128)(2,1)S(1)} %get-tuple-element.544), channel_id=1, source_target_pairs={{0,32},{16,48},{32,64},{48,80},{64,96},{80,112},{96,128},{112,144}... | collective-permute-start | bytes 589832 | tf_op jit(solution)/shard_map/ppermute | solution.py:383
  118.0 5.7 %collective-permute-start.12 = (bf16[6,128,128]{2,1,0:T(8,128)(2,1)S(1)}, bf16[6,128,128]{2,1,0:T(8,128)(2,1)S(1)}, u32[]{:S(2)}, u32[]{:S(2)}) collective-permute-start(bf16[6,128,128]{2,1,0:T(8,128)(2,1)S(1)} %get-tuple-element.545), channel_id=1, source_target_pairs={{0,448},{16,464},{32,96},{48,112},{64,0},{80,16},{96,160},{112,176... | collective-permute-start | bytes 589832 | tf_op jit(solution)/shard_map/ppermute | solution.py:383
  123.7 15.4 %collective-permute-done.10.refs_0_ = bf16[6,128,128]{2,1,0:T(8,128)(2,1)S(1)} collective-permute-done((bf16[6,128,128]{2,1,0:T(8,128)(2,1)S(1)}, bf16[6,128,128]{2,1,0:T(8,128)(2,1)S(1)}, u32[]{:S(2)}, u32[]{:S(2)}) %collective-permute-start.10) | collective-permute-done | bytes 196640 | tf_op jit(solution)/shard_map/ppermute | solution.py:383
  139.1 1.1 collective-permute-done.11.refs_1_
  140.3 7.8 %collective-permute-done.12.refs_2_ = bf16[6,128,128]{2,1,0:T(8,128)(2,1)S(1)} collective-permute-done((bf16[6,128,128]{2,1,0:T(8,128)(2,1)S(1)}, bf16[6,128,128]{2,1,0:T(8,128)(2,1)S(1)}, u32[]{:S(2)}, u32[]{:S(2)}) %collective-permute-start.12) | collective-permute-done | bytes 196640 | tf_op jit(solution)/shard_map/ppermute | solution.py:383
  148.1 1.8 %shard_map.131 = (f32[8,128,128]{2,1,0:T(8,128)}, bf16[8,128,128]{2,1,0:T(8,128)(2,1)}) custom-call(s32[18]{0:T(128)S(1)} %copy-done.15, s32[16]{0:T(128)S(1)} %copy-done.13, bf16[16,128,128]{2,1,0:T(8,128)(2,1)S(1)} %get-tuple-element.748.terms, bf16[6,128,128]{2,1,0:T(8,128)(2,1)S(1)} %collective-permute-done.10.refs_0_, ...), custom_call_target="tpu_custom_call" | custom-call | tf_op jit(solution)/shard_map/pallas_call | solution.py:99
  149.9 2.7 %collective-permute-start.13 = (bf16[8,128,128]{2,1,0:T(8,128)(2,1)}, bf16[8,128,128]{2,1,0:T(8,128)(2,1)S(1)}, u32[]{:S(2)}, u32[]{:S(2)}) collective-permute-start(bf16[8,128,128]{2,1,0:T(8,128)(2,1)} %get-tuple-element.549), channel_id=1, source_target_pairs={{0,16},{16,0},{32,48},{48,32},{64,80},{80,64},{96,112},{112,96},{1... | collective-permute-start | bytes 786440 | tf_op jit(solution)/shard_map/ppermute | solution.py:397
  153.3 1.3 iota_compare_fusion.2
  154.5 1.3 iota_compare_fusion
  155.8 4.4 %collective-permute-done.13 = bf16[8,128,128]{2,1,0:T(8,128)(2,1)S(1)} collective-permute-done((bf16[8,128,128]{2,1,0:T(8,128)(2,1)}, bf16[8,128,128]{2,1,0:T(8,128)(2,1)S(1)}, u32[]{:S(2)}, u32[]{:S(2)}) %collective-permute-start.13) | collective-permute-done | bytes 262176 | tf_op jit(solution)/shard_map/ppermute | solution.py:397
  162.8 1.3 select_select_fusion
  (54 shorter events, 9.8 us)
Async XLA Ops:
  0.6 2.1 %copy-start = (bf16[32,16384]{1,0:T(8,128)(2,1)S(1)}, bf16[32,16384]{1,0:T(8,128)(2,1)}, u32[]{:S(2)}) copy-start(bf16[32,16384]{1,0:T(8,128)(2,1)} %param.15) | copy-start | bytes 3145732
  4.3 49.6 %all-to-all-start = ((bf16[16,128,128]{2,1,0:T(8,128)(2,1)}), bf16[16,128,128]{2,1,0:T(8,128)(2,1)S(1)}, u32[]{:S(2)}, u32[]{:S(2)}) async-start(bf16[16,128,128]{2,1,0:T(8,128)(2,1)} %pad_maximum_fusion), calls=%async_computation | async-start | bytes 1048576 | tf_op jit(solution)/shard_map/all_to_all | solution.py:402
  17.6 9.8 %collective-permute-start.6 = (bf16[8,128,128]{2,1,0:T(8,128)(2,1)S(1)}, bf16[8,128,128]{2,1,0:T(8,128)(2,1)}, u32[]{:S(2)}, u32[]{:S(2)}) collective-permute-start(bf16[8,128,128]{2,1,0:T(8,128)(2,1)S(1)} %reshape.104.own), channel_id=1, source_target_pairs={{0,16},{16,0},{32,48},{48,32},{64,80},{80,64},{96,112},{112,96},{1... | collective-permute-start | bytes 786440 | tf_op jit(solution)/shard_map/ppermute | solution.py:397
  21.0 0.7 copy-start.19
  27.4 0.7 copy-start.14
  29.2 15.9 %collective-permute-start.7 = (bf16[6,128,128]{2,1,0:T(8,128)(2,1)S(1)}, bf16[6,128,128]{2,1,0:T(8,128)(2,1)S(1)}, u32[]{:S(2)}, u32[]{:S(2)}) collective-permute-start(bf16[6,128,128]{2,1,0:T(8,128)(2,1)S(1)} %get-tuple-element.535), channel_id=1, source_target_pairs={{0,32},{16,48},{32,64},{48,80},{64,96},{80,112},{96,128},{112,144}... | collective-permute-start | bytes 589832 | tf_op jit(solution)/shard_map/ppermute | solution.py:383
  32.2 17.2 %collective-permute-start.8 = (bf16[6,128,128]{2,1,0:T(8,128)(2,1)S(1)}, bf16[6,128,128]{2,1,0:T(8,128)(2,1)S(1)}, u32[]{:S(2)}, u32[]{:S(2)}) collective-permute-start(bf16[6,128,128]{2,1,0:T(8,128)(2,1)S(1)} %get-tuple-element.537), channel_id=1, source_target_pairs={{0,480},{16,496},{32,0},{48,16},{64,32},{80,48},{96,64},{112,80},{... | collective-permute-start | bytes 589832 | tf_op jit(solution)/shard_map/ppermute | solution.py:383
  35.1 16.8 %collective-permute-start.9 = (bf16[6,128,128]{2,1,0:T(8,128)(2,1)S(1)}, bf16[6,128,128]{2,1,0:T(8,128)(2,1)S(1)}, u32[]{:S(2)}, u32[]{:S(2)}) collective-permute-start(bf16[6,128,128]{2,1,0:T(8,128)(2,1)S(1)} %get-tuple-element.538), channel_id=1, source_target_pairs={{0,64},{16,80},{32,480},{48,496},{64,128},{80,144},{96,32},{112,48... | collective-permute-start | bytes 589832 | tf_op jit(solution)/shard_map/ppermute | solution.py:383
  46.7 5.1 %copy-start.13 = (s32[16]{0:T(128)S(1)}, s32[16]{0:T(128)}, u32[]{:S(2)}) copy-start(s32[16]{0:T(128)} %shard_map.122.found) | copy-start | bytes 196
  53.9 0.9 copy-start.3
  53.9 1.0 copy-start.8
  53.9 0.9 copy-start.12
  54.9 22.7 %copy-start.1 = (f32[8,256,128]{2,1,0:T(8,128)S(1)}, f32[8,256,128]{2,1,0:T(8,128)}, u32[]{:S(2)}) copy-start(f32[8,256,128]{2,1,0:T(8,128)} %constant.224.clone.spectrum) | copy-start | bytes 3145732
  58.2 19.4 %copy-start.6 = (bf16[2,128,128]{2,1,0:T(8,128)(2,1)S(1)}, bf16[2,128,128]{2,1,0:T(8,128)(2,1)}, u32[]{:S(2)}) copy-start(bf16[2,128,128]{2,1,0:T(8,128)(2,1)} %constant.223.clone.x_bwd) | copy-start | bytes 196612
  58.2 19.4 %copy-start.7 = (bf16[2,128,128]{2,1,0:T(8,128)(2,1)S(1)}, bf16[2,128,128]{2,1,0:T(8,128)(2,1)}, u32[]{:S(2)}) copy-start(bf16[2,128,128]{2,1,0:T(8,128)(2,1)} %constant.222.clone.x_fwd) | copy-start | bytes 196612
  85.8 15.2 %copy-start.2 = (bf16[2,256,256]{2,1,0:T(8,128)(2,1)S(1)}, bf16[2,256,256]{2,1,0:T(8,128)(2,1)}, u32[]{:S(2)}) copy-start(bf16[2,256,256]{2,1,0:T(8,128)(2,1)} %constant.221.clone.y_bwd) | copy-start | bytes 786436
  85.9 15.1 %copy-start.5 = (bf16[2,128,128]{2,1,0:T(8,128)(2,1)S(1)}, bf16[2,128,128]{2,1,0:T(8,128)(2,1)}, u32[]{:S(2)}) copy-start(bf16[2,128,128]{2,1,0:T(8,128)(2,1)} %constant.219.clone.z_bwd) | copy-start | bytes 196612
  85.9 15.1 %copy-start.17 = (bf16[16,128,128]{2,1,0:T(8,128)(2,1)S(1)}, bf16[16,128,128]{2,1,0:T(8,128)(2,1)}, u32[]{:S(2)}) copy-start(bf16[16,128,128]{2,1,0:T(8,128)(2,1)} %get-tuple-element.540.sources) | copy-start | bytes 1572868
  104.2 57.9 %all-to-all-start.3 = ((bf16[16,128,128]{2,1,0:T(8,128)(2,1)}), bf16[16,128,128]{2,1,0:T(8,128)(2,1)S(1)}, u32[]{:S(2)}, u32[]{:S(2)}) async-start(bf16[16,128,128]{2,1,0:T(8,128)(2,1)} %get-tuple-element.541), calls=%async_computation.3 | async-start | bytes 1048576 | tf_op jit(solution)/shard_map/all_to_all | solution.py:402
  112.2 26.9 %collective-permute-start.10 = (bf16[6,128,128]{2,1,0:T(8,128)(2,1)S(1)}, bf16[6,128,128]{2,1,0:T(8,128)(2,1)S(1)}, u32[]{:S(2)}, u32[]{:S(2)}) collective-permute-start(bf16[6,128,128]{2,1,0:T(8,128)(2,1)S(1)} %get-tuple-element.543), channel_id=1, source_target_pairs={{0,480},{16,496},{32,0},{48,16},{64,32},{80,48},{96,64},{112,80},{... | collective-permute-start | bytes 589832 | tf_op jit(solution)/shard_map/ppermute | solution.py:383
  115.7 24.6 %collective-permute-start.11 = (bf16[6,128,128]{2,1,0:T(8,128)(2,1)S(1)}, bf16[6,128,128]{2,1,0:T(8,128)(2,1)S(1)}, u32[]{:S(2)}, u32[]{:S(2)}) collective-permute-start(bf16[6,128,128]{2,1,0:T(8,128)(2,1)S(1)} %get-tuple-element.544), channel_id=1, source_target_pairs={{0,32},{16,48},{32,64},{48,80},{64,96},{80,112},{96,128},{112,144}... | collective-permute-start | bytes 589832 | tf_op jit(solution)/shard_map/ppermute | solution.py:383
  118.0 30.0 %copy-start.15 = (s32[18]{0:T(128)S(1)}, s32[18]{0:T(128)}, u32[]{:S(2)}) copy-start(s32[18]{0:T(128)} %shard_map.123.sent) | copy-start | bytes 220
  118.0 30.0 %collective-permute-start.12 = (bf16[6,128,128]{2,1,0:T(8,128)(2,1)S(1)}, bf16[6,128,128]{2,1,0:T(8,128)(2,1)S(1)}, u32[]{:S(2)}, u32[]{:S(2)}) collective-permute-start(bf16[6,128,128]{2,1,0:T(8,128)(2,1)S(1)} %get-tuple-element.545), channel_id=1, source_target_pairs={{0,448},{16,464},{32,96},{48,112},{64,0},{80,16},{96,160},{112,176... | collective-permute-start | bytes 589832 | tf_op jit(solution)/shard_map/ppermute | solution.py:383
  149.9 10.3 %collective-permute-start.13 = (bf16[8,128,128]{2,1,0:T(8,128)(2,1)}, bf16[8,128,128]{2,1,0:T(8,128)(2,1)S(1)}, u32[]{:S(2)}, u32[]{:S(2)}) collective-permute-start(bf16[8,128,128]{2,1,0:T(8,128)(2,1)} %get-tuple-element.549), channel_id=1, source_target_pairs={{0,16},{16,0},{32,48},{48,32},{64,80},{80,64},{96,112},{112,96},{1... | collective-permute-start | bytes 786440 | tf_op jit(solution)/shard_map/ppermute | solution.py:397
  161.3 0.8 copy-start.16

commit v12 on v11

--- a/solution.py
+++ b/solution.py
@@ -264,7 +264,7 @@
         square = value * value
         return norm + dot_of(square), power + dot_of(square * spectrum[j])
 
-    norm, power = lax.fori_loop(0, 8, start, (zero, zero))
+    norm, power = lax.fori_loop(0, 8, start, (zero, zero), unroll=2)
     norm, power = jnp.sum(norm), jnp.sum(power)
     steps, ratio = [norm / power], jnp.float32(0.0)
     for sweep in range(SWEEPS - 1):
@@ -284,7 +284,7 @@
             square = r * r
             return new + dot_of(square), power + dot_of(square * lam)
 
-        new, power = lax.fori_loop(0, 8, advance, (zero, zero))
+        new, power = lax.fori_loop(0, 8, advance, (zero, zero), unroll=2)
         new, power = jnp.sum(new), jnp.sum(power)
         ratio = new / norm
         steps.append(new / (power - ratio * new / step))
@@ -300,7 +300,7 @@
         out[:, pl.ds(pl.multiple_of(16 * j, 16), 16), :] = part.astype(out.dtype)
         return carry
 
-    lax.fori_loop(0, 8, finish, 0)
+    lax.fori_loop(0, 8, finish, 0, unroll=2)
 
 
 def term_kernel(place, pair_src, spectra, sources, wanted, z_bwd, y_bwd, terms, shares, queue):
@@ -488,8 +488,6 @@
     near = give_back(found)
     shares = along_ring(shares)
     mine, partner = lax.fori_loop(1, rounds, collect_in, collect(sent, found, near, ()))
-    owned = (mine + across(partner).astype(F32)).astype(BF16).reshape(sources.shape)
-
     (target_rows,) = vmem_call(
         target_kernel,
         [struct((4, ROW, ROW), BF16)],
@@ -497,7 +495,8 @@
         scalars=3,
         scratch=[pltpu.VMEM((4, ROW, ROW), F32)],
     )
-    flat = target_rows.reshape(4, targets.shape[1])
+    partner, flat = lax.optimization_barrier((across(partner), target_rows.reshape(4, targets.shape[1])))
+    owned = (mine + partner.astype(F32)).astype(BF16).reshape(sources.shape)
     slots = jnp.arange(targets.shape[0], dtype=jnp.int32)[:, None]
     summed = jnp.zeros(targets.shape, BF16)
     for p in range(4):

time: 165 us -> 163 us (0.988)
  the two profiles are of different devices: /device:TPU:64 before, /device:TPU:32 now
where the time goes in v12:
time: 163 us
  starting transfers between devices  48.8 us (30%)
  waiting for transfers between devices  41.9 us (26%)
  blocking collectives  34.4 us (21%)
  Pallas kernels  22.5 us (14%)
  local copies, waits for them, and re-layouts  6.92 us (4%)
  other arithmetic  6.37 us (4%)
  between operations  1.7 us (1%)
    ppermute x6, waiting for transfers between devices, hand_over(): lax.ppermute(packet, 'band', [(2 * z + x, 2 * ((z + sign * move(z)) % RIN...  34.9 us
    ppermute x6, starting transfers between devices, hand_over(): lax.ppermute(packet, 'band', [(2 * z + x, 2 * ((z + sign * move(z)) % RIN...  23.4 us
    all_to_all x2, starting transfers between devices, along_ring(): lax.all_to_all(value, 'band', 0, 0, axis_index_groups=groups, tiled=True)  20.1 us
    pallas_call x8, Pallas kernels, vmem_call(): pl.pallas_call(kernel, out_shape=outs, in_specs=[smem] * scalars + [whole...  19.6 us
    all_to_all x1, blocking collectives, per_device(): slabs = lax.all_to_all(spectra, 'dom', 0, 0, tiled=True)  19.3 us
    all_to_all x1, blocking collectives, per_device(): back = lax.all_to_all(solved, 'dom', 0, 0, tiled=True)  15.1 us
    ppermute x2, waiting for transfers between devices, across(): return lax.ppermute(value, 'band', [(i, i ^ 1) for i in range(32)])  7.02 us
    ppermute x2, starting transfers between devices, across(): return lax.ppermute(value, 'band', [(i, i ^ 1) for i in range(32)])  5.3 us
  transfers between devices with their start and end apart: 10, of which 7 were waited for; matrix products, arithmetic and copies ran while one was open for 3% of the time, Pallas kernels for 6%

profile of v12, /device:TPU:32, one launch (start us, length us, event | category | flops | bytes accessed | tf_op | source)
XLA Modules:
  0.0 162.6 jit_solution(6848320122192093986)
XLA Ops:
  0.6 0.8 reshape.99
  1.5 1.2 reshape.98.own
  4.3 14.2 %all-to-all-start = ((bf16[16,128,128]{2,1,0:T(8,128)(2,1)}), bf16[16,128,128]{2,1,0:T(8,128)(2,1)S(1)}, u32[]{:S(2)}, u32[]{:S(2)}) async-start(bf16[16,128,128]{2,1,0:T(8,128)(2,1)} %pad_maximum_fusion), calls=%async_computation | async-start | bytes 1048576 | tf_op jit(solution)/shard_map/all_to_all | solution.py:402
  18.5 3.4 %collective-permute-start.6 = (bf16[8,128,128]{2,1,0:T(8,128)(2,1)S(1)}, bf16[8,128,128]{2,1,0:T(8,128)(2,1)}, u32[]{:S(2)}, u32[]{:S(2)}) collective-permute-start(bf16[8,128,128]{2,1,0:T(8,128)(2,1)S(1)} %reshape.98.own), channel_id=1, source_target_pairs={{0,16},{16,0},{32,48},{48,32},{64,80},{80,64},{96,112},{112,96},{1... | collective-permute-start | bytes 786440 | tf_op jit(solution)/shard_map/ppermute | solution.py:397
  22.6 1.4 shard_map.123.found
  24.0 1.5 shard_map.122.sent
  25.5 2.8 %collective-permute-done.6.other = bf16[8,128,128]{2,1,0:T(8,128)(2,1)} collective-permute-done((bf16[8,128,128]{2,1,0:T(8,128)(2,1)S(1)}, bf16[8,128,128]{2,1,0:T(8,128)(2,1)}, u32[]{:S(2)}, u32[]{:S(2)}) %collective-permute-start.6) | collective-permute-done | bytes 262176 | tf_op jit(solution)/shard_map/ppermute | solution.py:397
  28.9 1.1 shard_map.124
  30.0 2.9 %collective-permute-start.7 = (bf16[6,128,128]{2,1,0:T(8,128)(2,1)S(1)}, bf16[6,128,128]{2,1,0:T(8,128)(2,1)S(1)}, u32[]{:S(2)}, u32[]{:S(2)}) collective-permute-start(bf16[6,128,128]{2,1,0:T(8,128)(2,1)S(1)} %get-tuple-element.537), channel_id=1, source_target_pairs={{0,32},{16,48},{32,64},{48,80},{64,96},{80,112},{96,128},{112,144}... | collective-permute-start | bytes 589832 | tf_op jit(solution)/shard_map/ppermute | solution.py:383
  33.0 2.9 %collective-permute-start.8 = (bf16[6,128,128]{2,1,0:T(8,128)(2,1)S(1)}, bf16[6,128,128]{2,1,0:T(8,128)(2,1)S(1)}, u32[]{:S(2)}, u32[]{:S(2)}) collective-permute-start(bf16[6,128,128]{2,1,0:T(8,128)(2,1)S(1)} %get-tuple-element.539), channel_id=1, source_target_pairs={{0,480},{16,496},{32,0},{48,16},{64,32},{80,48},{96,64},{112,80},{... | collective-permute-start | bytes 589832 | tf_op jit(solution)/shard_map/ppermute | solution.py:383
  35.9 6.7 %collective-permute-start.9 = (bf16[6,128,128]{2,1,0:T(8,128)(2,1)S(1)}, bf16[6,128,128]{2,1,0:T(8,128)(2,1)S(1)}, u32[]{:S(2)}, u32[]{:S(2)}) collective-permute-start(bf16[6,128,128]{2,1,0:T(8,128)(2,1)S(1)} %get-tuple-element.540), channel_id=1, source_target_pairs={{0,64},{16,80},{32,480},{48,496},{64,128},{80,144},{96,32},{112,48... | collective-permute-start | bytes 589832 | tf_op jit(solution)/shard_map/ppermute | solution.py:383
  42.6 5.7 %collective-permute-done.7.refs_0_ = bf16[6,128,128]{2,1,0:T(8,128)(2,1)S(1)} collective-permute-done((bf16[6,128,128]{2,1,0:T(8,128)(2,1)S(1)}, bf16[6,128,128]{2,1,0:T(8,128)(2,1)S(1)}, u32[]{:S(2)}, u32[]{:S(2)}) %collective-permute-start.7) | collective-permute-done | bytes 196640 | tf_op jit(solution)/shard_map/ppermute | solution.py:383
  50.1 4.6 %collective-permute-done.9.refs_2_ = bf16[6,128,128]{2,1,0:T(8,128)(2,1)S(1)} collective-permute-done((bf16[6,128,128]{2,1,0:T(8,128)(2,1)S(1)}, bf16[6,128,128]{2,1,0:T(8,128)(2,1)S(1)}, u32[]{:S(2)}, u32[]{:S(2)}) %collective-permute-start.9) | collective-permute-done | bytes 196640 | tf_op jit(solution)/shard_map/ppermute | solution.py:383
  54.7 2.0 %shard_map.125 = bf16[16,128,128]{2,1,0:T(8,128)(2,1)} custom-call(s32[16]{0:T(128)S(1)} %copy-done.13, bf16[8,128,128]{2,1,0:T(8,128)(2,1)S(1)} %reshape.98.own, bf16[8,128,128]{2,1,0:T(8,128)(2,1)} %collective-permute-done.6.other, bf16[6,128,128]{2,1,0:T(8,128)(2,1)S(1)} %collective-permute-done.7.refs_0_, ...), custom_call_target="tpu_custom_call" | custom-call | tf_op jit(solution)/shard_map/pallas_call | solution.py:99
  56.8 0.9 copy-done.3
  57.7 3.3 %shard_map.126 = bf16[16,128,128]{2,1,0:T(8,128)(2,1)S(1)} custom-call(s32[3]{0:T(128)S(1)} %copy-done.12, s32[2,64]{1,0:T(2,128)S(1)} %get-tuple-element.800, bf16[16,128,128]{2,1,0:T(8,128)(2,1)} %get-tuple-element.542.sources, bf16[16,128,128]{2,1,0:T(8,128)(2,1)S(1)} %all-to-all-done.wanted, bf16[2,128,128]{2,1,0:T(8,128)(2,1)S(1)} %copy-done.8, ...), custom_call_target="tpu_custom_call" | custom-call | tf_op jit(solution)/shard_map/pallas_call | solution.py:99
  61.0 19.3 %all_to_all.20.slabs = bf16[16,128,128]{2,1,0:T(8,128)(2,1)S(1)} all-to-all(bf16[16,128,128]{2,1,0:T(8,128)(2,1)S(1)} %shard_map.126), channel_id=1, replica_groups=mesh['band'=32,'dom'=16] {'dom'}, dimensions={0} | all-to-all | bytes 1048576 | tf_op jit(solution)/shard_map/all_to_all | solution.py:459
  80.4 6.7 %shard_map.127 = bf16[16,128,128]{2,1,0:T(8,128)(2,1)S(1)} custom-call(bf16[16,128,128]{2,1,0:T(8,128)(2,1)S(1)} %all_to_all.20.slabs, f32[8,256,128]{2,1,0:T(8,128)S(1)} %copy-done.1, bf16[2,128,128]{2,1,0:T(8,128)(2,1)S(1)} %copy-done.7, bf16[2,128,128]{2,1,0:T(8,128)(2,1)S(1)} %copy-done.6), custom_call_target="tpu_custom_call" | custom-call | tf_op jit(solution)/shard_map/pallas_call | solution.py:99
  87.1 15.1 %all_to_all.21.spectra = bf16[16,128,128]{2,1,0:T(8,128)(2,1)S(1)} all-to-all(bf16[16,128,128]{2,1,0:T(8,128)(2,1)S(1)} %shard_map.127), channel_id=1, replica_groups=mesh['band'=32,'dom'=16] {'dom'}, dimensions={0} | all-to-all | bytes 1048576 | tf_op jit(solution)/shard_map/all_to_all | solution.py:466
  102.2 3.2 %shard_map.128 = (bf16[16,128,128]{2,1,0:T(8,128)(2,1)S(1)}, bf16[16,128,128]{2,1,0:T(8,128)(2,1)}) custom-call(s32[3]{0:T(128)S(1)} %copy-done.12, s32[2,64]{1,0:T(2,128)S(1)} %get-tuple-element.800, bf16[16,128,128]{2,1,0:T(8,128)(2,1)S(1)} %all_to_all.21.spectra, bf16[16,128,128]{2,1,0:T(8,128)(2,1)S(1)} %copy-done.17, ...), custom_call_target="tpu_custom_call" | custom-call | tf_op jit(solution)/shard_map/pallas_call | solution.py:99
  105.4 6.0 %all-to-all-start.3 = ((bf16[16,128,128]{2,1,0:T(8,128)(2,1)}), bf16[16,128,128]{2,1,0:T(8,128)(2,1)S(1)}, u32[]{:S(2)}, u32[]{:S(2)}) async-start(bf16[16,128,128]{2,1,0:T(8,128)(2,1)} %get-tuple-element.550), calls=%async_computation.3 | async-start | bytes 1048576 | tf_op jit(solution)/shard_map/all_to_all | solution.py:402
  112.1 2.0 %collective-permute-start.10 = (bf16[6,128,128]{2,1,0:T(8,128)(2,1)S(1)}, bf16[6,128,128]{2,1,0:T(8,128)(2,1)S(1)}, u32[]{:S(2)}, u32[]{:S(2)}) collective-permute-start(bf16[6,128,128]{2,1,0:T(8,128)(2,1)S(1)} %get-tuple-element.544), channel_id=1, source_target_pairs={{0,480},{16,496},{32,0},{48,16},{64,32},{80,48},{96,64},{112,80},{... | collective-permute-start | bytes 589832 | tf_op jit(solution)/shard_map/ppermute | solution.py:383
  114.2 3.8 %collective-permute-start.11 = (bf16[6,128,128]{2,1,0:T(8,128)(2,1)S(1)}, bf16[6,128,128]{2,1,0:T(8,128)(2,1)S(1)}, u32[]{:S(2)}, u32[]{:S(2)}) collective-permute-start(bf16[6,128,128]{2,1,0:T(8,128)(2,1)S(1)} %get-tuple-element.545), channel_id=1, source_target_pairs={{0,32},{16,48},{32,64},{48,80},{64,96},{80,112},{96,128},{112,144}... | collective-permute-start | bytes 589832 | tf_op jit(solution)/shard_map/ppermute | solution.py:383
  118.0 5.0 %collective-permute-start.12 = (bf16[6,128,128]{2,1,0:T(8,128)(2,1)S(1)}, bf16[6,128,128]{2,1,0:T(8,128)(2,1)S(1)}, u32[]{:S(2)}, u32[]{:S(2)}) collective-permute-start(bf16[6,128,128]{2,1,0:T(8,128)(2,1)S(1)} %get-tuple-element.546), channel_id=1, source_target_pairs={{0,448},{16,464},{32,96},{48,112},{64,0},{80,16},{96,160},{112,176... | collective-permute-start | bytes 589832 | tf_op jit(solution)/shard_map/ppermute | solution.py:383
  123.0 17.3 %collective-permute-done.10.refs_0_ = bf16[6,128,128]{2,1,0:T(8,128)(2,1)S(1)} collective-permute-done((bf16[6,128,128]{2,1,0:T(8,128)(2,1)S(1)}, bf16[6,128,128]{2,1,0:T(8,128)(2,1)S(1)}, u32[]{:S(2)}, u32[]{:S(2)}) %collective-permute-start.10) | collective-permute-done | bytes 196640 | tf_op jit(solution)/shard_map/ppermute | solution.py:383
  140.6 7.0 %collective-permute-done.12.refs_2_ = bf16[6,128,128]{2,1,0:T(8,128)(2,1)S(1)} collective-permute-done((bf16[6,128,128]{2,1,0:T(8,128)(2,1)S(1)}, bf16[6,128,128]{2,1,0:T(8,128)(2,1)S(1)}, u32[]{:S(2)}, u32[]{:S(2)}) %collective-permute-start.12) | collective-permute-done | bytes 196640 | tf_op jit(solution)/shard_map/ppermute | solution.py:383
  147.6 1.8 %shard_map.130 = (f32[8,128,128]{2,1,0:T(8,128)}, bf16[8,128,128]{2,1,0:T(8,128)(2,1)}) custom-call(s32[18]{0:T(128)S(1)} %copy-done.15, s32[16]{0:T(128)S(1)} %copy-done.13, bf16[16,128,128]{2,1,0:T(8,128)(2,1)S(1)} %get-tuple-element.752.terms, bf16[6,128,128]{2,1,0:T(8,128)(2,1)S(1)} %collective-permute-done.10.refs_0_, ...), custom_call_target="tpu_custom_call" | custom-call | tf_op jit(solution)/shard_map/pallas_call | solution.py:99
  149.4 1.9 %collective-permute-start.13 = (bf16[8,128,128]{2,1,0:T(8,128)(2,1)}, bf16[8,128,128]{2,1,0:T(8,128)(2,1)S(1)}, u32[]{:S(2)}, u32[]{:S(2)}) collective-permute-start(bf16[8,128,128]{2,1,0:T(8,128)(2,1)} %get-tuple-element.549), channel_id=1, source_target_pairs={{0,16},{16,0},{32,48},{48,32},{64,80},{80,64},{96,112},{112,96},{1... | collective-permute-start | bytes 786440 | tf_op jit(solution)/shard_map/ppermute | solution.py:397
  152.0 1.3 iota_compare_fusion.2
  153.4 1.3 iota_compare_fusion
  155.5 4.3 %collective-permute-done.13 = bf16[8,128,128]{2,1,0:T(8,128)(2,1)S(1)} collective-permute-done((bf16[8,128,128]{2,1,0:T(8,128)(2,1)}, bf16[8,128,128]{2,1,0:T(8,128)(2,1)S(1)}, u32[]{:S(2)}, u32[]{:S(2)}) %collective-permute-start.13) | collective-permute-done | bytes 262176 | tf_op jit(solution)/shard_map/ppermute | solution.py:397
  161.3 1.3 select_select_fusion
  (57 shorter events, 8.0 us)
Async XLA Ops:
  0.6 2.1 %copy-start = (bf16[32,16384]{1,0:T(8,128)(2,1)S(1)}, bf16[32,16384]{1,0:T(8,128)(2,1)}, u32[]{:S(2)}) copy-start(bf16[32,16384]{1,0:T(8,128)(2,1)} %param.15) | copy-start | bytes 3145732
  4.3 52.4 %all-to-all-start = ((bf16[16,128,128]{2,1,0:T(8,128)(2,1)}), bf16[16,128,128]{2,1,0:T(8,128)(2,1)S(1)}, u32[]{:S(2)}, u32[]{:S(2)}) async-start(bf16[16,128,128]{2,1,0:T(8,128)(2,1)} %pad_maximum_fusion), calls=%async_computation | async-start | bytes 1048576 | tf_op jit(solution)/shard_map/all_to_all | solution.py:402
  18.5 9.8 %collective-permute-start.6 = (bf16[8,128,128]{2,1,0:T(8,128)(2,1)S(1)}, bf16[8,128,128]{2,1,0:T(8,128)(2,1)}, u32[]{:S(2)}, u32[]{:S(2)}) collective-permute-start(bf16[8,128,128]{2,1,0:T(8,128)(2,1)S(1)} %reshape.98.own), channel_id=1, source_target_pairs={{0,16},{16,0},{32,48},{48,32},{64,80},{80,64},{96,112},{112,96},{1... | collective-permute-start | bytes 786440 | tf_op jit(solution)/shard_map/ppermute | solution.py:397
  21.9 0.7 copy-start.20
  28.3 0.6 copy-start.14
  30.0 18.3 %collective-permute-start.7 = (bf16[6,128,128]{2,1,0:T(8,128)(2,1)S(1)}, bf16[6,128,128]{2,1,0:T(8,128)(2,1)S(1)}, u32[]{:S(2)}, u32[]{:S(2)}) collective-permute-start(bf16[6,128,128]{2,1,0:T(8,128)(2,1)S(1)} %get-tuple-element.537), channel_id=1, source_target_pairs={{0,32},{16,48},{32,64},{48,80},{64,96},{80,112},{96,128},{112,144}... | collective-permute-start | bytes 589832 | tf_op jit(solution)/shard_map/ppermute | solution.py:383
  33.0 17.1 %collective-permute-start.8 = (bf16[6,128,128]{2,1,0:T(8,128)(2,1)S(1)}, bf16[6,128,128]{2,1,0:T(8,128)(2,1)S(1)}, u32[]{:S(2)}, u32[]{:S(2)}) collective-permute-start(bf16[6,128,128]{2,1,0:T(8,128)(2,1)S(1)} %get-tuple-element.539), channel_id=1, source_target_pairs={{0,480},{16,496},{32,0},{48,16},{64,32},{80,48},{96,64},{112,80},{... | collective-permute-start | bytes 589832 | tf_op jit(solution)/shard_map/ppermute | solution.py:383
  35.9 18.8 %collective-permute-start.9 = (bf16[6,128,128]{2,1,0:T(8,128)(2,1)S(1)}, bf16[6,128,128]{2,1,0:T(8,128)(2,1)S(1)}, u32[]{:S(2)}, u32[]{:S(2)}) collective-permute-start(bf16[6,128,128]{2,1,0:T(8,128)(2,1)S(1)} %get-tuple-element.540), channel_id=1, source_target_pairs={{0,64},{16,80},{32,480},{48,496},{64,128},{80,144},{96,32},{112,48... | collective-permute-start | bytes 589832 | tf_op jit(solution)/shard_map/ppermute | solution.py:383
  50.1 4.7 %copy-start.13 = (s32[16]{0:T(128)S(1)}, s32[16]{0:T(128)}, u32[]{:S(2)}) copy-start(s32[16]{0:T(128)} %shard_map.123.found) | copy-start | bytes 196
  56.7 0.9 copy-start.3
  56.7 1.0 copy-start.8
  56.8 0.9 copy-start.12
  57.7 22.7 %copy-start.1 = (f32[8,256,128]{2,1,0:T(8,128)S(1)}, f32[8,256,128]{2,1,0:T(8,128)}, u32[]{:S(2)}) copy-start(f32[8,256,128]{2,1,0:T(8,128)} %constant.224.clone.spectrum) | copy-start | bytes 3145732
  61.0 19.4 %copy-start.6 = (bf16[2,128,128]{2,1,0:T(8,128)(2,1)S(1)}, bf16[2,128,128]{2,1,0:T(8,128)(2,1)}, u32[]{:S(2)}) copy-start(bf16[2,128,128]{2,1,0:T(8,128)(2,1)} %constant.223.clone.x_bwd) | copy-start | bytes 196612
  61.0 19.4 %copy-start.7 = (bf16[2,128,128]{2,1,0:T(8,128)(2,1)S(1)}, bf16[2,128,128]{2,1,0:T(8,128)(2,1)}, u32[]{:S(2)}) copy-start(bf16[2,128,128]{2,1,0:T(8,128)(2,1)} %constant.222.clone.x_fwd) | copy-start | bytes 196612
  87.1 15.2 %copy-start.2 = (bf16[2,256,256]{2,1,0:T(8,128)(2,1)S(1)}, bf16[2,256,256]{2,1,0:T(8,128)(2,1)}, u32[]{:S(2)}) copy-start(bf16[2,256,256]{2,1,0:T(8,128)(2,1)} %constant.221.clone.y_bwd) | copy-start | bytes 786436
  87.1 15.1 %copy-start.5 = (bf16[2,128,128]{2,1,0:T(8,128)(2,1)S(1)}, bf16[2,128,128]{2,1,0:T(8,128)(2,1)}, u32[]{:S(2)}) copy-start(bf16[2,128,128]{2,1,0:T(8,128)(2,1)} %constant.219.clone.z_bwd) | copy-start | bytes 196612
  87.1 15.1 %copy-start.17 = (bf16[16,128,128]{2,1,0:T(8,128)(2,1)S(1)}, bf16[16,128,128]{2,1,0:T(8,128)(2,1)}, u32[]{:S(2)}) copy-start(bf16[16,128,128]{2,1,0:T(8,128)(2,1)} %get-tuple-element.542.sources) | copy-start | bytes 1572868
  105.4 49.3 %all-to-all-start.3 = ((bf16[16,128,128]{2,1,0:T(8,128)(2,1)}), bf16[16,128,128]{2,1,0:T(8,128)(2,1)S(1)}, u32[]{:S(2)}, u32[]{:S(2)}) async-start(bf16[16,128,128]{2,1,0:T(8,128)(2,1)} %get-tuple-element.550), calls=%async_computation.3 | async-start | bytes 1048576 | tf_op jit(solution)/shard_map/all_to_all | solution.py:402
  112.1 28.2 %collective-permute-start.10 = (bf16[6,128,128]{2,1,0:T(8,128)(2,1)S(1)}, bf16[6,128,128]{2,1,0:T(8,128)(2,1)S(1)}, u32[]{:S(2)}, u32[]{:S(2)}) collective-permute-start(bf16[6,128,128]{2,1,0:T(8,128)(2,1)S(1)} %get-tuple-element.544), channel_id=1, source_target_pairs={{0,480},{16,496},{32,0},{48,16},{64,32},{80,48},{96,64},{112,80},{... | collective-permute-start | bytes 589832 | tf_op jit(solution)/shard_map/ppermute | solution.py:383
  114.2 26.4 %collective-permute-start.11 = (bf16[6,128,128]{2,1,0:T(8,128)(2,1)S(1)}, bf16[6,128,128]{2,1,0:T(8,128)(2,1)S(1)}, u32[]{:S(2)}, u32[]{:S(2)}) collective-permute-start(bf16[6,128,128]{2,1,0:T(8,128)(2,1)S(1)} %get-tuple-element.545), channel_id=1, source_target_pairs={{0,32},{16,48},{32,64},{48,80},{64,96},{80,112},{96,128},{112,144}... | collective-permute-start | bytes 589832 | tf_op jit(solution)/shard_map/ppermute | solution.py:383
  118.0 29.6 %copy-start.15 = (s32[18]{0:T(128)S(1)}, s32[18]{0:T(128)}, u32[]{:S(2)}) copy-start(s32[18]{0:T(128)} %shard_map.122.sent) | copy-start | bytes 220
  118.0 29.6 %collective-permute-start.12 = (bf16[6,128,128]{2,1,0:T(8,128)(2,1)S(1)}, bf16[6,128,128]{2,1,0:T(8,128)(2,1)S(1)}, u32[]{:S(2)}, u32[]{:S(2)}) collective-permute-start(bf16[6,128,128]{2,1,0:T(8,128)(2,1)S(1)} %get-tuple-element.546), channel_id=1, source_target_pairs={{0,448},{16,464},{32,96},{48,112},{64,0},{80,16},{96,160},{112,176... | collective-permute-start | bytes 589832 | tf_op jit(solution)/shard_map/ppermute | solution.py:383
  149.4 10.3 %collective-permute-start.13 = (bf16[8,128,128]{2,1,0:T(8,128)(2,1)}, bf16[8,128,128]{2,1,0:T(8,128)(2,1)S(1)}, u32[]{:S(2)}, u32[]{:S(2)}) collective-permute-start(bf16[8,128,128]{2,1,0:T(8,128)(2,1)} %get-tuple-element.549), channel_id=1, source_target_pairs={{0,16},{16,0},{32,48},{48,32},{64,80},{80,64},{96,112},{112,96},{1... | collective-permute-start | bytes 786440 | tf_op jit(solution)/shard_map/ppermute | solution.py:397
  153.3 1.4 copy-start.16
  153.3 6.4 %copy-start.19 = (f32[8,128,128]{2,1,0:T(8,128)S(1)}, f32[8,128,128]{2,1,0:T(8,128)}, u32[]{:S(2)}) copy-start(f32[8,128,128]{2,1,0:T(8,128)} %get-tuple-element.552) | copy-start | bytes 1572868

commit v13 on v11

--- a/solution.py
+++ b/solution.py
@@ -264,7 +264,7 @@
         square = value * value
         return norm + dot_of(square), power + dot_of(square * spectrum[j])
 
-    norm, power = lax.fori_loop(0, 8, start, (zero, zero))
+    norm, power = lax.fori_loop(0, 8, start, (zero, zero), unroll=4)
     norm, power = jnp.sum(norm), jnp.sum(power)
     steps, ratio = [norm / power], jnp.float32(0.0)
     for sweep in range(SWEEPS - 1):
@@ -284,7 +284,7 @@
             square = r * r
             return new + dot_of(square), power + dot_of(square * lam)
 
-        new, power = lax.fori_loop(0, 8, advance, (zero, zero))
+        new, power = lax.fori_loop(0, 8, advance, (zero, zero), unroll=4)
         new, power = jnp.sum(new), jnp.sum(power)
         ratio = new / norm
         steps.append(new / (power - ratio * new / step))
@@ -300,7 +300,7 @@
         out[:, pl.ds(pl.multiple_of(16 * j, 16), 16), :] = part.astype(out.dtype)
         return carry
 
-    lax.fori_loop(0, 8, finish, 0)
+    lax.fori_loop(0, 8, finish, 0, unroll=4)
 
 
 def term_kernel(place, pair_src, spectra, sources, wanted, z_bwd, y_bwd, terms, shares, queue):
@@ -488,8 +488,6 @@
     near = give_back(found)
     shares = along_ring(shares)
     mine, partner = lax.fori_loop(1, rounds, collect_in, collect(sent, found, near, ()))
-    owned = (mine + across(partner).astype(F32)).astype(BF16).reshape(sources.shape)
-
     (target_rows,) = vmem_call(
         target_kernel,
         [struct((4, ROW, ROW), BF16)],
@@ -502,6 +500,8 @@
     summed = jnp.zeros(targets.shape, BF16)
     for p in range(4):
         summed = jnp.where(slots == ids[p], flat[p][None, :], summed)
+    partner, summed = lax.optimization_barrier((across(partner), summed))
+    owned = (mine + partner.astype(F32)).astype(BF16).reshape(sources.shape)
     return summed, owned
 
 

time: 165 us -> 160 us (0.970)
  the two profiles are of different devices: /device:TPU:64 before, /device:TPU:32 now
where the time goes in v13:
time: 160 us; the launch traced here: 159 us
  starting transfers between devices  51.9 us (32%)
  waiting for transfers between devices  38.5 us (24%)
  blocking collectives  34.4 us (22%)
  Pallas kernels  20.2 us (13%)
  other arithmetic  6.29 us (4%)
  local copies, waits for them, and re-layouts  6.04 us (4%)
  between operations  1.66 us (1%)
    ppermute x6, waiting for transfers between devices, hand_over(): lax.ppermute(packet, 'band', [(2 * z + x, 2 * ((z + sign * move(z)) % RIN...  30.6 us
    ppermute x6, starting transfers between devices, hand_over(): lax.ppermute(packet, 'band', [(2 * z + x, 2 * ((z + sign * move(z)) % RIN...  23.5 us
    all_to_all x2, starting transfers between devices, along_ring(): lax.all_to_all(value, 'band', 0, 0, axis_index_groups=groups, tiled=True)  22.4 us
    all_to_all x1, blocking collectives, per_device(): slabs = lax.all_to_all(spectra, 'dom', 0, 0, tiled=True)  19.3 us
    pallas_call x8, Pallas kernels, vmem_call(): pl.pallas_call(kernel, out_shape=outs, in_specs=[smem] * scalars + [whole...  17.4 us
    all_to_all x1, blocking collectives, per_device(): back = lax.all_to_all(solved, 'dom', 0, 0, tiled=True)  15.1 us
    ppermute x2, waiting for transfers between devices, across(): return lax.ppermute(value, 'band', [(i, i ^ 1) for i in range(32)])  7.96 us
    ppermute x2, starting transfers between devices, across(): return lax.ppermute(value, 'band', [(i, i ^ 1) for i in range(32)])  6.02 us
  transfers between devices with their start and end apart: 10, of which 6 were waited for; matrix products, arithmetic and copies ran while one was open for 4% of the time, Pallas kernels for 6%

profile of v13, /device:TPU:32, one launch (start us, length us, event | category | flops | bytes accessed | tf_op | source)
XLA Modules:
  0.0 159.2 jit_solution(8344287842166892111)
XLA Ops:
  0.6 0.8 reshape.105
  1.5 1.2 reshape.104.own
  4.3 14.2 %all-to-all-start = ((bf16[16,128,128]{2,1,0:T(8,128)(2,1)}), bf16[16,128,128]{2,1,0:T(8,128)(2,1)S(1)}, u32[]{:S(2)}, u32[]{:S(2)}) async-start(bf16[16,128,128]{2,1,0:T(8,128)(2,1)} %pad_maximum_fusion), calls=%async_computation | async-start | bytes 1048576 | tf_op jit(solution)/shard_map/all_to_all | solution.py:402
  18.5 3.4 %collective-permute-start.6 = (bf16[8,128,128]{2,1,0:T(8,128)(2,1)S(1)}, bf16[8,128,128]{2,1,0:T(8,128)(2,1)}, u32[]{:S(2)}, u32[]{:S(2)}) collective-permute-start(bf16[8,128,128]{2,1,0:T(8,128)(2,1)S(1)} %reshape.104.own), channel_id=1, source_target_pairs={{0,16},{16,0},{32,48},{48,32},{64,80},{80,64},{96,112},{112,96},{1... | collective-permute-start | bytes 786440 | tf_op jit(solution)/shard_map/ppermute | solution.py:397
  22.6 1.4 shard_map.123.found
  24.0 1.5 shard_map.122.sent
  25.5 2.8 %collective-permute-done.6.other = bf16[8,128,128]{2,1,0:T(8,128)(2,1)} collective-permute-done((bf16[8,128,128]{2,1,0:T(8,128)(2,1)S(1)}, bf16[8,128,128]{2,1,0:T(8,128)(2,1)}, u32[]{:S(2)}, u32[]{:S(2)}) %collective-permute-start.6) | collective-permute-done | bytes 262176 | tf_op jit(solution)/shard_map/ppermute | solution.py:397
  28.8 1.1 shard_map.124
  30.0 2.9 %collective-permute-start.7 = (bf16[6,128,128]{2,1,0:T(8,128)(2,1)S(1)}, bf16[6,128,128]{2,1,0:T(8,128)(2,1)S(1)}, u32[]{:S(2)}, u32[]{:S(2)}) collective-permute-start(bf16[6,128,128]{2,1,0:T(8,128)(2,1)S(1)} %get-tuple-element.536), channel_id=1, source_target_pairs={{0,32},{16,48},{32,64},{48,80},{64,96},{80,112},{96,128},{112,144}... | collective-permute-start | bytes 589832 | tf_op jit(solution)/shard_map/ppermute | solution.py:383
  32.9 2.9 %collective-permute-start.8 = (bf16[6,128,128]{2,1,0:T(8,128)(2,1)S(1)}, bf16[6,128,128]{2,1,0:T(8,128)(2,1)S(1)}, u32[]{:S(2)}, u32[]{:S(2)}) collective-permute-start(bf16[6,128,128]{2,1,0:T(8,128)(2,1)S(1)} %get-tuple-element.538), channel_id=1, source_target_pairs={{0,480},{16,496},{32,0},{48,16},{64,32},{80,48},{96,64},{112,80},{... | collective-permute-start | bytes 589832 | tf_op jit(solution)/shard_map/ppermute | solution.py:383
  35.9 6.7 %collective-permute-start.9 = (bf16[6,128,128]{2,1,0:T(8,128)(2,1)S(1)}, bf16[6,128,128]{2,1,0:T(8,128)(2,1)S(1)}, u32[]{:S(2)}, u32[]{:S(2)}) collective-permute-start(bf16[6,128,128]{2,1,0:T(8,128)(2,1)S(1)} %get-tuple-element.539), channel_id=1, source_target_pairs={{0,64},{16,80},{32,480},{48,496},{64,128},{80,144},{96,32},{112,48... | collective-permute-start | bytes 589832 | tf_op jit(solution)/shard_map/ppermute | solution.py:383
  42.5 5.7 %collective-permute-done.7.refs_0_ = bf16[6,128,128]{2,1,0:T(8,128)(2,1)S(1)} collective-permute-done((bf16[6,128,128]{2,1,0:T(8,128)(2,1)S(1)}, bf16[6,128,128]{2,1,0:T(8,128)(2,1)S(1)}, u32[]{:S(2)}, u32[]{:S(2)}) %collective-permute-start.7) | collective-permute-done | bytes 196640 | tf_op jit(solution)/shard_map/ppermute | solution.py:383
  50.0 4.6 %collective-permute-done.9.refs_2_ = bf16[6,128,128]{2,1,0:T(8,128)(2,1)S(1)} collective-permute-done((bf16[6,128,128]{2,1,0:T(8,128)(2,1)S(1)}, bf16[6,128,128]{2,1,0:T(8,128)(2,1)S(1)}, u32[]{:S(2)}, u32[]{:S(2)}) %collective-permute-start.9) | collective-permute-done | bytes 196640 | tf_op jit(solution)/shard_map/ppermute | solution.py:383
  54.7 2.0 %shard_map.125 = bf16[16,128,128]{2,1,0:T(8,128)(2,1)} custom-call(s32[16]{0:T(128)S(1)} %copy-done.13, bf16[8,128,128]{2,1,0:T(8,128)(2,1)S(1)} %reshape.104.own, bf16[8,128,128]{2,1,0:T(8,128)(2,1)} %collective-permute-done.6.other, bf16[6,128,128]{2,1,0:T(8,128)(2,1)S(1)} %collective-permute-done.7.refs_0_, ...), custom_call_target="tpu_custom_call" | custom-call | tf_op jit(solution)/shard_map/pallas_call | solution.py:99
  56.7 0.9 copy-done.3
  57.6 2.7 %shard_map.126 = bf16[16,128,128]{2,1,0:T(8,128)(2,1)S(1)} custom-call(s32[3]{0:T(128)S(1)} %copy-done.12, s32[2,64]{1,0:T(2,128)S(1)} %get-tuple-element.800, bf16[16,128,128]{2,1,0:T(8,128)(2,1)} %get-tuple-element.541.sources, bf16[16,128,128]{2,1,0:T(8,128)(2,1)S(1)} %all-to-all-done.wanted, bf16[2,128,128]{2,1,0:T(8,128)(2,1)S(1)} %copy-done.8, ...), custom_call_target="tpu_custom_call" | custom-call | tf_op jit(solution)/shard_map/pallas_call | solution.py:99
  60.3 19.3 %all_to_all.20.slabs = bf16[16,128,128]{2,1,0:T(8,128)(2,1)S(1)} all-to-all(bf16[16,128,128]{2,1,0:T(8,128)(2,1)S(1)} %shard_map.126), channel_id=1, replica_groups=mesh['band'=32,'dom'=16] {'dom'}, dimensions={0} | all-to-all | bytes 1048576 | tf_op jit(solution)/shard_map/all_to_all | solution.py:459
  79.7 5.7 %shard_map.127 = bf16[16,128,128]{2,1,0:T(8,128)(2,1)S(1)} custom-call(bf16[16,128,128]{2,1,0:T(8,128)(2,1)S(1)} %all_to_all.20.slabs, f32[8,256,128]{2,1,0:T(8,128)S(1)} %copy-done.1, bf16[2,128,128]{2,1,0:T(8,128)(2,1)S(1)} %copy-done.7, bf16[2,128,128]{2,1,0:T(8,128)(2,1)S(1)} %copy-done.6), custom_call_target="tpu_custom_call" | custom-call | tf_op jit(solution)/shard_map/pallas_call | solution.py:99
  85.4 15.1 %all_to_all.21.spectra = bf16[16,128,128]{2,1,0:T(8,128)(2,1)S(1)} all-to-all(bf16[16,128,128]{2,1,0:T(8,128)(2,1)S(1)} %shard_map.127), channel_id=1, replica_groups=mesh['band'=32,'dom'=16] {'dom'}, dimensions={0} | all-to-all | bytes 1048576 | tf_op jit(solution)/shard_map/all_to_all | solution.py:466
  100.5 2.7 %shard_map.128 = (bf16[16,128,128]{2,1,0:T(8,128)(2,1)S(1)}, bf16[16,128,128]{2,1,0:T(8,128)(2,1)}) custom-call(s32[3]{0:T(128)S(1)} %copy-done.12, s32[2,64]{1,0:T(2,128)S(1)} %get-tuple-element.800, bf16[16,128,128]{2,1,0:T(8,128)(2,1)S(1)} %all_to_all.21.spectra, bf16[16,128,128]{2,1,0:T(8,128)(2,1)S(1)} %copy-done.17, ...), custom_call_target="tpu_custom_call" | custom-call | tf_op jit(solution)/shard_map/pallas_call | solution.py:99
  103.2 8.2 %all-to-all-start.3 = ((bf16[16,128,128]{2,1,0:T(8,128)(2,1)}), bf16[16,128,128]{2,1,0:T(8,128)(2,1)S(1)}, u32[]{:S(2)}, u32[]{:S(2)}) async-start(bf16[16,128,128]{2,1,0:T(8,128)(2,1)} %get-tuple-element.550), calls=%async_computation.3 | async-start | bytes 1048576 | tf_op jit(solution)/shard_map/all_to_all | solution.py:402
  112.8 2.2 %collective-permute-start.10 = (bf16[6,128,128]{2,1,0:T(8,128)(2,1)S(1)}, bf16[6,128,128]{2,1,0:T(8,128)(2,1)S(1)}, u32[]{:S(2)}, u32[]{:S(2)}) collective-permute-start(bf16[6,128,128]{2,1,0:T(8,128)(2,1)S(1)} %get-tuple-element.544), channel_id=1, source_target_pairs={{0,480},{16,496},{32,0},{48,16},{64,32},{80,48},{96,64},{112,80},{... | collective-permute-start | bytes 589832 | tf_op jit(solution)/shard_map/ppermute | solution.py:383
  115.0 3.7 %collective-permute-start.11 = (bf16[6,128,128]{2,1,0:T(8,128)(2,1)S(1)}, bf16[6,128,128]{2,1,0:T(8,128)(2,1)S(1)}, u32[]{:S(2)}, u32[]{:S(2)}) collective-permute-start(bf16[6,128,128]{2,1,0:T(8,128)(2,1)S(1)} %get-tuple-element.545), channel_id=1, source_target_pairs={{0,32},{16,48},{32,64},{48,80},{64,96},{80,112},{96,128},{112,144}... | collective-permute-start | bytes 589832 | tf_op jit(solution)/shard_map/ppermute | solution.py:383
  118.7 5.2 %collective-permute-start.12 = (bf16[6,128,128]{2,1,0:T(8,128)(2,1)S(1)}, bf16[6,128,128]{2,1,0:T(8,128)(2,1)S(1)}, u32[]{:S(2)}, u32[]{:S(2)}) collective-permute-start(bf16[6,128,128]{2,1,0:T(8,128)(2,1)S(1)} %get-tuple-element.546), channel_id=1, source_target_pairs={{0,448},{16,464},{32,96},{48,112},{64,0},{80,16},{96,160},{112,176... | collective-permute-start | bytes 589832 | tf_op jit(solution)/shard_map/ppermute | solution.py:383
  123.8 1.3 iota_compare_fusion.2
  125.2 1.2 iota_compare_fusion
  126.4 12.7 %collective-permute-done.10.refs_0_ = bf16[6,128,128]{2,1,0:T(8,128)(2,1)S(1)} collective-permute-done((bf16[6,128,128]{2,1,0:T(8,128)(2,1)S(1)}, bf16[6,128,128]{2,1,0:T(8,128)(2,1)S(1)}, u32[]{:S(2)}, u32[]{:S(2)}) %collective-permute-start.10) | collective-permute-done | bytes 196640 | tf_op jit(solution)/shard_map/ppermute | solution.py:383
  139.0 7.5 %collective-permute-done.12.refs_2_ = bf16[6,128,128]{2,1,0:T(8,128)(2,1)S(1)} collective-permute-done((bf16[6,128,128]{2,1,0:T(8,128)(2,1)S(1)}, bf16[6,128,128]{2,1,0:T(8,128)(2,1)S(1)}, u32[]{:S(2)}, u32[]{:S(2)}) %collective-permute-start.12) | collective-permute-done | bytes 196640 | tf_op jit(solution)/shard_map/ppermute | solution.py:383
  146.6 1.8 %shard_map.130 = (f32[8,128,128]{2,1,0:T(8,128)}, bf16[8,128,128]{2,1,0:T(8,128)(2,1)}) custom-call(s32[18]{0:T(128)S(1)} %copy-done.15, s32[16]{0:T(128)S(1)} %copy-done.13, bf16[16,128,128]{2,1,0:T(8,128)(2,1)S(1)} %get-tuple-element.752.terms, bf16[6,128,128]{2,1,0:T(8,128)(2,1)S(1)} %collective-permute-done.10.refs_0_, ...), custom_call_target="tpu_custom_call" | custom-call | tf_op jit(solution)/shard_map/pallas_call | solution.py:99
  148.4 2.6 %collective-permute-start.13 = (bf16[8,128,128]{2,1,0:T(8,128)(2,1)}, bf16[8,128,128]{2,1,0:T(8,128)(2,1)S(1)}, u32[]{:S(2)}, u32[]{:S(2)}) collective-permute-start(bf16[8,128,128]{2,1,0:T(8,128)(2,1)} %get-tuple-element.549), channel_id=1, source_target_pairs={{0,16},{16,0},{32,48},{48,32},{64,80},{80,64},{96,112},{112,96},{1... | collective-permute-start | bytes 786440 | tf_op jit(solution)/shard_map/ppermute | solution.py:397
  151.8 1.3 select_select_fusion
  153.1 5.2 %collective-permute-done.13 = bf16[8,128,128]{2,1,0:T(8,128)(2,1)S(1)} collective-permute-done((bf16[8,128,128]{2,1,0:T(8,128)(2,1)}, bf16[8,128,128]{2,1,0:T(8,128)(2,1)S(1)}, u32[]{:S(2)}, u32[]{:S(2)}) %collective-permute-start.13) | collective-permute-done | bytes 262176 | tf_op jit(solution)/shard_map/ppermute | solution.py:397
  (56 shorter events, 6.9 us)
Async XLA Ops:
  0.6 2.1 %copy-start = (bf16[32,16384]{1,0:T(8,128)(2,1)S(1)}, bf16[32,16384]{1,0:T(8,128)(2,1)}, u32[]{:S(2)}) copy-start(bf16[32,16384]{1,0:T(8,128)(2,1)} %param.15) | copy-start | bytes 3145732
  4.3 52.3 %all-to-all-start = ((bf16[16,128,128]{2,1,0:T(8,128)(2,1)}), bf16[16,128,128]{2,1,0:T(8,128)(2,1)S(1)}, u32[]{:S(2)}, u32[]{:S(2)}) async-start(bf16[16,128,128]{2,1,0:T(8,128)(2,1)} %pad_maximum_fusion), calls=%async_computation | async-start | bytes 1048576 | tf_op jit(solution)/shard_map/all_to_all | solution.py:402
  18.5 9.8 %collective-permute-start.6 = (bf16[8,128,128]{2,1,0:T(8,128)(2,1)S(1)}, bf16[8,128,128]{2,1,0:T(8,128)(2,1)}, u32[]{:S(2)}, u32[]{:S(2)}) collective-permute-start(bf16[8,128,128]{2,1,0:T(8,128)(2,1)S(1)} %reshape.104.own), channel_id=1, source_target_pairs={{0,16},{16,0},{32,48},{48,32},{64,80},{80,64},{96,112},{112,96},{1... | collective-permute-start | bytes 786440 | tf_op jit(solution)/shard_map/ppermute | solution.py:397
  21.9 0.7 copy-start.20
  28.3 0.6 copy-start.14
  30.0 18.3 %collective-permute-start.7 = (bf16[6,128,128]{2,1,0:T(8,128)(2,1)S(1)}, bf16[6,128,128]{2,1,0:T(8,128)(2,1)S(1)}, u32[]{:S(2)}, u32[]{:S(2)}) collective-permute-start(bf16[6,128,128]{2,1,0:T(8,128)(2,1)S(1)} %get-tuple-element.536), channel_id=1, source_target_pairs={{0,32},{16,48},{32,64},{48,80},{64,96},{80,112},{96,128},{112,144}... | collective-permute-start | bytes 589832 | tf_op jit(solution)/shard_map/ppermute | solution.py:383
  32.9 17.1 %collective-permute-start.8 = (bf16[6,128,128]{2,1,0:T(8,128)(2,1)S(1)}, bf16[6,128,128]{2,1,0:T(8,128)(2,1)S(1)}, u32[]{:S(2)}, u32[]{:S(2)}) collective-permute-start(bf16[6,128,128]{2,1,0:T(8,128)(2,1)S(1)} %get-tuple-element.538), channel_id=1, source_target_pairs={{0,480},{16,496},{32,0},{48,16},{64,32},{80,48},{96,64},{112,80},{... | collective-permute-start | bytes 589832 | tf_op jit(solution)/shard_map/ppermute | solution.py:383
  35.9 18.8 %collective-permute-start.9 = (bf16[6,128,128]{2,1,0:T(8,128)(2,1)S(1)}, bf16[6,128,128]{2,1,0:T(8,128)(2,1)S(1)}, u32[]{:S(2)}, u32[]{:S(2)}) collective-permute-start(bf16[6,128,128]{2,1,0:T(8,128)(2,1)S(1)} %get-tuple-element.539), channel_id=1, source_target_pairs={{0,64},{16,80},{32,480},{48,496},{64,128},{80,144},{96,32},{112,48... | collective-permute-start | bytes 589832 | tf_op jit(solution)/shard_map/ppermute | solution.py:383
  50.0 4.7 %copy-start.13 = (s32[16]{0:T(128)S(1)}, s32[16]{0:T(128)}, u32[]{:S(2)}) copy-start(s32[16]{0:T(128)} %shard_map.123.found) | copy-start | bytes 196
  56.6 0.9 copy-start.3
  56.6 1.0 copy-start.8
  56.6 0.9 copy-start.12
  57.6 22.1 %copy-start.1 = (f32[8,256,128]{2,1,0:T(8,128)S(1)}, f32[8,256,128]{2,1,0:T(8,128)}, u32[]{:S(2)}) copy-start(f32[8,256,128]{2,1,0:T(8,128)} %constant.224.clone.spectrum) | copy-start | bytes 3145732
  60.3 19.4 %copy-start.6 = (bf16[2,128,128]{2,1,0:T(8,128)(2,1)S(1)}, bf16[2,128,128]{2,1,0:T(8,128)(2,1)}, u32[]{:S(2)}) copy-start(bf16[2,128,128]{2,1,0:T(8,128)(2,1)} %constant.223.clone.x_bwd) | copy-start | bytes 196612
  60.3 19.4 %copy-start.7 = (bf16[2,128,128]{2,1,0:T(8,128)(2,1)S(1)}, bf16[2,128,128]{2,1,0:T(8,128)(2,1)}, u32[]{:S(2)}) copy-start(bf16[2,128,128]{2,1,0:T(8,128)(2,1)} %constant.222.clone.x_fwd) | copy-start | bytes 196612
  85.4 15.2 %copy-start.2 = (bf16[2,256,256]{2,1,0:T(8,128)(2,1)S(1)}, bf16[2,256,256]{2,1,0:T(8,128)(2,1)}, u32[]{:S(2)}) copy-start(bf16[2,256,256]{2,1,0:T(8,128)(2,1)} %constant.221.clone.y_bwd) | copy-start | bytes 786436
  85.4 15.1 %copy-start.5 = (bf16[2,128,128]{2,1,0:T(8,128)(2,1)S(1)}, bf16[2,128,128]{2,1,0:T(8,128)(2,1)}, u32[]{:S(2)}) copy-start(bf16[2,128,128]{2,1,0:T(8,128)(2,1)} %constant.219.clone.z_bwd) | copy-start | bytes 196612
  85.4 15.1 %copy-start.17 = (bf16[16,128,128]{2,1,0:T(8,128)(2,1)S(1)}, bf16[16,128,128]{2,1,0:T(8,128)(2,1)}, u32[]{:S(2)}) copy-start(bf16[16,128,128]{2,1,0:T(8,128)(2,1)} %get-tuple-element.541.sources) | copy-start | bytes 1572868
  103.2 47.9 %all-to-all-start.3 = ((bf16[16,128,128]{2,1,0:T(8,128)(2,1)}), bf16[16,128,128]{2,1,0:T(8,128)(2,1)S(1)}, u32[]{:S(2)}, u32[]{:S(2)}) async-start(bf16[16,128,128]{2,1,0:T(8,128)(2,1)} %get-tuple-element.550), calls=%async_computation.3 | async-start | bytes 1048576 | tf_op jit(solution)/shard_map/all_to_all | solution.py:402
  112.8 26.2 %collective-permute-start.10 = (bf16[6,128,128]{2,1,0:T(8,128)(2,1)S(1)}, bf16[6,128,128]{2,1,0:T(8,128)(2,1)S(1)}, u32[]{:S(2)}, u32[]{:S(2)}) collective-permute-start(bf16[6,128,128]{2,1,0:T(8,128)(2,1)S(1)} %get-tuple-element.544), channel_id=1, source_target_pairs={{0,480},{16,496},{32,0},{48,16},{64,32},{80,48},{96,64},{112,80},{... | collective-permute-start | bytes 589832 | tf_op jit(solution)/shard_map/ppermute | solution.py:383
  115.0 24.1 %collective-permute-start.11 = (bf16[6,128,128]{2,1,0:T(8,128)(2,1)S(1)}, bf16[6,128,128]{2,1,0:T(8,128)(2,1)S(1)}, u32[]{:S(2)}, u32[]{:S(2)}) collective-permute-start(bf16[6,128,128]{2,1,0:T(8,128)(2,1)S(1)} %get-tuple-element.545), channel_id=1, source_target_pairs={{0,32},{16,48},{32,64},{48,80},{64,96},{80,112},{96,128},{112,144}... | collective-permute-start | bytes 589832 | tf_op jit(solution)/shard_map/ppermute | solution.py:383
  118.7 27.9 %collective-permute-start.12 = (bf16[6,128,128]{2,1,0:T(8,128)(2,1)S(1)}, bf16[6,128,128]{2,1,0:T(8,128)(2,1)S(1)}, u32[]{:S(2)}, u32[]{:S(2)}) collective-permute-start(bf16[6,128,128]{2,1,0:T(8,128)(2,1)S(1)} %get-tuple-element.546), channel_id=1, source_target_pairs={{0,448},{16,464},{32,96},{48,112},{64,0},{80,16},{96,160},{112,176... | collective-permute-start | bytes 589832 | tf_op jit(solution)/shard_map/ppermute | solution.py:383
  125.2 21.4 %copy-start.15 = (s32[18]{0:T(128)S(1)}, s32[18]{0:T(128)}, u32[]{:S(2)}) copy-start(s32[18]{0:T(128)} %shard_map.122.sent) | copy-start | bytes 220
  148.4 2.7 %copy-start.16 = (s32[2,2]{1,0:T(2,128)S(1)}, s32[2,2]{1,0:T(2,128)}, u32[]{:S(2)}) copy-start(s32[2,2]{1,0:T(2,128)} %pair_tgt.1) | copy-start | bytes 52
  148.4 9.9 %collective-permute-start.13 = (bf16[8,128,128]{2,1,0:T(8,128)(2,1)}, bf16[8,128,128]{2,1,0:T(8,128)(2,1)S(1)}, u32[]{:S(2)}, u32[]{:S(2)}) collective-permute-start(bf16[8,128,128]{2,1,0:T(8,128)(2,1)} %get-tuple-element.549), channel_id=1, source_target_pairs={{0,16},{16,0},{32,48},{48,32},{64,80},{80,64},{96,112},{112,96},{1... | collective-permute-start | bytes 786440 | tf_op jit(solution)/shard_map/ppermute | solution.py:397
  151.8 6.5 %copy-start.19 = (f32[8,128,128]{2,1,0:T(8,128)S(1)}, f32[8,128,128]{2,1,0:T(8,128)}, u32[]{:S(2)}) copy-start(f32[8,128,128]{2,1,0:T(8,128)} %get-tuple-element.552) | copy-start | bytes 1572868

commit v14 on v13

--- a/solution.py
+++ b/solution.py
@@ -264,7 +264,7 @@
         square = value * value
         return norm + dot_of(square), power + dot_of(square * spectrum[j])
 
-    norm, power = lax.fori_loop(0, 8, start, (zero, zero), unroll=4)
+    norm, power = lax.fori_loop(0, 8, start, (zero, zero), unroll=8)
     norm, power = jnp.sum(norm), jnp.sum(power)
     steps, ratio = [norm / power], jnp.float32(0.0)
     for sweep in range(SWEEPS - 1):
@@ -284,7 +284,7 @@
             square = r * r
             return new + dot_of(square), power + dot_of(square * lam)
 
-        new, power = lax.fori_loop(0, 8, advance, (zero, zero), unroll=4)
+        new, power = lax.fori_loop(0, 8, advance, (zero, zero), unroll=8)
         new, power = jnp.sum(new), jnp.sum(power)
         ratio = new / norm
         steps.append(new / (power - ratio * new / step))
@@ -300,7 +300,7 @@
         out[:, pl.ds(pl.multiple_of(16 * j, 16), 16), :] = part.astype(out.dtype)
         return carry
 
-    lax.fori_loop(0, 8, finish, 0, unroll=4)
+    lax.fori_loop(0, 8, finish, 0, unroll=8)
 
 
 def term_kernel(place, pair_src, spectra, sources, wanted, z_bwd, y_bwd, terms, shares, queue):

time: 160 us -> 161 us (level)
  the two profiles are of different devices: /device:TPU:32 before, /device:TPU:1 now
where the time goes in v14:
time: 161 us; the launch traced here: 158 us
  starting transfers between devices  49.8 us (31%)
  waiting for transfers between devices  36.3 us (23%)
  blocking collectives  34.3 us (21%)
  Pallas kernels  24 us (15%)
  other arithmetic  6.29 us (4%)
  local copies, waits for them, and re-layouts  6.04 us (4%)
  between operations  1.65 us (1%)
    ppermute x6, waiting for transfers between devices, hand_over(): lax.ppermute(packet, 'band', [(2 * z + x, 2 * ((z + sign * move(z)) % RIN...  29.8 us
    ppermute x6, starting transfers between devices, hand_over(): lax.ppermute(packet, 'band', [(2 * z + x, 2 * ((z + sign * move(z)) % RIN...  23.6 us
    pallas_call x8, Pallas kernels, vmem_call(): pl.pallas_call(kernel, out_shape=outs, in_specs=[smem] * scalars + [whole...  21.1 us
    all_to_all x2, starting transfers between devices, along_ring(): lax.all_to_all(value, 'band', 0, 0, axis_index_groups=groups, tiled=True)  19.2 us
    all_to_all x1, blocking collectives, per_device(): slabs = lax.all_to_all(spectra, 'dom', 0, 0, tiled=True)  19.2 us
    all_to_all x1, blocking collectives, per_device(): back = lax.all_to_all(solved, 'dom', 0, 0, tiled=True)  15.1 us
    ppermute x2, starting transfers between devices, across(): return lax.ppermute(value, 'band', [(i, i ^ 1) for i in range(32)])  6.98 us
    ppermute x2, waiting for transfers between devices, across(): return lax.ppermute(value, 'band', [(i, i ^ 1) for i in range(32)])  6.52 us
  transfers between devices with their start and end apart: 10, of which 7 were waited for; matrix products, arithmetic and copies ran while one was open for 4% of the time, Pallas kernels for 6%

profile of v14, /device:TPU:1, one launch (start us, length us, event | category | flops | bytes accessed | tf_op | source)
XLA Modules:
  0.0 158.4 jit_solution(8881453381422269580)
XLA Ops:
  1.5 1.2 reshape.104.own
  4.3 15.6 %all-to-all-start = ((bf16[16,128,128]{2,1,0:T(8,128)(2,1)}), bf16[16,128,128]{2,1,0:T(8,128)(2,1)S(1)}, u32[]{:S(2)}, u32[]{:S(2)}) async-start(bf16[16,128,128]{2,1,0:T(8,128)(2,1)} %pad_maximum_fusion), calls=%async_computation | async-start | bytes 1048576 | tf_op jit(solution)/shard_map/all_to_all | solution.py:402
  19.9 3.1 %collective-permute-start.6 = (bf16[8,128,128]{2,1,0:T(8,128)(2,1)S(1)}, bf16[8,128,128]{2,1,0:T(8,128)(2,1)}, u32[]{:S(2)}, u32[]{:S(2)}) collective-permute-start(bf16[8,128,128]{2,1,0:T(8,128)(2,1)S(1)} %reshape.104.own), channel_id=1, source_target_pairs={{0,16},{16,0},{32,48},{48,32},{64,80},{80,64},{96,112},{112,96},{1... | collective-permute-start | bytes 786440 | tf_op jit(solution)/shard_map/ppermute | solution.py:397
  23.8 1.4 shard_map.123.found
  25.2 1.5 shard_map.122.sent
  26.7 2.1 %collective-permute-done.6.other = bf16[8,128,128]{2,1,0:T(8,128)(2,1)} collective-permute-done((bf16[8,128,128]{2,1,0:T(8,128)(2,1)S(1)}, bf16[8,128,128]{2,1,0:T(8,128)(2,1)}, u32[]{:S(2)}, u32[]{:S(2)}) %collective-permute-start.6) | collective-permute-done | bytes 262176 | tf_op jit(solution)/shard_map/ppermute | solution.py:397
  29.4 1.1 shard_map.124
  30.5 2.6 %collective-permute-start.7 = (bf16[6,128,128]{2,1,0:T(8,128)(2,1)S(1)}, bf16[6,128,128]{2,1,0:T(8,128)(2,1)S(1)}, u32[]{:S(2)}, u32[]{:S(2)}) collective-permute-start(bf16[6,128,128]{2,1,0:T(8,128)(2,1)S(1)} %get-tuple-element.536), channel_id=1, source_target_pairs={{0,32},{16,48},{32,64},{48,80},{64,96},{80,112},{96,128},{112,144}... | collective-permute-start | bytes 589832 | tf_op jit(solution)/shard_map/ppermute | solution.py:383
  33.2 4.9 %collective-permute-start.8 = (bf16[6,128,128]{2,1,0:T(8,128)(2,1)S(1)}, bf16[6,128,128]{2,1,0:T(8,128)(2,1)S(1)}, u32[]{:S(2)}, u32[]{:S(2)}) collective-permute-start(bf16[6,128,128]{2,1,0:T(8,128)(2,1)S(1)} %get-tuple-element.538), channel_id=1, source_target_pairs={{0,480},{16,496},{32,0},{48,16},{64,32},{80,48},{96,64},{112,80},{... | collective-permute-start | bytes 589832 | tf_op jit(solution)/shard_map/ppermute | solution.py:383
  38.1 1.9 %collective-permute-start.9 = (bf16[6,128,128]{2,1,0:T(8,128)(2,1)S(1)}, bf16[6,128,128]{2,1,0:T(8,128)(2,1)S(1)}, u32[]{:S(2)}, u32[]{:S(2)}) collective-permute-start(bf16[6,128,128]{2,1,0:T(8,128)(2,1)S(1)} %get-tuple-element.539), channel_id=1, source_target_pairs={{0,64},{16,80},{32,480},{48,496},{64,128},{80,144},{96,32},{112,48... | collective-permute-start | bytes 589832 | tf_op jit(solution)/shard_map/ppermute | solution.py:383
  40.1 11.4 %collective-permute-done.7.refs_0_ = bf16[6,128,128]{2,1,0:T(8,128)(2,1)S(1)} collective-permute-done((bf16[6,128,128]{2,1,0:T(8,128)(2,1)S(1)}, bf16[6,128,128]{2,1,0:T(8,128)(2,1)S(1)}, u32[]{:S(2)}, u32[]{:S(2)}) %collective-permute-start.7) | collective-permute-done | bytes 196640 | tf_op jit(solution)/shard_map/ppermute | solution.py:383
  53.2 3.1 %collective-permute-done.9.refs_2_ = bf16[6,128,128]{2,1,0:T(8,128)(2,1)S(1)} collective-permute-done((bf16[6,128,128]{2,1,0:T(8,128)(2,1)S(1)}, bf16[6,128,128]{2,1,0:T(8,128)(2,1)S(1)}, u32[]{:S(2)}, u32[]{:S(2)}) %collective-permute-start.9) | collective-permute-done | bytes 196640 | tf_op jit(solution)/shard_map/ppermute | solution.py:383
  56.2 2.1 %shard_map.125 = bf16[16,128,128]{2,1,0:T(8,128)(2,1)} custom-call(s32[16]{0:T(128)S(1)} %copy-done.13, bf16[8,128,128]{2,1,0:T(8,128)(2,1)S(1)} %reshape.104.own, bf16[8,128,128]{2,1,0:T(8,128)(2,1)} %collective-permute-done.6.other, bf16[6,128,128]{2,1,0:T(8,128)(2,1)S(1)} %collective-permute-done.7.refs_0_, ...), custom_call_target="tpu_custom_call" | custom-call | tf_op jit(solution)/shard_map/pallas_call | solution.py:99
  58.3 0.9 copy-done.3
  59.2 3.9 %shard_map.126 = bf16[16,128,128]{2,1,0:T(8,128)(2,1)S(1)} custom-call(s32[3]{0:T(128)S(1)} %copy-done.12, s32[2,64]{1,0:T(2,128)S(1)} %get-tuple-element.800, bf16[16,128,128]{2,1,0:T(8,128)(2,1)} %get-tuple-element.541.sources, bf16[16,128,128]{2,1,0:T(8,128)(2,1)S(1)} %all-to-all-done.wanted, bf16[2,128,128]{2,1,0:T(8,128)(2,1)S(1)} %copy-done.8, ...), custom_call_target="tpu_custom_call" | custom-call | tf_op jit(solution)/shard_map/pallas_call | solution.py:99
  63.2 19.2 %all_to_all.20.slabs = bf16[16,128,128]{2,1,0:T(8,128)(2,1)S(1)} all-to-all(bf16[16,128,128]{2,1,0:T(8,128)(2,1)S(1)} %shard_map.126), channel_id=1, replica_groups=mesh['band'=32,'dom'=16] {'dom'}, dimensions={0} | all-to-all | bytes 1048576 | tf_op jit(solution)/shard_map/all_to_all | solution.py:459
  82.4 6.9 %shard_map.127 = bf16[16,128,128]{2,1,0:T(8,128)(2,1)S(1)} custom-call(bf16[16,128,128]{2,1,0:T(8,128)(2,1)S(1)} %all_to_all.20.slabs, f32[8,256,128]{2,1,0:T(8,128)S(1)} %copy-done.1, bf16[2,128,128]{2,1,0:T(8,128)(2,1)S(1)} %copy-done.7, bf16[2,128,128]{2,1,0:T(8,128)(2,1)S(1)} %copy-done.6), custom_call_target="tpu_custom_call" | custom-call | tf_op jit(solution)/shard_map/pallas_call | solution.py:99
  89.3 15.1 %all_to_all.21.spectra = bf16[16,128,128]{2,1,0:T(8,128)(2,1)S(1)} all-to-all(bf16[16,128,128]{2,1,0:T(8,128)(2,1)S(1)} %shard_map.127), channel_id=1, replica_groups=mesh['band'=32,'dom'=16] {'dom'}, dimensions={0} | all-to-all | bytes 1048576 | tf_op jit(solution)/shard_map/all_to_all | solution.py:466
  104.5 3.7 %shard_map.128 = (bf16[16,128,128]{2,1,0:T(8,128)(2,1)S(1)}, bf16[16,128,128]{2,1,0:T(8,128)(2,1)}) custom-call(s32[3]{0:T(128)S(1)} %copy-done.12, s32[2,64]{1,0:T(2,128)S(1)} %get-tuple-element.800, bf16[16,128,128]{2,1,0:T(8,128)(2,1)S(1)} %all_to_all.21.spectra, bf16[16,128,128]{2,1,0:T(8,128)(2,1)S(1)} %copy-done.17, ...), custom_call_target="tpu_custom_call" | custom-call | tf_op jit(solution)/shard_map/pallas_call | solution.py:99
  108.2 3.5 %all-to-all-start.3 = ((bf16[16,128,128]{2,1,0:T(8,128)(2,1)}), bf16[16,128,128]{2,1,0:T(8,128)(2,1)S(1)}, u32[]{:S(2)}, u32[]{:S(2)}) async-start(bf16[16,128,128]{2,1,0:T(8,128)(2,1)} %get-tuple-element.550), calls=%async_computation.3 | async-start | bytes 1048576 | tf_op jit(solution)/shard_map/all_to_all | solution.py:402
  113.3 7.1 %collective-permute-start.10 = (bf16[6,128,128]{2,1,0:T(8,128)(2,1)S(1)}, bf16[6,128,128]{2,1,0:T(8,128)(2,1)S(1)}, u32[]{:S(2)}, u32[]{:S(2)}) collective-permute-start(bf16[6,128,128]{2,1,0:T(8,128)(2,1)S(1)} %get-tuple-element.544), channel_id=1, source_target_pairs={{0,480},{16,496},{32,0},{48,16},{64,32},{80,48},{96,64},{112,80},{... | collective-permute-start | bytes 589832 | tf_op jit(solution)/shard_map/ppermute | solution.py:383
  120.4 1.9 %collective-permute-start.11 = (bf16[6,128,128]{2,1,0:T(8,128)(2,1)S(1)}, bf16[6,128,128]{2,1,0:T(8,128)(2,1)S(1)}, u32[]{:S(2)}, u32[]{:S(2)}) collective-permute-start(bf16[6,128,128]{2,1,0:T(8,128)(2,1)S(1)} %get-tuple-element.545), channel_id=1, source_target_pairs={{0,32},{16,48},{32,64},{48,80},{64,96},{80,112},{96,128},{112,144}... | collective-permute-start | bytes 589832 | tf_op jit(solution)/shard_map/ppermute | solution.py:383
  122.3 5.1 %collective-permute-start.12 = (bf16[6,128,128]{2,1,0:T(8,128)(2,1)S(1)}, bf16[6,128,128]{2,1,0:T(8,128)(2,1)S(1)}, u32[]{:S(2)}, u32[]{:S(2)}) collective-permute-start(bf16[6,128,128]{2,1,0:T(8,128)(2,1)S(1)} %get-tuple-element.546), channel_id=1, source_target_pairs={{0,448},{16,464},{32,96},{48,112},{64,0},{80,16},{96,160},{112,176... | collective-permute-start | bytes 589832 | tf_op jit(solution)/shard_map/ppermute | solution.py:383
  127.4 1.3 iota_compare_fusion.2
  128.8 1.2 iota_compare_fusion
  130.0 10.6 %collective-permute-done.10.refs_0_ = bf16[6,128,128]{2,1,0:T(8,128)(2,1)S(1)} collective-permute-done((bf16[6,128,128]{2,1,0:T(8,128)(2,1)S(1)}, bf16[6,128,128]{2,1,0:T(8,128)(2,1)S(1)}, u32[]{:S(2)}, u32[]{:S(2)}) %collective-permute-start.10) | collective-permute-done | bytes 196640 | tf_op jit(solution)/shard_map/ppermute | solution.py:383
  140.6 2.9 %collective-permute-done.11.refs_1_ = bf16[6,128,128]{2,1,0:T(8,128)(2,1)S(1)} collective-permute-done((bf16[6,128,128]{2,1,0:T(8,128)(2,1)S(1)}, bf16[6,128,128]{2,1,0:T(8,128)(2,1)S(1)}, u32[]{:S(2)}, u32[]{:S(2)}) %collective-permute-start.11) | collective-permute-done | bytes 196640 | tf_op jit(solution)/shard_map/ppermute | solution.py:383
  143.4 2.0 %collective-permute-done.12.refs_2_ = bf16[6,128,128]{2,1,0:T(8,128)(2,1)S(1)} collective-permute-done((bf16[6,128,128]{2,1,0:T(8,128)(2,1)S(1)}, bf16[6,128,128]{2,1,0:T(8,128)(2,1)S(1)}, u32[]{:S(2)}, u32[]{:S(2)}) %collective-permute-start.12) | collective-permute-done | bytes 196640 | tf_op jit(solution)/shard_map/ppermute | solution.py:383
  145.4 1.8 %shard_map.130 = (f32[8,128,128]{2,1,0:T(8,128)}, bf16[8,128,128]{2,1,0:T(8,128)(2,1)}) custom-call(s32[18]{0:T(128)S(1)} %copy-done.15, s32[16]{0:T(128)S(1)} %copy-done.13, bf16[16,128,128]{2,1,0:T(8,128)(2,1)S(1)} %get-tuple-element.752.terms, bf16[6,128,128]{2,1,0:T(8,128)(2,1)S(1)} %collective-permute-done.10.refs_0_, ...), custom_call_target="tpu_custom_call" | custom-call | tf_op jit(solution)/shard_map/pallas_call | solution.py:99
  147.2 3.9 %collective-permute-start.13 = (bf16[8,128,128]{2,1,0:T(8,128)(2,1)}, bf16[8,128,128]{2,1,0:T(8,128)(2,1)S(1)}, u32[]{:S(2)}, u32[]{:S(2)}) collective-permute-start(bf16[8,128,128]{2,1,0:T(8,128)(2,1)} %get-tuple-element.549), channel_id=1, source_target_pairs={{0,16},{16,0},{32,48},{48,32},{64,80},{80,64},{96,112},{112,96},{1... | collective-permute-start | bytes 786440 | tf_op jit(solution)/shard_map/ppermute | solution.py:397
  151.8 1.3 select_select_fusion
  153.1 4.4 %collective-permute-done.13 = bf16[8,128,128]{2,1,0:T(8,128)(2,1)S(1)} collective-permute-done((bf16[8,128,128]{2,1,0:T(8,128)(2,1)}, bf16[8,128,128]{2,1,0:T(8,128)(2,1)S(1)}, u32[]{:S(2)}, u32[]{:S(2)}) %collective-permute-start.13) | collective-permute-done | bytes 262176 | tf_op jit(solution)/shard_map/ppermute | solution.py:397
  (56 shorter events, 7.9 us)
Async XLA Ops:
  0.6 2.1 %copy-start = (bf16[32,16384]{1,0:T(8,128)(2,1)S(1)}, bf16[32,16384]{1,0:T(8,128)(2,1)}, u32[]{:S(2)}) copy-start(bf16[32,16384]{1,0:T(8,128)(2,1)} %param.15) | copy-start | bytes 3145732
  4.3 54.0 %all-to-all-start = ((bf16[16,128,128]{2,1,0:T(8,128)(2,1)}), bf16[16,128,128]{2,1,0:T(8,128)(2,1)S(1)}, u32[]{:S(2)}, u32[]{:S(2)}) async-start(bf16[16,128,128]{2,1,0:T(8,128)(2,1)} %pad_maximum_fusion), calls=%async_computation | async-start | bytes 1048576 | tf_op jit(solution)/shard_map/all_to_all | solution.py:402
  19.9 8.8 %collective-permute-start.6 = (bf16[8,128,128]{2,1,0:T(8,128)(2,1)S(1)}, bf16[8,128,128]{2,1,0:T(8,128)(2,1)}, u32[]{:S(2)}, u32[]{:S(2)}) collective-permute-start(bf16[8,128,128]{2,1,0:T(8,128)(2,1)S(1)} %reshape.104.own), channel_id=1, source_target_pairs={{0,16},{16,0},{32,48},{48,32},{64,80},{80,64},{96,112},{112,96},{1... | collective-permute-start | bytes 786440 | tf_op jit(solution)/shard_map/ppermute | solution.py:397
  23.1 0.7 copy-start.20
  28.8 0.6 copy-start.14
  30.5 20.9 %collective-permute-start.7 = (bf16[6,128,128]{2,1,0:T(8,128)(2,1)S(1)}, bf16[6,128,128]{2,1,0:T(8,128)(2,1)S(1)}, u32[]{:S(2)}, u32[]{:S(2)}) collective-permute-start(bf16[6,128,128]{2,1,0:T(8,128)(2,1)S(1)} %get-tuple-element.536), channel_id=1, source_target_pairs={{0,32},{16,48},{32,64},{48,80},{64,96},{80,112},{96,128},{112,144}... | collective-permute-start | bytes 589832 | tf_op jit(solution)/shard_map/ppermute | solution.py:383
  33.2 20.0 %collective-permute-start.8 = (bf16[6,128,128]{2,1,0:T(8,128)(2,1)S(1)}, bf16[6,128,128]{2,1,0:T(8,128)(2,1)S(1)}, u32[]{:S(2)}, u32[]{:S(2)}) collective-permute-start(bf16[6,128,128]{2,1,0:T(8,128)(2,1)S(1)} %get-tuple-element.538), channel_id=1, source_target_pairs={{0,480},{16,496},{32,0},{48,16},{64,32},{80,48},{96,64},{112,80},{... | collective-permute-start | bytes 589832 | tf_op jit(solution)/shard_map/ppermute | solution.py:383
  38.1 18.1 %collective-permute-start.9 = (bf16[6,128,128]{2,1,0:T(8,128)(2,1)S(1)}, bf16[6,128,128]{2,1,0:T(8,128)(2,1)S(1)}, u32[]{:S(2)}, u32[]{:S(2)}) collective-permute-start(bf16[6,128,128]{2,1,0:T(8,128)(2,1)S(1)} %get-tuple-element.539), channel_id=1, source_target_pairs={{0,64},{16,80},{32,480},{48,496},{64,128},{80,144},{96,32},{112,48... | collective-permute-start | bytes 589832 | tf_op jit(solution)/shard_map/ppermute | solution.py:383
  53.1 3.1 %copy-start.13 = (s32[16]{0:T(128)S(1)}, s32[16]{0:T(128)}, u32[]{:S(2)}) copy-start(s32[16]{0:T(128)} %shard_map.123.found) | copy-start | bytes 196
  58.3 0.9 copy-start.3
  58.3 1.0 copy-start.8
  58.3 0.9 copy-start.12
  59.2 23.1 %copy-start.1 = (f32[8,256,128]{2,1,0:T(8,128)S(1)}, f32[8,256,128]{2,1,0:T(8,128)}, u32[]{:S(2)}) copy-start(f32[8,256,128]{2,1,0:T(8,128)} %constant.224.clone.spectrum) | copy-start | bytes 3145732
  63.2 19.2 %copy-start.6 = (bf16[2,128,128]{2,1,0:T(8,128)(2,1)S(1)}, bf16[2,128,128]{2,1,0:T(8,128)(2,1)}, u32[]{:S(2)}) copy-start(bf16[2,128,128]{2,1,0:T(8,128)(2,1)} %constant.223.clone.x_bwd) | copy-start | bytes 196612
  63.2 19.2 %copy-start.7 = (bf16[2,128,128]{2,1,0:T(8,128)(2,1)S(1)}, bf16[2,128,128]{2,1,0:T(8,128)(2,1)}, u32[]{:S(2)}) copy-start(bf16[2,128,128]{2,1,0:T(8,128)(2,1)} %constant.222.clone.x_fwd) | copy-start | bytes 196612
  89.3 15.2 %copy-start.2 = (bf16[2,256,256]{2,1,0:T(8,128)(2,1)S(1)}, bf16[2,256,256]{2,1,0:T(8,128)(2,1)}, u32[]{:S(2)}) copy-start(bf16[2,256,256]{2,1,0:T(8,128)(2,1)} %constant.221.clone.y_bwd) | copy-start | bytes 786436
  89.3 15.1 %copy-start.5 = (bf16[2,128,128]{2,1,0:T(8,128)(2,1)S(1)}, bf16[2,128,128]{2,1,0:T(8,128)(2,1)}, u32[]{:S(2)}) copy-start(bf16[2,128,128]{2,1,0:T(8,128)(2,1)} %constant.219.clone.z_bwd) | copy-start | bytes 196612
  89.3 15.1 %copy-start.17 = (bf16[16,128,128]{2,1,0:T(8,128)(2,1)S(1)}, bf16[16,128,128]{2,1,0:T(8,128)(2,1)}, u32[]{:S(2)}) copy-start(bf16[16,128,128]{2,1,0:T(8,128)(2,1)} %get-tuple-element.541.sources) | copy-start | bytes 1572868
  108.2 42.9 %all-to-all-start.3 = ((bf16[16,128,128]{2,1,0:T(8,128)(2,1)}), bf16[16,128,128]{2,1,0:T(8,128)(2,1)S(1)}, u32[]{:S(2)}, u32[]{:S(2)}) async-start(bf16[16,128,128]{2,1,0:T(8,128)(2,1)} %get-tuple-element.550), calls=%async_computation.3 | async-start | bytes 1048576 | tf_op jit(solution)/shard_map/all_to_all | solution.py:402
  113.3 27.3 %collective-permute-start.10 = (bf16[6,128,128]{2,1,0:T(8,128)(2,1)S(1)}, bf16[6,128,128]{2,1,0:T(8,128)(2,1)S(1)}, u32[]{:S(2)}, u32[]{:S(2)}) collective-permute-start(bf16[6,128,128]{2,1,0:T(8,128)(2,1)S(1)} %get-tuple-element.544), channel_id=1, source_target_pairs={{0,480},{16,496},{32,0},{48,16},{64,32},{80,48},{96,64},{112,80},{... | collective-permute-start | bytes 589832 | tf_op jit(solution)/shard_map/ppermute | solution.py:383
  120.4 23.1 %collective-permute-start.11 = (bf16[6,128,128]{2,1,0:T(8,128)(2,1)S(1)}, bf16[6,128,128]{2,1,0:T(8,128)(2,1)S(1)}, u32[]{:S(2)}, u32[]{:S(2)}) collective-permute-start(bf16[6,128,128]{2,1,0:T(8,128)(2,1)S(1)} %get-tuple-element.545), channel_id=1, source_target_pairs={{0,32},{16,48},{32,64},{48,80},{64,96},{80,112},{96,128},{112,144}... | collective-permute-start | bytes 589832 | tf_op jit(solution)/shard_map/ppermute | solution.py:383
  122.3 23.1 %collective-permute-start.12 = (bf16[6,128,128]{2,1,0:T(8,128)(2,1)S(1)}, bf16[6,128,128]{2,1,0:T(8,128)(2,1)S(1)}, u32[]{:S(2)}, u32[]{:S(2)}) collective-permute-start(bf16[6,128,128]{2,1,0:T(8,128)(2,1)S(1)} %get-tuple-element.546), channel_id=1, source_target_pairs={{0,448},{16,464},{32,96},{48,112},{64,0},{80,16},{96,160},{112,176... | collective-permute-start | bytes 589832 | tf_op jit(solution)/shard_map/ppermute | solution.py:383
  128.8 16.6 %copy-start.15 = (s32[18]{0:T(128)S(1)}, s32[18]{0:T(128)}, u32[]{:S(2)}) copy-start(s32[18]{0:T(128)} %shard_map.122.sent) | copy-start | bytes 220
  147.2 3.9 %copy-start.16 = (s32[2,2]{1,0:T(2,128)S(1)}, s32[2,2]{1,0:T(2,128)}, u32[]{:S(2)}) copy-start(s32[2,2]{1,0:T(2,128)} %pair_tgt.1) | copy-start | bytes 52
  147.2 10.3 %collective-permute-start.13 = (bf16[8,128,128]{2,1,0:T(8,128)(2,1)}, bf16[8,128,128]{2,1,0:T(8,128)(2,1)S(1)}, u32[]{:S(2)}, u32[]{:S(2)}) collective-permute-start(bf16[8,128,128]{2,1,0:T(8,128)(2,1)} %get-tuple-element.549), channel_id=1, source_target_pairs={{0,16},{16,0},{32,48},{48,32},{64,80},{80,64},{96,112},{112,96},{1... | collective-permute-start | bytes 786440 | tf_op jit(solution)/shard_map/ppermute | solution.py:397
  151.8 5.7 %copy-start.19 = (f32[8,128,128]{2,1,0:T(8,128)S(1)}, f32[8,128,128]{2,1,0:T(8,128)}, u32[]{:S(2)}) copy-start(f32[8,128,128]{2,1,0:T(8,128)} %get-tuple-element.552) | copy-start | bytes 1572868

commit v15 on v13

--- a/solution.py
+++ b/solution.py
@@ -472,8 +472,8 @@
         scratch=[pltpu.SMEM((16,), jnp.int32)],
     )
 
-    def give_back(found):
-        return hand_over(vmem_call(pack_terms_kernel, packets, (found, terms), scalars=1), -1)
+    def pack_terms_in(found):
+        return vmem_call(pack_terms_kernel, packets, (found, terms), scalars=1)
 
     def collect(sent, found, near, before):
         outs = [struct((8, ROW, ROW), F32), struct((8, ROW, ROW), BF16)]
@@ -483,9 +483,10 @@
 
     def collect_in(turn, before):
         found = found_in(turn)
-        return collect(sent_in(turn), found, give_back(found), tuple(before))
-
-    near = give_back(found)
+        return collect(sent_in(turn), found, hand_over(pack_terms_in(found), -1), tuple(before))
+
+    packed, shares = lax.optimization_barrier((pack_terms_in(found), shares))
+    near = hand_over(packed, -1)
     shares = along_ring(shares)
     mine, partner = lax.fori_loop(1, rounds, collect_in, collect(sent, found, near, ()))
     (target_rows,) = vmem_call(

time: 160 us -> 160 us (level)
  the two profiles are of different devices: /device:TPU:32 before, /device:TPU:1 now
where the time goes in v15:
time: 160 us; the launch traced here: 157 us
  starting transfers between devices  51.2 us (32%)
  waiting for transfers between devices  36.6 us (23%)
  blocking collectives  34.3 us (21%)
  Pallas kernels  21.4 us (13%)
  other arithmetic  6.29 us (4%)
  local copies, waits for them, and re-layouts  6.04 us (4%)
  between operations  1.66 us (1%)
    ppermute x6, waiting for transfers between devices, hand_over(): lax.ppermute(packet, 'band', [(2 * z + x, 2 * ((z + sign * move(z)) % RIN...  30.3 us
    ppermute x6, starting transfers between devices, hand_over(): lax.ppermute(packet, 'band', [(2 * z + x, 2 * ((z + sign * move(z)) % RIN...  24.4 us
    all_to_all x2, starting transfers between devices, along_ring(): lax.all_to_all(value, 'band', 0, 0, axis_index_groups=groups, tiled=True)  20.3 us
    all_to_all x1, blocking collectives, per_device(): slabs = lax.all_to_all(spectra, 'dom', 0, 0, tiled=True)  19.2 us
    pallas_call x8, Pallas kernels, vmem_call(): pl.pallas_call(kernel, out_shape=outs, in_specs=[smem] * scalars + [whole...  18.5 us
    all_to_all x1, blocking collectives, per_device(): back = lax.all_to_all(solved, 'dom', 0, 0, tiled=True)  15.1 us
    ppermute x2, starting transfers between devices, across(): return lax.ppermute(value, 'band', [(i, i ^ 1) for i in range(32)])  6.5 us
    ppermute x2, waiting for transfers between devices, across(): return lax.ppermute(value, 'band', [(i, i ^ 1) for i in range(32)])  6.29 us
  transfers between devices with their start and end apart: 10, of which 6 were waited for; matrix products, arithmetic and copies ran while one was open for 4% of the time, Pallas kernels for 5%

profile of v15, /device:TPU:1, one launch (start us, length us, event | category | flops | bytes accessed | tf_op | source)
XLA Modules:
  0.0 157.5 jit_solution(8839892144215911197)
XLA Ops:
  0.6 0.8 reshape.105
  1.5 1.2 reshape.104.own
  4.3 15.6 %all-to-all-start = ((bf16[16,128,128]{2,1,0:T(8,128)(2,1)}), bf16[16,128,128]{2,1,0:T(8,128)(2,1)S(1)}, u32[]{:S(2)}, u32[]{:S(2)}) async-start(bf16[16,128,128]{2,1,0:T(8,128)(2,1)} %pad_maximum_fusion), calls=%async_computation | async-start | bytes 1048576 | tf_op jit(solution)/shard_map/all_to_all | solution.py:402
  19.9 3.1 %collective-permute-start.6 = (bf16[8,128,128]{2,1,0:T(8,128)(2,1)S(1)}, bf16[8,128,128]{2,1,0:T(8,128)(2,1)}, u32[]{:S(2)}, u32[]{:S(2)}) collective-permute-start(bf16[8,128,128]{2,1,0:T(8,128)(2,1)S(1)} %reshape.104.own), channel_id=1, source_target_pairs={{0,16},{16,0},{32,48},{48,32},{64,80},{80,64},{96,112},{112,96},{1... | collective-permute-start | bytes 786440 | tf_op jit(solution)/shard_map/ppermute | solution.py:397
  23.8 1.4 shard_map.123.found
  25.2 1.5 shard_map.122.sent
  26.7 2.1 %collective-permute-done.6.other = bf16[8,128,128]{2,1,0:T(8,128)(2,1)} collective-permute-done((bf16[8,128,128]{2,1,0:T(8,128)(2,1)S(1)}, bf16[8,128,128]{2,1,0:T(8,128)(2,1)}, u32[]{:S(2)}, u32[]{:S(2)}) %collective-permute-start.6) | collective-permute-done | bytes 262176 | tf_op jit(solution)/shard_map/ppermute | solution.py:397
  29.4 1.1 shard_map.124
  30.5 2.7 %collective-permute-start.7 = (bf16[6,128,128]{2,1,0:T(8,128)(2,1)S(1)}, bf16[6,128,128]{2,1,0:T(8,128)(2,1)S(1)}, u32[]{:S(2)}, u32[]{:S(2)}) collective-permute-start(bf16[6,128,128]{2,1,0:T(8,128)(2,1)S(1)} %get-tuple-element.540), channel_id=1, source_target_pairs={{0,32},{16,48},{32,64},{48,80},{64,96},{80,112},{96,128},{112,144}... | collective-permute-start | bytes 589832 | tf_op jit(solution)/shard_map/ppermute | solution.py:383
  33.2 4.9 %collective-permute-start.8 = (bf16[6,128,128]{2,1,0:T(8,128)(2,1)S(1)}, bf16[6,128,128]{2,1,0:T(8,128)(2,1)S(1)}, u32[]{:S(2)}, u32[]{:S(2)}) collective-permute-start(bf16[6,128,128]{2,1,0:T(8,128)(2,1)S(1)} %get-tuple-element.542), channel_id=1, source_target_pairs={{0,480},{16,496},{32,0},{48,16},{64,32},{80,48},{96,64},{112,80},{... | collective-permute-start | bytes 589832 | tf_op jit(solution)/shard_map/ppermute | solution.py:383
  38.1 1.9 %collective-permute-start.9 = (bf16[6,128,128]{2,1,0:T(8,128)(2,1)S(1)}, bf16[6,128,128]{2,1,0:T(8,128)(2,1)S(1)}, u32[]{:S(2)}, u32[]{:S(2)}) collective-permute-start(bf16[6,128,128]{2,1,0:T(8,128)(2,1)S(1)} %get-tuple-element.543), channel_id=1, source_target_pairs={{0,64},{16,80},{32,480},{48,496},{64,128},{80,144},{96,32},{112,48... | collective-permute-start | bytes 589832 | tf_op jit(solution)/shard_map/ppermute | solution.py:383
  40.1 11.4 %collective-permute-done.7.refs_0_ = bf16[6,128,128]{2,1,0:T(8,128)(2,1)S(1)} collective-permute-done((bf16[6,128,128]{2,1,0:T(8,128)(2,1)S(1)}, bf16[6,128,128]{2,1,0:T(8,128)(2,1)S(1)}, u32[]{:S(2)}, u32[]{:S(2)}) %collective-permute-start.7) | collective-permute-done | bytes 196640 | tf_op jit(solution)/shard_map/ppermute | solution.py:383
  53.2 3.1 %collective-permute-done.9.refs_2_ = bf16[6,128,128]{2,1,0:T(8,128)(2,1)S(1)} collective-permute-done((bf16[6,128,128]{2,1,0:T(8,128)(2,1)S(1)}, bf16[6,128,128]{2,1,0:T(8,128)(2,1)S(1)}, u32[]{:S(2)}, u32[]{:S(2)}) %collective-permute-start.9) | collective-permute-done | bytes 196640 | tf_op jit(solution)/shard_map/ppermute | solution.py:383
  56.2 2.0 %shard_map.125 = bf16[16,128,128]{2,1,0:T(8,128)(2,1)} custom-call(s32[16]{0:T(128)S(1)} %copy-done.13, bf16[8,128,128]{2,1,0:T(8,128)(2,1)S(1)} %reshape.104.own, bf16[8,128,128]{2,1,0:T(8,128)(2,1)} %collective-permute-done.6.other, bf16[6,128,128]{2,1,0:T(8,128)(2,1)S(1)} %collective-permute-done.7.refs_0_, ...), custom_call_target="tpu_custom_call" | custom-call | tf_op jit(solution)/shard_map/pallas_call | solution.py:99
  58.3 0.9 copy-done.3
  59.2 3.3 %shard_map.126 = bf16[16,128,128]{2,1,0:T(8,128)(2,1)S(1)} custom-call(s32[3]{0:T(128)S(1)} %copy-done.12, s32[2,64]{1,0:T(2,128)S(1)} %get-tuple-element.808, bf16[16,128,128]{2,1,0:T(8,128)(2,1)} %get-tuple-element.545.sources, bf16[16,128,128]{2,1,0:T(8,128)(2,1)S(1)} %all-to-all-done.wanted, bf16[2,128,128]{2,1,0:T(8,128)(2,1)S(1)} %copy-done.8, ...), custom_call_target="tpu_custom_call" | custom-call | tf_op jit(solution)/shard_map/pallas_call | solution.py:99
  62.6 19.2 %all_to_all.20.slabs = bf16[16,128,128]{2,1,0:T(8,128)(2,1)S(1)} all-to-all(bf16[16,128,128]{2,1,0:T(8,128)(2,1)S(1)} %shard_map.126), channel_id=1, replica_groups=mesh['band'=32,'dom'=16] {'dom'}, dimensions={0} | all-to-all | bytes 1048576 | tf_op jit(solution)/shard_map/all_to_all | solution.py:459
  81.7 5.7 %shard_map.127 = bf16[16,128,128]{2,1,0:T(8,128)(2,1)S(1)} custom-call(bf16[16,128,128]{2,1,0:T(8,128)(2,1)S(1)} %all_to_all.20.slabs, f32[8,256,128]{2,1,0:T(8,128)S(1)} %copy-done.1, bf16[2,128,128]{2,1,0:T(8,128)(2,1)S(1)} %copy-done.7, bf16[2,128,128]{2,1,0:T(8,128)(2,1)S(1)} %copy-done.6), custom_call_target="tpu_custom_call" | custom-call | tf_op jit(solution)/shard_map/pallas_call | solution.py:99
  87.5 15.1 %all_to_all.21.spectra = bf16[16,128,128]{2,1,0:T(8,128)(2,1)S(1)} all-to-all(bf16[16,128,128]{2,1,0:T(8,128)(2,1)S(1)} %shard_map.127), channel_id=1, replica_groups=mesh['band'=32,'dom'=16] {'dom'}, dimensions={0} | all-to-all | bytes 1048576 | tf_op jit(solution)/shard_map/all_to_all | solution.py:466
  102.6 3.2 %shard_map.128 = (bf16[16,128,128]{2,1,0:T(8,128)(2,1)S(1)}, bf16[16,128,128]{2,1,0:T(8,128)(2,1)}) custom-call(s32[3]{0:T(128)S(1)} %copy-done.12, s32[2,64]{1,0:T(2,128)S(1)} %get-tuple-element.808, bf16[16,128,128]{2,1,0:T(8,128)(2,1)S(1)} %all_to_all.21.spectra, bf16[16,128,128]{2,1,0:T(8,128)(2,1)S(1)} %copy-done.17, ...), custom_call_target="tpu_custom_call" | custom-call | tf_op jit(solution)/shard_map/pallas_call | solution.py:99
  106.5 4.7 %all-to-all-start.3 = ((bf16[16,128,128]{2,1,0:T(8,128)(2,1)}), bf16[16,128,128]{2,1,0:T(8,128)(2,1)S(1)}, u32[]{:S(2)}, u32[]{:S(2)}) async-start(bf16[16,128,128]{2,1,0:T(8,128)(2,1)} %get-tuple-element.558), calls=%async_computation.3 | async-start | bytes 1048576 | tf_op jit(solution)/shard_map/all_to_all | solution.py:402
  111.9 5.9 %collective-permute-start.10 = (bf16[6,128,128]{2,1,0:T(8,128)(2,1)S(1)}, bf16[6,128,128]{2,1,0:T(8,128)(2,1)S(1)}, u32[]{:S(2)}, u32[]{:S(2)}) collective-permute-start(bf16[6,128,128]{2,1,0:T(8,128)(2,1)S(1)} %get-tuple-element.552), channel_id=1, source_target_pairs={{0,480},{16,496},{32,0},{48,16},{64,32},{80,48},{96,64},{112,80},{... | collective-permute-start | bytes 589832 | tf_op jit(solution)/shard_map/ppermute | solution.py:383
  117.8 1.9 %collective-permute-start.11 = (bf16[6,128,128]{2,1,0:T(8,128)(2,1)S(1)}, bf16[6,128,128]{2,1,0:T(8,128)(2,1)S(1)}, u32[]{:S(2)}, u32[]{:S(2)}) collective-permute-start(bf16[6,128,128]{2,1,0:T(8,128)(2,1)S(1)} %get-tuple-element.553), channel_id=1, source_target_pairs={{0,32},{16,48},{32,64},{48,80},{64,96},{80,112},{96,128},{112,144}... | collective-permute-start | bytes 589832 | tf_op jit(solution)/shard_map/ppermute | solution.py:383
  119.7 7.1 %collective-permute-start.12 = (bf16[6,128,128]{2,1,0:T(8,128)(2,1)S(1)}, bf16[6,128,128]{2,1,0:T(8,128)(2,1)S(1)}, u32[]{:S(2)}, u32[]{:S(2)}) collective-permute-start(bf16[6,128,128]{2,1,0:T(8,128)(2,1)S(1)} %get-tuple-element.554), channel_id=1, source_target_pairs={{0,448},{16,464},{32,96},{48,112},{64,0},{80,16},{96,160},{112,176... | collective-permute-start | bytes 589832 | tf_op jit(solution)/shard_map/ppermute | solution.py:383
  126.8 1.3 iota_compare_fusion.2
  128.1 1.2 iota_compare_fusion
  129.3 13.2 %collective-permute-done.10.refs_0_ = bf16[6,128,128]{2,1,0:T(8,128)(2,1)S(1)} collective-permute-done((bf16[6,128,128]{2,1,0:T(8,128)(2,1)S(1)}, bf16[6,128,128]{2,1,0:T(8,128)(2,1)S(1)}, u32[]{:S(2)}, u32[]{:S(2)}) %collective-permute-start.10) | collective-permute-done | bytes 196640 | tf_op jit(solution)/shard_map/ppermute | solution.py:383
  142.6 2.7 %collective-permute-done.12.refs_2_ = bf16[6,128,128]{2,1,0:T(8,128)(2,1)S(1)} collective-permute-done((bf16[6,128,128]{2,1,0:T(8,128)(2,1)S(1)}, bf16[6,128,128]{2,1,0:T(8,128)(2,1)S(1)}, u32[]{:S(2)}, u32[]{:S(2)}) %collective-permute-start.12) | collective-permute-done | bytes 196640 | tf_op jit(solution)/shard_map/ppermute | solution.py:383
  145.2 1.8 %shard_map.130 = (f32[8,128,128]{2,1,0:T(8,128)}, bf16[8,128,128]{2,1,0:T(8,128)(2,1)}) custom-call(s32[18]{0:T(128)S(1)} %copy-done.15, s32[16]{0:T(128)S(1)} %copy-done.13, bf16[16,128,128]{2,1,0:T(8,128)(2,1)S(1)} %get-tuple-element.760.terms, bf16[6,128,128]{2,1,0:T(8,128)(2,1)S(1)} %collective-permute-done.10.refs_0_, ...), custom_call_target="tpu_custom_call" | custom-call | tf_op jit(solution)/shard_map/pallas_call | solution.py:99
  147.0 3.4 %collective-permute-start.13 = (bf16[8,128,128]{2,1,0:T(8,128)(2,1)}, bf16[8,128,128]{2,1,0:T(8,128)(2,1)S(1)}, u32[]{:S(2)}, u32[]{:S(2)}) collective-permute-start(bf16[8,128,128]{2,1,0:T(8,128)(2,1)} %get-tuple-element.557), channel_id=1, source_target_pairs={{0,16},{16,0},{32,48},{48,32},{64,80},{80,64},{96,112},{112,96},{1... | collective-permute-start | bytes 786440 | tf_op jit(solution)/shard_map/ppermute | solution.py:397
  151.1 1.3 select_select_fusion
  152.4 4.2 %collective-permute-done.13 = bf16[8,128,128]{2,1,0:T(8,128)(2,1)S(1)} collective-permute-done((bf16[8,128,128]{2,1,0:T(8,128)(2,1)}, bf16[8,128,128]{2,1,0:T(8,128)(2,1)S(1)}, u32[]{:S(2)}, u32[]{:S(2)}) %collective-permute-start.13) | collective-permute-done | bytes 262176 | tf_op jit(solution)/shard_map/ppermute | solution.py:397
  (56 shorter events, 6.9 us)
Async XLA Ops:
  0.6 2.1 %copy-start = (bf16[32,16384]{1,0:T(8,128)(2,1)S(1)}, bf16[32,16384]{1,0:T(8,128)(2,1)}, u32[]{:S(2)}) copy-start(bf16[32,16384]{1,0:T(8,128)(2,1)} %param.15) | copy-start | bytes 3145732
  4.3 54.0 %all-to-all-start = ((bf16[16,128,128]{2,1,0:T(8,128)(2,1)}), bf16[16,128,128]{2,1,0:T(8,128)(2,1)S(1)}, u32[]{:S(2)}, u32[]{:S(2)}) async-start(bf16[16,128,128]{2,1,0:T(8,128)(2,1)} %pad_maximum_fusion), calls=%async_computation | async-start | bytes 1048576 | tf_op jit(solution)/shard_map/all_to_all | solution.py:402
  19.9 8.8 %collective-permute-start.6 = (bf16[8,128,128]{2,1,0:T(8,128)(2,1)S(1)}, bf16[8,128,128]{2,1,0:T(8,128)(2,1)}, u32[]{:S(2)}, u32[]{:S(2)}) collective-permute-start(bf16[8,128,128]{2,1,0:T(8,128)(2,1)S(1)} %reshape.104.own), channel_id=1, source_target_pairs={{0,16},{16,0},{32,48},{48,32},{64,80},{80,64},{96,112},{112,96},{1... | collective-permute-start | bytes 786440 | tf_op jit(solution)/shard_map/ppermute | solution.py:397
  23.1 0.7 copy-start.20
  28.8 0.6 copy-start.14
  30.5 20.9 %collective-permute-start.7 = (bf16[6,128,128]{2,1,0:T(8,128)(2,1)S(1)}, bf16[6,128,128]{2,1,0:T(8,128)(2,1)S(1)}, u32[]{:S(2)}, u32[]{:S(2)}) collective-permute-start(bf16[6,128,128]{2,1,0:T(8,128)(2,1)S(1)} %get-tuple-element.540), channel_id=1, source_target_pairs={{0,32},{16,48},{32,64},{48,80},{64,96},{80,112},{96,128},{112,144}... | collective-permute-start | bytes 589832 | tf_op jit(solution)/shard_map/ppermute | solution.py:383
  33.2 20.0 %collective-permute-start.8 = (bf16[6,128,128]{2,1,0:T(8,128)(2,1)S(1)}, bf16[6,128,128]{2,1,0:T(8,128)(2,1)S(1)}, u32[]{:S(2)}, u32[]{:S(2)}) collective-permute-start(bf16[6,128,128]{2,1,0:T(8,128)(2,1)S(1)} %get-tuple-element.542), channel_id=1, source_target_pairs={{0,480},{16,496},{32,0},{48,16},{64,32},{80,48},{96,64},{112,80},{... | collective-permute-start | bytes 589832 | tf_op jit(solution)/shard_map/ppermute | solution.py:383
  38.1 18.1 %collective-permute-start.9 = (bf16[6,128,128]{2,1,0:T(8,128)(2,1)S(1)}, bf16[6,128,128]{2,1,0:T(8,128)(2,1)S(1)}, u32[]{:S(2)}, u32[]{:S(2)}) collective-permute-start(bf16[6,128,128]{2,1,0:T(8,128)(2,1)S(1)} %get-tuple-element.543), channel_id=1, source_target_pairs={{0,64},{16,80},{32,480},{48,496},{64,128},{80,144},{96,32},{112,48... | collective-permute-start | bytes 589832 | tf_op jit(solution)/shard_map/ppermute | solution.py:383
  53.1 3.1 %copy-start.13 = (s32[16]{0:T(128)S(1)}, s32[16]{0:T(128)}, u32[]{:S(2)}) copy-start(s32[16]{0:T(128)} %shard_map.123.found) | copy-start | bytes 196
  58.3 0.9 copy-start.3
  58.3 1.0 copy-start.8
  58.3 0.9 copy-start.12
  59.2 22.5 %copy-start.1 = (f32[8,256,128]{2,1,0:T(8,128)S(1)}, f32[8,256,128]{2,1,0:T(8,128)}, u32[]{:S(2)}) copy-start(f32[8,256,128]{2,1,0:T(8,128)} %constant.224.clone.spectrum) | copy-start | bytes 3145732
  62.5 19.2 %copy-start.6 = (bf16[2,128,128]{2,1,0:T(8,128)(2,1)S(1)}, bf16[2,128,128]{2,1,0:T(8,128)(2,1)}, u32[]{:S(2)}) copy-start(bf16[2,128,128]{2,1,0:T(8,128)(2,1)} %constant.223.clone.x_bwd) | copy-start | bytes 196612
  62.5 19.2 %copy-start.7 = (bf16[2,128,128]{2,1,0:T(8,128)(2,1)S(1)}, bf16[2,128,128]{2,1,0:T(8,128)(2,1)}, u32[]{:S(2)}) copy-start(bf16[2,128,128]{2,1,0:T(8,128)(2,1)} %constant.222.clone.x_fwd) | copy-start | bytes 196612
  87.4 15.2 %copy-start.2 = (bf16[2,256,256]{2,1,0:T(8,128)(2,1)S(1)}, bf16[2,256,256]{2,1,0:T(8,128)(2,1)}, u32[]{:S(2)}) copy-start(bf16[2,256,256]{2,1,0:T(8,128)(2,1)} %constant.221.clone.y_bwd) | copy-start | bytes 786436
  87.4 15.1 %copy-start.5 = (bf16[2,128,128]{2,1,0:T(8,128)(2,1)S(1)}, bf16[2,128,128]{2,1,0:T(8,128)(2,1)}, u32[]{:S(2)}) copy-start(bf16[2,128,128]{2,1,0:T(8,128)(2,1)} %constant.219.clone.z_bwd) | copy-start | bytes 196612
  87.4 15.1 %copy-start.17 = (bf16[16,128,128]{2,1,0:T(8,128)(2,1)S(1)}, bf16[16,128,128]{2,1,0:T(8,128)(2,1)}, u32[]{:S(2)}) copy-start(bf16[16,128,128]{2,1,0:T(8,128)(2,1)} %get-tuple-element.545.sources) | copy-start | bytes 1572868
  106.5 43.9 %all-to-all-start.3 = ((bf16[16,128,128]{2,1,0:T(8,128)(2,1)}), bf16[16,128,128]{2,1,0:T(8,128)(2,1)S(1)}, u32[]{:S(2)}, u32[]{:S(2)}) async-start(bf16[16,128,128]{2,1,0:T(8,128)(2,1)} %get-tuple-element.558), calls=%async_computation.3 | async-start | bytes 1048576 | tf_op jit(solution)/shard_map/all_to_all | solution.py:402
  111.9 30.7 %collective-permute-start.10 = (bf16[6,128,128]{2,1,0:T(8,128)(2,1)S(1)}, bf16[6,128,128]{2,1,0:T(8,128)(2,1)S(1)}, u32[]{:S(2)}, u32[]{:S(2)}) collective-permute-start(bf16[6,128,128]{2,1,0:T(8,128)(2,1)S(1)} %get-tuple-element.552), channel_id=1, source_target_pairs={{0,480},{16,496},{32,0},{48,16},{64,32},{80,48},{96,64},{112,80},{... | collective-permute-start | bytes 589832 | tf_op jit(solution)/shard_map/ppermute | solution.py:383
  117.8 24.8 %collective-permute-start.11 = (bf16[6,128,128]{2,1,0:T(8,128)(2,1)S(1)}, bf16[6,128,128]{2,1,0:T(8,128)(2,1)S(1)}, u32[]{:S(2)}, u32[]{:S(2)}) collective-permute-start(bf16[6,128,128]{2,1,0:T(8,128)(2,1)S(1)} %get-tuple-element.553), channel_id=1, source_target_pairs={{0,32},{16,48},{32,64},{48,80},{64,96},{80,112},{96,128},{112,144}... | collective-permute-start | bytes 589832 | tf_op jit(solution)/shard_map/ppermute | solution.py:383
  119.7 25.5 %collective-permute-start.12 = (bf16[6,128,128]{2,1,0:T(8,128)(2,1)S(1)}, bf16[6,128,128]{2,1,0:T(8,128)(2,1)S(1)}, u32[]{:S(2)}, u32[]{:S(2)}) collective-permute-start(bf16[6,128,128]{2,1,0:T(8,128)(2,1)S(1)} %get-tuple-element.554), channel_id=1, source_target_pairs={{0,448},{16,464},{32,96},{48,112},{64,0},{80,16},{96,160},{112,176... | collective-permute-start | bytes 589832 | tf_op jit(solution)/shard_map/ppermute | solution.py:383
  128.1 17.1 %copy-start.15 = (s32[18]{0:T(128)S(1)}, s32[18]{0:T(128)}, u32[]{:S(2)}) copy-start(s32[18]{0:T(128)} %shard_map.122.sent) | copy-start | bytes 220
  147.0 3.4 %copy-start.16 = (s32[2,2]{1,0:T(2,128)S(1)}, s32[2,2]{1,0:T(2,128)}, u32[]{:S(2)}) copy-start(s32[2,2]{1,0:T(2,128)} %pair_tgt.1) | copy-start | bytes 52
  147.0 9.6 %collective-permute-start.13 = (bf16[8,128,128]{2,1,0:T(8,128)(2,1)}, bf16[8,128,128]{2,1,0:T(8,128)(2,1)S(1)}, u32[]{:S(2)}, u32[]{:S(2)}) collective-permute-start(bf16[8,128,128]{2,1,0:T(8,128)(2,1)} %get-tuple-element.557), channel_id=1, source_target_pairs={{0,16},{16,0},{32,48},{48,32},{64,80},{80,64},{96,112},{112,96},{1... | collective-permute-start | bytes 786440 | tf_op jit(solution)/shard_map/ppermute | solution.py:397
  151.1 5.5 %copy-start.19 = (f32[8,128,128]{2,1,0:T(8,128)S(1)}, f32[8,128,128]{2,1,0:T(8,128)}, u32[]{:S(2)}) copy-start(f32[8,128,128]{2,1,0:T(8,128)} %get-tuple-element.560) | copy-start | bytes 1572868
